TPU v7x, 32 devices: a whole 2x2x4 slice. The times are simulated.
32 devices in a mesh: groups: 2 (over y), atoms: 4 (over z), pair: 2 (over x), samp: 2 (over core).
Axes of the slice: x: 2, y: 2, z: 4, core: 2. Of those that a mesh axis runs over, the one named last changes fastest.
Arguments:
- atom_single: bfloat16 [24, 2048, 128], P(('groups', 'pair', 'samp'), 'atoms'), parts along dimension 0, may hold values from -6 to 6
- atom_cond: bfloat16 [4096, 128], P(('groups', 'atoms')), parts along dimension 0, may hold values from -6 to 6
- pair_cond: bfloat16 [512, 256, 128], P(('groups', 'pair'), 'atoms'), parts along dimension 0, may hold values from -6 to 6
- atom_counts: int32 [8, 64], P('groups'), parts along dimension 0, may hold values from 1 to 24, 512 in all within a row
- ada_attn_scale: bfloat16 [128, 128], replicated, may hold values from -0.5 to 0.5
- ada_attn_shift: bfloat16 [128, 128], replicated, may hold values from -0.5 to 0.5
- w_query: bfloat16 [128, 128], replicated, may hold values from -4 to 4
- w_key: bfloat16 [128, 128], replicated, may hold values from -4 to 4
- w_value: bfloat16 [128, 128], replicated, may hold values from -0.5 to 0.5
- w_gate: bfloat16 [128, 128], replicated, may hold values from -0.5 to 0.5
- w_out: bfloat16 [128, 128], replicated, may hold values from -0.5 to 0.5
- attn_gate: bfloat16 [128, 128], replicated, may hold values from -0.5 to 0.5
- w_pair: bfloat16 [128, 4], replicated, may hold values from -0.5 to 0.5
- ada_trans_scale: bfloat16 [128, 128], replicated, may hold values from -0.5 to 0.5
- ada_trans_shift: bfloat16 [128, 128], replicated, may hold values from -0.5 to 0.5
- w_swish: bfloat16 [128, 256], replicated, may hold values from -0.5 to 0.5
- w_linear: bfloat16 [128, 256], replicated, may hold values from -0.5 to 0.5
- w_down: bfloat16 [256, 128], replicated, may hold values from -0.375 to 0.375
- trans_gate: bfloat16 [128, 128], replicated, may hold values from -0.5 to 0.5
Outputs:
- updated: bfloat16 [24, 2048, 128], P(('groups', 'pair', 'samp'), 'atoms'), parts along dimension 0
There are 2 independent parts, one for each index of `groups`. A program takes and returns all parts, laid end to end along the dimension named above; an argument that names none is the same for every part. Nothing has to cross between parts.
Inputs may be any that keep to these rules, and one draw needn't show every extreme that they name: Row j of atom_counts gives the atoms of tokens j * 64 to (j + 1) * 64 - 1; every row sums to 512 and holds at least one count equal to 24.
All inputs are finite; a program needn't handle non-finite values.
Results may differ from a plain program's by a relative error of at most 0.0094.
Values may be sent and summed in bfloat16 or wider, within the bound.
No kernel may reach another device: no remote copies, remote signals or barrier semaphores. Data moves between devices by JAX's collectives and lax.ppermute only.
A program may use at most 64 MiB of HBM per device.

v0:
```python
import math

import jax
import jax.numpy as jnp
from jax import lax
from jax.sharding import PartitionSpec as P

Q_WIN = 32
K_WIN = 128
EDGE = 48


EPSILON = 1e-05
MASKED = -1e30


def padded(cells, sides, width):
    for axis, dim in sides:
        count = lax.axis_size(axis)
        ends = count - 1
        head = lax.slice_in_dim(cells, 0, width, axis=dim)
        tail = lax.slice_in_dim(cells, cells.shape[dim] - width, cells.shape[dim], axis=dim)
        cells = jnp.concatenate(
            [
                lax.ppermute(tail, axis, [(i, (i + 1) % count) for i in range(ends)]),
                cells,
                lax.ppermute(head, axis, [((i + 1) % count, i) for i in range(ends)]),
            ],
            axis=dim,
        )
    return cells


def from_root(value, axis, root):
    mine = lax.axis_index(axis) == root
    return lax.psum(jnp.where(mine, value, jnp.zeros_like(value)), axis)


def layer_norm(values):
    values = values.astype(jnp.float32)
    centred = values - jnp.mean(values, axis=-1, keepdims=True)
    return centred * lax.rsqrt(jnp.mean(centred * centred, axis=-1, keepdims=True) + EPSILON)


def project(matrix_rows, weight):
    flattened = matrix_rows.reshape(-1, matrix_rows.shape[-1])
    mixed = jnp.dot(flattened, weight, preferred_element_type=jnp.float32)
    return mixed.reshape(matrix_rows.shape[:-1] + (weight.shape[1],))


def windowed(matrix_rows, axis_pos, windows):
    span_count = K_WIN // Q_WIN
    dims_in = matrix_rows.shape
    grouped = matrix_rows.reshape(
        dims_in[:axis_pos] + (windows + span_count - 1, Q_WIN) + dims_in[axis_pos + 1 :]
    )
    shifted_parts = [
        lax.slice_in_dim(grouped, offset, offset + windows, axis=axis_pos)
        for offset in range(span_count)
    ]
    return jnp.concatenate(shifted_parts, axis=axis_pos + 1)


def shards(
    atom_single,
    atom_cond,
    pair_cond,
    atom_counts,
    ada_attn_scale,
    ada_attn_shift,
    w_query,
    w_key,
    w_value,
    w_gate,
    w_out,
    attn_gate,
    w_pair,
    ada_trans_scale,
    ada_trans_shift,
    w_swish,
    w_linear,
    w_down,
    trans_gate,
):
    device_at = lax.axis_index("atoms")
    blocks = lax.axis_size("atoms")
    samples, atoms_here, width = atom_single.shape
    tok_here = atom_counts.shape[1]
    head_count = w_pair.shape[1]
    head_dim = width // head_count
    windows = atoms_here // Q_WIN
    cond_norm = layer_norm(atom_cond).astype(jnp.bfloat16)
    single_norm = layer_norm(atom_single)
    normed = (
        jax.nn.sigmoid(project(cond_norm, ada_attn_scale)) * single_norm
        + project(cond_norm, ada_attn_shift)
    ).astype(jnp.bfloat16)
    stacked = jnp.stack(
        [project(normed, w_key).astype(jnp.bfloat16), project(normed, w_value).astype(jnp.bfloat16)]
    )
    halo_pair = padded(stacked, (("atoms", 2),), EDGE)
    keys_ext = halo_pair[0]
    values_ext = halo_pair[1]
    normed_trans = (
        jax.nn.sigmoid(project(cond_norm, ada_trans_scale)) * single_norm
        + project(cond_norm, ada_trans_shift)
    ).astype(jnp.bfloat16)
    hidden = (jax.nn.silu(project(normed_trans, w_swish)) * project(normed_trans, w_linear)).astype(
        jnp.bfloat16
    )
    transition = jax.nn.sigmoid(project(cond_norm, trans_gate)) * project(hidden, w_down)
    pair_norm = layer_norm(pair_cond).astype(jnp.bfloat16)
    pair_tile = jnp.einsum(
        "rcp,ph->hrc", pair_norm, w_pair, preferred_element_type=jnp.float32
    ).astype(jnp.bfloat16)
    rows_pair = pair_tile.shape[1]
    widened = padded(pair_tile, (("atoms", 2),), tok_here)
    owner_row = device_at * tok_here // rows_pair
    row_start = device_at * tok_here - owner_row * rows_pair
    picked = lax.dynamic_slice_in_dim(widened, row_start, tok_here, 1)
    token_bias = from_root(picked, "pair", owner_row)
    span_len = atoms_here + 2 * EDGE
    position = device_at * atoms_here - EDGE + jnp.arange(span_len, dtype=jnp.int32)
    block_of = jnp.floor_divide(position, atoms_here)
    relative = jnp.clip(block_of - device_at + 1, 0, 2)
    row_pick = jnp.clip(device_at - 1 + jnp.arange(3, dtype=jnp.int32), 0, blocks - 1)
    counts_near = jnp.take(atom_counts, row_pick, axis=0)
    starts_near = jnp.cumsum(counts_near, axis=1) - counts_near
    offset_in = position - block_of * atoms_here
    starts_for = jnp.take(starts_near, relative, axis=0)
    within = jnp.sum((starts_for <= offset_in[:, None]).astype(jnp.int32), axis=1) - 1
    column = relative * tok_here + within
    is_valid = (position >= 0) & (position < blocks * atoms_here)
    row_hot = (
        within[EDGE : EDGE + atoms_here, None] == jnp.arange(tok_here, dtype=jnp.int32)[None, :]
    ).astype(jnp.bfloat16)
    col_hot = (
        (column[:, None] == jnp.arange(3 * tok_here, dtype=jnp.int32)[None, :]) & is_valid[:, None]
    ).astype(jnp.bfloat16)
    row_bias = jnp.einsum(
        "at,htc->hac", row_hot, token_bias, preferred_element_type=jnp.float32
    ).astype(jnp.bfloat16)
    row_bias = row_bias.reshape(head_count, windows, Q_WIN, 3 * tok_here)
    col_win = windowed(col_hot, 0, windows)
    atom_bias = jnp.einsum("hwqc,wkc->whqk", row_bias, col_win, preferred_element_type=jnp.float32)
    valid_win = windowed(is_valid, 0, windows)
    queries = (
        project(normed, w_query)
        .astype(jnp.bfloat16)
        .reshape(samples, windows, Q_WIN, head_count, head_dim)
    )
    key_win = windowed(keys_ext, 1, windows).reshape(samples, windows, K_WIN, head_count, head_dim)
    value_win = windowed(values_ext, 1, windows).reshape(
        samples, windows, K_WIN, head_count, head_dim
    )
    inv_root = 1.0 / math.sqrt(head_dim)
    scores = (
        jnp.einsum("swqhd,swkhd->swhqk", queries, key_win, preferred_element_type=jnp.float32)
        * inv_root
        + atom_bias[None]
    )
    scores = jnp.where(valid_win[None, :, None, None, :], scores, MASKED)
    row_max = jnp.max(scores, axis=-1, keepdims=True)
    raised = jnp.exp(scores - row_max)
    probs = (raised / jnp.sum(raised, axis=-1, keepdims=True)).astype(jnp.bfloat16)
    attended = jnp.einsum(
        "swhqk,swkhd->swqhd", probs, value_win, preferred_element_type=jnp.float32
    )
    attended = attended.reshape(samples, atoms_here, width)
    gated_out = (jax.nn.sigmoid(project(normed, w_gate)) * attended).astype(jnp.bfloat16)
    attention = jax.nn.sigmoid(project(cond_norm, attn_gate)) * project(gated_out, w_out)
    return (attention + transition).astype(jnp.bfloat16)


def solution(mesh):
    return jax.shard_map(
        shards,
        mesh=mesh,
        in_specs=(
            P(("groups", "pair", "samp"), "atoms", None),
            P(("groups", "atoms"), None),
            P(("groups", "pair"), "atoms", None),
            P("groups", None),
            P(),
            P(),
            P(),
            P(),
            P(),
            P(),
            P(),
            P(),
            P(),
            P(),
            P(),
            P(),
            P(),
            P(),
            P(),
        ),
        out_specs=P(("groups", "pair", "samp"), "atoms", None),
        check_vma=False,
    )
```

profile of v0, /device:TPU:0, one launch (start us, length us, event | category | flops | bytes accessed | tf_op | source)
XLA Modules:
  0.0 108.2 jit_solution(8134953778965902301)
XLA Ops:
  6.5 2.9 %convert_reduce_fusion = f32[128,64]{1,0:T(8,128)S(1)} fusion(bf16[128,64,128]{2,1,0:T(8,128)(2,1)} %param.21), kind=kLoop, calls=%fused_computation.4 | loop fusion | flops 2088960 | bytes 2129920 | tf_op jit(solution)/shard_map/reduce_sum | solution.py:41
  9.5 2.7 %fusion.3 = f32[128,64]{1,0:T(8,128)S(1)} fusion(bf16[128,64,128]{2,1,0:T(8,128)(2,1)S(1)} %copy-done.1, f32[128,64]{1,0:T(8,128)S(1)} %broadcast_multiply_fusion), kind=kLoop, calls=%fused_computation.7 | loop fusion | flops 4186112 | bytes 2162688 | tf_op jit(solution)/shard_map/reduce_sum | solution.py:42
  12.2 2.9 %fusion.6 = bf16[128,64,4]{1,2,0:T(4,128)(2,1)S(1)} fusion(bf16[128,64,128]{2,1,0:T(8,128)(2,1)S(1)} %copy-done.1, f32[128,64]{1,0:T(8,128)S(1)} %add_rsqrt_fusion, f32[128,64]{1,0:T(8,128)S(1)} %broadcast_multiply_fusion, bf16[128,4]{0,1:T(4,128)(2,1)S(1)} %copy-done.29), kind=kOutput, calls=%fused_computation.13 | convolution fusion | flops 12582912 | bytes 2229248 | tf_op jit(solution)/shard_map/rcp,ph->hrc/dot_general | solution.py:113
  15.3 5.6 %collective-permute-start.2 = (bf16[4,128,64]{1,0,2:T(4,128)(2,1)S(1)}, bf16[4,128,64]{1,0,2:T(4,128)(2,1)}, u32[]{:S(2)}, u32[]{:S(2)}) collective-permute-start(bf16[4,128,64]{1,0,2:T(4,128)(2,1)S(1)} %bitcast.84), channel_id=1, source_target_pairs={{0,4},{4,8},{8,12},{1,5},{5,9},{9,13},{2,6},{6,10},{10,14},{3,7},{... | collective-permute-start | bytes 196616 | tf_op jit(solution)/shard_map/ppermute | solution.py:25
  20.8 1.3 %collective-permute-start.3 = (bf16[4,128,64]{1,0,2:T(4,128)(2,1)S(1)}, bf16[4,128,64]{1,0,2:T(4,128)(2,1)}, u32[]{:S(2)}, u32[]{:S(2)}) collective-permute-start(bf16[4,128,64]{1,0,2:T(4,128)(2,1)S(1)} %bitcast.85), channel_id=1, source_target_pairs={{4,0},{8,4},{12,8},{5,1},{9,5},{13,9},{6,2},{10,6},{14,10},{7,3},{... | collective-permute-start | bytes 196616 | tf_op jit(solution)/shard_map/ppermute | solution.py:27
  22.3 0.2 fusion.62
  22.6 0.3 fusion.35
  23.1 0.3 fusion.110
  23.6 0.5 fusion.49
  24.2 0.5 fusion.46
  24.7 0.2 fusion.25
  25.0 0.2 fusion.26
  25.2 0.7 pad_maximum_fusion.4
  25.9 5.2 %collective-permute-start = (bf16[2,3,48,128]{3,2,1,0:T(8,128)(2,1)}, bf16[2,3,48,128]{3,2,1,0:T(8,128)(2,1)}, u32[]{:S(2)}, u32[]{:S(2)}) collective-permute-start(bf16[2,3,48,128]{3,2,1,0:T(8,128)(2,1)} %get-tuple-element.7), channel_id=1, source_target_pairs={{0,4},{4,8},{8,12},{1,5},{5,9},{9,13},{2,6},{6,10},{10,14},{3,7},{... | collective-permute-start | bytes 221192 | tf_op jit(solution)/shard_map/ppermute | solution.py:25
  31.0 1.5 %collective-permute-start.1 = (bf16[2,3,48,128]{3,2,1,0:T(8,128)(2,1)}, bf16[2,3,48,128]{3,2,1,0:T(8,128)(2,1)}, u32[]{:S(2)}, u32[]{:S(2)}) collective-permute-start(bf16[2,3,48,128]{3,2,1,0:T(8,128)(2,1)} %get-tuple-element.8), channel_id=1, source_target_pairs={{4,0},{8,4},{12,8},{5,1},{9,5},{13,9},{6,2},{10,6},{14,10},{7,3},{... | collective-permute-start | bytes 221192 | tf_op jit(solution)/shard_map/ppermute | solution.py:27
  32.7 0.6 gather_fusion
  33.3 0.2 reduce_window_sum.11
  33.7 1.6 %gather_fusion.1 = s32[608,64]{1,0:T(8,128)S(1)} fusion(s32[3,64]{1,0:T(4,128)S(1)} %fusion.134, s32[1024]{0:T(1024)S(1)} %pad_clamp_fusion), kind=kCustom, calls=%fused_computation.1 | custom fusion | bytes 313728 | tf_op jit(solution)/shard_map/jit(_take)/gather | solution.py:130
  35.3 0.3 convert_reduce_fusion.3
  35.7 0.7 slice.99
  36.3 0.2 fusion.58
  36.6 0.8 fusion.117
  37.4 1.3 %copy.32 = bf16[16,32,192]{1,2,0:T(8,128)(2,1)S(1)} copy(bf16[16,32,192]{2,1,0:T(8,128)(2,1)} %bitcast.83) | data formatting | bytes 393216 | tf_op jit(solution)/shard_map/slice | solution.py:58
  38.7 1.2 %copy.33 = bf16[16,32,192]{1,2,0:T(8,128)(2,1)} copy(bf16[16,32,192]{2,1,0:T(8,128)(2,1)S(1)} %bitcast.82) | data formatting | bytes 393216 | tf_op jit(solution)/shard_map/slice | solution.py:58
  39.9 1.2 %copy.34 = bf16[16,32,192]{1,2,0:T(8,128)(2,1)} copy(bf16[16,32,192]{2,1,0:T(8,128)(2,1)S(1)} %bitcast.81) | data formatting | bytes 393216 | tf_op jit(solution)/shard_map/slice | solution.py:58
  41.1 1.2 %copy.35 = bf16[16,32,192]{1,2,0:T(8,128)(2,1)} copy(bf16[16,32,192]{2,1,0:T(8,128)(2,1)S(1)} %bitcast.80) | data formatting | bytes 393216 | tf_op jit(solution)/shard_map/slice | solution.py:58
  42.3 1.0 convolution_convert_fusion.1
  43.3 1.8 %reshape.228 = bf16[3,16,32,4,32]{4,3,2,1,0:T(4,128)(2,1)} reshape(bf16[3,512,128]{2,1,0:T(8,128)(2,1)S(1)} %convolution_convert_fusion.1) | data formatting | bytes 786432 | tf_op jit(solution)/shard_map/reshape | solution.py:150
  45.2 1.0 fusion.38
  46.2 0.3 fusion.106
  46.5 0.3 fusion.29
  46.9 1.0 fusion.32
  48.0 1.8 %fusion.69 = f32[3,512,256]{2,1,0:T(8,128)} fusion(bf16[128,256]{1,0:T(8,128)(2,1)S(1)} %copy-done, bf16[3,512,128]{2,1,0:T(8,128)(2,1)S(1)} %copy-done.2, f32[512,128]{1,0:T(8,128)S(1)} %fusion.106, f32[512,128]{1,0:T(8,128)S(1)} %fusion.29, f32[3,512]{1,0:T(4,128)S(1)} %copy-done.13, f32[3,512]{1,0:T(4,128)S(1)} %broadcast_multiply_fusion.1), kind=kOutput, calls=%fused_computation.103 | convolution fusion | flops 101842944 | bytes 2568192 | tf_op jit(solution)/shard_map/dot_general | solution.py:47
  49.8 1.7 %fusion.64 = bf16[4,64,192]{1,0,2:T(4,128)(2,1)} fusion(s32[]{:T(128)S(6)} %select_n.83, bf16[4,128,64]{1,0,2:T(4,128)(2,1)} %collective-permute-done.3, bf16[4,128,64]{1,0,2:T(4,128)(2,1)S(1)} %bitcast.86, bf16[4,128,64]{1,0,2:T(4,128)(2,1)} %collective-permute-done.2, pred[]{:T(512)S(6)} %eq.14), kind=kLoop, calls=%fused_computation.95 | loop fusion | flops 344064 | bytes 294917 | tf_op jit(solution)/shard_map/jit(_where)/select_n | solution.py:36
  51.6 1.0 pad_maximum_fusion.2
  52.7 0.3 fusion.115
  53.1 1.7 %copy.27 = bf16[3,16,128,128]{2,3,1,0:T(8,128)(2,1)} copy(bf16[3,16,128,128]{3,2,1,0:T(8,128)(2,1)S(1)} %pad_maximum_fusion.1) | data formatting | bytes 3145728 | tf_op jit(solution)/shard_map/concatenate | solution.py:61
  55.2 1.6 %copy.26 = bf16[3,16,128,128]{2,3,1,0:T(8,128)(2,1)} copy(bf16[3,16,128,128]{3,2,1,0:T(8,128)(2,1)S(1)} %pad_maximum_fusion) | data formatting | bytes 3145728 | tf_op jit(solution)/shard_map/concatenate | solution.py:61
  56.8 19.4 %all-reduce.2.cloned.1.call-done = bf16[4,64,192]{1,0,2:T(4,128)(2,1)} async-done(((bf16[4,64,192]{1,0,2:T(4,128)(2,1)}), bf16[4,64,192]{1,0,2:T(4,128)(2,1)}) %all-reduce.2.cloned.1.call-update) | async-done | bytes 98320 | tf_op jit(solution)/shard_map/psum | solution.py:36
  76.2 2.2 %fusion.18 = bf16[4,512,192]{1,2,0:T(8,128)(2,1)} fusion(bf16[4,64,192]{1,0,2:T(4,128)(2,1)} %all-reduce.2.cloned.1.call-done, s32[512]{0:T(512)S(1)} %copy-done.22), kind=kOutput, calls=%fused_computation.30 | convolution fusion | flops 50757632 | bytes 886784 | tf_op jit(solution)/shard_map/at,htc->hac/dot_general | solution.py:140
  78.3 1.4 %copy.31 = bf16[4,512,192]{2,1,0:T(8,128)(2,1)S(1)} copy(bf16[4,512,192]{1,2,0:T(8,128)(2,1)} %fusion.18) | data formatting | bytes 1572864 | tf_op jit(solution)/shard_map/convert_element_type | solution.py:142
  79.8 3.5 %fusion.39 = f32[16,4,32,128]{3,2,1,0:T(8,128)} fusion(bf16[4,16,32,192]{3,2,1,0:T(8,128)(2,1)S(1)} %bitcast.77, bf16[16,32,192]{1,2,0:T(8,128)(2,1)} %copy.35, bf16[16,32,192]{1,2,0:T(8,128)(2,1)} %copy.34, bf16[16,32,192]{1,2,0:T(8,128)(2,1)S(1)} %copy-done.5, bf16[16,32,192]{1,2,0:T(8,128)(2,1)S(1)} %copy.32), kind=kOutput, calls=%fused_computation.60 | convolution fusion | flops 103809024 | bytes 2621440 | tf_op jit(solution)/shard_map/hwqc,wkc->whqk/dot_general | solution.py:145
  83.3 5.0 %fusion.119 = (f32[3,16,4,32]{3,2,1,0:T(4,128)S(1)}, f32[3,16,4,32,128]{4,3,2,1,0:T(8,128)}) fusion(f32[16,4,32,128]{3,2,1,0:T(8,128)} %fusion.39, pred[16,128]{1,0:T(8,128)(4,1)S(1)} %pad_add_fusion, bf16[3,16,128,4,32]{2,4,3,1,0:T(8,128)(2,1)} %bitcast.78, bf16[3,16,32,4,32]{4,3,2,1,0:T(4,128)(2,1)} %reshape.228), kind=kOutput, calls=%fused_computation.168 | convolution fusion | flops 54263936 | bytes 6187008 | tf_op jit(solution)/shard_map/sub | solution.py:164
  88.3 2.9 %convolution_bitcast_fusion = f32[3,16,32,4,32]{2,4,3,1,0:T(8,128)S(1)} fusion(bf16[3,16,128,4,32]{2,4,3,1,0:T(8,128)(2,1)S(1)} %bitcast.79, f32[3,16,4,32,128]{4,3,2,1,0:T(8,128)} %get-tuple-element.28, f32[3,16,4,32]{3,2,1,0:T(4,128)S(1)} %get-tuple-element.27), kind=kOutput, calls=%fused_computation.16 | convolution fusion | flops 51904512 | bytes 5529600 | tf_op jit(solution)/shard_map/swhqk,swkhd->swqhd/dot_general | solution.py:166
  91.2 2.2 %copy.37 = f32[3,16,32,4,32]{2,1,4,3,0:T(8,128)S(1)} copy(f32[3,16,32,4,32]{2,4,3,1,0:T(8,128)S(1)} %convolution_bitcast_fusion) | data formatting | bytes 1572864 | tf_op jit(solution)/shard_map/swhqk,swkhd->swqhd/transpose | solution.py:166
  93.4 2.1 %reshape.231 = f32[3,512,128]{1,2,0:T(8,128)} reshape(f32[3,16,32,4,32]{2,1,4,3,0:T(8,128)S(1)} %copy.37) | data formatting | bytes 1572864 | tf_op jit(solution)/shard_map/reshape | solution.py:169
  95.6 3.1 %convolution_multiply_fusion.1 = f32[3,512,128]{2,1,0:T(8,128)} fusion(f32[3,512,128]{1,2,0:T(8,128)} %reshape.231, bf16[3,512,128]{2,1,0:T(8,128)(2,1)} %copy-done.4, f32[512,128]{1,0:T(8,128)} %fusion.38, bf16[128,128]{1,0:T(8,128)(2,1)} %param.29, bf16[128,128]{1,0:T(8,128)(2,1)} %param.28), kind=kOutput, calls=%fused_computation.31 | convolution fusion | flops 101842944 | bytes 2293760 | tf_op jit(solution)/shard_map/dot_general | solution.py:47
  98.7 2.7 %fusion.24 = bf16[3,512,128]{2,1,0:T(8,128)(2,1)} fusion(f32[3,512,128]{2,1,0:T(8,128)} %convolution_multiply_fusion.1, f32[3,512,256]{2,1,0:T(8,128)S(1)} %copy-done.7, f32[512,128]{1,0:T(8,128)S(1)} %copy-done.30, bf16[256,128]{1,0:T(8,128)(2,1)S(1)} %copy-done.23, bf16[128,256]{1,0:T(8,128)(2,1)S(1)} %copy-done.24, ...), kind=kOutput, calls=%fused_computation.38 | convolution fusion | flops 205455360 | bytes 4075520 | tf_op jit(solution)/shard_map/dot_general | solution.py:47
  (94 shorter events, 1.9 us)
Async XLA Ops:
  6.5 41.4 %copy-start = (bf16[128,256]{1,0:T(8,128)(2,1)S(1)}, bf16[128,256]{1,0:T(8,128)(2,1)}, u32[]{:S(2)}) copy-start(bf16[128,256]{1,0:T(8,128)(2,1)} %param.35) | copy-start | bytes 196612
  6.5 2.9 %copy-start.1 = (bf16[128,64,128]{2,1,0:T(8,128)(2,1)S(1)}, bf16[128,64,128]{2,1,0:T(8,128)(2,1)}, u32[]{:S(2)}) copy-start(bf16[128,64,128]{2,1,0:T(8,128)(2,1)} %param.21) | copy-start | bytes 6291460
  6.5 5.7 %copy-start.29 = (bf16[128,4]{0,1:T(4,128)(2,1)S(1)}, bf16[128,4]{0,1:T(4,128)(2,1)}, u32[]{:S(2)}) copy-start(bf16[128,4]{0,1:T(4,128)(2,1)} %param.31) | copy-start | bytes 3076
  6.5 69.6 %all-reduce.2.cloned.1.call-start = ((), (), s32[]{:S(2)}) async-start(), calls=%async_computation | async-start | bytes 393216 | tf_op jit(solution)/shard_map/psum | solution.py:36
  12.2 9.9 %copy-start.6 = (bf16[512,128]{1,0:T(8,128)(2,1)S(1)}, bf16[512,128]{1,0:T(8,128)(2,1)}, u32[]{:S(2)}) copy-start(bf16[512,128]{1,0:T(8,128)(2,1)} %param.20) | copy-start | bytes 393220
  12.2 10.3 %copy-start.25 = (bf16[128,128]{1,0:T(8,128)(2,1)S(1)}, bf16[128,128]{1,0:T(8,128)(2,1)}, u32[]{:S(2)}) copy-start(bf16[128,128]{1,0:T(8,128)(2,1)} %param.23) | copy-start | bytes 98308
  12.2 10.9 %copy-start.18 = (bf16[128,128]{1,0:T(8,128)(2,1)S(1)}, bf16[128,128]{1,0:T(8,128)(2,1)}, u32[]{:S(2)}) copy-start(bf16[128,128]{1,0:T(8,128)(2,1)} %param.24) | copy-start | bytes 98308
  15.2 8.3 %copy-start.2 = (bf16[3,512,128]{2,1,0:T(8,128)(2,1)S(1)}, bf16[3,512,128]{2,1,0:T(8,128)(2,1)}, u32[]{:S(2)}) copy-start(bf16[3,512,128]{2,1,0:T(8,128)(2,1)} %param.19) | copy-start | bytes 1179652
  15.3 34.5 %collective-permute-start.2 = (bf16[4,128,64]{1,0,2:T(4,128)(2,1)S(1)}, bf16[4,128,64]{1,0,2:T(4,128)(2,1)}, u32[]{:S(2)}, u32[]{:S(2)}) collective-permute-start(bf16[4,128,64]{1,0,2:T(4,128)(2,1)S(1)} %bitcast.84), channel_id=1, source_target_pairs={{0,4},{4,8},{8,12},{1,5},{5,9},{9,13},{2,6},{6,10},{10,14},{3,7},{... | collective-permute-start | bytes 196616 | tf_op jit(solution)/shard_map/ppermute | solution.py:25
  20.8 29.0 %collective-permute-start.3 = (bf16[4,128,64]{1,0,2:T(4,128)(2,1)S(1)}, bf16[4,128,64]{1,0,2:T(4,128)(2,1)}, u32[]{:S(2)}, u32[]{:S(2)}) collective-permute-start(bf16[4,128,64]{1,0,2:T(4,128)(2,1)S(1)} %bitcast.85), channel_id=1, source_target_pairs={{4,0},{8,4},{12,8},{5,1},{9,5},{13,9},{6,2},{10,6},{14,10},{7,3},{... | collective-permute-start | bytes 196616 | tf_op jit(solution)/shard_map/ppermute | solution.py:27
  22.3 1.9 %copy-start.14 = (f32[512]{0:T(512)}, f32[512]{0:T(512)S(1)}, u32[]{:S(2)}) copy-start(f32[512]{0:T(512)S(1)} %broadcast_multiply_fusion.2) | copy-start | bytes 6148
  22.5 0.6 copy-start.20
  22.5 2.1 %copy-start.16 = (bf16[128,128]{1,0:T(8,128)(2,1)S(1)}, bf16[128,128]{1,0:T(8,128)(2,1)}, u32[]{:S(2)}) copy-start(bf16[128,128]{1,0:T(8,128)(2,1)} %param.26) | copy-start | bytes 98308
  23.1 1.8 %copy-start.17 = (bf16[128,128]{1,0:T(8,128)(2,1)S(1)}, bf16[128,128]{1,0:T(8,128)(2,1)}, u32[]{:S(2)}) copy-start(bf16[128,128]{1,0:T(8,128)(2,1)} %param.27) | copy-start | bytes 98308
  24.2 1.7 %copy-start.12 = (f32[3,512]{1,0:T(4,128)}, f32[3,512]{1,0:T(4,128)S(1)}, u32[]{:S(2)}) copy-start(f32[3,512]{1,0:T(4,128)S(1)} %add_rsqrt_fusion.1) | copy-start | bytes 18436
  24.2 8.5 %copy-start.11 = (s32[4,64]{1,0:T(4,128)S(1)}, s32[4,64]{1,0:T(4,128)}, u32[]{:S(2)}) copy-start(s32[4,64]{1,0:T(4,128)} %param.22) | copy-start | bytes 3076
  24.7 17.6 %copy-start.4 = (bf16[3,512,128]{2,1,0:T(8,128)(2,1)}, bf16[3,512,128]{2,1,0:T(8,128)(2,1)S(1)}, u32[]{:S(2)}) copy-start(bf16[3,512,128]{2,1,0:T(8,128)(2,1)S(1)} %fusion.46) | copy-start | bytes 1179652
  25.9 25.7 %collective-permute-start = (bf16[2,3,48,128]{3,2,1,0:T(8,128)(2,1)}, bf16[2,3,48,128]{3,2,1,0:T(8,128)(2,1)}, u32[]{:S(2)}, u32[]{:S(2)}) collective-permute-start(bf16[2,3,48,128]{3,2,1,0:T(8,128)(2,1)} %get-tuple-element.7), channel_id=1, source_target_pairs={{0,4},{4,8},{8,12},{1,5},{5,9},{9,13},{2,6},{6,10},{10,14},{3,7},{... | collective-permute-start | bytes 221192 | tf_op jit(solution)/shard_map/ppermute | solution.py:25
  31.0 20.5 %collective-permute-start.1 = (bf16[2,3,48,128]{3,2,1,0:T(8,128)(2,1)}, bf16[2,3,48,128]{3,2,1,0:T(8,128)(2,1)}, u32[]{:S(2)}, u32[]{:S(2)}) collective-permute-start(bf16[2,3,48,128]{3,2,1,0:T(8,128)(2,1)} %get-tuple-element.8), channel_id=1, source_target_pairs={{4,0},{8,4},{12,8},{5,1},{9,5},{13,9},{6,2},{10,6},{14,10},{7,3},{... | collective-permute-start | bytes 221192 | tf_op jit(solution)/shard_map/ppermute | solution.py:27
  41.1 4.1 %copy-start.15 = (f32[512]{0:T(512)S(1)}, f32[512]{0:T(512)}, u32[]{:S(2)}) copy-start(f32[512]{0:T(512)} %copy-done.14) | copy-start | bytes 6148
  41.1 4.1 %copy-start.21 = (f32[512]{0:T(512)S(1)}, f32[512]{0:T(512)}, u32[]{:S(2)}) copy-start(f32[512]{0:T(512)} %copy-done.20) | copy-start | bytes 6148
  41.1 4.1 %copy-start.26 = (bf16[128,128]{1,0:T(8,128)(2,1)S(1)}, bf16[128,128]{1,0:T(8,128)(2,1)}, u32[]{:S(2)}) copy-start(bf16[128,128]{1,0:T(8,128)(2,1)} %param.30) | copy-start | bytes 98308
  42.3 3.9 %copy-start.19 = (bf16[128,128]{1,0:T(8,128)(2,1)S(1)}, bf16[128,128]{1,0:T(8,128)(2,1)}, u32[]{:S(2)}) copy-start(bf16[128,128]{1,0:T(8,128)(2,1)} %param.33) | copy-start | bytes 98308
  43.3 3.2 %copy-start.27 = (bf16[128,128]{1,0:T(8,128)(2,1)S(1)}, bf16[128,128]{1,0:T(8,128)(2,1)}, u32[]{:S(2)}) copy-start(bf16[128,128]{1,0:T(8,128)(2,1)} %param.32) | copy-start | bytes 98308
  45.2 1.7 %copy-start.28 = (bf16[128,128]{1,0:T(8,128)(2,1)S(1)}, bf16[128,128]{1,0:T(8,128)(2,1)}, u32[]{:S(2)}) copy-start(bf16[128,128]{1,0:T(8,128)(2,1)} %param.37) | copy-start | bytes 98308
  45.2 2.8 %copy-start.13 = (f32[3,512]{1,0:T(4,128)S(1)}, f32[3,512]{1,0:T(4,128)}, u32[]{:S(2)}) copy-start(f32[3,512]{1,0:T(4,128)} %copy-done.12) | copy-start | bytes 18436
  46.9 2.8 %copy-start.9 = (f32[512,128]{1,0:T(8,128)}, f32[512,128]{1,0:T(8,128)S(1)}, u32[]{:S(2)}) copy-start(f32[512,128]{1,0:T(8,128)S(1)} %fusion.29) | copy-start | bytes 786436
  55.2 21.0 %copy-start.22 = (s32[512]{0:T(512)S(1)}, s32[512]{0:T(512)}, u32[]{:S(2)}) copy-start(s32[512]{0:T(512)} %slice.99) | copy-start | bytes 6148
  56.8 23.0 %copy-start.5 = (bf16[16,32,192]{1,2,0:T(8,128)(2,1)S(1)}, bf16[16,32,192]{1,2,0:T(8,128)(2,1)}, u32[]{:S(2)}) copy-start(bf16[16,32,192]{1,2,0:T(8,128)(2,1)} %copy.33) | copy-start | bytes 589828
  83.3 5.1 %copy-start.8 = (bf16[3,16,128,128]{2,3,1,0:T(8,128)(2,1)S(1)}, bf16[3,16,128,128]{2,3,1,0:T(8,128)(2,1)}, u32[]{:S(2)}) copy-start(bf16[3,16,128,128]{2,3,1,0:T(8,128)(2,1)} %copy.26) | copy-start | bytes 4718596
  95.5 3.1 %copy-start.3 = (bf16[3,512,128]{2,1,0:T(8,128)(2,1)S(1)}, bf16[3,512,128]{2,1,0:T(8,128)(2,1)}, u32[]{:S(2)}) copy-start(bf16[3,512,128]{2,1,0:T(8,128)(2,1)} %param.19) | copy-start | bytes 1179652
  95.5 3.1 %copy-start.7 = (f32[3,512,256]{2,1,0:T(8,128)S(1)}, f32[3,512,256]{2,1,0:T(8,128)}, u32[]{:S(2)}) copy-start(f32[3,512,256]{2,1,0:T(8,128)} %fusion.69) | copy-start | bytes 4718596
  95.5 3.1 %copy-start.10 = (f32[512,128]{1,0:T(8,128)S(1)}, f32[512,128]{1,0:T(8,128)}, u32[]{:S(2)}) copy-start(f32[512,128]{1,0:T(8,128)} %copy-done.9) | copy-start | bytes 786436
  95.5 3.1 %copy-start.23 = (bf16[256,128]{1,0:T(8,128)(2,1)S(1)}, bf16[256,128]{1,0:T(8,128)(2,1)}, u32[]{:S(2)}) copy-start(bf16[256,128]{1,0:T(8,128)(2,1)} %param.36) | copy-start | bytes 196612
  95.5 3.1 %copy-start.24 = (bf16[128,256]{1,0:T(8,128)(2,1)S(1)}, bf16[128,256]{1,0:T(8,128)(2,1)}, u32[]{:S(2)}) copy-start(bf16[128,256]{1,0:T(8,128)(2,1)} %param.34) | copy-start | bytes 196612
  95.6 3.1 %copy-start.30 = (f32[512,128]{1,0:T(8,128)S(1)}, f32[512,128]{1,0:T(8,128)}, u32[]{:S(2)}) copy-start(f32[512,128]{1,0:T(8,128)} %fusion.32) | copy-start | bytes 786436
Sparse Core Ops, SparseCore 0:
  51.7 24.4 all-reduce.1
where the time goes:
time: 109 us; the launch traced here: 108 us
  matrix products  28.9 us (27%)
  local copies, waits for them, and re-layouts  20.3 us (19%)
  waiting for transfers between devices  19.4 us (18%)
  between operations  14 us (13%)
  starting transfers between devices  13.5 us (12%)
  other arithmetic  12.1 us (11%)
    psum x1, waiting for transfers between devices, from_root(): return lax.psum(jnp.where(mine, value, jnp.zeros_like(value)), axis)  19.4 us
    dot_general x12, matrix products, project(): mixed = jnp.dot(flattened, weight, preferred_element_type=jnp.float32)  12.4 us
    ppermute x2, starting transfers between devices, padded(): lax.ppermute(tail, axis, [(i, (i + 1) % count) for i in range(ends)])  10.7 us
    slice x8, local copies, waits for them, and re-layouts, windowed(): lax.slice_in_dim(grouped, offset, offset + windows, axis=axis_pos)  6.16 us
    sub x1, matrix products, shards(): raised = jnp.exp(scores - row_max)  5.04 us
    dot_general x1, matrix products, shards(): jnp.einsum('hwqc,wkc->whqk', row_bias, col_win, preferred_element_type=jn...  3.5 us
    reduce_sum x3, other arithmetic, layer_norm(): jnp.mean(centred * centred, axis=-1, keepdims=True) + EPSILON  3.43 us
    concatenate x2, local copies, waits for them, and re-layouts, windowed(): return jnp.concatenate(shifted_parts, axis=axis_pos + 1)  3.25 us
  transfers between devices with their start and end apart: 5, of which 1 were waited for; matrix products, arithmetic and copies ran while one was open for 25% of the time, Pallas kernels for 0%

commit v1 on v0

v1 whole, which is shorter than its diff:
```python
import functools
import math

import jax
import jax.numpy as jnp
from jax import lax
from jax.experimental import pallas as pl
from jax.experimental.pallas import tpu as pltpu
from jax.sharding import PartitionSpec as P

Q_WIN = 32
K_WIN = 128
EDGE = 48
GROUP = 32

EPSILON = 1e-05
MASKED = -1e30
LOG2E = math.log2(math.e)
BF16 = jnp.bfloat16
F32 = jnp.float32
LAST = (((1,), (1,)), ((), ()))
VMEM = pl.BlockSpec(memory_space=pltpu.VMEM)


def dot(a, b):
    return jnp.dot(a, b, preferred_element_type=F32)


def iota(shape, dim):
    return lax.broadcasted_iota(jnp.int32, shape, dim)


def centring(width):
    same = iota((width, width), 0) == iota((width, width), 1)
    return jnp.where(same, 1.0 - 1.0 / width, -1.0 / width).astype(BF16)


def averaging(width):
    return jnp.full((width, width), 1.0 / width, BF16)


def layer_norm(rows):
    width = rows.shape[-1]
    centred = dot(rows, centring(width))
    variance = dot((centred * centred).astype(BF16), averaging(width))
    return centred * lax.rsqrt(variance + EPSILON)


def sigmoid(values):
    return 1.0 / (1.0 + jnp.exp2(values * -LOG2E))


def pair_kernel(heads, pair_ref, w_pair_ref, out_ref):
    group, cols, width = pair_ref.shape
    half = group // 2
    lanes = heads * group
    centre = centring(width)
    blank = jnp.zeros((width, width), BF16)
    centre2 = jnp.concatenate(
        [jnp.concatenate([centre, blank], 1), jnp.concatenate([blank, centre], 1)], 0
    )
    spread = (iota((heads, lanes), 1) // group == iota((heads, lanes), 0)).astype(BF16)
    weight = dot(w_pair_ref[...], spread).astype(BF16)
    blank = jnp.zeros((width, lanes), BF16)
    mean = jnp.full((width, lanes), 1.0 / width, BF16)
    mix = jnp.concatenate(
        [jnp.concatenate([weight, blank], 1), jnp.concatenate([blank, mean], 1)], 0
    )
    pair = pair_ref[...]
    both = jnp.concatenate(
        [pair[:half].reshape(half * cols, width), pair[half:].reshape(half * cols, width)], 1
    )
    centred = dot(both, centre2)
    rounded = centred.astype(BF16)
    squares = (centred * centred).astype(BF16)
    slot = iota((cols, 2 * lanes), 1) % group
    total = jnp.zeros((cols, 2 * lanes), F32)
    for part in range(2):
        cut = slice(part * width, (part + 1) * width)
        mixed = dot(jnp.concatenate([rounded[:, cut], squares[:, cut]], 1), mix)
        mixed = mixed.reshape(half, cols, 2 * lanes)
        for index in range(half):
            total = jnp.where(slot == part * half + index, mixed[index], total)
    out_ref[0, 0] = (total[:, :lanes] * lax.rsqrt(total[:, lanes:] + EPSILON)).astype(BF16)


def pair_bias(pair_cond, w_pair, tok_here):
    rows, cols, width = pair_cond.shape
    heads = w_pair.shape[1]
    groups = tok_here // GROUP
    return pl.pallas_call(
        functools.partial(pair_kernel, heads),
        grid=(rows // GROUP,),
        in_specs=[
            pl.BlockSpec((GROUP, cols, width), lambda i: (i, 0, 0)),
            pl.BlockSpec((width, heads), lambda i: (0, 0)),
        ],
        out_specs=pl.BlockSpec(
            (1, 1, cols, heads * GROUP), lambda i: (i // groups, i % groups, 0, 0)
        ),
        out_shape=jax.ShapeDtypeStruct(
            (rows // tok_here, groups, cols, heads * GROUP), BF16
        ),
        compiler_params=pltpu.CompilerParams(vmem_limit_bytes=40 << 20),
        cost_estimate=pl.CostEstimate(
            flops=rows * cols * width * width * 4,
            bytes_accessed=rows * cols * width * 2,
            transcendentals=0,
        ),
    )(pair_cond, w_pair)


def project_kernel(
    single_ref,
    cond_ref,
    edge_prev_ref,
    edge_next_ref,
    ada_attn_scale,
    ada_attn_shift,
    w_query,
    w_key,
    w_value,
    w_gate,
    attn_gate,
    ada_trans_scale,
    ada_trans_shift,
    w_swish,
    w_linear,
    w_down,
    trans_gate,
    query_ref,
    key_ref,
    value_ref,
    gate_ref,
    open_ref,
    trans_ref,
):
    samples, atoms_here, width = single_ref.shape
    hidden_width = w_swish.shape[1]
    step = 128

    def attn_norm(cond, single):
        ada = dot(cond, jnp.concatenate([ada_attn_scale[...], ada_attn_shift[...]], 1))
        scale, shift = sigmoid(ada[:, :width])[None], ada[None, :, width:]
        rows = single.shape[1]
        return (scale * single.reshape(samples, rows, width) + shift).astype(BF16)

    def keys_values(normed):
        both = dot(
            normed.reshape(-1, width), jnp.concatenate([w_key[...], w_value[...]], 1)
        ).astype(BF16)
        both = both.reshape(samples, -1, 2 * width)
        return both[:, :, :width], both[:, :, width:]

    for place, edge_ref in ((0, edge_prev_ref), (EDGE + atoms_here, edge_next_ref)):
        edge = edge_ref[...].reshape(samples + 1, EDGE, width)
        normal = layer_norm(edge.reshape(-1, width)).reshape(samples + 1, EDGE, width)
        keys, values = keys_values(
            attn_norm(normal[samples].astype(BF16), normal[:samples])
        )
        key_ref[:, place : place + EDGE, :] = keys
        value_ref[:, place : place + EDGE, :] = values

    @pl.loop(0, atoms_here // step)
    def _(turn):
        start = pl.multiple_of(turn * step, step)
        at = pl.ds(start, step)
        cond = layer_norm(cond_ref[at, :]).astype(BF16)
        single = layer_norm(single_ref[:, at, :].reshape(-1, width))
        single = single.reshape(samples, step, width)
        normed = attn_norm(cond, single)
        keys, values = keys_values(normed)
        at_ext = pl.ds(pl.multiple_of(start + EDGE, 16), step)
        key_ref[:, at_ext, :] = keys
        value_ref[:, at_ext, :] = values
        both = dot(
            normed.reshape(-1, width), jnp.concatenate([w_query[...], w_gate[...]], 1)
        ).reshape(samples, step, 2 * width)
        query_ref[:, at, :] = both[:, :, :width].astype(BF16)
        gate_ref[:, at, :] = sigmoid(both[:, :, width:])
        gates = dot(cond, jnp.concatenate([attn_gate[...], trans_gate[...]], 1))
        open_ref[at, :] = sigmoid(gates[:, :width])
        ada = dot(cond, jnp.concatenate([ada_trans_scale[...], ada_trans_shift[...]], 1))
        normed_trans = (sigmoid(ada[:, :width])[None] * single + ada[None, :, width:]).astype(BF16)
        flat = normed_trans.reshape(-1, width)
        swish = dot(flat, w_swish[...])
        hidden = (swish * sigmoid(swish) * dot(flat, w_linear[...])).astype(BF16)
        down = dot(hidden, w_down[...]).reshape(samples, step, width)
        trans_ref[:, at, :] = sigmoid(gates[:, width:])[None] * down


def attend_kernel(
    heads,
    blocks,
    at_ref,
    query_ref,
    key_ref,
    value_ref,
    gate_ref,
    open_ref,
    trans_ref,
    counts_ref,
    prev_ref,
    own_ref,
    next_ref,
    w_out_ref,
    out_ref,
    near_ref,
    gated_ref,
):
    samples, atoms_here, width = query_ref.shape
    tok_here = counts_ref.shape[1]
    head_dim = width // heads
    windows = atoms_here // Q_WIN
    lanes = heads * tok_here
    rows = heads * Q_WIN
    device_at = at_ref[0]
    ends = atoms_here * blocks

    def bounds(block, token, reach):
        counts = counts_ref[pl.ds(block, 1), :].astype(F32).astype(BF16)
        counts = jnp.broadcast_to(counts, (8, tok_here))
        before = iota((tok_here, reach), 0)
        first = dot(counts, (before < token).astype(BF16))[:1]
        last = dot(counts, (before <= token).astype(BF16))[:1]
        return first.astype(jnp.int32), last.astype(jnp.int32)

    def expand(block, place, count, offset, tile_ref):
        token = iota((tok_here, tok_here), 1)
        first, last = bounds(block, token, tok_here)
        position = iota((count, tok_here), 0) + offset
        hot = ((first <= position) & (position < last)).astype(F32).astype(BF16)
        tile = tile_ref[...].reshape(tok_here // GROUP, tok_here, heads * GROUP)
        tile = jnp.concatenate([tile[index] for index in range(tok_here // GROUP)], 1)
        near_ref[place : place + count, :] = dot(hot, tile).astype(BF16)

    expand(jnp.maximum(device_at - 1, 0), 0, EDGE, atoms_here - EDGE, prev_ref)
    expand(device_at, EDGE, atoms_here, 0, own_ref)
    expand(jnp.minimum(device_at + 1, blocks - 1), EDGE + atoms_here, EDGE, 0, next_ref)

    lane = iota((tok_here, lanes), 1)
    token = lane // (heads * GROUP) * GROUP + lane % GROUP
    first, last = bounds(device_at, token, lanes)
    lane_head = iota((rows, lanes), 1) // GROUP % heads
    row_head = iota((rows, lanes), 0) // Q_WIN
    same_head = (lane_head == row_head).astype(F32).astype(BF16)
    own_head = (iota((rows, width), 1) // head_dim == iota((rows, width), 0) // Q_WIN)
    own_head = own_head.astype(F32).astype(BF16)
    channel_head = iota((Q_WIN, 2 * width), 1) % width // head_dim
    ones = jnp.ones((K_WIN, width), BF16)
    scaling = LOG2E / math.sqrt(head_dim)

    @pl.loop(0, windows)
    def _(window):
        start = pl.multiple_of(window * Q_WIN, Q_WIN)
        position = iota((Q_WIN, lanes), 0) + start
        hot = ((first <= position) & (position < last)).astype(F32).astype(BF16)
        pick = jnp.concatenate([hot] * heads, 0) * same_head
        bias = lax.dot_general(
            pick, near_ref[pl.ds(start, K_WIN), :], LAST, preferred_element_type=F32
        )
        key_at = iota((rows, K_WIN), 1) + (device_at * atoms_here + start - EDGE)
        bias = jnp.where((key_at >= 0) & (key_at < ends), bias * LOG2E, MASKED)
        for sample in range(samples):
            query = query_ref[sample, pl.ds(start, Q_WIN), :]
            query = jnp.concatenate([query] * heads, 0) * own_head
            keys = key_ref[sample, pl.ds(start, K_WIN), :]
            values = value_ref[sample, pl.ds(start, K_WIN), :]
            scores = lax.dot_general(query, keys, LAST, preferred_element_type=F32)
            scores = scores * scaling + bias
            raised = jnp.exp2(scores - jnp.max(scores, axis=-1, keepdims=True)).astype(BF16)
            mixed = dot(raised, jnp.concatenate([values, ones], 1))
            picked = mixed[:Q_WIN]
            for head in range(1, heads):
                picked = jnp.where(
                    channel_head == head, mixed[head * Q_WIN : (head + 1) * Q_WIN], picked
                )
            attended = picked[:, :width] / picked[:, width:]
            gate = gate_ref[sample, pl.ds(start, Q_WIN), :]
            gated_ref[sample, pl.ds(start, Q_WIN), :] = (gate * attended).astype(BF16)

    for sample in range(samples):
        mixed = dot(gated_ref[sample], w_out_ref[...])
        out_ref[sample] = (open_ref[...] * mixed + trans_ref[sample]).astype(BF16)


def shards(
    atom_single,
    atom_cond,
    pair_cond,
    atom_counts,
    ada_attn_scale,
    ada_attn_shift,
    w_query,
    w_key,
    w_value,
    w_gate,
    w_out,
    attn_gate,
    w_pair,
    ada_trans_scale,
    ada_trans_shift,
    w_swish,
    w_linear,
    w_down,
    trans_gate,
):
    device_at = lax.axis_index("atoms")
    blocks = lax.axis_size("atoms")
    samples, atoms_here, width = atom_single.shape
    tok_here = atom_counts.shape[1]
    heads = w_pair.shape[1]
    groups = tok_here // GROUP
    rows_pair = pair_cond.shape[0] // tok_here
    at = device_at.astype(jnp.int32).reshape(1)

    def edge(cut):
        return jnp.concatenate([atom_single[:, cut], atom_cond[None, cut]], 0)

    edges = jnp.stack([edge(slice(0, EDGE)), edge(slice(atoms_here - EDGE, atoms_here))])
    edges = lax.all_gather(edges, "atoms")
    tiles = pair_bias(pair_cond, w_pair, tok_here)
    tiles = lax.all_gather(tiles, ("pair", "atoms"))

    weights = (
        ada_attn_scale,
        ada_attn_shift,
        w_query,
        w_key,
        w_value,
        w_gate,
        attn_gate,
        ada_trans_scale,
        ada_trans_shift,
        w_swish,
        w_linear,
        w_down,
        trans_gate,
    )
    whole = lambda array: pl.BlockSpec(array.shape, lambda i, at: (0,) * array.ndim)
    spot = (1, 1, samples + 1, EDGE, width)
    ext = atoms_here + 2 * EDGE
    shapes = [
        jax.ShapeDtypeStruct((samples, atoms_here, width), BF16),
        jax.ShapeDtypeStruct((samples, ext, width), BF16),
        jax.ShapeDtypeStruct((samples, ext, width), BF16),
        jax.ShapeDtypeStruct((samples, atoms_here, width), F32),
        jax.ShapeDtypeStruct((atoms_here, width), F32),
        jax.ShapeDtypeStruct((samples, atoms_here, width), F32),
    ]
    projected = pl.pallas_call(
        project_kernel_at,
        grid_spec=pltpu.PrefetchScalarGridSpec(
            num_scalar_prefetch=1,
            grid=(1,),
            in_specs=[
                whole(atom_single),
                whole(atom_cond),
                pl.BlockSpec(spot, lambda i, at: (jnp.maximum(at[0] - 1, 0), 1, 0, 0, 0)),
                pl.BlockSpec(spot, lambda i, at: (jnp.minimum(at[0] + 1, blocks - 1), 0, 0, 0, 0)),
            ]
            + [whole(weight) for weight in weights],
            out_specs=[whole(shape) for shape in shapes],
        ),
        out_shape=shapes,
        compiler_params=pltpu.CompilerParams(vmem_limit_bytes=40 << 20),
        cost_estimate=pl.CostEstimate(
            flops=samples * atoms_here * width * width * 24,
            bytes_accessed=4 << 20,
            transcendentals=0,
        ),
    )(at, atom_single, atom_cond, edges, edges, *weights)

    tile_spot = (1, 1, groups, tok_here, heads * GROUP)

    def tile_at(shift):
        def index(i, at):
            column = jnp.clip(at[0] + shift, 0, blocks - 1)
            return at[0] // rows_pair * blocks + column, at[0] % rows_pair, 0, 0, 0

        return pl.BlockSpec(tile_spot, index)

    return pl.pallas_call(
        functools.partial(attend_kernel, heads, blocks),
        grid_spec=pltpu.PrefetchScalarGridSpec(
            num_scalar_prefetch=1,
            grid=(1,),
            in_specs=[whole(shape) for shape in shapes]
            + [whole(atom_counts), tile_at(-1), tile_at(0), tile_at(1), whole(w_out)],
            out_specs=whole(shapes[0]),
            scratch_shapes=[
                pltpu.VMEM((ext, heads * tok_here), BF16),
                pltpu.VMEM((samples, atoms_here, width), BF16),
            ],
        ),
        out_shape=shapes[0],
        compiler_params=pltpu.CompilerParams(vmem_limit_bytes=40 << 20),
        cost_estimate=pl.CostEstimate(
            flops=samples * atoms_here * width * width * 12,
            bytes_accessed=4 << 20,
            transcendentals=0,
        ),
    )(at, *projected, atom_counts, tiles, tiles, tiles, w_out)


def project_kernel_at(at_ref, *refs):
    project_kernel(*refs)


def solution(mesh):
    return jax.shard_map(
        shards,
        mesh=mesh,
        in_specs=(
            P(("groups", "pair", "samp"), "atoms", None),
            P(("groups", "atoms"), None),
            P(("groups", "pair"), "atoms", None),
            P("groups", None),
        )
        + (P(),) * 15,
        out_specs=P(("groups", "pair", "samp"), "atoms", None),
        check_vma=False,
    )
```

time: 109 us -> 88.5 us (0.81)
  blocking collectives: 0 us -> 50 us
  matrix products: 28.9 us -> 0 us
  waiting for transfers between devices: 19.4 us -> 0 us
  Pallas kernels: 0 us -> 19.3 us
  between operations: 14 us -> 0.12 us
  starting transfers between devices: 13.5 us -> 0 us
  other arithmetic: 12.1 us -> 0.02 us
  local copies, waits for them, and re-layouts: 20.3 us -> 18 us
    all_gather x0 -> x2, blocking collectives: none -> 50 us  [the longest x1 33.2 us: shards(): tiles = lax.all_gather(tiles, ('pair', 'atoms'))]
    dot_general x16 -> x0, matrix products: 23.9 us -> none  [the longest x12 12.4 us: project(): mixed = jnp.dot(flattened, weight, preferred_element_type=jnp.float32)]
    psum x1 -> x0, waiting for transfers between devices: 19.4 us -> none  [from_root(): return lax.psum(jnp.where(mine, value, jnp.zeros_like(value)), axis)]
    pallas_call x0 -> x3, Pallas kernels: none -> 19.3 us  [the longest x1 11.8 us: shards(): pl.pallas_call(functools.partial(attend_kernel, heads, blocks), grid_spec...]
    unnamed x62 -> x57, local copies, waits for them, and re-layouts: 0.36 us -> 16.3 us
    ppermute x4 -> x0, starting transfers between devices: 13.5 us -> none  [the longest x2 10.7 us: padded(): lax.ppermute(tail, axis, [(i, (i + 1) % count) for i in range(ends)])]
    reduce_sum x7 -> x0, other arithmetic: 6.97 us -> none  [the longest x3 3.43 us: layer_norm(): jnp.mean(centred * centred, axis=-1, keepdims=True) + EPSILON]
    slice x10 -> x1, local copies, waits for them, and re-layouts: 6.88 us -> 0.94 us  [edge(): return jnp.concatenate([atom_single[:, cut], atom_cond[None, cut]], 0)]
  transfers between devices with their start and end apart: 5 -> 0, of which waited for: 1 -> 0; matrix products, arithmetic and copies ran while one was open for 25% -> 0% of each run, Pallas kernels for 0% -> 0%
where the time goes in v1:
time: 88.5 us; the launch traced here: 87.4 us
  blocking collectives  50 us (56%)
  Pallas kernels  19.3 us (22%)
  local copies, waits for them, and re-layouts  18 us (20%)
    all_gather x1, blocking collectives, shards(): tiles = lax.all_gather(tiles, ('pair', 'atoms'))  33.2 us
    all_gather x1, blocking collectives, shards(): edges = lax.all_gather(edges, 'atoms')  16.8 us
    unnamed x57, local copies, waits for them, and re-layouts  16.3 us
    pallas_call x1, Pallas kernels, shards(): pl.pallas_call(functools.partial(attend_kernel, heads, blocks), grid_spec...  11.8 us
    pallas_call x1, Pallas kernels, shards(): pl.pallas_call(project_kernel_at, grid_spec=pltpu.PrefetchScalarGridSpec(...  4.98 us
    pallas_call x1, Pallas kernels, pair_bias(): pl.pallas_call(functools.partial(pair_kernel, heads), grid=(rows // GROUP...  2.55 us

profile of v1, /device:TPU:0, one launch (start us, length us, event | category | flops | bytes accessed | tf_op | source)
XLA Modules:
  0.0 87.4 jit_solution(10719157118152322863)
XLA Ops:
  0.0 0.0 copy-start
  0.0 0.9 %fusion = (bf16[3,48,128]{2,1,0:T(8,128)(2,1)S(1)}, bf16[3,48,128]{2,1,0:T(8,128)(2,1)S(1)}) fusion(bf16[3,512,128]{2,1,0:T(8,128)(2,1)} %refs_0_.1), kind=kLoop, calls=%fused_computation.5 | loop fusion | bytes 147456 | tf_op jit(solution)/shard_map/slice | solution.py:318
  0.9 0.7 slice_bitcast_fusion.1
  1.7 16.8 %all-gather = bf16[8,4,48,128]{3,2,1,0:T(8,128)(2,1)} all-gather(bf16[2,4,48,128]{3,2,1,0:T(8,128)(2,1)S(1)} %pad_maximum_fusion), channel_id=2, replica_groups=mesh['groups'=2,'atoms'=4,'pair'=2,'samp'=2] {'atoms'}, dimensions={0}, use_global_device_ids=true | all-gather | bytes 491520 | tf_op jit(solution)/shard_map/all_gather | solution.py:321
  18.5 0.0 copy-start.7
  18.5 1.0 %copy-done.7 = bf16[8,4,48,128]{3,2,1,0:T(8,128)(2,1)S(1)} copy-done((bf16[8,4,48,128]{3,2,1,0:T(8,128)(2,1)S(1)}, bf16[8,4,48,128]{3,2,1,0:T(8,128)(2,1)}, u32[]{:S(2)}) %copy-start.7) | copy-done | bytes 393240
  19.5 0.0 copy-start.11
  19.5 1.0 %copy-done.11 = bf16[3,512,128]{2,1,0:T(8,128)(2,1)S(1)} copy-done((bf16[3,512,128]{2,1,0:T(8,128)(2,1)S(1)}, bf16[3,512,128]{2,1,0:T(8,128)(2,1)}, u32[]{:S(2)}) %copy-start.11) | copy-done | bytes 393240
  20.5 0.0 copy-start.12
  20.5 0.9 %copy-done.12 = bf16[512,128]{1,0:T(8,128)(2,1)S(1)} copy-done((bf16[512,128]{1,0:T(8,128)(2,1)S(1)}, bf16[512,128]{1,0:T(8,128)(2,1)}, u32[]{:S(2)}) %copy-start.12) | copy-done | bytes 131096
  21.4 0.0 copy-start.14
  21.4 0.8 copy-done.14
  22.2 0.0 copy-start.15
  22.2 0.8 copy-done.15
  23.1 0.0 copy-start.16
  23.1 0.8 copy-done.16
  23.9 0.0 copy-start.17
  23.9 0.8 copy-done.17
  24.7 0.8 copy-done.18
  25.4 0.8 copy-done.19
  26.2 0.8 copy-done.20
  26.9 0.8 copy-done.21
  27.7 0.8 copy-done.22
  28.4 0.8 copy-done.23
  29.2 0.8 copy-done.24
  30.0 0.8 copy-done.25
  30.7 0.8 copy-done.26
  31.5 5.0 %shard_map.181 = (bf16[3,512,128]{2,1,0:T(8,128)(2,1)S(1)}, bf16[3,608,128]{2,1,0:T(8,128)(2,1)S(1)}, bf16[3,608,128]{2,1,0:T(8,128)(2,1)S(1)}, f32[3,512,128]{2...) custom-call(s32[1]{0:T(128)} %bitcast.at_ref, bf16[3,512,128]{2,1,0:T(8,128)(2,1)S(1)} %copy-done.11, ...), custom_call_target="tpu_custom_call" | custom-call | flops 603979776 | bytes 4194304 | tf_op jit(solution)/shard_map/pallas_call | solution.py:351
  36.5 0.0 copy-start.1
  36.5 0.9 %copy-done.1 = f32[3,512,128]{2,1,0:T(8,128)} copy-done((f32[3,512,128]{2,1,0:T(8,128)}, f32[3,512,128]{2,1,0:T(8,128)S(1)}, u32[]{:S(2)}) %copy-start.1) | copy-done | bytes 786456
  37.4 0.8 copy-done.3
  38.2 0.7 copy-done.5
  38.9 0.7 copy-done.8
  39.6 0.0 copy-done.27
  39.6 0.1 copy.21.w_pair_ref
  39.8 0.0 copy-done
  39.8 0.0 copy-start.4
  39.8 0.0 copy-start.6
  39.8 0.0 copy-start.9
  39.8 2.6 %shard_map.182 = bf16[2,2,64,128]{3,2,1,0:T(8,128)(2,1)S(1)} custom-call(bf16[128,64,128]{2,1,0:T(8,128)(2,1)S(1)} %copy-done, bf16[128,4]{1,0:T(8,128)(2,1)S(1)} %copy.21.w_pair_ref), custom_call_target="tpu_custom_call" | custom-call | flops 536870912 | bytes 2097152 | tf_op jit(solution)/shard_map/pallas_call | solution.py:91
  42.4 33.2 %all-gather.1 = bf16[16,2,64,128]{3,2,1,0:T(8,128)(2,1)S(1)} all-gather(bf16[2,2,64,128]{3,2,1,0:T(8,128)(2,1)S(1)} %shard_map.182), channel_id=3, replica_groups=mesh['groups'=2,'atoms'=4,'pair'=2,'samp'=2] {'pair','atoms'}, dimensions={0}, use_global_device_ids=true | all-gather | bytes 589824 | tf_op jit(solution)/shard_map/all_gather | solution.py:323
  75.6 0.0 copy-done.10
  75.6 0.0 copy-done.13
  75.6 0.0 copy-done.2
  75.6 0.0 copy-done.4
  75.6 0.0 copy-done.6
  75.6 0.0 copy-done.9
  75.6 11.8 %shard_map.183 = bf16[3,512,128]{2,1,0:T(8,128)(2,1)} custom-call(s32[1]{0:T(128)} %bitcast.at_ref, bf16[3,512,128]{2,1,0:T(8,128)(2,1)S(1)} %copy-done.6, bf16[3,608,128]{2,1,0:T(8,128)(2,1)S(1)} %get-tuple-element.12.key_ref, bf16[3,608,128]{2,1,0:T(8,128)(2,1)S(1)} %copy-done.4, f32[3,512,128]{2,1,0:T(8,128)S(1)} %get-tuple-element.14.gate_ref, ...), custom_call_target="tpu_custom_call" | custom-call | flops 301989888 | bytes 4194304 | tf_op jit(solution)/shard_map/pallas_call | solution.py:383
  (18 shorter events, 0.1 us)
Async XLA Ops:
  0.0 39.8 %copy-start = (bf16[128,64,128]{2,1,0:T(8,128)(2,1)S(1)}, bf16[128,64,128]{2,1,0:T(8,128)(2,1)}, u32[]{:S(2)}) copy-start(bf16[128,64,128]{2,1,0:T(8,128)(2,1)} %pair_ref.1) | copy-start | bytes 6291460
  18.5 1.0 %copy-start.7 = (bf16[8,4,48,128]{3,2,1,0:T(8,128)(2,1)S(1)}, bf16[8,4,48,128]{3,2,1,0:T(8,128)(2,1)}, u32[]{:S(2)}) copy-start(bf16[8,4,48,128]{3,2,1,0:T(8,128)(2,1)} %all-gather) | copy-start | bytes 1179652
  19.5 1.0 %copy-start.11 = (bf16[3,512,128]{2,1,0:T(8,128)(2,1)S(1)}, bf16[3,512,128]{2,1,0:T(8,128)(2,1)}, u32[]{:S(2)}) copy-start(bf16[3,512,128]{2,1,0:T(8,128)(2,1)} %refs_0_.1) | copy-start | bytes 1179652
  20.5 0.9 %copy-start.12 = (bf16[512,128]{1,0:T(8,128)(2,1)S(1)}, bf16[512,128]{1,0:T(8,128)(2,1)}, u32[]{:S(2)}) copy-start(bf16[512,128]{1,0:T(8,128)(2,1)} %refs_1_.1) | copy-start | bytes 393220
  21.4 0.8 copy-start.14
  22.2 0.8 copy-start.15
  23.1 0.8 copy-start.16
  23.9 0.8 copy-start.17
  24.7 0.8 copy-start.18
  25.4 0.8 copy-start.19
  26.2 0.8 copy-start.20
  26.9 0.8 copy-start.21
  27.7 0.8 copy-start.22
  28.4 0.8 copy-start.23
  29.2 0.8 copy-start.24
  30.0 0.8 copy-start.25
  30.7 0.8 copy-start.26
  31.5 8.2 %copy-start.27 = (bf16[128,4]{0,1:T(4,128)(2,1)S(1)}, bf16[128,4]{0,1:T(4,128)(2,1)}, u32[]{:S(2)}) copy-start(bf16[128,4]{0,1:T(4,128)(2,1)} %param.31) | copy-start | bytes 3076
  31.5 44.1 %copy-start.10 = (bf16[128,128]{1,0:T(8,128)(2,1)S(1)}, bf16[128,128]{1,0:T(8,128)(2,1)}, u32[]{:S(2)}) copy-start(bf16[128,128]{1,0:T(8,128)(2,1)} %w_out_ref.1) | copy-start | bytes 98308
  31.5 44.1 %copy-start.13 = (s32[4,64]{1,0:T(4,128)S(1)}, s32[4,64]{1,0:T(4,128)}, u32[]{:S(2)}) copy-start(s32[4,64]{1,0:T(4,128)} %counts_ref.1) | copy-start | bytes 3076
  36.5 0.9 %copy-start.1 = (f32[3,512,128]{2,1,0:T(8,128)}, f32[3,512,128]{2,1,0:T(8,128)S(1)}, u32[]{:S(2)}) copy-start(f32[3,512,128]{2,1,0:T(8,128)S(1)} %get-tuple-element.16.trans_ref) | copy-start | bytes 2359300
  37.4 0.8 copy-start.3
  38.2 0.7 copy-start.5
  38.9 0.7 copy-start.8
  39.8 35.8 %copy-start.2 = (f32[3,512,128]{2,1,0:T(8,128)S(1)}, f32[3,512,128]{2,1,0:T(8,128)}, u32[]{:S(2)}) copy-start(f32[3,512,128]{2,1,0:T(8,128)} %copy-done.1) | copy-start | bytes 2359300
  39.8 35.8 %copy-start.4 = (bf16[3,608,128]{2,1,0:T(8,128)(2,1)S(1)}, bf16[3,608,128]{2,1,0:T(8,128)(2,1)}, u32[]{:S(2)}) copy-start(bf16[3,608,128]{2,1,0:T(8,128)(2,1)} %copy-done.3) | copy-start | bytes 1400836
  39.8 35.8 %copy-start.6 = (bf16[3,512,128]{2,1,0:T(8,128)(2,1)S(1)}, bf16[3,512,128]{2,1,0:T(8,128)(2,1)}, u32[]{:S(2)}) copy-start(bf16[3,512,128]{2,1,0:T(8,128)(2,1)} %copy-done.5) | copy-start | bytes 1179652
  39.8 35.8 %copy-start.9 = (f32[512,128]{1,0:T(8,128)S(1)}, f32[512,128]{1,0:T(8,128)}, u32[]{:S(2)}) copy-start(f32[512,128]{1,0:T(8,128)} %copy-done.8) | copy-start | bytes 786436

commit v2 on v1

--- a/solution.py
+++ b/solution.py
@@ -19,7 +19,7 @@
 BF16 = jnp.bfloat16
 F32 = jnp.float32
 LAST = (((1,), (1,)), ((), ()))
-VMEM = pl.BlockSpec(memory_space=pltpu.VMEM)
+VMEM_LIMIT = 62 << 20
 
 
 def dot(a, b):
@@ -101,7 +101,7 @@
         out_shape=jax.ShapeDtypeStruct(
             (rows // tok_here, groups, cols, heads * GROUP), BF16
         ),
-        compiler_params=pltpu.CompilerParams(vmem_limit_bytes=40 << 20),
+        compiler_params=pltpu.CompilerParams(vmem_limit_bytes=VMEM_LIMIT),
         cost_estimate=pl.CostEstimate(
             flops=rows * cols * width * width * 4,
             bytes_accessed=rows * cols * width * 2,
@@ -250,34 +250,42 @@
     ones = jnp.ones((K_WIN, width), BF16)
     scaling = LOG2E / math.sqrt(head_dim)
 
-    @pl.loop(0, windows)
-    def _(window):
-        start = pl.multiple_of(window * Q_WIN, Q_WIN)
-        position = iota((Q_WIN, lanes), 0) + start
-        hot = ((first <= position) & (position < last)).astype(F32).astype(BF16)
-        pick = jnp.concatenate([hot] * heads, 0) * same_head
-        bias = lax.dot_general(
-            pick, near_ref[pl.ds(start, K_WIN), :], LAST, preferred_element_type=F32
-        )
-        key_at = iota((rows, K_WIN), 1) + (device_at * atoms_here + start - EDGE)
-        bias = jnp.where((key_at >= 0) & (key_at < ends), bias * LOG2E, MASKED)
-        for sample in range(samples):
-            query = query_ref[sample, pl.ds(start, Q_WIN), :]
+    batch = math.gcd(windows, 4)
+
+    @pl.loop(0, windows // batch)
+    def _(turn):
+        starts = [pl.multiple_of((turn * batch + i) * Q_WIN, Q_WIN) for i in range(batch)]
+        biases = []
+        for start in starts:
+            position = iota((Q_WIN, lanes), 0) + start
+            hot = ((first <= position) & (position < last)).astype(F32).astype(BF16)
+            pick = jnp.concatenate([hot] * heads, 0) * same_head
+            bias = lax.dot_general(
+                pick, near_ref[pl.ds(start, K_WIN), :], LAST, preferred_element_type=F32
+            )
+            key_at = iota((rows, K_WIN), 1) + (device_at * atoms_here + start - EDGE)
+            biases.append(jnp.where((key_at >= 0) & (key_at < ends), bias * LOG2E, MASKED))
+        units = [(sample, i) for i in range(batch) for sample in range(samples)]
+        scores = []
+        for sample, i in units:
+            query = query_ref[sample, pl.ds(starts[i], Q_WIN), :]
             query = jnp.concatenate([query] * heads, 0) * own_head
-            keys = key_ref[sample, pl.ds(start, K_WIN), :]
-            values = value_ref[sample, pl.ds(start, K_WIN), :]
-            scores = lax.dot_general(query, keys, LAST, preferred_element_type=F32)
-            scores = scores * scaling + bias
-            raised = jnp.exp2(scores - jnp.max(scores, axis=-1, keepdims=True)).astype(BF16)
-            mixed = dot(raised, jnp.concatenate([values, ones], 1))
+            keys = key_ref[sample, pl.ds(starts[i], K_WIN), :]
+            product = lax.dot_general(query, keys, LAST, preferred_element_type=F32)
+            scores.append(product * scaling + biases[i])
+        tops = [jnp.max(score, axis=-1, keepdims=True) for score in scores]
+        raised = [jnp.exp2(score - top).astype(BF16) for score, top in zip(scores, tops)]
+        for (sample, i), weight in zip(units, raised):
+            values = value_ref[sample, pl.ds(starts[i], K_WIN), :]
+            mixed = dot(weight, jnp.concatenate([values, ones], 1))
             picked = mixed[:Q_WIN]
             for head in range(1, heads):
                 picked = jnp.where(
                     channel_head == head, mixed[head * Q_WIN : (head + 1) * Q_WIN], picked
                 )
             attended = picked[:, :width] / picked[:, width:]
-            gate = gate_ref[sample, pl.ds(start, Q_WIN), :]
-            gated_ref[sample, pl.ds(start, Q_WIN), :] = (gate * attended).astype(BF16)
+            gate = gate_ref[sample, pl.ds(starts[i], Q_WIN), :]
+            gated_ref[sample, pl.ds(starts[i], Q_WIN), :] = (gate * attended).astype(BF16)
 
     for sample in range(samples):
         mixed = dot(gated_ref[sample], w_out_ref[...])
@@ -317,10 +325,12 @@
     def edge(cut):
         return jnp.concatenate([atom_single[:, cut], atom_cond[None, cut]], 0)
 
-    edges = jnp.stack([edge(slice(0, EDGE)), edge(slice(atoms_here - EDGE, atoms_here))])
-    edges = lax.all_gather(edges, "atoms")
+    head, tail = edge(slice(0, EDGE)), edge(slice(atoms_here - EDGE, atoms_here))
+    above = (jnp.arange(blocks) < device_at)[:, None, None, None]
+    edges = lax.all_to_all(jnp.where(above, head[None], tail[None]), "atoms", 0, 0)
     tiles = pair_bias(pair_cond, w_pair, tok_here)
-    tiles = lax.all_gather(tiles, ("pair", "atoms"))
+    tiles = jnp.tile(tiles, (lax.axis_size("pair") * blocks // rows_pair, 1, 1, 1))
+    tiles = lax.all_to_all(tiles, ("pair", "atoms"), 0, 0)
 
     weights = (
         ada_attn_scale,
@@ -338,7 +348,7 @@
         trans_gate,
     )
     whole = lambda array: pl.BlockSpec(array.shape, lambda i, at: (0,) * array.ndim)
-    spot = (1, 1, samples + 1, EDGE, width)
+    spot = (1, samples + 1, EDGE, width)
     ext = atoms_here + 2 * EDGE
     shapes = [
         jax.ShapeDtypeStruct((samples, atoms_here, width), BF16),
@@ -356,14 +366,14 @@
             in_specs=[
                 whole(atom_single),
                 whole(atom_cond),
-                pl.BlockSpec(spot, lambda i, at: (jnp.maximum(at[0] - 1, 0), 1, 0, 0, 0)),
-                pl.BlockSpec(spot, lambda i, at: (jnp.minimum(at[0] + 1, blocks - 1), 0, 0, 0, 0)),
+                pl.BlockSpec(spot, lambda i, at: (jnp.maximum(at[0] - 1, 0), 0, 0, 0)),
+                pl.BlockSpec(spot, lambda i, at: (jnp.minimum(at[0] + 1, blocks - 1), 0, 0, 0)),
             ]
             + [whole(weight) for weight in weights],
             out_specs=[whole(shape) for shape in shapes],
         ),
         out_shape=shapes,
-        compiler_params=pltpu.CompilerParams(vmem_limit_bytes=40 << 20),
+        compiler_params=pltpu.CompilerParams(vmem_limit_bytes=VMEM_LIMIT),
         cost_estimate=pl.CostEstimate(
             flops=samples * atoms_here * width * width * 24,
             bytes_accessed=4 << 20,
@@ -371,12 +381,12 @@
         ),
     )(at, atom_single, atom_cond, edges, edges, *weights)
 
-    tile_spot = (1, 1, groups, tok_here, heads * GROUP)
+    tile_spot = (1, groups, tok_here, heads * GROUP)
 
     def tile_at(shift):
         def index(i, at):
             column = jnp.clip(at[0] + shift, 0, blocks - 1)
-            return at[0] // rows_pair * blocks + column, at[0] % rows_pair, 0, 0, 0
+            return at[0] // rows_pair * blocks + column, 0, 0, 0
 
         return pl.BlockSpec(tile_spot, index)
 
@@ -394,7 +404,7 @@
             ],
         ),
         out_shape=shapes[0],
-        compiler_params=pltpu.CompilerParams(vmem_limit_bytes=40 << 20),
+        compiler_params=pltpu.CompilerParams(vmem_limit_bytes=VMEM_LIMIT),
         cost_estimate=pl.CostEstimate(
             flops=samples * atoms_here * width * width * 12,
             bytes_accessed=4 << 20,

time: 88.5 us -> 39.4 us (0.45)
  blocking collectives: 50 us -> 0 us
  local copies, waits for them, and re-layouts: 18 us -> 5.27 us
  starting transfers between devices: 0 us -> 10.9 us
  waiting for transfers between devices: 0 us -> 3.29 us
    all_gather x2 -> x0, blocking collectives: 50 us -> none  [the longest x1 33.2 us: shards(): tiles = lax.all_gather(tiles, ('pair', 'atoms'))]
    unnamed x57 -> x5, local copies, waits for them, and re-layouts: 16.3 us -> 2.11 us
    all_to_all x0 -> x2, starting transfers between devices: none -> 10.9 us  [the longest x1 6.32 us: shards(): lax.all_to_all(jnp.where(above, head[None], tail[None]), 'atoms', 0, 0)]
    pallas_call x1, Pallas kernels: 11.8 us -> 6.31 us  [shards(): pl.pallas_call(functools.partial(attend_kernel, heads, blocks), grid_spec...]
    all_to_all x0 -> x2, waiting for transfers between devices: none -> 3.29 us  [the longest x1 1.85 us: shards(): tiles = lax.all_to_all(tiles, ('pair', 'atoms'), 0, 0)]
    pallas_call x1, Pallas kernels: 4.98 us -> 7.55 us  [shards(): pl.pallas_call(project_kernel_at, grid_spec=pltpu.PrefetchScalarGridSpec(...]
    pallas_call x1, Pallas kernels: 2.55 us -> 4.67 us  [pair_bias(): pl.pallas_call(functools.partial(pair_kernel, heads), grid=(rows // GROUP...]
    another operation x0 -> x1, local copies, waits for them, and re-layouts: none -> 1.64 us  [shards(): jnp.tile(tiles, (lax.axis_size('pair') * blocks // rows_pair, 1, 1, 1))]
  transfers between devices with their start and end apart: 0 -> 2, of which waited for: 0 -> 2; matrix products, arithmetic and copies ran while one was open for 0% -> 4% of each run, Pallas kernels for 0% -> 32%
where the time goes in v2:
time: 39.4 us; the launch traced here: 38.8 us
  Pallas kernels  18.5 us (47%)
  starting transfers between devices  10.9 us (28%)
  local copies, waits for them, and re-layouts  5.27 us (13%)
  waiting for transfers between devices  3.29 us (8%)
  other arithmetic  0.78 us (2%)
    pallas_call x1, Pallas kernels, shards(): pl.pallas_call(project_kernel_at, grid_spec=pltpu.PrefetchScalarGridSpec(...  7.55 us
    all_to_all x1, starting transfers between devices, shards(): lax.all_to_all(jnp.where(above, head[None], tail[None]), 'atoms', 0, 0)  6.32 us
    pallas_call x1, Pallas kernels, shards(): pl.pallas_call(functools.partial(attend_kernel, heads, blocks), grid_spec...  6.31 us
    pallas_call x1, Pallas kernels, pair_bias(): pl.pallas_call(functools.partial(pair_kernel, heads), grid=(rows // GROUP...  4.67 us
    all_to_all x1, starting transfers between devices, shards(): tiles = lax.all_to_all(tiles, ('pair', 'atoms'), 0, 0)  4.59 us
    unnamed x5, local copies, waits for them, and re-layouts  2.11 us
    all_to_all x1, waiting for transfers between devices, shards(): tiles = lax.all_to_all(tiles, ('pair', 'atoms'), 0, 0)  1.85 us
    another operation x1, local copies, waits for them, and re-layouts, shards(): jnp.tile(tiles, (lax.axis_size('pair') * blocks // rows_pair, 1, 1, 1))  1.64 us
  transfers between devices with their start and end apart: 2, of which 2 were waited for; matrix products, arithmetic and copies ran while one was open for 4% of the time, Pallas kernels for 32%

profile of v2, /device:TPU:0, one launch (start us, length us, event | category | flops | bytes accessed | tf_op | source)
XLA Modules:
  0.0 38.8 jit_solution(7912243886594932750)
XLA Ops:
  0.0 0.7 %slice_bitcast_fusion.1 = (bf16[1,48,128]{2,1,0:T(8,128)(2,1)S(1)}, bf16[1,48,128]{2,1,0:T(8,128)(2,1)S(1)}) fusion(bf16[512,128]{1,0:T(8,128)(2,1)} %refs_1_.1), kind=kLoop, calls=%fused_computation.4 | loop fusion | bytes 49152 | tf_op jit(solution)/shard_map/broadcast_in_dim | solution.py:326
  0.7 0.8 %fusion = (bf16[3,48,128]{2,1,0:T(8,128)(2,1)S(1)}, bf16[3,48,128]{2,1,0:T(8,128)(2,1)S(1)}) fusion(bf16[3,512,128]{2,1,0:T(8,128)(2,1)} %refs_0_.1), kind=kLoop, calls=%fused_computation.6 | loop fusion | bytes 147456 | tf_op jit(solution)/shard_map/slice | solution.py:326
  1.5 0.8 %broadcast_select_fusion = bf16[4,4,48,128]{3,2,1,0:T(8,128)(2,1)} fusion(pred[4]{0:T(512)(128)(4,1)S(1)} %iota_compare_fusion, bf16[4,48,128]{2,1,0:T(8,128)(2,1)S(1)} %get-tuple-element.22, bf16[4,48,128]{2,1,0:T(8,128)(2,1)S(1)} %get-tuple-element.21), kind=kLoop, calls=%fused_computation | loop fusion | flops 98304 | bytes 294916 | tf_op jit(solution)/shard_map/jit(_where)/select_n | solution.py:330
  2.3 6.3 %all-to-all-start = ((bf16[4,4,48,128]{3,2,1,0:T(8,128)(2,1)}), bf16[4,4,48,128]{3,2,1,0:T(8,128)(2,1)S(1)}, u32[]{:S(2)}, u32[]{:S(2)}) async-start(bf16[4,4,48,128]{3,2,1,0:T(8,128)(2,1)} %broadcast_select_fusion), calls=%async_computation | async-start | bytes 393216 | tf_op jit(solution)/shard_map/all_to_all | solution.py:330
  8.6 1.4 %copy.20.w_pair_ref = bf16[128,4]{1,0:T(8,128)(2,1)} copy(bf16[128,4]{0,1:T(4,128)(2,1)} %param.31) | data formatting | bytes 2048 | tf_op args[12]
  10.0 4.7 %shard_map.182 = bf16[2,2,64,128]{3,2,1,0:T(8,128)(2,1)} custom-call(bf16[128,64,128]{2,1,0:T(8,128)(2,1)} %pair_ref.1, bf16[128,4]{1,0:T(8,128)(2,1)} %copy.20.w_pair_ref), custom_call_target="tpu_custom_call" | custom-call | flops 536870912 | bytes 2097152 | tf_op jit(solution)/shard_map/pallas_call | solution.py:91
  14.7 1.4 %all-to-all-done.refs_2_.refs_3_ = bf16[4,4,48,128]{3,2,1,0:T(8,128)(2,1)S(1)} async-done(((bf16[4,4,48,128]{3,2,1,0:T(8,128)(2,1)}), bf16[4,4,48,128]{3,2,1,0:T(8,128)(2,1)S(1)}, u32[]{:S(2)}, u32[]{:S(2)}) %all-to-all-start) | async-done | bytes 196640 | tf_op jit(solution)/shard_map/all_to_all | solution.py:330
  16.1 0.0 copy-start.1
  16.1 1.6 %tile.4 = bf16[4,2,2,64,128]{4,3,2,1,0:T(8,128)(2,1)} broadcast(bf16[2,2,64,128]{3,2,1,0:T(8,128)(2,1)} %shard_map.182), dimensions={1,2,3,4} | broadcast | bytes 327680 | tf_op jit(solution)/shard_map/tile | solution.py:332
  17.8 4.6 %all-to-all-start.1 = ((bf16[8,2,64,128]{3,2,1,0:T(8,128)(2,1)}), bf16[8,2,64,128]{3,2,1,0:T(8,128)(2,1)S(1)}, u32[]{:S(2)}, u32[]{:S(2)}) async-start(bf16[8,2,64,128]{3,2,1,0:T(8,128)(2,1)} %bitcast.3), calls=%async_computation.1 | async-start | bytes 524288 | tf_op jit(solution)/shard_map/all_to_all | solution.py:333
  22.4 0.0 copy-done.1
  22.4 7.5 %shard_map.181 = (bf16[3,512,128]{2,1,0:T(8,128)(2,1)}, bf16[3,608,128]{2,1,0:T(8,128)(2,1)}, bf16[3,608,128]{2,1,0:T(8,128)(2,1)}, f32[3,512,128]{2,1,0:T(8,128...) custom-call(s32[1]{0:T(128)} %bitcast.at_ref, bf16[3,512,128]{2,1,0:T(8,128)(2,1)} %refs_0_.1, bf16[512,128]{1,0:T(8,128)(2,1)} %refs_1_.1, ...), custom_call_target="tpu_custom_call" | custom-call | flops 603979776 | bytes 4194304 | tf_op jit(solution)/shard_map/pallas_call | solution.py:361
  29.9 1.8 %all-to-all-done.1.prev_ref.own_ref.next_ref = bf16[8,2,64,128]{3,2,1,0:T(8,128)(2,1)S(1)} async-done(((bf16[8,2,64,128]{3,2,1,0:T(8,128)(2,1)}), bf16[8,2,64,128]{3,2,1,0:T(8,128)(2,1)S(1)}, u32[]{:S(2)}, u32[]{:S(2)}) %all-to-all-start.1) | async-done | bytes 262176 | tf_op jit(solution)/shard_map/all_to_all | solution.py:333
  31.8 0.0 copy-start
  31.8 0.7 %copy-done = bf16[8,2,64,128]{3,2,1,0:T(8,128)(2,1)} copy-done((bf16[8,2,64,128]{3,2,1,0:T(8,128)(2,1)}, bf16[8,2,64,128]{3,2,1,0:T(8,128)(2,1)S(1)}, u32[]{:S(2)}) %copy-start) | copy-done | bytes 262168
  32.5 6.3 %shard_map.183 = bf16[3,512,128]{2,1,0:T(8,128)(2,1)} custom-call(s32[1]{0:T(128)} %bitcast.at_ref, bf16[3,512,128]{2,1,0:T(8,128)(2,1)} %get-tuple-element.11.query_ref, bf16[3,608,128]{2,1,0:T(8,128)(2,1)} %get-tuple-element.12.key_ref, bf16[3,608,128]{2,1,0:T(8,128)(2,1)} %get-tuple-element.13.value_ref, f32[3,512,128]{2,1,0:T(8,128)} %get-tuple-element.14.gate_ref, ...), custom_call_target="tpu_custom_call" | custom-call | flops 301989888 | bytes 4194304 | tf_op jit(solution)/shard_map/pallas_call | solution.py:393
  (2 shorter events, 0.0 us)
Async XLA Ops:
  2.3 13.8 %all-to-all-start = ((bf16[4,4,48,128]{3,2,1,0:T(8,128)(2,1)}), bf16[4,4,48,128]{3,2,1,0:T(8,128)(2,1)S(1)}, u32[]{:S(2)}, u32[]{:S(2)}) async-start(bf16[4,4,48,128]{3,2,1,0:T(8,128)(2,1)} %broadcast_select_fusion), calls=%async_computation | async-start | bytes 393216 | tf_op jit(solution)/shard_map/all_to_all | solution.py:330
  16.1 6.2 %copy-start.1 = (bf16[4,4,48,128]{3,2,1,0:T(8,128)(2,1)}, bf16[4,4,48,128]{3,2,1,0:T(8,128)(2,1)S(1)}, u32[]{:S(2)}) copy-start(bf16[4,4,48,128]{3,2,1,0:T(8,128)(2,1)S(1)} %all-to-all-done.refs_2_.refs_3_) | copy-start | bytes 589828
  17.8 14.0 %all-to-all-start.1 = ((bf16[8,2,64,128]{3,2,1,0:T(8,128)(2,1)}), bf16[8,2,64,128]{3,2,1,0:T(8,128)(2,1)S(1)}, u32[]{:S(2)}, u32[]{:S(2)}) async-start(bf16[8,2,64,128]{3,2,1,0:T(8,128)(2,1)} %bitcast.3), calls=%async_computation.1 | async-start | bytes 524288 | tf_op jit(solution)/shard_map/all_to_all | solution.py:333
  31.8 0.7 %copy-start = (bf16[8,2,64,128]{3,2,1,0:T(8,128)(2,1)}, bf16[8,2,64,128]{3,2,1,0:T(8,128)(2,1)S(1)}, u32[]{:S(2)}) copy-start(bf16[8,2,64,128]{3,2,1,0:T(8,128)(2,1)S(1)} %all-to-all-done.1.prev_ref.own_ref.next_ref) | copy-start | bytes 786436

commit v3 on v2

v3 whole, which is shorter than its diff:
```python
import functools
import math

import jax
import jax.numpy as jnp
from jax import lax
from jax.experimental import pallas as pl
from jax.experimental.pallas import tpu as pltpu
from jax.sharding import PartitionSpec as P

Q_WIN = 32
K_WIN = 128
EDGE = 48
GROUP = 32

EPSILON = 1e-05
MASKED = -1e30
LOG2E = math.log2(math.e)
BF16 = jnp.bfloat16
F32 = jnp.float32
LAST = (((1,), (1,)), ((), ()))
VMEM_LIMIT = 32 << 20
IN_VMEM = pl.BlockSpec(memory_space=pltpu.VMEM)
IN_HBM = pl.BlockSpec(memory_space=pltpu.HBM)
IN_SMEM = pl.BlockSpec(memory_space=pltpu.SMEM)


def dot(a, b):
    return jnp.dot(a, b, preferred_element_type=F32)


def iota(shape, dim):
    return lax.broadcasted_iota(jnp.int32, shape, dim)


def twice(matrix):
    blank = jnp.zeros_like(matrix)
    return jnp.concatenate(
        [jnp.concatenate([matrix, blank], 1), jnp.concatenate([blank, matrix], 1)], 0
    )


def side_by_side(rows):
    half = rows.shape[0] // 2
    return jnp.concatenate([rows[:half], rows[half:]], 1)


def centring(width):
    same = iota((width, width), 0) == iota((width, width), 1)
    return jnp.where(same, 1.0 - 1.0 / width, -1.0 / width).astype(BF16)


def averaging(width):
    return jnp.full((width, width), 1.0 / width, BF16)


def layer_norm(rows):
    width = rows.shape[1]
    centred = dot(side_by_side(rows), twice(centring(width)))
    variance = dot((centred * centred).astype(BF16), twice(averaging(width)))
    normal = centred * lax.rsqrt(variance + EPSILON)
    return jnp.concatenate([normal[:, :width], normal[:, width:]], 0)


def sigmoid(values):
    return pl.reciprocal(1.0 + jnp.exp2(values * -LOG2E), approx=True)


def attn_norm(cond, single, ada):
    width = single.shape[-1]
    mixed = dot(cond, ada)
    return (sigmoid(mixed[:, :width])[None] * single + mixed[None, :, width:]).astype(BF16)


def pair_kernel(
    tok_here,
    blocks,
    packing,
    at_ref,
    w_pair_ref,
    pair_hbm,
    single_hbm,
    cond_hbm,
    *refs,
):
    count = sum(len(names) for names in packing)
    weights_hbm, refs = refs[:count], refs[count:]
    tiles_ref, edges_hbm, single_ref, cond_ref = refs[:4]
    packed_refs, refs = refs[4 : 4 + len(packing)], refs[4 + len(packing) :]
    pair_ref, pair_sem, sem = refs
    rows, cols, width = pair_ref.shape
    heads = w_pair_ref.shape[0]
    samples, atoms_here, _ = single_ref.shape
    group = GROUP
    chunks = rows // group
    half = group // 2
    lanes = heads * group
    device_at = at_ref[0]

    pair_copies = [
        pltpu.make_async_copy(
            pair_hbm.at[pl.ds(i * group, group)],
            pair_ref.at[pl.ds(i * group, group)],
            pair_sem.at[i],
        )
        for i in range(chunks)
    ]
    for copy in pair_copies:
        copy.start()
    moves = [(single_hbm, single_ref), (cond_hbm, cond_ref)]
    for place, cut in (
        (jnp.maximum(device_at - 1, 0), pl.ds(0, EDGE)),
        (jnp.minimum(device_at + 1, blocks - 1), pl.ds(atoms_here - EDGE, EDGE)),
    ):
        moves.append((single_hbm.at[:, cut], edges_hbm.at[place, pl.ds(0, samples)]))
        moves.append((cond_hbm.at[cut], edges_hbm.at[place, samples]))
    index = 0
    for names, packed in zip(packing, packed_refs):
        offset = 0
        for _ in names:
            source = weights_hbm[index]
            span = source.shape[1]
            moves.append((source, packed.at[:, pl.ds(offset, span)]))
            offset += span
            index += 1
    copies = [
        pltpu.make_async_copy(source, target, sem.at[i])
        for i, (source, target) in enumerate(moves)
    ]
    for copy in copies:
        copy.start()

    centre = twice(centring(width))
    w_pair = w_pair_ref[...].astype(F32)
    spread = jnp.concatenate(
        [jnp.broadcast_to(w_pair[h : h + 1], (group, width)) for h in range(heads)], 0
    )
    weight = spread.T.astype(BF16)
    mean = jnp.full((width, lanes), 1.0 / width, BF16)
    blank = jnp.zeros((width, lanes), BF16)
    mix = jnp.concatenate(
        [jnp.concatenate([weight, blank], 1), jnp.concatenate([blank, mean], 1)], 0
    )
    slot = iota((cols, 2 * lanes), 1) % group
    per_block = tok_here // group
    owners = rows // tok_here
    for chunk in range(chunks):
        pair_copies[chunk].wait()
        pair = pair_ref[chunk * group : (chunk + 1) * group].reshape(group * cols, width)
        centred = dot(side_by_side(pair), centre)
        rounded = centred.astype(BF16)
        squares = (centred * centred).astype(BF16)
        total = jnp.zeros((cols, 2 * lanes), F32)
        for part in range(2):
            cut = slice(part * width, (part + 1) * width)
            mixed = dot(jnp.concatenate([rounded[:, cut], squares[:, cut]], 1), mix)
            mixed = mixed.reshape(half, cols, 2 * lanes)
            for i in range(half):
                total = jnp.where(slot == part * half + i, mixed[i], total)
        bias = (total[:, :lanes] * lax.rsqrt(total[:, lanes:] + EPSILON)).astype(BF16)
        owner, part = divmod(chunk, per_block)
        for target in range(owner, tiles_ref.shape[0], owners):
            tiles_ref[target, part] = bias
    for copy in copies:
        copy.wait()


def project_kernel(
    single_ref,
    cond_ref,
    ada_attn,
    ada_trans,
    gates_ref,
    w_kv,
    w_qg,
    w_up,
    w_down,
    query_ref,
    key_ref,
    value_ref,
    gate_ref,
    open_ref,
    trans_ref,
):
    samples, atoms_here, width = single_ref.shape
    hidden_width = w_down.shape[0]
    step = math.gcd(atoms_here, 256)
    for start in range(0, atoms_here, step):
        at = slice(start, start + step)
        cond = layer_norm(cond_ref[at, :]).astype(BF16)
        single = layer_norm(single_ref[:, at, :].reshape(-1, width))
        single = single.reshape(samples, step, width)
        normed = attn_norm(cond, single, ada_attn[...]).reshape(-1, width)
        both = dot(normed, w_kv[...]).astype(BF16).reshape(samples, step, 2 * width)
        key_ref[:, at, :] = both[:, :, :width]
        value_ref[:, at, :] = both[:, :, width:]
        both = dot(normed, w_qg[...]).reshape(samples, step, 2 * width)
        query_ref[:, at, :] = both[:, :, :width].astype(BF16)
        gate_ref[:, at, :] = sigmoid(both[:, :, width:])
        gates = dot(cond, gates_ref[...])
        open_ref[at, :] = sigmoid(gates[:, :width])
        normed = attn_norm(cond, single, ada_trans[...]).reshape(-1, width)
        swish = dot(normed, w_up[:, :hidden_width])
        hidden = (swish * sigmoid(swish) * dot(normed, w_up[:, hidden_width:])).astype(BF16)
        down = dot(hidden, w_down[...]).reshape(samples, step, width)
        trans_ref[:, at, :] = sigmoid(gates[:, width:])[None] * down


def attend_kernel(
    heads,
    blocks,
    owners,
    at_ref,
    counts_ref,
    query_ref,
    own_key_ref,
    own_value_ref,
    gate_ref,
    open_ref,
    trans_ref,
    ada_attn,
    w_kv,
    w_out_ref,
    edges_hbm,
    tiles_hbm,
    out_ref,
    key_ref,
    value_ref,
    near_ref,
    gated_ref,
    edges_ref,
    tiles_ref,
    sem,
):
    samples, atoms_here, width = query_ref.shape
    tok_here = counts_ref.shape[1]
    head_dim = width // heads
    windows = atoms_here // Q_WIN
    lanes = heads * tok_here
    rows = heads * Q_WIN
    device_at = at_ref[0]
    ends = atoms_here * blocks
    around = [jnp.maximum(device_at - 1, 0), device_at, jnp.minimum(device_at + 1, blocks - 1)]

    copies = [
        pltpu.make_async_copy(edges_hbm.at[place], edges_ref.at[side], sem.at[side])
        for side, place in enumerate((around[0], around[2]))
    ]
    for i, place in enumerate(around):
        source = tiles_hbm.at[device_at // owners * blocks + place]
        copies.append(pltpu.make_async_copy(source, tiles_ref.at[i], sem.at[2 + i]))
    for copy in copies:
        copy.start()

    key_ref[:, EDGE : EDGE + atoms_here, :] = own_key_ref[...]
    value_ref[:, EDGE : EDGE + atoms_here, :] = own_value_ref[...]

    def bounds(block, token, reach):
        counts = counts_ref[pl.ds(block, 1), :].astype(F32).astype(BF16)
        counts = jnp.broadcast_to(counts, (8, tok_here))
        before = iota((tok_here, reach), 0)
        first = dot(counts, (before < token).astype(BF16))[:1]
        last = dot(counts, (before <= token).astype(BF16))[:1]
        return first.astype(jnp.int32), last.astype(jnp.int32)

    def hot_rows(block, count, offset):
        token = iota((tok_here, tok_here), 1)
        first, last = bounds(block, token, tok_here)
        position = iota((count, tok_here), 0) + offset
        return ((first <= position) & (position < last)).astype(F32).astype(BF16)

    spans = ((0, EDGE, atoms_here - EDGE), (EDGE, atoms_here, 0), (EDGE + atoms_here, EDGE, 0))
    hots = [hot_rows(block, span[1], span[2]) for block, span in zip(around, spans)]

    copies[0].wait()
    copies[1].wait()
    normal = layer_norm(edges_ref[...].reshape(-1, width))
    normal = normal.reshape(2, samples + 1, EDGE, width)
    for side, place in enumerate((0, EDGE + atoms_here)):
        cond = normal[side, samples].astype(BF16)
        normed = attn_norm(cond, normal[side, :samples], ada_attn[...])
        both = dot(normed.reshape(-1, width), w_kv[...]).astype(BF16)
        both = both.reshape(samples, EDGE, 2 * width)
        key_ref[:, place : place + EDGE, :] = both[:, :, :width]
        value_ref[:, place : place + EDGE, :] = both[:, :, width:]

    for i, (place, count, _) in enumerate(spans):
        copies[2 + i].wait()
        tile = jnp.concatenate([tiles_ref[i, part] for part in range(tok_here // GROUP)], 1)
        near_ref[place : place + count, :] = dot(hots[i], tile).astype(BF16)

    lane = iota((tok_here, lanes), 1)
    token = lane // (heads * GROUP) * GROUP + lane % GROUP
    first, last = bounds(device_at, token, lanes)
    lane_head = iota((rows, lanes), 1) // GROUP % heads
    row_head = iota((rows, lanes), 0) // Q_WIN
    same_head = (lane_head == row_head).astype(F32).astype(BF16)
    own_head = (iota((rows, width), 1) // head_dim == iota((rows, width), 0) // Q_WIN)
    own_head = own_head.astype(F32).astype(BF16)
    channel_head = iota((Q_WIN, 2 * width), 1) % width // head_dim
    ones = jnp.ones((K_WIN, width), BF16)
    scaling = LOG2E / math.sqrt(head_dim)

    batch = math.gcd(windows, 4)

    @pl.loop(0, windows // batch)
    def _(turn):
        starts = [pl.multiple_of((turn * batch + i) * Q_WIN, Q_WIN) for i in range(batch)]
        biases = []
        for start in starts:
            position = iota((Q_WIN, lanes), 0) + start
            hot = ((first <= position) & (position < last)).astype(F32).astype(BF16)
            pick = jnp.concatenate([hot] * heads, 0) * same_head
            bias = lax.dot_general(
                pick, near_ref[pl.ds(start, K_WIN), :], LAST, preferred_element_type=F32
            )
            key_at = iota((rows, K_WIN), 1) + (device_at * atoms_here + start - EDGE)
            biases.append(jnp.where((key_at >= 0) & (key_at < ends), bias * LOG2E, MASKED))
        units = [(sample, i) for i in range(batch) for sample in range(samples)]
        scores = []
        for sample, i in units:
            query = query_ref[sample, pl.ds(starts[i], Q_WIN), :]
            query = jnp.concatenate([query] * heads, 0) * own_head
            keys = key_ref[sample, pl.ds(starts[i], K_WIN), :]
            product = lax.dot_general(query, keys, LAST, preferred_element_type=F32)
            scores.append(product * scaling + biases[i])
        tops = [jnp.max(score, axis=-1, keepdims=True) for score in scores]
        raised = [jnp.exp2(score - top).astype(BF16) for score, top in zip(scores, tops)]
        for (sample, i), weight in zip(units, raised):
            values = value_ref[sample, pl.ds(starts[i], K_WIN), :]
            mixed = dot(weight, jnp.concatenate([values, ones], 1))
            picked = mixed[:Q_WIN]
            for head in range(1, heads):
                picked = jnp.where(
                    channel_head == head, mixed[head * Q_WIN : (head + 1) * Q_WIN], picked
                )
            attended = picked[:, :width] * pl.reciprocal(picked[:, width:], approx=True)
            gate = gate_ref[sample, pl.ds(starts[i], Q_WIN), :]
            gated_ref[sample, pl.ds(starts[i], Q_WIN), :] = (gate * attended).astype(BF16)

    for sample in range(samples):
        mixed = dot(gated_ref[sample], w_out_ref[...])
        out_ref[sample] = (open_ref[...] * mixed + trans_ref[sample]).astype(BF16)


def shards(
    atom_single,
    atom_cond,
    pair_cond,
    atom_counts,
    ada_attn_scale,
    ada_attn_shift,
    w_query,
    w_key,
    w_value,
    w_gate,
    w_out,
    attn_gate,
    w_pair,
    ada_trans_scale,
    ada_trans_shift,
    w_swish,
    w_linear,
    w_down,
    trans_gate,
):
    device_at = lax.axis_index("atoms")
    blocks = lax.axis_size("atoms")
    samples, atoms_here, width = atom_single.shape
    tok_here = atom_counts.shape[1]
    heads = w_pair.shape[1]
    groups = tok_here // GROUP
    pairs = lax.axis_size("pair")
    rows_pair = pair_cond.shape[0] // tok_here
    at = device_at.astype(jnp.int32).reshape(1)
    in_hbm = lambda array: pltpu.with_memory_space_constraint(array, pltpu.HBM)
    in_vmem = lambda array: pltpu.with_memory_space_constraint(array, pltpu.VMEM)

    packing = (
        (ada_attn_scale, ada_attn_shift),
        (ada_trans_scale, ada_trans_shift),
        (attn_gate, trans_gate),
        (w_key, w_value),
        (w_query, w_gate),
        (w_swish, w_linear),
        (w_down,),
        (w_out,),
    )
    flat = [array for arrays in packing for array in arrays]
    rows, cols, _ = pair_cond.shape
    lanes = heads * GROUP
    shapes = [
        jax.ShapeDtypeStruct((pairs * blocks, groups, cols, lanes), BF16),
        pltpu.HBM((blocks, samples + 1, EDGE, width), BF16),
        pltpu.VMEM(atom_single.shape, BF16),
        pltpu.VMEM(atom_cond.shape, BF16),
    ] + [
        pltpu.VMEM((arrays[0].shape[0], sum(a.shape[1] for a in arrays)), BF16)
        for arrays in packing
    ]
    made = pl.pallas_call(
        functools.partial(pair_kernel, tok_here, blocks, [(0,) * len(a) for a in packing]),
        in_specs=[IN_SMEM, IN_VMEM] + [IN_HBM] * (3 + len(flat)),
        out_specs=[IN_VMEM, IN_HBM] + [IN_VMEM] * (2 + len(packing)),
        out_shape=shapes,
        scratch_shapes=[
            pltpu.VMEM(pair_cond.shape, BF16),
            pltpu.SemaphoreType.DMA((rows // GROUP,)),
            pltpu.SemaphoreType.DMA((6 + len(flat),)),
        ],
        compiler_params=pltpu.CompilerParams(vmem_limit_bytes=VMEM_LIMIT),
        cost_estimate=pl.CostEstimate(
            flops=rows * cols * width * width * 4,
            bytes_accessed=rows * cols * width * 2,
            transcendentals=0,
        ),
    )(at, w_pair.T, *map(in_hbm, (pair_cond, atom_single, atom_cond, *flat)))
    tiles, edges, single, cond, *packed = made
    ada_attn, ada_trans, gates, w_kv, w_qg, w_up, w_down, w_out = packed
    tiles = lax.all_to_all(tiles, ("pair", "atoms"), 0, 0)
    edges = lax.all_to_all(edges, "atoms", 0, 0)

    wide = (samples, atoms_here, width)
    shapes = [pltpu.VMEM(wide, BF16)] * 3 + [
        pltpu.VMEM(wide, F32),
        pltpu.VMEM((atoms_here, width), F32),
        pltpu.VMEM(wide, F32),
    ]
    operands = (single, cond, ada_attn, ada_trans, gates, w_kv, w_qg, w_up, w_down)
    projected = pl.pallas_call(
        project_kernel,
        in_specs=[IN_VMEM] * len(operands),
        out_specs=[IN_VMEM] * len(shapes),
        out_shape=shapes,
        compiler_params=pltpu.CompilerParams(vmem_limit_bytes=VMEM_LIMIT),
        cost_estimate=pl.CostEstimate(
            flops=samples * atoms_here * width * width * 24,
            bytes_accessed=4 << 20,
            transcendentals=0,
        ),
    )(*map(in_vmem, operands))

    ext = atoms_here + 2 * EDGE
    operands = (*projected, ada_attn, w_kv, w_out)
    return pl.pallas_call(
        functools.partial(attend_kernel, heads, blocks, rows_pair),
        in_specs=[IN_SMEM, IN_VMEM] + [IN_VMEM] * len(operands) + [IN_HBM] * 2,
        out_specs=IN_VMEM,
        out_shape=jax.ShapeDtypeStruct(wide, BF16),
        scratch_shapes=[
            pltpu.VMEM((samples, ext, width), BF16),
            pltpu.VMEM((samples, ext, width), BF16),
            pltpu.VMEM((ext, heads * tok_here), BF16),
            pltpu.VMEM(wide, BF16),
            pltpu.VMEM((2, samples + 1, EDGE, width), BF16),
            pltpu.VMEM((3, groups, cols, lanes), BF16),
            pltpu.SemaphoreType.DMA((5,)),
        ],
        compiler_params=pltpu.CompilerParams(vmem_limit_bytes=VMEM_LIMIT),
        cost_estimate=pl.CostEstimate(
            flops=samples * atoms_here * width * width * 12,
            bytes_accessed=4 << 20,
            transcendentals=0,
        ),
    )(at, atom_counts, *map(in_vmem, operands), in_hbm(edges), in_hbm(tiles))


def solution(mesh):
    return jax.shard_map(
        shards,
        mesh=mesh,
        in_specs=(
            P(("groups", "pair", "samp"), "atoms", None),
            P(("groups", "atoms"), None),
            P(("groups", "pair"), "atoms", None),
            P("groups", None),
        )
        + (P(),) * 15,
        out_specs=P(("groups", "pair", "samp"), "atoms", None),
        check_vma=False,
    )
```

time: 39.4 us -> 42.4 us (1.076)
  blocking collectives: 0 us -> 14 us
  starting transfers between devices: 10.9 us -> 4.04 us
  Pallas kernels: 18.5 us -> 13.5 us
  local copies, waits for them, and re-layouts: 5.27 us -> 6.8 us
  other arithmetic: 0.78 us -> 0 us
    all_to_all x0 -> x1, blocking collectives: none -> 14 us  [shards(): edges = lax.all_to_all(edges, 'atoms', 0, 0)]
    all_to_all x1 -> x0, starting transfers between devices: 6.32 us -> none  [shards(): lax.all_to_all(jnp.where(above, head[None], tail[None]), 'atoms', 0, 0)]
    pallas_call x3, Pallas kernels: 18.5 us -> 13.5 us  [the longest x1 6.03 us: shards(): pl.pallas_call(functools.partial(attend_kernel, heads, blocks, rows_pair)...]
    unnamed x5 -> x20, local copies, waits for them, and re-layouts: 2.11 us -> 6.8 us
    another operation x1 -> x0, local copies, waits for them, and re-layouts: 1.64 us -> none  [shards(): jnp.tile(tiles, (lax.axis_size('pair') * blocks // rows_pair, 1, 1, 1))]
    all_to_all x1, waiting for transfers between devices: 1.85 us -> 3.42 us  [shards(): tiles = lax.all_to_all(tiles, ('pair', 'atoms'), 0, 0)]
    all_to_all x1 -> x0, waiting for transfers between devices: 1.44 us -> none  [shards(): lax.all_to_all(jnp.where(above, head[None], tail[None]), 'atoms', 0, 0)]
    slice x1 -> x0, local copies, waits for them, and re-layouts: 0.79 us -> none  [edge(): return jnp.concatenate([atom_single[:, cut], atom_cond[None, cut]], 0)]
  transfers between devices with their start and end apart: 2 -> 1, of which waited for: 2 -> 1; matrix products, arithmetic and copies ran while one was open for 4% -> 0% of each run, Pallas kernels for 32% -> 6%
where the time goes in v3:
time: 42.4 us; the launch traced here: 41.8 us
  blocking collectives  14 us (33%)
  Pallas kernels  13.5 us (32%)
  local copies, waits for them, and re-layouts  6.8 us (16%)
  starting transfers between devices  4.04 us (10%)
  waiting for transfers between devices  3.42 us (8%)
    all_to_all x1, blocking collectives, shards(): edges = lax.all_to_all(edges, 'atoms', 0, 0)  14 us
    unnamed x20, local copies, waits for them, and re-layouts  6.8 us
    pallas_call x1, Pallas kernels, shards(): pl.pallas_call(functools.partial(attend_kernel, heads, blocks, rows_pair)...  6.03 us
    pallas_call x1, Pallas kernels, shards(): pl.pallas_call(functools.partial(pair_kernel, tok_here, blocks, [(0,) * l...  5.02 us
    all_to_all x1, starting transfers between devices, shards(): tiles = lax.all_to_all(tiles, ('pair', 'atoms'), 0, 0)  4.04 us
    all_to_all x1, waiting for transfers between devices, shards(): tiles = lax.all_to_all(tiles, ('pair', 'atoms'), 0, 0)  3.42 us
    pallas_call x1, Pallas kernels, shards(): pl.pallas_call(project_kernel, in_specs=[IN_VMEM] * len(operands), out_sp...  2.44 us
  transfers between devices with their start and end apart: 1, of which 1 were waited for; matrix products, arithmetic and copies ran while one was open for 0% of the time, Pallas kernels for 6%

profile of v3, /device:TPU:0, one launch (start us, length us, event | category | flops | bytes accessed | tf_op | source)
XLA Modules:
  0.0 41.8 jit_solution(14485362064145909788)
XLA Ops:
  0.0 0.0 copy-start.1
  0.0 0.7 %copy-done.1 = bf16[128,4]{0,1:T(4,128)(2,1)S(1)} copy-done((bf16[128,4]{0,1:T(4,128)(2,1)S(1)}, bf16[128,4]{0,1:T(4,128)(2,1)}, u32[]{:S(2)}) %copy-start.1) | copy-done | bytes 1048
  0.7 5.0 %shard_map.181 = (bf16[8,2,64,128]{3,2,1,0:T(8,128)(2,1)}, bf16[4,4,48,128]{3,2,1,0:T(8,128)(2,1)}, bf16[3,512,128]{2,1,0:T(8,128)(2,1)S(1)}, bf16[512,128]{1,0:...) custom-call(s32[1]{0:T(128)} %bitcast.at_ref, ...), custom_call_target="tpu_custom_call" | custom-call | flops 536870912 | bytes 2097152 | tf_op jit(solution)/shard_map/pallas_call | solution.py:401
  5.7 0.0 copy-start.2
  5.7 0.7 %copy-done.2 = bf16[3,512,128]{2,1,0:T(8,128)(2,1)} copy-done((bf16[3,512,128]{2,1,0:T(8,128)(2,1)}, bf16[3,512,128]{2,1,0:T(8,128)(2,1)S(1)}, u32[]{:S(2)}) %copy-start.2) | copy-done | bytes 393240
  6.5 0.0 copy-start.4
  6.5 0.6 %copy-done.4 = bf16[128,256]{1,0:T(8,128)(2,1)} copy-done((bf16[128,256]{1,0:T(8,128)(2,1)}, bf16[128,256]{1,0:T(8,128)(2,1)S(1)}, u32[]{:S(2)}) %copy-start.4) | copy-done | bytes 65560
  7.1 0.0 copy-start.6
  7.1 0.6 %copy-done.6 = bf16[128,256]{1,0:T(8,128)(2,1)} copy-done((bf16[128,256]{1,0:T(8,128)(2,1)}, bf16[128,256]{1,0:T(8,128)(2,1)S(1)}, u32[]{:S(2)}) %copy-start.6) | copy-done | bytes 65560
  7.7 0.0 copy-start.8
  7.7 0.6 %copy-done.8 = bf16[256,128]{1,0:T(8,128)(2,1)} copy-done((bf16[256,128]{1,0:T(8,128)(2,1)}, bf16[256,128]{1,0:T(8,128)(2,1)S(1)}, u32[]{:S(2)}) %copy-start.8) | copy-done | bytes 65560
  8.3 0.0 copy-start
  8.3 14.0 %all_to_all.10.edges_hbm = bf16[4,4,48,128]{3,2,1,0:T(8,128)(2,1)} all-to-all(bf16[4,4,48,128]{3,2,1,0:T(8,128)(2,1)} %get-tuple-element.39), channel_id=1, replica_groups=mesh['groups'=2,'atoms'=4,'pair'=2,'samp'=2] {'atoms'}, dimensions={0} | all-to-all | bytes 393216 | tf_op jit(solution)/shard_map/all_to_all | solution.py:421
  22.4 4.0 %all-to-all-start.1 = ((bf16[8,2,64,128]{3,2,1,0:T(8,128)(2,1)}), bf16[8,2,64,128]{3,2,1,0:T(8,128)(2,1)}, u32[]{:S(2)}, u32[]{:S(2)}) async-start(bf16[8,2,64,128]{3,2,1,0:T(8,128)(2,1)} %get-tuple-element.40), calls=%async_computation.1 | async-start | bytes 524288 | tf_op jit(solution)/shard_map/all_to_all | solution.py:420
  26.4 0.0 copy-start.3
  26.4 1.0 %copy-done.3 = bf16[3,512,128]{2,1,0:T(8,128)(2,1)S(1)} copy-done((bf16[3,512,128]{2,1,0:T(8,128)(2,1)S(1)}, bf16[3,512,128]{2,1,0:T(8,128)(2,1)}, u32[]{:S(2)}) %copy-start.3) | copy-done | bytes 393240
  27.4 0.0 copy-start.5
  27.4 0.8 %copy-done.5 = bf16[128,256]{1,0:T(8,128)(2,1)S(1)} copy-done((bf16[128,256]{1,0:T(8,128)(2,1)S(1)}, bf16[128,256]{1,0:T(8,128)(2,1)}, u32[]{:S(2)}) %copy-start.5) | copy-done | bytes 65560
  28.3 0.0 copy-start.7
  28.3 0.8 %copy-done.7 = bf16[128,256]{1,0:T(8,128)(2,1)S(1)} copy-done((bf16[128,256]{1,0:T(8,128)(2,1)S(1)}, bf16[128,256]{1,0:T(8,128)(2,1)}, u32[]{:S(2)}) %copy-start.7) | copy-done | bytes 65560
  29.1 0.0 copy-start.9
  29.1 0.8 %copy-done.9 = bf16[256,128]{1,0:T(8,128)(2,1)S(1)} copy-done((bf16[256,128]{1,0:T(8,128)(2,1)S(1)}, bf16[256,128]{1,0:T(8,128)(2,1)}, u32[]{:S(2)}) %copy-start.9) | copy-done | bytes 65560
  29.9 2.4 %shard_map.182 = (bf16[3,512,128]{2,1,0:T(8,128)(2,1)S(1)}, bf16[3,512,128]{2,1,0:T(8,128)(2,1)S(1)}, bf16[3,512,128]{2,1,0:T(8,128)(2,1)S(1)}, f32[3,512,128]{2...) custom-call(bf16[3,512,128]{2,1,0:T(8,128)(2,1)S(1)} %copy-done.3, ...), custom_call_target="tpu_custom_call" | custom-call | flops 603979776 | bytes 4194304 | tf_op jit(solution)/shard_map/pallas_call | solution.py:430
  32.4 3.4 %all-to-all-done.1.tiles_hbm = bf16[8,2,64,128]{3,2,1,0:T(8,128)(2,1)} async-done(((bf16[8,2,64,128]{3,2,1,0:T(8,128)(2,1)}), bf16[8,2,64,128]{3,2,1,0:T(8,128)(2,1)}, u32[]{:S(2)}, u32[]{:S(2)}) %all-to-all-start.1) | async-done | bytes 262176 | tf_op jit(solution)/shard_map/all_to_all | solution.py:420
  35.8 0.0 copy-done
  35.8 6.0 %shard_map.183 = bf16[3,512,128]{2,1,0:T(8,128)(2,1)} custom-call(s32[1]{0:T(128)} %bitcast.at_ref, s32[4,64]{1,0:T(4,128)S(1)} %copy-done, bf16[3,512,128]{2,1,0:T(8,128)(2,1)S(1)} %get-tuple-element.32.query_ref, bf16[3,512,128]{2,1,0:T(8,128)(2,1)S(1)} %get-tuple-element.33.own_key_ref, bf16[3,512,128]{2,1,0:T(8,128)(2,1)S(1)} %get-tuple-element.34.own_value_ref, ...), custom_call_target="tpu_custom_call" | custom-call | flops 301989888 | bytes 4194304 | tf_op jit(solution)/shard_map/pallas_call | solution.py:445
Async XLA Ops:
  0.0 0.7 %copy-start.1 = (bf16[128,4]{0,1:T(4,128)(2,1)S(1)}, bf16[128,4]{0,1:T(4,128)(2,1)}, u32[]{:S(2)}) copy-start(bf16[128,4]{0,1:T(4,128)(2,1)} %param.31) | copy-start | bytes 3076
  5.7 0.7 %copy-start.2 = (bf16[3,512,128]{2,1,0:T(8,128)(2,1)}, bf16[3,512,128]{2,1,0:T(8,128)(2,1)S(1)}, u32[]{:S(2)}) copy-start(bf16[3,512,128]{2,1,0:T(8,128)(2,1)S(1)} %get-tuple-element.23.single_ref) | copy-start | bytes 1179652
  6.5 0.6 %copy-start.4 = (bf16[128,256]{1,0:T(8,128)(2,1)}, bf16[128,256]{1,0:T(8,128)(2,1)S(1)}, u32[]{:S(2)}) copy-start(bf16[128,256]{1,0:T(8,128)(2,1)S(1)} %get-tuple-element.27.gates_ref) | copy-start | bytes 196612
  7.1 0.6 %copy-start.6 = (bf16[128,256]{1,0:T(8,128)(2,1)}, bf16[128,256]{1,0:T(8,128)(2,1)S(1)}, u32[]{:S(2)}) copy-start(bf16[128,256]{1,0:T(8,128)(2,1)S(1)} %get-tuple-element.29.w_qg) | copy-start | bytes 196612
  7.7 0.6 %copy-start.8 = (bf16[256,128]{1,0:T(8,128)(2,1)}, bf16[256,128]{1,0:T(8,128)(2,1)S(1)}, u32[]{:S(2)}) copy-start(bf16[256,128]{1,0:T(8,128)(2,1)S(1)} %get-tuple-element.31.w_down) | copy-start | bytes 196612
  8.3 27.5 %copy-start = (s32[4,64]{1,0:T(4,128)S(1)}, s32[4,64]{1,0:T(4,128)}, u32[]{:S(2)}) copy-start(s32[4,64]{1,0:T(4,128)} %counts_ref.1) | copy-start | bytes 3076
  22.4 13.4 %all-to-all-start.1 = ((bf16[8,2,64,128]{3,2,1,0:T(8,128)(2,1)}), bf16[8,2,64,128]{3,2,1,0:T(8,128)(2,1)}, u32[]{:S(2)}, u32[]{:S(2)}) async-start(bf16[8,2,64,128]{3,2,1,0:T(8,128)(2,1)} %get-tuple-element.40), calls=%async_computation.1 | async-start | bytes 524288 | tf_op jit(solution)/shard_map/all_to_all | solution.py:420
  26.4 1.0 %copy-start.3 = (bf16[3,512,128]{2,1,0:T(8,128)(2,1)S(1)}, bf16[3,512,128]{2,1,0:T(8,128)(2,1)}, u32[]{:S(2)}) copy-start(bf16[3,512,128]{2,1,0:T(8,128)(2,1)} %copy-done.2) | copy-start | bytes 1179652
  27.4 0.8 %copy-start.5 = (bf16[128,256]{1,0:T(8,128)(2,1)S(1)}, bf16[128,256]{1,0:T(8,128)(2,1)}, u32[]{:S(2)}) copy-start(bf16[128,256]{1,0:T(8,128)(2,1)} %copy-done.4) | copy-start | bytes 196612
  28.3 0.8 %copy-start.7 = (bf16[128,256]{1,0:T(8,128)(2,1)S(1)}, bf16[128,256]{1,0:T(8,128)(2,1)}, u32[]{:S(2)}) copy-start(bf16[128,256]{1,0:T(8,128)(2,1)} %copy-done.6) | copy-start | bytes 196612
  29.1 0.8 %copy-start.9 = (bf16[256,128]{1,0:T(8,128)(2,1)S(1)}, bf16[256,128]{1,0:T(8,128)(2,1)}, u32[]{:S(2)}) copy-start(bf16[256,128]{1,0:T(8,128)(2,1)} %copy-done.8) | copy-start | bytes 196612

commit v4 on v3

--- a/solution.py
+++ b/solution.py
@@ -72,12 +72,44 @@
     return (sigmoid(mixed[:, :width])[None] * single + mixed[None, :, width:]).astype(BF16)
 
 
+def edge_kernel(
+    blocks, at_ref, single_hbm, cond_hbm, w_pair_hbm, edges_hbm, mix_ref, w_pair_ref, sem
+):
+    samples, atoms_here, width = single_hbm.shape
+    device_at = at_ref[0]
+    copies = []
+    for place, cut in (
+        (jnp.maximum(device_at - 1, 0), pl.ds(0, EDGE)),
+        (jnp.minimum(device_at + 1, blocks - 1), pl.ds(atoms_here - EDGE, EDGE)),
+    ):
+        for source, target in (
+            (single_hbm.at[:, cut], edges_hbm.at[place, pl.ds(0, samples)]),
+            (cond_hbm.at[cut], edges_hbm.at[place, samples]),
+        ):
+            copies.append(pltpu.make_async_copy(source, target, sem.at[len(copies)]))
+    copies.append(pltpu.make_async_copy(w_pair_hbm, w_pair_ref, sem.at[len(copies)]))
+    for copy in copies:
+        copy.start()
+    copies.pop().wait()
+    heads = w_pair_ref.shape[0]
+    w_pair = w_pair_ref[...].astype(F32)
+    spread = jnp.concatenate(
+        [jnp.broadcast_to(w_pair[h : h + 1], (GROUP, width)) for h in range(heads)], 0
+    )
+    weight = spread.T.astype(BF16)
+    mean = jnp.full((width, heads * GROUP), 1.0 / width, BF16)
+    blank = jnp.zeros((width, heads * GROUP), BF16)
+    mix_ref[...] = jnp.concatenate(
+        [jnp.concatenate([weight, blank], 1), jnp.concatenate([blank, mean], 1)], 0
+    )
+    for copy in copies:
+        copy.wait()
+
+
 def pair_kernel(
     tok_here,
-    blocks,
     packing,
-    at_ref,
-    w_pair_ref,
+    mix_ref,
     pair_hbm,
     single_hbm,
     cond_hbm,
@@ -85,35 +117,22 @@
 ):
     count = sum(len(names) for names in packing)
     weights_hbm, refs = refs[:count], refs[count:]
-    tiles_ref, edges_hbm, single_ref, cond_ref = refs[:4]
-    packed_refs, refs = refs[4 : 4 + len(packing)], refs[4 + len(packing) :]
+    tiles_ref, single_ref, cond_ref = refs[:3]
+    packed_refs, refs = refs[3 : 3 + len(packing)], refs[3 + len(packing) :]
     pair_ref, pair_sem, sem = refs
     rows, cols, width = pair_ref.shape
-    heads = w_pair_ref.shape[0]
-    samples, atoms_here, _ = single_ref.shape
     group = GROUP
     chunks = rows // group
     half = group // 2
-    lanes = heads * group
-    device_at = at_ref[0]
-
-    pair_copies = [
-        pltpu.make_async_copy(
-            pair_hbm.at[pl.ds(i * group, group)],
-            pair_ref.at[pl.ds(i * group, group)],
-            pair_sem.at[i],
-        )
-        for i in range(chunks)
-    ]
-    for copy in pair_copies:
-        copy.start()
+    lanes = mix_ref.shape[1] // 2
+
+    def pair_copy(i):
+        at = pl.ds(i * group, group)
+        return pltpu.make_async_copy(pair_hbm.at[at], pair_ref.at[at], pair_sem.at[i])
+
+    for i in range(chunks):
+        pair_copy(i).start()
     moves = [(single_hbm, single_ref), (cond_hbm, cond_ref)]
-    for place, cut in (
-        (jnp.maximum(device_at - 1, 0), pl.ds(0, EDGE)),
-        (jnp.minimum(device_at + 1, blocks - 1), pl.ds(atoms_here - EDGE, EDGE)),
-    ):
-        moves.append((single_hbm.at[:, cut], edges_hbm.at[place, pl.ds(0, samples)]))
-        moves.append((cond_hbm.at[cut], edges_hbm.at[place, samples]))
     index = 0
     for names, packed in zip(packing, packed_refs):
         offset = 0
@@ -131,36 +150,28 @@
         copy.start()
 
     centre = twice(centring(width))
-    w_pair = w_pair_ref[...].astype(F32)
-    spread = jnp.concatenate(
-        [jnp.broadcast_to(w_pair[h : h + 1], (group, width)) for h in range(heads)], 0
-    )
-    weight = spread.T.astype(BF16)
-    mean = jnp.full((width, lanes), 1.0 / width, BF16)
-    blank = jnp.zeros((width, lanes), BF16)
-    mix = jnp.concatenate(
-        [jnp.concatenate([weight, blank], 1), jnp.concatenate([blank, mean], 1)], 0
-    )
     slot = iota((cols, 2 * lanes), 1) % group
     per_block = tok_here // group
     owners = rows // tok_here
-    for chunk in range(chunks):
-        pair_copies[chunk].wait()
-        pair = pair_ref[chunk * group : (chunk + 1) * group].reshape(group * cols, width)
+
+    @pl.loop(0, chunks)
+    def _(chunk):
+        pair_copy(chunk).wait()
+        pair = pair_ref[pl.ds(chunk * group, group)].reshape(group * cols, width)
         centred = dot(side_by_side(pair), centre)
         rounded = centred.astype(BF16)
         squares = (centred * centred).astype(BF16)
         total = jnp.zeros((cols, 2 * lanes), F32)
         for part in range(2):
             cut = slice(part * width, (part + 1) * width)
-            mixed = dot(jnp.concatenate([rounded[:, cut], squares[:, cut]], 1), mix)
+            mixed = dot(jnp.concatenate([rounded[:, cut], squares[:, cut]], 1), mix_ref[...])
             mixed = mixed.reshape(half, cols, 2 * lanes)
             for i in range(half):
                 total = jnp.where(slot == part * half + i, mixed[i], total)
         bias = (total[:, :lanes] * lax.rsqrt(total[:, lanes:] + EPSILON)).astype(BF16)
-        owner, part = divmod(chunk, per_block)
-        for target in range(owner, tiles_ref.shape[0], owners):
-            tiles_ref[target, part] = bias
+        for target in range(0, tiles_ref.shape[0], owners):
+            tiles_ref[target + chunk // per_block, chunk % per_block] = bias
+
     for copy in copies:
         copy.wait()
 
@@ -196,14 +207,14 @@
         value_ref[:, at, :] = both[:, :, width:]
         both = dot(normed, w_qg[...]).reshape(samples, step, 2 * width)
         query_ref[:, at, :] = both[:, :, :width].astype(BF16)
-        gate_ref[:, at, :] = sigmoid(both[:, :, width:])
+        gate_ref[:, at, :] = sigmoid(both[:, :, width:]).astype(BF16)
         gates = dot(cond, gates_ref[...])
-        open_ref[at, :] = sigmoid(gates[:, :width])
+        open_ref[at, :] = sigmoid(gates[:, :width]).astype(BF16)
         normed = attn_norm(cond, single, ada_trans[...]).reshape(-1, width)
         swish = dot(normed, w_up[:, :hidden_width])
         hidden = (swish * sigmoid(swish) * dot(normed, w_up[:, hidden_width:])).astype(BF16)
         down = dot(hidden, w_down[...]).reshape(samples, step, width)
-        trans_ref[:, at, :] = sigmoid(gates[:, width:])[None] * down
+        trans_ref[:, at, :] = (sigmoid(gates[:, width:])[None] * down).astype(BF16)
 
 
 def attend_kernel(
@@ -221,16 +232,13 @@
     ada_attn,
     w_kv,
     w_out_ref,
-    edges_hbm,
-    tiles_hbm,
+    edges_ref,
+    tiles_ref,
     out_ref,
     key_ref,
     value_ref,
     near_ref,
     gated_ref,
-    edges_ref,
-    tiles_ref,
-    sem,
 ):
     samples, atoms_here, width = query_ref.shape
     tok_here = counts_ref.shape[1]
@@ -242,16 +250,6 @@
     ends = atoms_here * blocks
     around = [jnp.maximum(device_at - 1, 0), device_at, jnp.minimum(device_at + 1, blocks - 1)]
 
-    copies = [
-        pltpu.make_async_copy(edges_hbm.at[place], edges_ref.at[side], sem.at[side])
-        for side, place in enumerate((around[0], around[2]))
-    ]
-    for i, place in enumerate(around):
-        source = tiles_hbm.at[device_at // owners * blocks + place]
-        copies.append(pltpu.make_async_copy(source, tiles_ref.at[i], sem.at[2 + i]))
-    for copy in copies:
-        copy.start()
-
     key_ref[:, EDGE : EDGE + atoms_here, :] = own_key_ref[...]
     value_ref[:, EDGE : EDGE + atoms_here, :] = own_value_ref[...]
 
@@ -272,9 +270,8 @@
     spans = ((0, EDGE, atoms_here - EDGE), (EDGE, atoms_here, 0), (EDGE + atoms_here, EDGE, 0))
     hots = [hot_rows(block, span[1], span[2]) for block, span in zip(around, spans)]
 
-    copies[0].wait()
-    copies[1].wait()
-    normal = layer_norm(edges_ref[...].reshape(-1, width))
+    edges = jnp.concatenate([edges_ref[around[0]], edges_ref[around[2]]], 0)
+    normal = layer_norm(edges.reshape(-1, width))
     normal = normal.reshape(2, samples + 1, EDGE, width)
     for side, place in enumerate((0, EDGE + atoms_here)):
         cond = normal[side, samples].astype(BF16)
@@ -285,8 +282,10 @@
         value_ref[:, place : place + EDGE, :] = both[:, :, width:]
 
     for i, (place, count, _) in enumerate(spans):
-        copies[2 + i].wait()
-        tile = jnp.concatenate([tiles_ref[i, part] for part in range(tok_here // GROUP)], 1)
+        place_from = device_at // owners * blocks + around[i]
+        tile = jnp.concatenate(
+            [tiles_ref[place_from, part] for part in range(tok_here // GROUP)], 1
+        )
         near_ref[place : place + count, :] = dot(hots[i], tile).astype(BF16)
 
     lane = iota((tok_here, lanes), 1)
@@ -335,12 +334,12 @@
                     channel_head == head, mixed[head * Q_WIN : (head + 1) * Q_WIN], picked
                 )
             attended = picked[:, :width] * pl.reciprocal(picked[:, width:], approx=True)
-            gate = gate_ref[sample, pl.ds(starts[i], Q_WIN), :]
+            gate = gate_ref[sample, pl.ds(starts[i], Q_WIN), :].astype(F32)
             gated_ref[sample, pl.ds(starts[i], Q_WIN), :] = (gate * attended).astype(BF16)
 
     for sample in range(samples):
         mixed = dot(gated_ref[sample], w_out_ref[...])
-        out_ref[sample] = (open_ref[...] * mixed + trans_ref[sample]).astype(BF16)
+        out_ref[sample] = (open_ref[...].astype(F32) * mixed + trans_ref[sample].astype(F32)).astype(BF16)
 
 
 def shards(
@@ -390,23 +389,33 @@
     rows, cols, _ = pair_cond.shape
     lanes = heads * GROUP
     shapes = [
-        jax.ShapeDtypeStruct((pairs * blocks, groups, cols, lanes), BF16),
-        pltpu.HBM((blocks, samples + 1, EDGE, width), BF16),
+        pltpu.VMEM((pairs * blocks, groups, cols, lanes), BF16),
         pltpu.VMEM(atom_single.shape, BF16),
         pltpu.VMEM(atom_cond.shape, BF16),
     ] + [
         pltpu.VMEM((arrays[0].shape[0], sum(a.shape[1] for a in arrays)), BF16)
         for arrays in packing
     ]
+    edges, mix = pl.pallas_call(
+        functools.partial(edge_kernel, blocks),
+        in_specs=[IN_SMEM] + [IN_HBM] * 3,
+        out_specs=[IN_HBM, IN_VMEM],
+        out_shape=[
+            pltpu.HBM((blocks, samples + 1, EDGE, width), BF16),
+            pltpu.VMEM((2 * width, 2 * lanes), BF16),
+        ],
+        scratch_shapes=[pltpu.VMEM((heads, width), BF16), pltpu.SemaphoreType.DMA((5,))],
+    )(at, *map(in_hbm, (atom_single, atom_cond, w_pair.T)))
+    edges = lax.all_to_all(edges, "atoms", 0, 0)
     made = pl.pallas_call(
-        functools.partial(pair_kernel, tok_here, blocks, [(0,) * len(a) for a in packing]),
-        in_specs=[IN_SMEM, IN_VMEM] + [IN_HBM] * (3 + len(flat)),
-        out_specs=[IN_VMEM, IN_HBM] + [IN_VMEM] * (2 + len(packing)),
+        functools.partial(pair_kernel, tok_here, [(0,) * len(a) for a in packing]),
+        in_specs=[IN_VMEM] + [IN_HBM] * (3 + len(flat)),
+        out_specs=[IN_VMEM] * (3 + len(packing)),
         out_shape=shapes,
         scratch_shapes=[
             pltpu.VMEM(pair_cond.shape, BF16),
             pltpu.SemaphoreType.DMA((rows // GROUP,)),
-            pltpu.SemaphoreType.DMA((6 + len(flat),)),
+            pltpu.SemaphoreType.DMA((2 + len(flat),)),
         ],
         compiler_params=pltpu.CompilerParams(vmem_limit_bytes=VMEM_LIMIT),
         cost_estimate=pl.CostEstimate(
@@ -414,17 +423,15 @@
             bytes_accessed=rows * cols * width * 2,
             transcendentals=0,
         ),
-    )(at, w_pair.T, *map(in_hbm, (pair_cond, atom_single, atom_cond, *flat)))
-    tiles, edges, single, cond, *packed = made
+    )(in_vmem(mix), *map(in_hbm, (pair_cond, atom_single, atom_cond, *flat)))
+    tiles, single, cond, *packed = made
     ada_attn, ada_trans, gates, w_kv, w_qg, w_up, w_down, w_out = packed
     tiles = lax.all_to_all(tiles, ("pair", "atoms"), 0, 0)
-    edges = lax.all_to_all(edges, "atoms", 0, 0)
 
     wide = (samples, atoms_here, width)
-    shapes = [pltpu.VMEM(wide, BF16)] * 3 + [
-        pltpu.VMEM(wide, F32),
-        pltpu.VMEM((atoms_here, width), F32),
-        pltpu.VMEM(wide, F32),
+    shapes = [pltpu.VMEM(wide, BF16)] * 4 + [
+        pltpu.VMEM((atoms_here, width), BF16),
+        pltpu.VMEM(wide, BF16),
     ]
     operands = (single, cond, ada_attn, ada_trans, gates, w_kv, w_qg, w_up, w_down)
     projected = pl.pallas_call(
@@ -432,6 +439,7 @@
         in_specs=[IN_VMEM] * len(operands),
         out_specs=[IN_VMEM] * len(shapes),
         out_shape=shapes,
+        input_output_aliases={0: 0, 1: 4},
         compiler_params=pltpu.CompilerParams(vmem_limit_bytes=VMEM_LIMIT),
         cost_estimate=pl.CostEstimate(
             flops=samples * atoms_here * width * width * 24,
@@ -441,10 +449,10 @@
     )(*map(in_vmem, operands))
 
     ext = atoms_here + 2 * EDGE
-    operands = (*projected, ada_attn, w_kv, w_out)
+    operands = (*projected, ada_attn, w_kv, w_out, edges, tiles)
     return pl.pallas_call(
         functools.partial(attend_kernel, heads, blocks, rows_pair),
-        in_specs=[IN_SMEM, IN_VMEM] + [IN_VMEM] * len(operands) + [IN_HBM] * 2,
+        in_specs=[IN_SMEM] + [IN_VMEM] * (1 + len(operands)),
         out_specs=IN_VMEM,
         out_shape=jax.ShapeDtypeStruct(wide, BF16),
         scratch_shapes=[
@@ -452,9 +460,6 @@
             pltpu.VMEM((samples, ext, width), BF16),
             pltpu.VMEM((ext, heads * tok_here), BF16),
             pltpu.VMEM(wide, BF16),
-            pltpu.VMEM((2, samples + 1, EDGE, width), BF16),
-            pltpu.VMEM((3, groups, cols, lanes), BF16),
-            pltpu.SemaphoreType.DMA((5,)),
         ],
         compiler_params=pltpu.CompilerParams(vmem_limit_bytes=VMEM_LIMIT),
         cost_estimate=pl.CostEstimate(
@@ -462,7 +467,7 @@
             bytes_accessed=4 << 20,
             transcendentals=0,
         ),
-    )(at, atom_counts, *map(in_vmem, operands), in_hbm(edges), in_hbm(tiles))
+    )(at, atom_counts, *map(in_vmem, operands))
 
 
 def solution(mesh):

time: 42.4 us -> 36.1 us (0.85)
  blocking collectives: 14 us -> 0 us
  local copies, waits for them, and re-layouts: 6.8 us -> 0.01 us
  waiting for transfers between devices: 3.42 us -> 9.6 us
  starting transfers between devices: 4.04 us -> 9.95 us
  Pallas kernels: 13.5 us -> 16.1 us
    all_to_all x1 -> x0, blocking collectives: 14 us -> none  [shards(): edges = lax.all_to_all(edges, 'atoms', 0, 0)]
    unnamed x20 -> x2, local copies, waits for them, and re-layouts: 6.8 us -> 0.01 us
    all_to_all x0 -> x1, starting transfers between devices: none -> 6.33 us  [shards(): edges = lax.all_to_all(edges, 'atoms', 0, 0)]
    pallas_call x1 -> x2, Pallas kernels: 5.02 us -> 8.93 us  [the longest x1 4.81 us: shards(): pl.pallas_call(functools.partial(pair_kernel, tok_here, [(0,) * len(a) fo...]
    all_to_all x1, waiting for transfers between devices: 3.42 us -> 6.92 us  [shards(): tiles = lax.all_to_all(tiles, ('pair', 'atoms'), 0, 0)]
    all_to_all x0 -> x1, waiting for transfers between devices: none -> 2.68 us  [shards(): edges = lax.all_to_all(edges, 'atoms', 0, 0)]
    pallas_call x1, Pallas kernels: 6.03 us -> 4.76 us  [shards(): pl.pallas_call(functools.partial(attend_kernel, heads, blocks, rows_pair)...]
  transfers between devices with their start and end apart: 1 -> 2, of which waited for: 1 -> 2; matrix products, arithmetic and copies ran while one was open for 0% -> 0% of each run, Pallas kernels for 6% -> 20%
where the time goes in v4:
time: 36.1 us; the launch traced here: 35.7 us
  Pallas kernels  16.1 us (45%)
  starting transfers between devices  9.95 us (28%)
  waiting for transfers between devices  9.6 us (27%)
    all_to_all x1, waiting for transfers between devices, shards(): tiles = lax.all_to_all(tiles, ('pair', 'atoms'), 0, 0)  6.92 us
    all_to_all x1, starting transfers between devices, shards(): edges = lax.all_to_all(edges, 'atoms', 0, 0)  6.33 us
    pallas_call x1, Pallas kernels, shards(): pl.pallas_call(functools.partial(pair_kernel, tok_here, [(0,) * len(a) fo...  4.81 us
    pallas_call x1, Pallas kernels, shards(): pl.pallas_call(functools.partial(attend_kernel, heads, blocks, rows_pair)...  4.76 us
    pallas_call x1, Pallas kernels, shards(): pl.pallas_call(functools.partial(edge_kernel, blocks), in_specs=[IN_SMEM]...  4.12 us
    all_to_all x1, starting transfers between devices, shards(): tiles = lax.all_to_all(tiles, ('pair', 'atoms'), 0, 0)  3.62 us
    all_to_all x1, waiting for transfers between devices, shards(): edges = lax.all_to_all(edges, 'atoms', 0, 0)  2.68 us
    pallas_call x1, Pallas kernels, shards(): pl.pallas_call(project_kernel, in_specs=[IN_VMEM] * len(operands), out_sp...  2.45 us
  transfers between devices with their start and end apart: 2, of which 2 were waited for; matrix products, arithmetic and copies ran while one was open for 0% of the time, Pallas kernels for 20%

profile of v4, /device:TPU:0, one launch (start us, length us, event | category | flops | bytes accessed | tf_op | source)
XLA Modules:
  0.0 35.7 jit_solution(5155544473859331703)
XLA Ops:
  0.0 4.1 %shard_map.181 = (bf16[4,4,48,128]{3,2,1,0:T(8,128)(2,1)}, bf16[256,256]{1,0:T(8,128)(2,1)S(1)}) custom-call(s32[1]{0:T(128)} %bitcast.at_ref, bf16[3,512,128]{2,1,0:T(8,128)(2,1)} %single_hbm.3, bf16[512,128]{1,0:T(8,128)(2,1)} %cond_hbm.3, bf16[4,128]{1,0:T(4,128)(2,1)} %bitcast.2), custom_call_target="tpu_custom_call" | custom-call | tf_op jit(solution)/shard_map/pallas_call | solution.py:399
  4.1 6.3 %all-to-all-start = ((bf16[4,4,48,128]{3,2,1,0:T(8,128)(2,1)}), bf16[4,4,48,128]{3,2,1,0:T(8,128)(2,1)S(1)}, u32[]{:S(2)}, u32[]{:S(2)}) async-start(bf16[4,4,48,128]{3,2,1,0:T(8,128)(2,1)} %get-tuple-element.41), calls=%async_computation | async-start | bytes 393216 | tf_op jit(solution)/shard_map/all_to_all | solution.py:409
  10.5 4.8 %shard_map.182 = (bf16[8,2,64,128]{3,2,1,0:T(8,128)(2,1)}, bf16[3,512,128]{2,1,0:T(8,128)(2,1)S(1)}, bf16[512,128]{1,0:T(8,128)(2,1)S(1)}, bf16[128,256]{1,0:T(8...) custom-call(bf16[256,256]{1,0:T(8,128)(2,1)S(1)} %get-tuple-element., ...), custom_call_target="tpu_custom_call" | custom-call | flops 536870912 | bytes 2097152 | tf_op jit(solution)/shard_map/pallas_call | solution.py:410
  15.3 0.0 copy-start
  15.3 2.7 %all-to-all-done.edges_ref = bf16[4,4,48,128]{3,2,1,0:T(8,128)(2,1)S(1)} async-done(((bf16[4,4,48,128]{3,2,1,0:T(8,128)(2,1)}), bf16[4,4,48,128]{3,2,1,0:T(8,128)(2,1)S(1)}, u32[]{:S(2)}, u32[]{:S(2)}) %all-to-all-start) | async-done | bytes 196640 | tf_op jit(solution)/shard_map/all_to_all | solution.py:409
  18.0 3.6 %all-to-all-start.1 = ((bf16[8,2,64,128]{3,2,1,0:T(8,128)(2,1)}), bf16[8,2,64,128]{3,2,1,0:T(8,128)(2,1)S(1)}, u32[]{:S(2)}, u32[]{:S(2)}) async-start(bf16[8,2,64,128]{3,2,1,0:T(8,128)(2,1)} %get-tuple-element.42), calls=%async_computation.1 | async-start | bytes 524288 | tf_op jit(solution)/shard_map/all_to_all | solution.py:429
  21.6 2.5 %shard_map.183 = (bf16[3,512,128]{2,1,0:T(8,128)(2,1)S(1)}, bf16[3,512,128]{2,1,0:T(8,128)(2,1)S(1)}, bf16[3,512,128]{2,1,0:T(8,128)(2,1)S(1)}, bf16[3,512,128]{...) custom-call(bf16[3,512,128]{2,1,0:T(8,128)(2,1)S(1)} %get-tuple-elem, ...), custom_call_target="tpu_custom_call", output_to_operand_aliasing={{0}: (0, {}), {4}: (1, {})} | custom-call | flops 603979776 | bytes 4194304 | tf_op jit(solution)/shard_map/pallas_call | solution.py:437
  24.1 6.9 %all-to-all-done.1.tiles_ref = bf16[8,2,64,128]{3,2,1,0:T(8,128)(2,1)S(1)} async-done(((bf16[8,2,64,128]{3,2,1,0:T(8,128)(2,1)}), bf16[8,2,64,128]{3,2,1,0:T(8,128)(2,1)S(1)}, u32[]{:S(2)}, u32[]{:S(2)}) %all-to-all-start.1) | async-done | bytes 262176 | tf_op jit(solution)/shard_map/all_to_all | solution.py:429
  31.0 0.0 copy-done
  31.0 4.8 %shard_map.184 = bf16[3,512,128]{2,1,0:T(8,128)(2,1)} custom-call(s32[1]{0:T(128)} %bitcast.at_ref, s32[4,64]{1,0:T(4,128)S(1)} %copy-done, bf16[3,512,128]{2,1,0:T(8,128)(2,1)S(1)} %get-tuple-element.34.query_ref, bf16[3,512,128]{2,1,0:T(8,128)(2,1)S(1)} %get-tuple-element.35.own_key_ref, bf16[3,512,128]{2,1,0:T(8,128)(2,1)S(1)} %get-tuple-element.36.own_value_ref, ...), custom_call_target="tpu_custom_call" | custom-call | flops 301989888 | bytes 4194304 | tf_op jit(solution)/shard_map/pallas_call | solution.py:453
Async XLA Ops:
  4.1 13.8 %all-to-all-start = ((bf16[4,4,48,128]{3,2,1,0:T(8,128)(2,1)}), bf16[4,4,48,128]{3,2,1,0:T(8,128)(2,1)S(1)}, u32[]{:S(2)}, u32[]{:S(2)}) async-start(bf16[4,4,48,128]{3,2,1,0:T(8,128)(2,1)} %get-tuple-element.41), calls=%async_computation | async-start | bytes 393216 | tf_op jit(solution)/shard_map/all_to_all | solution.py:409
  15.3 15.7 %copy-start = (s32[4,64]{1,0:T(4,128)S(1)}, s32[4,64]{1,0:T(4,128)}, u32[]{:S(2)}) copy-start(s32[4,64]{1,0:T(4,128)} %counts_ref.1) | copy-start | bytes 3076
  18.0 13.0 %all-to-all-start.1 = ((bf16[8,2,64,128]{3,2,1,0:T(8,128)(2,1)}), bf16[8,2,64,128]{3,2,1,0:T(8,128)(2,1)S(1)}, u32[]{:S(2)}, u32[]{:S(2)}) async-start(bf16[8,2,64,128]{3,2,1,0:T(8,128)(2,1)} %get-tuple-element.42), calls=%async_computation.1 | async-start | bytes 524288 | tf_op jit(solution)/shard_map/all_to_all | solution.py:429

commit v5 on v3

--- a/solution.py
+++ b/solution.py
@@ -72,52 +72,34 @@
     return (sigmoid(mixed[:, :width])[None] * single + mixed[None, :, width:]).astype(BF16)
 
 
-def pair_kernel(
-    tok_here,
-    blocks,
-    packing,
-    at_ref,
-    w_pair_ref,
-    pair_hbm,
-    single_hbm,
-    cond_hbm,
-    *refs,
-):
-    count = sum(len(names) for names in packing)
+def pair_kernel(tok_here, packing, w_pair_hbm, pair_hbm, single_hbm, cond_hbm, *refs):
+    count = sum(packing)
     weights_hbm, refs = refs[:count], refs[count:]
-    tiles_ref, edges_hbm, single_ref, cond_ref = refs[:4]
-    packed_refs, refs = refs[4 : 4 + len(packing)], refs[4 + len(packing) :]
-    pair_ref, pair_sem, sem = refs
+    tiles_ref, down_ref, up_ref, single_ref, cond_ref = refs[:5]
+    packed_refs, refs = refs[5 : 5 + len(packing)], refs[5 + len(packing) :]
+    w_pair_ref, pair_ref, pair_sem, sem = refs
     rows, cols, width = pair_ref.shape
     heads = w_pair_ref.shape[0]
     samples, atoms_here, _ = single_ref.shape
     group = GROUP
-    chunks = rows // group
+    lanes = heads * group
     half = group // 2
-    lanes = heads * group
-    device_at = at_ref[0]
-
-    pair_copies = [
-        pltpu.make_async_copy(
-            pair_hbm.at[pl.ds(i * group, group)],
-            pair_ref.at[pl.ds(i * group, group)],
-            pair_sem.at[i],
-        )
-        for i in range(chunks)
-    ]
-    for copy in pair_copies:
-        copy.start()
-    moves = [(single_hbm, single_ref), (cond_hbm, cond_ref)]
-    for place, cut in (
-        (jnp.maximum(device_at - 1, 0), pl.ds(0, EDGE)),
-        (jnp.minimum(device_at + 1, blocks - 1), pl.ds(atoms_here - EDGE, EDGE)),
-    ):
-        moves.append((single_hbm.at[:, cut], edges_hbm.at[place, pl.ds(0, samples)]))
-        moves.append((cond_hbm.at[cut], edges_hbm.at[place, samples]))
+    pieces = rows // half
+
+    def pair_copy(i):
+        at = pl.ds(i * half, half)
+        return pltpu.make_async_copy(pair_hbm.at[at], pair_ref.at[at], pair_sem.at[i])
+
+    moves = [(w_pair_hbm, w_pair_ref), (single_hbm, single_ref), (cond_hbm, cond_ref)]
+    for send_ref, start in ((down_ref, 0), (up_ref, atoms_here - EDGE)):
+        cut = pl.ds(start, EDGE)
+        for sample in range(samples):
+            moves.append((single_hbm.at[sample, cut], send_ref.at[pl.ds(sample * EDGE, EDGE)]))
+        moves.append((cond_hbm.at[cut], send_ref.at[pl.ds(samples * EDGE, EDGE)]))
     index = 0
-    for names, packed in zip(packing, packed_refs):
+    for number, packed in zip(packing, packed_refs):
         offset = 0
-        for _ in names:
+        for _ in range(number):
             source = weights_hbm[index]
             span = source.shape[1]
             moves.append((source, packed.at[:, pl.ds(offset, span)]))
@@ -127,10 +109,12 @@
         pltpu.make_async_copy(source, target, sem.at[i])
         for i, (source, target) in enumerate(moves)
     ]
-    for copy in copies:
-        copy.start()
+    copies[0].start()
+    for i in range(4):
+        pair_copy(i).start()
 
     centre = twice(centring(width))
+    copies[0].wait()
     w_pair = w_pair_ref[...].astype(F32)
     spread = jnp.concatenate(
         [jnp.broadcast_to(w_pair[h : h + 1], (group, width)) for h in range(heads)], 0
@@ -143,10 +127,23 @@
     )
     slot = iota((cols, 2 * lanes), 1) % group
     per_block = tok_here // group
-    owners = rows // tok_here
-    for chunk in range(chunks):
-        pair_copies[chunk].wait()
-        pair = pair_ref[chunk * group : (chunk + 1) * group].reshape(group * cols, width)
+
+    @pl.loop(0, rows // group)
+    def _(chunk):
+        for part in range(2):
+            piece = chunk * 2 + part
+            pair_copy(piece).wait()
+
+            @pl.when(piece + 4 < pieces)
+            def _():
+                pair_copy(piece + 4).start()
+
+        @pl.when(chunk == 0)
+        def _():
+            for copy in copies[1:]:
+                copy.start()
+
+        pair = pair_ref[pl.ds(chunk * group, group)].reshape(group * cols, width)
         centred = dot(side_by_side(pair), centre)
         rounded = centred.astype(BF16)
         squares = (centred * centred).astype(BF16)
@@ -158,27 +155,21 @@
             for i in range(half):
                 total = jnp.where(slot == part * half + i, mixed[i], total)
         bias = (total[:, :lanes] * lax.rsqrt(total[:, lanes:] + EPSILON)).astype(BF16)
-        owner, part = divmod(chunk, per_block)
-        for target in range(owner, tiles_ref.shape[0], owners):
-            tiles_ref[target, part] = bias
-    for copy in copies:
+        tiles_ref[chunk // per_block, chunk % per_block] = bias
+
+    for copy in copies[1:]:
         copy.wait()
 
 
-def project_kernel(
+def transition_kernel(
     single_ref,
     cond_ref,
     ada_attn,
     ada_trans,
     gates_ref,
-    w_kv,
-    w_qg,
     w_up,
     w_down,
-    query_ref,
-    key_ref,
-    value_ref,
-    gate_ref,
+    normed_ref,
     open_ref,
     trans_ref,
 ):
@@ -190,27 +181,54 @@
         cond = layer_norm(cond_ref[at, :]).astype(BF16)
         single = layer_norm(single_ref[:, at, :].reshape(-1, width))
         single = single.reshape(samples, step, width)
-        normed = attn_norm(cond, single, ada_attn[...]).reshape(-1, width)
+        normed_ref[:, at, :] = attn_norm(cond, single, ada_attn[...])
+        gates = dot(cond, gates_ref[...])
+        open_ref[at, :] = sigmoid(gates[:, :width]).astype(BF16)
+        normed = attn_norm(cond, single, ada_trans[...]).reshape(-1, width)
+        swish = dot(normed, w_up[:, :hidden_width])
+        hidden = (swish * sigmoid(swish) * dot(normed, w_up[:, hidden_width:])).astype(BF16)
+        down = dot(hidden, w_down[...]).reshape(samples, step, width)
+        trans_ref[:, at, :] = (sigmoid(gates[:, width:])[None] * down).astype(BF16)
+
+
+def tile_of(own_ref, other_ref, pair_at, row_block):
+    owners, groups, cols, lanes = own_ref.shape
+    place, part = row_block // owners, row_block % owners
+    other = other_ref[0, part] if other_ref.shape[0] == 1 else other_ref[place, part]
+    return jnp.where(place == pair_at, own_ref[part], other)
+
+
+def select_kernel(blocks, at_ref, pair_ref, own_ref, other_ref, down_in, up_in, _, down_ref, up_ref, __):
+    del down_in, up_in
+    _, groups, cols, lanes = own_ref.shape
+    rows = groups * cols
+    for send_ref, row_block in (
+        (down_ref, jnp.maximum(at_ref[0] - 1, 0)),
+        (up_ref, jnp.minimum(at_ref[0] + 1, blocks - 1)),
+    ):
+        tile = tile_of(own_ref, other_ref, pair_ref[0], row_block)
+        send_ref[send_ref.shape[0] - rows :, :] = tile.reshape(rows, lanes)
+
+
+def project_kernel(normed_ref, w_kv, w_qg, query_ref, key_ref, value_ref, gate_ref):
+    samples, atoms_here, width = normed_ref.shape
+    step = math.gcd(atoms_here, 256)
+    for start in range(0, atoms_here, step):
+        at = slice(start, start + step)
+        normed = normed_ref[:, at, :].reshape(-1, width)
         both = dot(normed, w_kv[...]).astype(BF16).reshape(samples, step, 2 * width)
         key_ref[:, at, :] = both[:, :, :width]
         value_ref[:, at, :] = both[:, :, width:]
         both = dot(normed, w_qg[...]).reshape(samples, step, 2 * width)
         query_ref[:, at, :] = both[:, :, :width].astype(BF16)
-        gate_ref[:, at, :] = sigmoid(both[:, :, width:])
-        gates = dot(cond, gates_ref[...])
-        open_ref[at, :] = sigmoid(gates[:, :width])
-        normed = attn_norm(cond, single, ada_trans[...]).reshape(-1, width)
-        swish = dot(normed, w_up[:, :hidden_width])
-        hidden = (swish * sigmoid(swish) * dot(normed, w_up[:, hidden_width:])).astype(BF16)
-        down = dot(hidden, w_down[...]).reshape(samples, step, width)
-        trans_ref[:, at, :] = sigmoid(gates[:, width:])[None] * down
+        gate_ref[:, at, :] = sigmoid(both[:, :, width:]).astype(BF16)
 
 
 def attend_kernel(
     heads,
     blocks,
-    owners,
     at_ref,
+    pair_ref,
     counts_ref,
     query_ref,
     own_key_ref,
@@ -221,16 +239,15 @@
     ada_attn,
     w_kv,
     w_out_ref,
-    edges_hbm,
-    tiles_hbm,
+    own_ref,
+    other_ref,
+    prev_ref,
+    next_ref,
     out_ref,
     key_ref,
     value_ref,
     near_ref,
     gated_ref,
-    edges_ref,
-    tiles_ref,
-    sem,
 ):
     samples, atoms_here, width = query_ref.shape
     tok_here = counts_ref.shape[1]
@@ -242,16 +259,6 @@
     ends = atoms_here * blocks
     around = [jnp.maximum(device_at - 1, 0), device_at, jnp.minimum(device_at + 1, blocks - 1)]
 
-    copies = [
-        pltpu.make_async_copy(edges_hbm.at[place], edges_ref.at[side], sem.at[side])
-        for side, place in enumerate((around[0], around[2]))
-    ]
-    for i, place in enumerate(around):
-        source = tiles_hbm.at[device_at // owners * blocks + place]
-        copies.append(pltpu.make_async_copy(source, tiles_ref.at[i], sem.at[2 + i]))
-    for copy in copies:
-        copy.start()
-
     key_ref[:, EDGE : EDGE + atoms_here, :] = own_key_ref[...]
     value_ref[:, EDGE : EDGE + atoms_here, :] = own_value_ref[...]
 
@@ -272,9 +279,8 @@
     spans = ((0, EDGE, atoms_here - EDGE), (EDGE, atoms_here, 0), (EDGE + atoms_here, EDGE, 0))
     hots = [hot_rows(block, span[1], span[2]) for block, span in zip(around, spans)]
 
-    copies[0].wait()
-    copies[1].wait()
-    normal = layer_norm(edges_ref[...].reshape(-1, width))
+    count = (samples + 1) * EDGE
+    normal = layer_norm(jnp.concatenate([prev_ref[:count], next_ref[:count]], 0))
     normal = normal.reshape(2, samples + 1, EDGE, width)
     for side, place in enumerate((0, EDGE + atoms_here)):
         cond = normal[side, samples].astype(BF16)
@@ -284,9 +290,11 @@
         key_ref[:, place : place + EDGE, :] = both[:, :, :width]
         value_ref[:, place : place + EDGE, :] = both[:, :, width:]
 
+    held = tile_of(own_ref, other_ref, pair_ref[0], device_at)
+    tiles = [prev_ref[count:], held, next_ref[count:]]
     for i, (place, count, _) in enumerate(spans):
-        copies[2 + i].wait()
-        tile = jnp.concatenate([tiles_ref[i, part] for part in range(tok_here // GROUP)], 1)
+        tile = tiles[i].reshape(tok_here // GROUP, tok_here, heads * GROUP)
+        tile = jnp.concatenate([tile[part] for part in range(tok_here // GROUP)], 1)
         near_ref[place : place + count, :] = dot(hots[i], tile).astype(BF16)
 
     lane = iota((tok_here, lanes), 1)
@@ -335,12 +343,12 @@
                     channel_head == head, mixed[head * Q_WIN : (head + 1) * Q_WIN], picked
                 )
             attended = picked[:, :width] * pl.reciprocal(picked[:, width:], approx=True)
-            gate = gate_ref[sample, pl.ds(starts[i], Q_WIN), :]
+            gate = gate_ref[sample, pl.ds(starts[i], Q_WIN), :].astype(F32)
             gated_ref[sample, pl.ds(starts[i], Q_WIN), :] = (gate * attended).astype(BF16)
 
     for sample in range(samples):
         mixed = dot(gated_ref[sample], w_out_ref[...])
-        out_ref[sample] = (open_ref[...] * mixed + trans_ref[sample]).astype(BF16)
+        out_ref[sample] = (open_ref[...].astype(F32) * mixed + trans_ref[sample].astype(F32)).astype(BF16)
 
 
 def shards(
@@ -371,8 +379,9 @@
     heads = w_pair.shape[1]
     groups = tok_here // GROUP
     pairs = lax.axis_size("pair")
-    rows_pair = pair_cond.shape[0] // tok_here
+    owners = pair_cond.shape[0] // tok_here
     at = device_at.astype(jnp.int32).reshape(1)
+    pair_at = lax.axis_index("pair").astype(jnp.int32).reshape(1)
     in_hbm = lambda array: pltpu.with_memory_space_constraint(array, pltpu.HBM)
     in_vmem = lambda array: pltpu.with_memory_space_constraint(array, pltpu.VMEM)
 
@@ -389,62 +398,86 @@
     flat = [array for arrays in packing for array in arrays]
     rows, cols, _ = pair_cond.shape
     lanes = heads * GROUP
+    wide = (samples, atoms_here, width)
+    params = pltpu.CompilerParams(vmem_limit_bytes=VMEM_LIMIT)
+
+    def cost(products):
+        return pl.CostEstimate(flops=2 * products, bytes_accessed=4 << 20, transcendentals=0)
+
+    sent = pltpu.VMEM(((samples + 1) * EDGE + groups * cols, lanes), BF16)
     shapes = [
-        jax.ShapeDtypeStruct((pairs * blocks, groups, cols, lanes), BF16),
-        pltpu.HBM((blocks, samples + 1, EDGE, width), BF16),
-        pltpu.VMEM(atom_single.shape, BF16),
+        pltpu.VMEM((owners, groups, cols, lanes), BF16),
+        sent,
+        sent,
+        pltpu.VMEM(wide, BF16),
         pltpu.VMEM(atom_cond.shape, BF16),
     ] + [
         pltpu.VMEM((arrays[0].shape[0], sum(a.shape[1] for a in arrays)), BF16)
         for arrays in packing
     ]
     made = pl.pallas_call(
-        functools.partial(pair_kernel, tok_here, blocks, [(0,) * len(a) for a in packing]),
-        in_specs=[IN_SMEM, IN_VMEM] + [IN_HBM] * (3 + len(flat)),
-        out_specs=[IN_VMEM, IN_HBM] + [IN_VMEM] * (2 + len(packing)),
+        functools.partial(pair_kernel, tok_here, [len(arrays) for arrays in packing]),
+        in_specs=[IN_HBM] * (4 + len(flat)),
+        out_specs=[IN_VMEM] * len(shapes),
         out_shape=shapes,
         scratch_shapes=[
+            pltpu.VMEM((heads, width), BF16),
             pltpu.VMEM(pair_cond.shape, BF16),
-            pltpu.SemaphoreType.DMA((rows // GROUP,)),
-            pltpu.SemaphoreType.DMA((6 + len(flat),)),
+            pltpu.SemaphoreType.DMA((2 * rows // GROUP,)),
+            pltpu.SemaphoreType.DMA((3 + 2 * (samples + 1) + len(flat),)),
         ],
-        compiler_params=pltpu.CompilerParams(vmem_limit_bytes=VMEM_LIMIT),
-        cost_estimate=pl.CostEstimate(
-            flops=rows * cols * width * width * 4,
-            bytes_accessed=rows * cols * width * 2,
-            transcendentals=0,
-        ),
-    )(at, w_pair.T, *map(in_hbm, (pair_cond, atom_single, atom_cond, *flat)))
-    tiles, edges, single, cond, *packed = made
+        compiler_params=params,
+        cost_estimate=cost(rows * cols * width * width * 2),
+    )(*map(in_hbm, (w_pair.T, pair_cond, atom_single, atom_cond, *flat)))
+    own, down, up, single, cond, *packed = made
     ada_attn, ada_trans, gates, w_kv, w_qg, w_up, w_down, w_out = packed
-    tiles = lax.all_to_all(tiles, ("pair", "atoms"), 0, 0)
-    edges = lax.all_to_all(edges, "atoms", 0, 0)
-
-    wide = (samples, atoms_here, width)
-    shapes = [pltpu.VMEM(wide, BF16)] * 3 + [
-        pltpu.VMEM(wide, F32),
-        pltpu.VMEM((atoms_here, width), F32),
-        pltpu.VMEM(wide, F32),
-    ]
-    operands = (single, cond, ada_attn, ada_trans, gates, w_kv, w_qg, w_up, w_down)
+    if pairs == 2:
+        other = lax.ppermute(own, "pair", [(0, 1), (1, 0)])[None]
+    else:
+        other = lax.all_gather(own, "pair")
+
+    operands = (single, cond, ada_attn, ada_trans, gates, w_up, w_down)
+    normed, opened, trans = pl.pallas_call(
+        transition_kernel,
+        in_specs=[IN_VMEM] * len(operands),
+        out_specs=[IN_VMEM] * 3,
+        out_shape=[
+            pltpu.VMEM(wide, BF16),
+            pltpu.VMEM((atoms_here, width), BF16),
+            pltpu.VMEM(wide, BF16),
+        ],
+        compiler_params=params,
+        cost_estimate=cost(samples * atoms_here * width * width * 10),
+    )(*map(in_vmem, operands))
+
+    operands = (own, other, down, up, normed)
+    down, up, normed = pl.pallas_call(
+        functools.partial(select_kernel, blocks),
+        in_specs=[IN_SMEM] * 2 + [IN_VMEM] * len(operands),
+        out_specs=[IN_VMEM] * 3,
+        out_shape=[sent, sent, pltpu.VMEM(wide, BF16)],
+        input_output_aliases={4: 0, 5: 1, 6: 2},
+        compiler_params=params,
+    )(at, pair_at, *map(in_vmem, operands))
+    steps = range(blocks - 1)
+    from_prev = lax.ppermute(up, "atoms", [(i, i + 1) for i in steps])
+    from_next = lax.ppermute(down, "atoms", [(i + 1, i) for i in steps])
+
+    operands = (normed, w_kv, w_qg)
     projected = pl.pallas_call(
         project_kernel,
         in_specs=[IN_VMEM] * len(operands),
-        out_specs=[IN_VMEM] * len(shapes),
-        out_shape=shapes,
-        compiler_params=pltpu.CompilerParams(vmem_limit_bytes=VMEM_LIMIT),
-        cost_estimate=pl.CostEstimate(
-            flops=samples * atoms_here * width * width * 24,
-            bytes_accessed=4 << 20,
-            transcendentals=0,
-        ),
+        out_specs=[IN_VMEM] * 4,
+        out_shape=[pltpu.VMEM(wide, BF16)] * 4,
+        compiler_params=params,
+        cost_estimate=cost(samples * atoms_here * width * width * 10),
     )(*map(in_vmem, operands))
 
     ext = atoms_here + 2 * EDGE
-    operands = (*projected, ada_attn, w_kv, w_out)
+    operands = (*projected, opened, trans, ada_attn, w_kv, w_out, own, other, from_prev, from_next)
     return pl.pallas_call(
-        functools.partial(attend_kernel, heads, blocks, rows_pair),
-        in_specs=[IN_SMEM, IN_VMEM] + [IN_VMEM] * len(operands) + [IN_HBM] * 2,
+        functools.partial(attend_kernel, heads, blocks),
+        in_specs=[IN_SMEM] * 2 + [IN_VMEM] * (1 + len(operands)),
         out_specs=IN_VMEM,
         out_shape=jax.ShapeDtypeStruct(wide, BF16),
         scratch_shapes=[
@@ -452,17 +485,10 @@
             pltpu.VMEM((samples, ext, width), BF16),
             pltpu.VMEM((ext, heads * tok_here), BF16),
             pltpu.VMEM(wide, BF16),
-            pltpu.VMEM((2, samples + 1, EDGE, width), BF16),
-            pltpu.VMEM((3, groups, cols, lanes), BF16),
-            pltpu.SemaphoreType.DMA((5,)),
         ],
-        compiler_params=pltpu.CompilerParams(vmem_limit_bytes=VMEM_LIMIT),
-        cost_estimate=pl.CostEstimate(
-            flops=samples * atoms_here * width * width * 12,
-            bytes_accessed=4 << 20,
-            transcendentals=0,
-        ),
-    )(at, atom_counts, *map(in_vmem, operands), in_hbm(edges), in_hbm(tiles))
+        compiler_params=params,
+        cost_estimate=cost(samples * atoms_here * width * width * 12),
+    )(at, pair_at, atom_counts, *map(in_vmem, operands))
 
 
 def solution(mesh):

time: 42.4 us -> 24.6 us (0.58); the launches traced: 41.8 us -> 24.5 us
  blocking collectives: 14 us -> 0 us
  local copies, waits for them, and re-layouts: 6.8 us -> 0.01 us
  starting transfers between devices: 4.04 us -> 8.31 us
  Pallas kernels: 13.5 us -> 11.2 us
  waiting for transfers between devices: 3.42 us -> 4.88 us
    all_to_all x1 -> x0, blocking collectives: 14 us -> none  [shards(): edges = lax.all_to_all(edges, 'atoms', 0, 0)]
    ppermute x0 -> x3, starting transfers between devices: none -> 8.31 us  [the longest x1 4.01 us: shards(): from_prev = lax.ppermute(up, 'atoms', [(i, i + 1) for i in steps])]
    unnamed x20 -> x2, local copies, waits for them, and re-layouts: 6.8 us -> 0.01 us
    ppermute x0 -> x3, waiting for transfers between devices: none -> 4.88 us  [the longest x1 4.3 us: shards(): from_next = lax.ppermute(down, 'atoms', [(i + 1, i) for i in steps])]
    all_to_all x1 -> x0, starting transfers between devices: 4.04 us -> none  [shards(): tiles = lax.all_to_all(tiles, ('pair', 'atoms'), 0, 0)]
    all_to_all x1 -> x0, waiting for transfers between devices: 3.42 us -> none  [shards(): tiles = lax.all_to_all(tiles, ('pair', 'atoms'), 0, 0)]
    pallas_call x1, Pallas kernels: 2.44 us -> 0.57 us  [shards(): pl.pallas_call(project_kernel, in_specs=[IN_VMEM] * len(operands), out_sp...]
    pallas_call x2 -> x4, Pallas kernels: 11 us -> 10.7 us  [the longest x1 4.76 us: shards(): pl.pallas_call(functools.partial(attend_kernel, heads, blocks), in_specs=...]
  transfers between devices with their start and end apart: 1 -> 3, of which waited for: 1 -> 3; matrix products, arithmetic and copies ran while one was open for 0% -> 0% of each run, Pallas kernels for 6% -> 10%
where the time goes in v5:
time: 24.6 us; the launch traced here: 24.5 us
  Pallas kernels  11.2 us (46%)
  starting transfers between devices  8.31 us (34%)
  waiting for transfers between devices  4.88 us (20%)
    pallas_call x1, Pallas kernels, shards(): pl.pallas_call(functools.partial(attend_kernel, heads, blocks), in_specs=...  4.76 us
    ppermute x1, waiting for transfers between devices, shards(): from_next = lax.ppermute(down, 'atoms', [(i + 1, i) for i in steps])  4.3 us
    pallas_call x1, Pallas kernels, shards(): pl.pallas_call(functools.partial(pair_kernel, tok_here, [len(arrays) for...  4.06 us
    ppermute x1, starting transfers between devices, shards(): from_prev = lax.ppermute(up, 'atoms', [(i, i + 1) for i in steps])  4.01 us
    ppermute x1, starting transfers between devices, shards(): other = lax.ppermute(own, 'pair', [(0, 1), (1, 0)])[None]  3 us
    pallas_call x1, Pallas kernels, shards(): pl.pallas_call(transition_kernel, in_specs=[IN_VMEM] * len(operands), out...  1.82 us
    ppermute x1, starting transfers between devices, shards(): from_next = lax.ppermute(down, 'atoms', [(i + 1, i) for i in steps])  1.29 us
    pallas_call x1, Pallas kernels, shards(): pl.pallas_call(project_kernel, in_specs=[IN_VMEM] * len(operands), out_sp...  0.57 us
  transfers between devices with their start and end apart: 3, of which 3 were waited for; matrix products, arithmetic and copies ran while one was open for 0% of the time, Pallas kernels for 10%

profile of v5, /device:TPU:0, one launch (start us, length us, event | category | flops | bytes accessed | tf_op | source)
XLA Modules:
  0.0 24.5 jit_solution(2131961518329820186)
XLA Ops:
  0.0 4.1 %shard_map.181 = (bf16[2,2,64,128]{3,2,1,0:T(8,128)(2,1)S(1)}, bf16[320,128]{1,0:T(8,128)(2,1)S(1)}, bf16[320,128]{1,0:T(8,128)(2,1)S(1)}, bf16[3,512,128]{2,1,0...) custom-call(bf16[4,128]{1,0:T(4,128)(2,1)} %bitcast.6, ...), custom_call_target="tpu_custom_call" | custom-call | flops 536870912 | bytes 4194304 | tf_op jit(solution)/shard_map/pallas_call | solution.py:418
  4.1 3.0 %collective-permute-start = (bf16[2,2,64,128]{3,2,1,0:T(8,128)(2,1)S(1)}, bf16[2,2,64,128]{3,2,1,0:T(8,128)(2,1)S(1)}, u32[]{:S(2)}, u32[]{:S(2)}) collective-permute-start(bf16[2,2,64,128]{3,2,1,0:T(8,128)(2,1)S(1)} %get-tuple-element.28.own_ref), channel_id=1, source_target_pairs={{0,2},{2,0},{1,3},{3,1},{4,6},{6,4},{5,7},{7,5},{8,10},{10,8},{9,1... | collective-permute-start | bytes 196616 | tf_op jit(solution)/shard_map/ppermute | solution.py:435
  7.1 0.0 copy-start
  7.1 1.8 %shard_map.182 = (bf16[3,512,128]{2,1,0:T(8,128)(2,1)S(1)}, bf16[512,128]{1,0:T(8,128)(2,1)S(1)}, bf16[3,512,128]{2,1,0:T(8,128)(2,1)S(1)}) custom-call(bf16[3,512,128]{2,1,0:T(8,128)(2,1)S(1)} %get-tuple-element.31.single_ref, bf16[512,128]{1,0:T(8,128)(2,1)S(1)} %get-tuple-element.32.cond_ref, bf16[128,256]{1,0:T(8,128)(2,1)S(1)} %get-tuple-element.33.ada_attn, ...), custom_call_target="tpu_custom_call" | custom-call | flops 503316480 | bytes 4194304 | tf_op jit(solution)/shard_map/pallas_call | solution.py:440
  8.9 0.4 %collective-permute-done = bf16[2,2,64,128]{3,2,1,0:T(8,128)(2,1)S(1)} collective-permute-done((bf16[2,2,64,128]{3,2,1,0:T(8,128)(2,1)S(1)}, bf16[2,2,64,128]{3,2,1,0:T(8,128)(2,1)S(1)}, u32[]{:S(2)}, u32[]{:S(2)}) %collective-permute-start) | collective-permute-done | bytes 65568 | tf_op jit(solution)/shard_map/ppermute | solution.py:435
  9.3 4.0 %collective-permute-start.1 = (bf16[320,128]{1,0:T(8,128)(2,1)S(1)}, bf16[320,128]{1,0:T(8,128)(2,1)S(1)}, u32[]{:S(2)}, u32[]{:S(2)}) collective-permute-start(bf16[320,128]{1,0:T(8,128)(2,1)S(1)} %get-tuple-element.49), channel_id=1, source_target_pairs={{0,4},{4,8},{8,12},{1,5},{5,9},{9,13},{2,6},{6,10},{10,14},{3,7},{... | collective-permute-start | bytes 245768 | tf_op jit(solution)/shard_map/ppermute | solution.py:463
  13.4 1.3 %collective-permute-start.2 = (bf16[320,128]{1,0:T(8,128)(2,1)S(1)}, bf16[320,128]{1,0:T(8,128)(2,1)S(1)}, u32[]{:S(2)}, u32[]{:S(2)}) collective-permute-start(bf16[320,128]{1,0:T(8,128)(2,1)S(1)} %get-tuple-element.50), channel_id=1, source_target_pairs={{4,0},{8,4},{12,8},{5,1},{9,5},{13,9},{6,2},{10,6},{14,10},{7,3},{... | collective-permute-start | bytes 245768 | tf_op jit(solution)/shard_map/ppermute | solution.py:464
  14.7 0.6 %shard_map.184 = (bf16[3,512,128]{2,1,0:T(8,128)(2,1)S(1)}, bf16[3,512,128]{2,1,0:T(8,128)(2,1)S(1)}, bf16[3,512,128]{2,1,0:T(8,128)(2,1)S(1)}, bf16[3,512,128]{2,1,0:T(8,128)(2,1)S(1)}) custom-call(bf16[3,512,128]{2,1,0:T(8,128)(2,1)S(1)} %get-tuple-element.39.normed_ref, bf16[128,256]{1,0:T(8,128)(2,1)S(1)} %get-tuple-element.40.w_kv, ...), custom_call_target="tpu_custom_call" | custom-call | flops 503316480 | bytes 4194304 | tf_op jit(solution)/shard_map/pallas_call | solution.py:467
  15.2 0.2 collective-permute-done.1.prev_ref
  15.4 4.3 %collective-permute-done.2.next_ref = bf16[320,128]{1,0:T(8,128)(2,1)S(1)} collective-permute-done((bf16[320,128]{1,0:T(8,128)(2,1)S(1)}, bf16[320,128]{1,0:T(8,128)(2,1)S(1)}, u32[]{:S(2)}, u32[]{:S(2)}) %collective-permute-start.2) | collective-permute-done | bytes 81952 | tf_op jit(solution)/shard_map/ppermute | solution.py:464
  19.7 0.0 copy-done
  19.7 4.8 %shard_map.185 = bf16[3,512,128]{2,1,0:T(8,128)(2,1)} custom-call(s32[1]{0:T(128)} %bitcast.at_ref, s32[1]{0:T(128)} %bitcast.1.pair_ref, s32[4,64]{1,0:T(4,128)S(1)} %copy-done, bf16[3,512,128]{2,1,0:T(8,128)(2,1)S(1)} %get-tuple-element.42.query_ref, bf16[3,512,128]{2,1,0:T(8,128)(2,1)S(1)} %get-tuple-element.43.own_key_ref, ...), custom_call_target="tpu_custom_call" | custom-call | flops 603979776 | bytes 4194304 | tf_op jit(solution)/shard_map/pallas_call | solution.py:478
  (1 shorter events, 0.0 us)
Async XLA Ops:
  4.1 5.2 %collective-permute-start = (bf16[2,2,64,128]{3,2,1,0:T(8,128)(2,1)S(1)}, bf16[2,2,64,128]{3,2,1,0:T(8,128)(2,1)S(1)}, u32[]{:S(2)}, u32[]{:S(2)}) collective-permute-start(bf16[2,2,64,128]{3,2,1,0:T(8,128)(2,1)S(1)} %get-tuple-element.28.own_ref), channel_id=1, source_target_pairs={{0,2},{2,0},{1,3},{3,1},{4,6},{6,4},{5,7},{7,5},{8,10},{10,8},{9,1... | collective-permute-start | bytes 196616 | tf_op jit(solution)/shard_map/ppermute | solution.py:435
  7.1 12.6 %copy-start = (s32[4,64]{1,0:T(4,128)S(1)}, s32[4,64]{1,0:T(4,128)}, u32[]{:S(2)}) copy-start(s32[4,64]{1,0:T(4,128)} %counts_ref.1) | copy-start | bytes 3076
  9.3 6.1 %collective-permute-start.1 = (bf16[320,128]{1,0:T(8,128)(2,1)S(1)}, bf16[320,128]{1,0:T(8,128)(2,1)S(1)}, u32[]{:S(2)}, u32[]{:S(2)}) collective-permute-start(bf16[320,128]{1,0:T(8,128)(2,1)S(1)} %get-tuple-element.49), channel_id=1, source_target_pairs={{0,4},{4,8},{8,12},{1,5},{5,9},{9,13},{2,6},{6,10},{10,14},{3,7},{... | collective-permute-start | bytes 245768 | tf_op jit(solution)/shard_map/ppermute | solution.py:463
  13.4 6.3 %collective-permute-start.2 = (bf16[320,128]{1,0:T(8,128)(2,1)S(1)}, bf16[320,128]{1,0:T(8,128)(2,1)S(1)}, u32[]{:S(2)}, u32[]{:S(2)}) collective-permute-start(bf16[320,128]{1,0:T(8,128)(2,1)S(1)} %get-tuple-element.50), channel_id=1, source_target_pairs={{4,0},{8,4},{12,8},{5,1},{9,5},{13,9},{6,2},{10,6},{14,10},{7,3},{... | collective-permute-start | bytes 245768 | tf_op jit(solution)/shard_map/ppermute | solution.py:464

commit v6 on v5

v6 whole, which is shorter than its diff:
```python
import functools
import math

import jax
import jax.numpy as jnp
from jax import lax
from jax.experimental import pallas as pl
from jax.experimental.pallas import tpu as pltpu
from jax.sharding import PartitionSpec as P

Q_WIN = 32
K_WIN = 128
EDGE = 48
GROUP = 32

EPSILON = 1e-05
MASKED = -1e30
LOG2E = math.log2(math.e)
BF16 = jnp.bfloat16
F32 = jnp.float32
LAST = (((1,), (1,)), ((), ()))
VMEM_LIMIT = 32 << 20
IN_VMEM = pl.BlockSpec(memory_space=pltpu.VMEM)
IN_HBM = pl.BlockSpec(memory_space=pltpu.HBM)
IN_SMEM = pl.BlockSpec(memory_space=pltpu.SMEM)


def dot(a, b):
    return jnp.dot(a, b, preferred_element_type=F32)


def iota(shape, dim):
    return lax.broadcasted_iota(jnp.int32, shape, dim)


def twice(matrix):
    blank = jnp.zeros_like(matrix)
    return jnp.concatenate(
        [jnp.concatenate([matrix, blank], 1), jnp.concatenate([blank, matrix], 1)], 0
    )


def side_by_side(rows):
    half = rows.shape[0] // 2
    return jnp.concatenate([rows[:half], rows[half:]], 1)


def centring(width):
    same = iota((width, width), 0) == iota((width, width), 1)
    return jnp.where(same, 1.0 - 1.0 / width, -1.0 / width).astype(BF16)


def averaging(width):
    return jnp.full((width, width), 1.0 / width, BF16)


def layer_norm(rows):
    width = rows.shape[1]
    centred = dot(side_by_side(rows), twice(centring(width)))
    variance = dot((centred * centred).astype(BF16), twice(averaging(width)))
    normal = centred * lax.rsqrt(variance + EPSILON)
    return jnp.concatenate([normal[:, :width], normal[:, width:]], 0)


def sigmoid(values):
    return pl.reciprocal(1.0 + jnp.exp2(values * -LOG2E), approx=True)


def attn_norm(cond, single, ada):
    width = single.shape[-1]
    mixed = dot(cond, ada)
    return (sigmoid(mixed[:, :width])[None] * single + mixed[None, :, width:]).astype(BF16)


def pair_kernel(tok_here, packing, at_ref, w_pair_hbm, pair_hbm, single_hbm, cond_hbm, *refs):
    count = sum(packing)
    weights_hbm, refs = refs[:count], refs[count:]
    tiles_ref, near_ref, far_ref, single_ref, cond_ref = refs[:5]
    packed_refs, refs = refs[5 : 5 + len(packing)], refs[5 + len(packing) :]
    w_pair_ref, pair_ref, pair_sem, sem = refs
    rows, cols, width = pair_ref.shape
    heads = w_pair_ref.shape[0]
    samples, atoms_here, _ = single_ref.shape
    group = GROUP
    lanes = heads * group
    half = group // 2
    pieces = rows // half

    def pair_copy(i):
        at = pl.ds(i * half, half)
        return pltpu.make_async_copy(pair_hbm.at[at], pair_ref.at[at], pair_sem.at[i])

    moves = [(w_pair_hbm, w_pair_ref), (single_hbm, single_ref), (cond_hbm, cond_ref)]
    for send_ref, parity in ((near_ref, 1), (far_ref, 0)):
        start = jnp.where(at_ref[0] % 2 == parity, 0, atoms_here - EDGE)
        cut = pl.ds(pl.multiple_of(start, 16), EDGE)
        for sample in range(samples):
            moves.append((single_hbm.at[sample, cut], send_ref.at[pl.ds(sample * EDGE, EDGE)]))
        moves.append((cond_hbm.at[cut], send_ref.at[pl.ds(samples * EDGE, EDGE)]))
    index = 0
    for number, packed in zip(packing, packed_refs):
        offset = 0
        for _ in range(number):
            source = weights_hbm[index]
            span = source.shape[1]
            moves.append((source, packed.at[:, pl.ds(offset, span)]))
            offset += span
            index += 1
    copies = [
        pltpu.make_async_copy(source, target, sem.at[i])
        for i, (source, target) in enumerate(moves)
    ]
    copies[0].start()
    for i in range(4):
        pair_copy(i).start()

    centre = twice(centring(width))
    copies[0].wait()
    w_pair = w_pair_ref[...].astype(F32)
    spread = jnp.concatenate(
        [jnp.broadcast_to(w_pair[h : h + 1], (group, width)) for h in range(heads)], 0
    )
    weight = spread.T.astype(BF16)
    mean = jnp.full((width, lanes), 1.0 / width, BF16)
    blank = jnp.zeros((width, lanes), BF16)
    mix = jnp.concatenate(
        [jnp.concatenate([weight, blank], 1), jnp.concatenate([blank, mean], 1)], 0
    )
    slot = iota((cols, 2 * lanes), 1) % group
    per_block = tok_here // group

    @pl.loop(0, rows // group)
    def _(chunk):
        for part in range(2):
            piece = chunk * 2 + part
            pair_copy(piece).wait()

            @pl.when(piece + 4 < pieces)
            def _():
                pair_copy(piece + 4).start()

        @pl.when(chunk == 0)
        def _():
            for copy in copies[1:]:
                copy.start()

        pair = pair_ref[pl.ds(chunk * group, group)].reshape(group * cols, width)
        centred = dot(side_by_side(pair), centre)
        rounded = centred.astype(BF16)
        squares = (centred * centred).astype(BF16)
        total = jnp.zeros((cols, 2 * lanes), F32)
        for part in range(2):
            cut = slice(part * width, (part + 1) * width)
            mixed = dot(jnp.concatenate([rounded[:, cut], squares[:, cut]], 1), mix)
            mixed = mixed.reshape(half, cols, 2 * lanes)
            for i in range(half):
                total = jnp.where(slot == part * half + i, mixed[i], total)
        bias = (total[:, :lanes] * lax.rsqrt(total[:, lanes:] + EPSILON)).astype(BF16)
        tiles_ref[chunk // per_block, chunk % per_block] = bias

    for copy in copies[1:]:
        copy.wait()


def project_kernel(
    single_ref,
    cond_ref,
    ada_attn,
    ada_trans,
    gates_ref,
    w_kv,
    w_qg,
    w_up,
    w_down,
    query_ref,
    key_ref,
    value_ref,
    gate_ref,
    open_ref,
    trans_ref,
):
    samples, atoms_here, width = single_ref.shape
    hidden_width = w_down.shape[0]
    step = math.gcd(atoms_here, 256)
    for start in range(0, atoms_here, step):
        at = slice(start, start + step)
        cond = layer_norm(cond_ref[at, :]).astype(BF16)
        single = layer_norm(single_ref[:, at, :].reshape(-1, width))
        single = single.reshape(samples, step, width)
        normed = attn_norm(cond, single, ada_attn[...]).reshape(-1, width)
        both = dot(normed, w_kv[...]).astype(BF16).reshape(samples, step, 2 * width)
        key_ref[:, at, :] = both[:, :, :width]
        value_ref[:, at, :] = both[:, :, width:]
        both = dot(normed, w_qg[...]).reshape(samples, step, 2 * width)
        query_ref[:, at, :] = both[:, :, :width].astype(BF16)
        gate_ref[:, at, :] = sigmoid(both[:, :, width:]).astype(BF16)
        gates = dot(cond, gates_ref[...])
        open_ref[at, :] = sigmoid(gates[:, :width]).astype(BF16)
        normed = attn_norm(cond, single, ada_trans[...]).reshape(-1, width)
        swish = dot(normed, w_up[:, :hidden_width])
        hidden = (swish * sigmoid(swish) * dot(normed, w_up[:, hidden_width:])).astype(BF16)
        down = dot(hidden, w_down[...]).reshape(samples, step, width)
        trans_ref[:, at, :] = (sigmoid(gates[:, width:])[None] * down).astype(BF16)


def tile_of(own_ref, other_ref, pair_at, row_block):
    owners, groups, cols, lanes = own_ref.shape
    place, part = row_block // owners, row_block % owners
    other = other_ref[0, part] if other_ref.shape[0] == 1 else other_ref[place, part]
    return jnp.where(place == pair_at, own_ref[part], other)


def select_kernel(blocks, at_ref, pair_ref, own_ref, other_ref, *refs):
    near_ref, far_ref, _, held_ref = refs[3:]
    groups, cols, lanes = own_ref.shape[1:]
    rows = groups * cols
    device_at, pair_at = at_ref[0], pair_ref[0]
    for send_ref, parity in ((near_ref, 0), (far_ref, 1)):
        beside = jnp.where(device_at % 2 == parity, device_at + 1, device_at - 1)
        tile = tile_of(own_ref, other_ref, pair_at, jnp.clip(beside, 0, blocks - 1))
        send_ref[send_ref.shape[0] - rows :, :] = tile.reshape(rows, lanes)
    held_ref[...] = tile_of(own_ref, other_ref, pair_at, device_at).reshape(rows, lanes)


def bounds(counts_ref, block, token):
    tok_here = counts_ref.shape[1]
    counts = counts_ref[pl.ds(block, 1), :].astype(F32).astype(BF16)
    counts = jnp.broadcast_to(counts, (8, tok_here))
    before = iota((tok_here, token.shape[1]), 0)
    first = dot(counts, (before < token).astype(BF16))[:1]
    last = dot(counts, (before <= token).astype(BF16))[:1]
    return first.astype(jnp.int32), last.astype(jnp.int32)


def one_hot(reach, offset, count):
    first, last = reach
    position = iota((count, first.shape[1]), 0) + offset
    return ((first <= position) & (position < last)).astype(F32).astype(BF16)


def expand(hot, tile, tok_here):
    tile = tile.reshape(tok_here // GROUP, tok_here, tile.shape[-1])
    tile = jnp.concatenate([tile[part] for part in range(tok_here // GROUP)], 1)
    return dot(hot, tile).astype(BF16)


def attend(heads, reach, windows, query_ref, gate_ref, gated_ref):
    samples, _, width = query_ref.shape
    head_dim = width // heads
    lanes = reach[0].shape[1]
    rows = heads * Q_WIN
    lane_head = iota((rows, lanes), 1) // GROUP % heads
    row_head = iota((rows, lanes), 0) // Q_WIN
    same_head = (lane_head == row_head).astype(F32).astype(BF16)
    own_head = iota((rows, width), 1) // head_dim == iota((rows, width), 0) // Q_WIN
    own_head = own_head.astype(F32).astype(BF16)
    channel_head = iota((Q_WIN, 2 * width), 1) % width // head_dim
    ones = jnp.ones((K_WIN, width), BF16)
    scaling = LOG2E / math.sqrt(head_dim)

    biases = []
    for start, _, near, mask in windows:
        pick = jnp.concatenate([one_hot(reach, start, Q_WIN)] * heads, 0) * same_head
        bias = lax.dot_general(pick, near, LAST, preferred_element_type=F32) * LOG2E
        biases.append(bias if mask is None else jnp.where(mask, bias, MASKED))
    units = [(sample, i) for i in range(len(windows)) for sample in range(samples)]
    scores = []
    for sample, i in units:
        query = query_ref[sample, pl.ds(windows[i][0], Q_WIN), :]
        query = jnp.concatenate([query] * heads, 0) * own_head
        keys = windows[i][1](sample)[0]
        product = lax.dot_general(query, keys, LAST, preferred_element_type=F32)
        scores.append(product * scaling + biases[i])
    tops = [jnp.max(score, axis=-1, keepdims=True) for score in scores]
    raised = [jnp.exp2(score - top).astype(BF16) for score, top in zip(scores, tops)]
    for (sample, i), weight in zip(units, raised):
        values = windows[i][1](sample)[1]
        mixed = dot(weight, jnp.concatenate([values, ones], 1))
        picked = mixed[:Q_WIN]
        for head in range(1, heads):
            picked = jnp.where(
                channel_head == head, mixed[head * Q_WIN : (head + 1) * Q_WIN], picked
            )
        attended = picked[:, :width] * pl.reciprocal(picked[:, width:], approx=True)
        at = pl.ds(windows[i][0], Q_WIN)
        gate = gate_ref[sample, at, :].astype(F32)
        gated_ref[sample, at, :] = (gate * attended).astype(BF16)


def close(sample, cut, gated_ref, open_ref, trans_ref, w_out_ref):
    mixed = dot(gated_ref[sample, cut, :], w_out_ref[...])
    opened, trans = open_ref[cut, :].astype(F32), trans_ref[sample, cut, :].astype(F32)
    return (opened * mixed + trans).astype(BF16)


def row_tokens(heads, tok_here):
    lane = iota((tok_here, heads * tok_here), 1)
    return lane // (heads * GROUP) * GROUP + lane % GROUP


def inner_kernel(
    heads,
    at_ref,
    counts_ref,
    query_ref,
    key_ref,
    value_ref,
    gate_ref,
    open_ref,
    trans_ref,
    w_out_ref,
    held_ref,
    out_ref,
    near_ref,
    gated_ref,
):
    samples, atoms_here, width = query_ref.shape
    tok_here = counts_ref.shape[1]
    device_at = at_ref[0]
    hot = one_hot(
        bounds(counts_ref, device_at, iota((tok_here, tok_here), 1)), 0, atoms_here
    )
    near_ref[...] = expand(hot, held_ref[...], tok_here)
    reach = bounds(counts_ref, device_at, row_tokens(heads, tok_here))
    skip = -(-EDGE // Q_WIN)
    inner = atoms_here // Q_WIN - 2 * skip
    batch = math.gcd(inner, 4)

    @pl.loop(0, inner // batch)
    def _(turn):
        windows = []
        for i in range(batch):
            start = pl.multiple_of((turn * batch + i + skip) * Q_WIN, Q_WIN)
            cut = pl.ds(pl.multiple_of(start - EDGE, 16), K_WIN)
            parts = lambda sample, cut=cut: (key_ref[sample, cut, :], value_ref[sample, cut, :])
            windows.append((start, parts, near_ref[cut, :], None))
        attend(heads, reach, windows, query_ref, gate_ref, gated_ref)

    cut = slice(skip * Q_WIN, atoms_here - skip * Q_WIN)
    for sample in range(samples):
        out_ref[sample] = close(sample, cut, gated_ref, open_ref, trans_ref, w_out_ref)


def outer_kernel(
    heads,
    blocks,
    at_ref,
    counts_ref,
    query_ref,
    own_key_ref,
    own_value_ref,
    gate_ref,
    open_ref,
    trans_ref,
    w_out_ref,
    held_ref,
    inner_ref,
    ada_attn,
    w_kv,
    first_ref,
    second_ref,
    out_hbm,
    key_ref,
    value_ref,
    near_ref,
    gated_ref,
    out_ref,
    sem,
):
    samples, atoms_here, width = query_ref.shape
    tok_here = counts_ref.shape[1]
    device_at = at_ref[0]
    ends = atoms_here * blocks
    skip = -(-EDGE // Q_WIN)
    margin = skip * Q_WIN
    reach_keys = key_ref.shape[2]
    inside = reach_keys - EDGE

    whole = pltpu.make_async_copy(
        inner_ref, out_hbm.at[:, pl.ds(margin, atoms_here - 2 * margin)], sem.at[0]
    )
    whole.start()

    even = device_at % 2 == 0
    first, second = first_ref[...], second_ref[...]
    arrived = (jnp.where(even, second, first), jnp.where(even, first, second))
    count = (samples + 1) * EDGE
    normal = layer_norm(jnp.concatenate([rows[:count] for rows in arrived], 0))
    normal = normal.reshape(2, samples + 1, EDGE, width)
    token = iota((tok_here, tok_here), 1)
    own_reach = bounds(counts_ref, device_at, token)
    sides = (
        (jnp.maximum(device_at - 1, 0), atoms_here - EDGE, 0, EDGE, 0),
        (jnp.minimum(device_at + 1, blocks - 1), 0, inside, 0, atoms_here - inside),
    )
    for side, (block, offset, place, own_place, own_start) in enumerate(sides):
        cond = normal[side, samples].astype(BF16)
        normed = attn_norm(cond, normal[side, :samples], ada_attn[...])
        both = dot(normed.reshape(-1, width), w_kv[...]).astype(BF16)
        both = both.reshape(samples, EDGE, 2 * width)
        for ref, own_ref, edge in (
            (key_ref, own_key_ref, both[:, :, :width]),
            (value_ref, own_value_ref, both[:, :, width:]),
        ):
            ref[side, :, place : place + EDGE, :] = edge
            ref[side, :, own_place : own_place + inside, :] = own_ref[
                :, own_start : own_start + inside, :
            ]
        hot = one_hot(bounds(counts_ref, block, token), offset, EDGE)
        near_ref[side, place : place + EDGE, :] = expand(hot, arrived[side][count:], tok_here)
        hot = one_hot(own_reach, own_start, inside)
        near_ref[side, own_place : own_place + inside, :] = expand(hot, held_ref[...], tok_here)

    reach = bounds(counts_ref, device_at, row_tokens(heads, tok_here))
    windows = []
    for side in range(2):
        for i in range(skip):
            start = i * Q_WIN + side * (atoms_here - margin)
            cut = slice(i * Q_WIN, i * Q_WIN + K_WIN)
            parts = lambda sample, side=side, cut=cut: (
                key_ref[side, sample, cut, :],
                value_ref[side, sample, cut, :],
            )
            key_at = iota((heads * Q_WIN, K_WIN), 1) + (device_at * atoms_here + start - EDGE)
            mask = (key_at >= 0) & (key_at < ends)
            windows.append((start, parts, near_ref[side, cut, :], mask))
    attend(heads, reach, windows, query_ref, gate_ref, gated_ref)
    copies = []
    for side in range(2):
        cut = slice(side * (atoms_here - margin), side * (atoms_here - margin) + margin)
        for sample in range(samples):
            out_ref[side, sample] = close(sample, cut, gated_ref, open_ref, trans_ref, w_out_ref)
        target = out_hbm.at[:, pl.ds(side * (atoms_here - margin), margin)]
        copies.append(pltpu.make_async_copy(out_ref.at[side], target, sem.at[1 + side]))
        copies[-1].start()
    for copy in copies:
        copy.wait()
    whole.wait()


def shards(
    atom_single,
    atom_cond,
    pair_cond,
    atom_counts,
    ada_attn_scale,
    ada_attn_shift,
    w_query,
    w_key,
    w_value,
    w_gate,
    w_out,
    attn_gate,
    w_pair,
    ada_trans_scale,
    ada_trans_shift,
    w_swish,
    w_linear,
    w_down,
    trans_gate,
):
    device_at = lax.axis_index("atoms")
    blocks = lax.axis_size("atoms")
    samples, atoms_here, width = atom_single.shape
    tok_here = atom_counts.shape[1]
    heads = w_pair.shape[1]
    groups = tok_here // GROUP
    pairs = lax.axis_size("pair")
    owners = pair_cond.shape[0] // tok_here
    at = device_at.astype(jnp.int32).reshape(1)
    pair_at = lax.axis_index("pair").astype(jnp.int32).reshape(1)
    in_hbm = lambda array: pltpu.with_memory_space_constraint(array, pltpu.HBM)
    in_vmem = lambda array: pltpu.with_memory_space_constraint(array, pltpu.VMEM)

    packing = (
        (ada_attn_scale, ada_attn_shift),
        (ada_trans_scale, ada_trans_shift),
        (attn_gate, trans_gate),
        (w_key, w_value),
        (w_query, w_gate),
        (w_swish, w_linear),
        (w_down,),
        (w_out,),
    )
    flat = [array for arrays in packing for array in arrays]
    rows, cols, _ = pair_cond.shape
    lanes = heads * GROUP
    wide = (samples, atoms_here, width)
    params = pltpu.CompilerParams(vmem_limit_bytes=VMEM_LIMIT)

    def cost(products):
        return pl.CostEstimate(flops=2 * products, bytes_accessed=4 << 20, transcendentals=0)

    sent = pltpu.VMEM(((samples + 1) * EDGE + groups * cols, lanes), BF16)
    shapes = [
        pltpu.VMEM((owners, groups, cols, lanes), BF16),
        sent,
        sent,
        pltpu.VMEM(wide, BF16),
        pltpu.VMEM(atom_cond.shape, BF16),
    ] + [
        pltpu.VMEM((arrays[0].shape[0], sum(a.shape[1] for a in arrays)), BF16)
        for arrays in packing
    ]
    made = pl.pallas_call(
        functools.partial(pair_kernel, tok_here, [len(arrays) for arrays in packing]),
        in_specs=[IN_SMEM] + [IN_HBM] * (4 + len(flat)),
        out_specs=[IN_VMEM] * len(shapes),
        out_shape=shapes,
        scratch_shapes=[
            pltpu.VMEM((heads, width), BF16),
            pltpu.VMEM(pair_cond.shape, BF16),
            pltpu.SemaphoreType.DMA((2 * rows // GROUP,)),
            pltpu.SemaphoreType.DMA((3 + 2 * (samples + 1) + len(flat),)),
        ],
        compiler_params=params,
        cost_estimate=cost(rows * cols * width * width * 2),
    )(at, *map(in_hbm, (w_pair.T, pair_cond, atom_single, atom_cond, *flat)))
    own, near, far, single, cond, *packed = made
    ada_attn, ada_trans, gates, w_kv, w_qg, w_up, w_down, w_out = packed
    if pairs == 2:
        other = lax.ppermute(own, "pair", [(0, 1), (1, 0)])[None]
    else:
        other = lax.all_gather(own, "pair")

    operands = (single, cond, ada_attn, ada_trans, gates, w_kv, w_qg, w_up, w_down)
    query, keys, values, gate, opened, trans = pl.pallas_call(
        project_kernel,
        in_specs=[IN_VMEM] * len(operands),
        out_specs=[IN_VMEM] * 6,
        out_shape=[pltpu.VMEM(wide, BF16)] * 4
        + [pltpu.VMEM((atoms_here, width), BF16), pltpu.VMEM(wide, BF16)],
        compiler_params=params,
        cost_estimate=cost(samples * atoms_here * width * width * 20),
    )(*map(in_vmem, operands))

    operands = (own, other, near, far, opened)
    near, far, opened, held = pl.pallas_call(
        functools.partial(select_kernel, blocks),
        in_specs=[IN_SMEM] * 2 + [IN_VMEM] * len(operands),
        out_specs=[IN_VMEM] * 4,
        out_shape=[
            sent,
            sent,
            pltpu.VMEM((atoms_here, width), BF16),
            pltpu.VMEM((groups * cols, lanes), BF16),
        ],
        input_output_aliases={4: 0, 5: 1, 6: 2},
        compiler_params=params,
    )(at, pair_at, *map(in_vmem, operands))

    def swap(value, start):
        sides = [(i, i + 1) for i in range(start, blocks - 1, 2)]
        return lax.ppermute(value, "atoms", sides + [(j, i) for i, j in sides])

    first, second = swap(near, 0), swap(far, 1)

    margin = -(-EDGE // Q_WIN) * Q_WIN
    operands = (query, keys, values, gate, opened, trans, w_out, held)
    inner = pl.pallas_call(
        functools.partial(inner_kernel, heads),
        in_specs=[IN_SMEM] + [IN_VMEM] * (1 + len(operands)),
        out_specs=IN_VMEM,
        out_shape=pltpu.VMEM((samples, atoms_here - 2 * margin, width), BF16),
        scratch_shapes=[
            pltpu.VMEM((atoms_here, heads * tok_here), BF16),
            pltpu.VMEM(wide, BF16),
        ],
        compiler_params=params,
        cost_estimate=cost(samples * atoms_here * width * width * 12),
    )(at, atom_counts, *map(in_vmem, operands))

    reach = margin - Q_WIN + K_WIN
    operands += (inner, ada_attn, w_kv, first, second)
    return pl.pallas_call(
        functools.partial(outer_kernel, heads, blocks),
        in_specs=[IN_SMEM] + [IN_VMEM] * (1 + len(operands)),
        out_specs=IN_HBM,
        out_shape=pltpu.HBM(wide, BF16),
        scratch_shapes=[
            pltpu.VMEM((2, samples, reach, width), BF16),
            pltpu.VMEM((2, samples, reach, width), BF16),
            pltpu.VMEM((2, reach, heads * tok_here), BF16),
            pltpu.VMEM(wide, BF16),
            pltpu.VMEM((2, samples, margin, width), BF16),
            pltpu.SemaphoreType.DMA((3,)),
        ],
        compiler_params=params,
        cost_estimate=cost(samples * atoms_here * width * width * 4),
    )(at, atom_counts, *map(in_vmem, operands))


def solution(mesh):
    return jax.shard_map(
        shards,
        mesh=mesh,
        in_specs=(
            P(("groups", "pair", "samp"), "atoms", None),
            P(("groups", "atoms"), None),
            P(("groups", "pair"), "atoms", None),
            P("groups", None),
        )
        + (P(),) * 15,
        out_specs=P(("groups", "pair", "samp"), "atoms", None),
        check_vma=False,
    )
```

time: 24.6 us -> 19 us (0.77)
  the two profiles are of different devices: /device:TPU:0 before, /device:TPU:18 now
where the time goes in v6:
time: 19 us; the launch traced here: 18.9 us
  Pallas kernels  11.8 us (62%)
  starting transfers between devices  4.14 us (22%)
  waiting for transfers between devices  2.86 us (15%)
    pallas_call x1, Pallas kernels, shards(): pl.pallas_call(functools.partial(pair_kernel, tok_here, [len(arrays) for...  4.15 us
    ppermute x2, starting transfers between devices, swap(): return lax.ppermute(value, 'atoms', sides + [(j, i) for i, j in sides])  3.55 us
    pallas_call x1, Pallas kernels, shards(): pl.pallas_call(functools.partial(inner_kernel, heads), in_specs=[IN_SMEM]...  2.79 us
    pallas_call x1, Pallas kernels, shards(): pl.pallas_call(project_kernel, in_specs=[IN_VMEM] * len(operands), out_sp...  2.46 us
    pallas_call x1, Pallas kernels, shards(): pl.pallas_call(functools.partial(outer_kernel, heads, blocks), in_specs=[...  2.38 us
    ppermute x2, waiting for transfers between devices, swap(): return lax.ppermute(value, 'atoms', sides + [(j, i) for i, j in sides])  1.59 us
    ppermute x1, waiting for transfers between devices, shards(): other = lax.ppermute(own, 'pair', [(0, 1), (1, 0)])[None]  1.27 us
    ppermute x1, starting transfers between devices, shards(): other = lax.ppermute(own, 'pair', [(0, 1), (1, 0)])[None]  0.6 us
  transfers between devices with their start and end apart: 3, of which 2 were waited for; matrix products, arithmetic and copies ran while one was open for 0% of the time, Pallas kernels for 28%

profile of v6, /device:TPU:18, one launch (start us, length us, event | category | flops | bytes accessed | tf_op | source)
XLA Modules:
  0.0 18.9 jit_solution(15766131067714875681)
XLA Ops:
  0.0 4.2 %shard_map.181 = (bf16[2,2,64,128]{3,2,1,0:T(8,128)(2,1)S(1)}, bf16[320,128]{1,0:T(8,128)(2,1)S(1)}, bf16[320,128]{1,0:T(8,128)(2,1)S(1)}, bf16[3,512,128]{2,1,0...) custom-call(s32[1]{0:T(128)} %bitcast.at_ref, ...), custom_call_target="tpu_custom_call" | custom-call | flops 536870912 | bytes 4194304 | tf_op jit(solution)/shard_map/pallas_call | solution.py:505
  4.2 0.6 %collective-permute-start = (bf16[2,2,64,128]{3,2,1,0:T(8,128)(2,1)S(1)}, bf16[2,2,64,128]{3,2,1,0:T(8,128)(2,1)S(1)}, u32[]{:S(2)}, u32[]{:S(2)}) collective-permute-start(bf16[2,2,64,128]{3,2,1,0:T(8,128)(2,1)S(1)} %get-tuple-element.41.own_ref), channel_id=1, source_target_pairs={{0,2},{2,0},{1,3},{3,1},{4,6},{6,4},{5,7},{7,5},{8,10},{10,8},{9,1... | collective-permute-start | bytes 196616 | tf_op jit(solution)/shard_map/ppermute | solution.py:522
  4.8 0.0 copy-start
  4.8 2.5 %shard_map.182 = (bf16[3,512,128]{2,1,0:T(8,128)(2,1)S(1)}, bf16[3,512,128]{2,1,0:T(8,128)(2,1)S(1)}, bf16[3,512,128]{2,1,0:T(8,128)(2,1)S(1)}, bf16[3,512,128]{...) custom-call(bf16[3,512,128]{2,1,0:T(8,128)(2,1)S(1)} %get-tuple-element.28.single_ref, ...), custom_call_target="tpu_custom_call" | custom-call | flops 1006632960 | bytes 4194304 | tf_op jit(solution)/shard_map/pallas_call | solution.py:527
  7.2 1.3 %collective-permute-done = bf16[2,2,64,128]{3,2,1,0:T(8,128)(2,1)S(1)} collective-permute-done((bf16[2,2,64,128]{3,2,1,0:T(8,128)(2,1)S(1)}, bf16[2,2,64,128]{3,2,1,0:T(8,128)(2,1)S(1)}, u32[]{:S(2)}, u32[]{:S(2)}) %collective-permute-start) | collective-permute-done | bytes 65568 | tf_op jit(solution)/shard_map/ppermute | solution.py:522
  8.5 1.6 %collective-permute-start.1 = (bf16[320,128]{1,0:T(8,128)(2,1)S(1)}, bf16[320,128]{1,0:T(8,128)(2,1)S(1)}, u32[]{:S(2)}, u32[]{:S(2)}) collective-permute-start(bf16[320,128]{1,0:T(8,128)(2,1)S(1)} %get-tuple-element.49), channel_id=1, source_target_pairs={{0,4},{8,12},{4,0},{12,8},{1,5},{9,13},{5,1},{13,9},{2,6},{10,14},... | collective-permute-start | bytes 245768 | tf_op jit(solution)/shard_map/ppermute | solution.py:554
  10.2 1.9 %collective-permute-start.2 = (bf16[320,128]{1,0:T(8,128)(2,1)S(1)}, bf16[320,128]{1,0:T(8,128)(2,1)S(1)}, u32[]{:S(2)}, u32[]{:S(2)}) collective-permute-start(bf16[320,128]{1,0:T(8,128)(2,1)S(1)} %get-tuple-element.50), channel_id=1, source_target_pairs={{4,8},{8,4},{5,9},{9,5},{6,10},{10,6},{7,11},{11,7},{20,24},{24,20... | collective-permute-start | bytes 245768 | tf_op jit(solution)/shard_map/ppermute | solution.py:554
  12.1 0.0 copy-done
  12.1 2.8 %shard_map.184.inner_ref = bf16[3,384,128]{2,1,0:T(8,128)(2,1)S(1)} custom-call(s32[1]{0:T(128)} %bitcast.at_ref, s32[4,64]{1,0:T(4,128)S(1)} %copy-done, bf16[3,512,128]{2,1,0:T(8,128)(2,1)S(1)} %get-tuple-element.37.query_ref, bf16[3,512,128]{2,1,0:T(8,128)(2,1)S(1)} %get-tuple-element.38.key_ref.own_key_ref, ...), custom_call_target="tpu_custom_call" | custom-call | flops 603979776 | bytes 4194304 | tf_op jit(solution)/shard_map/pallas_call | solution.py:560
  14.9 0.0 collective-permute-done.1.first_ref
  14.9 1.6 %collective-permute-done.2.second_ref = bf16[320,128]{1,0:T(8,128)(2,1)S(1)} collective-permute-done((bf16[320,128]{1,0:T(8,128)(2,1)S(1)}, bf16[320,128]{1,0:T(8,128)(2,1)S(1)}, u32[]{:S(2)}, u32[]{:S(2)}) %collective-permute-start.2) | collective-permute-done | bytes 81952 | tf_op jit(solution)/shard_map/ppermute | solution.py:554
  16.5 2.4 %shard_map.185 = bf16[3,512,128]{2,1,0:T(8,128)(2,1)} custom-call(s32[1]{0:T(128)} %bitcast.at_ref, s32[4,64]{1,0:T(4,128)S(1)} %copy-done, bf16[3,512,128]{2,1,0:T(8,128)(2,1)S(1)} %get-tuple-element.37.query_ref, bf16[3,512,128]{2,1,0:T(8,128)(2,1)S(1)} %get-tuple-element.38.key_ref.own_key_ref, ...), custom_call_target="tpu_custom_call" | custom-call | flops 201326592 | bytes 4194304 | tf_op jit(solution)/shard_map/pallas_call | solution.py:575
  (1 shorter events, 0.0 us)
Async XLA Ops:
  4.2 4.3 %collective-permute-start = (bf16[2,2,64,128]{3,2,1,0:T(8,128)(2,1)S(1)}, bf16[2,2,64,128]{3,2,1,0:T(8,128)(2,1)S(1)}, u32[]{:S(2)}, u32[]{:S(2)}) collective-permute-start(bf16[2,2,64,128]{3,2,1,0:T(8,128)(2,1)S(1)} %get-tuple-element.41.own_ref), channel_id=1, source_target_pairs={{0,2},{2,0},{1,3},{3,1},{4,6},{6,4},{5,7},{7,5},{8,10},{10,8},{9,1... | collective-permute-start | bytes 196616 | tf_op jit(solution)/shard_map/ppermute | solution.py:522
  4.8 7.3 %copy-start = (s32[4,64]{1,0:T(4,128)S(1)}, s32[4,64]{1,0:T(4,128)}, u32[]{:S(2)}) copy-start(s32[4,64]{1,0:T(4,128)} %counts_ref.3) | copy-start | bytes 3076
  8.5 6.4 %collective-permute-start.1 = (bf16[320,128]{1,0:T(8,128)(2,1)S(1)}, bf16[320,128]{1,0:T(8,128)(2,1)S(1)}, u32[]{:S(2)}, u32[]{:S(2)}) collective-permute-start(bf16[320,128]{1,0:T(8,128)(2,1)S(1)} %get-tuple-element.49), channel_id=1, source_target_pairs={{0,4},{8,12},{4,0},{12,8},{1,5},{9,13},{5,1},{13,9},{2,6},{10,14},... | collective-permute-start | bytes 245768 | tf_op jit(solution)/shard_map/ppermute | solution.py:554
  10.2 6.3 %collective-permute-start.2 = (bf16[320,128]{1,0:T(8,128)(2,1)S(1)}, bf16[320,128]{1,0:T(8,128)(2,1)S(1)}, u32[]{:S(2)}, u32[]{:S(2)}) collective-permute-start(bf16[320,128]{1,0:T(8,128)(2,1)S(1)} %get-tuple-element.50), channel_id=1, source_target_pairs={{4,8},{8,4},{5,9},{9,5},{6,10},{10,6},{7,11},{11,7},{20,24},{24,20... | collective-permute-start | bytes 245768 | tf_op jit(solution)/shard_map/ppermute | solution.py:554

commit v7 on v6

--- a/solution.py
+++ b/solution.py
@@ -72,31 +72,25 @@
     return (sigmoid(mixed[:, :width])[None] * single + mixed[None, :, width:]).astype(BF16)
 
 
-def pair_kernel(tok_here, packing, at_ref, w_pair_hbm, pair_hbm, single_hbm, cond_hbm, *refs):
+def pair_kernel(packing, core_ref, w_pair_hbm, pair_hbm, single_hbm, cond_hbm, *refs):
     count = sum(packing)
     weights_hbm, refs = refs[:count], refs[count:]
-    tiles_ref, near_ref, far_ref, single_ref, cond_ref = refs[:5]
-    packed_refs, refs = refs[5 : 5 + len(packing)], refs[5 + len(packing) :]
+    tile_ref, single_ref, cond_ref = refs[:3]
+    packed_refs, refs = refs[3 : 3 + len(packing)], refs[3 + len(packing) :]
     w_pair_ref, pair_ref, pair_sem, sem = refs
     rows, cols, width = pair_ref.shape
     heads = w_pair_ref.shape[0]
-    samples, atoms_here, _ = single_ref.shape
     group = GROUP
     lanes = heads * group
     half = group // 2
     pieces = rows // half
+    row_start = core_ref[0] * rows
 
     def pair_copy(i):
-        at = pl.ds(i * half, half)
-        return pltpu.make_async_copy(pair_hbm.at[at], pair_ref.at[at], pair_sem.at[i])
+        source = pair_hbm.at[pl.ds(row_start + i * half, half)]
+        return pltpu.make_async_copy(source, pair_ref.at[pl.ds(i * half, half)], pair_sem.at[i])
 
     moves = [(w_pair_hbm, w_pair_ref), (single_hbm, single_ref), (cond_hbm, cond_ref)]
-    for send_ref, parity in ((near_ref, 1), (far_ref, 0)):
-        start = jnp.where(at_ref[0] % 2 == parity, 0, atoms_here - EDGE)
-        cut = pl.ds(pl.multiple_of(start, 16), EDGE)
-        for sample in range(samples):
-            moves.append((single_hbm.at[sample, cut], send_ref.at[pl.ds(sample * EDGE, EDGE)]))
-        moves.append((cond_hbm.at[cut], send_ref.at[pl.ds(samples * EDGE, EDGE)]))
     index = 0
     for number, packed in zip(packing, packed_refs):
         offset = 0
@@ -111,7 +105,7 @@
         for i, (source, target) in enumerate(moves)
     ]
     copies[0].start()
-    for i in range(4):
+    for i in range(pieces):
         pair_copy(i).start()
 
     centre = twice(centring(width))
@@ -127,17 +121,11 @@
         [jnp.concatenate([weight, blank], 1), jnp.concatenate([blank, mean], 1)], 0
     )
     slot = iota((cols, 2 * lanes), 1) % group
-    per_block = tok_here // group
 
     @pl.loop(0, rows // group)
     def _(chunk):
         for part in range(2):
-            piece = chunk * 2 + part
-            pair_copy(piece).wait()
-
-            @pl.when(piece + 4 < pieces)
-            def _():
-                pair_copy(piece + 4).start()
+            pair_copy(chunk * 2 + part).wait()
 
         @pl.when(chunk == 0)
         def _():
@@ -156,13 +144,14 @@
             for i in range(half):
                 total = jnp.where(slot == part * half + i, mixed[i], total)
         bias = (total[:, :lanes] * lax.rsqrt(total[:, lanes:] + EPSILON)).astype(BF16)
-        tiles_ref[chunk // per_block, chunk % per_block] = bias
+        tile_ref[chunk] = bias
 
     for copy in copies[1:]:
         copy.wait()
 
 
 def project_kernel(
+    at_ref,
     single_ref,
     cond_ref,
     ada_attn,
@@ -178,6 +167,8 @@
     gate_ref,
     open_ref,
     trans_ref,
+    near_ref,
+    far_ref,
 ):
     samples, atoms_here, width = single_ref.shape
     hidden_width = w_down.shape[0]
@@ -201,25 +192,36 @@
         hidden = (swish * sigmoid(swish) * dot(normed, w_up[:, hidden_width:])).astype(BF16)
         down = dot(hidden, w_down[...]).reshape(samples, step, width)
         trans_ref[:, at, :] = (sigmoid(gates[:, width:])[None] * down).astype(BF16)
-
-
-def tile_of(own_ref, other_ref, pair_at, row_block):
-    owners, groups, cols, lanes = own_ref.shape
-    place, part = row_block // owners, row_block % owners
-    other = other_ref[0, part] if other_ref.shape[0] == 1 else other_ref[place, part]
-    return jnp.where(place == pair_at, own_ref[part], other)
-
-
-def select_kernel(blocks, at_ref, pair_ref, own_ref, other_ref, *refs):
-    near_ref, far_ref, _, held_ref = refs[3:]
-    groups, cols, lanes = own_ref.shape[1:]
+    even = at_ref[0] % 2 == 0
+    for i, ref in enumerate((key_ref, value_ref)):
+        for sample in range(samples):
+            head, tail = ref[sample, :EDGE, :], ref[sample, atoms_here - EDGE :, :]
+            place = (2 * sample + i) * EDGE
+            near_ref[place : place + EDGE, :] = jnp.where(even, tail, head)
+            far_ref[place : place + EDGE, :] = jnp.where(even, head, tail)
+
+
+def tile_of(refs, place, row_block):
+    if len(refs) == 1:
+        return refs[0][row_block]
+    pair_at, core_at = place
+    owners = 2
+    mine, theirs, across, diagonal = [ref[...] for ref in refs]
+    near = jnp.where(row_block % owners == core_at, mine, theirs)
+    far = jnp.where(row_block % owners == core_at, across, diagonal)
+    return jnp.where(row_block // owners == pair_at, near, far)
+
+
+def select_kernel(blocks, at_ref, pair_ref, core_ref, *refs):
+    *tile_refs, _, __, ___, near_ref, far_ref, ____, held_ref = refs
+    groups, cols, lanes = tile_refs[0].shape[-3:]
     rows = groups * cols
-    device_at, pair_at = at_ref[0], pair_ref[0]
+    device_at, place = at_ref[0], (pair_ref[0], core_ref[0])
     for send_ref, parity in ((near_ref, 0), (far_ref, 1)):
         beside = jnp.where(device_at % 2 == parity, device_at + 1, device_at - 1)
-        tile = tile_of(own_ref, other_ref, pair_at, jnp.clip(beside, 0, blocks - 1))
+        tile = tile_of(tile_refs, place, jnp.clip(beside, 0, blocks - 1))
         send_ref[send_ref.shape[0] - rows :, :] = tile.reshape(rows, lanes)
-    held_ref[...] = tile_of(own_ref, other_ref, pair_at, device_at).reshape(rows, lanes)
+    held_ref[...] = tile_of(tile_refs, place, device_at).reshape(rows, lanes)
 
 
 def bounds(counts_ref, block, token):
@@ -355,8 +357,6 @@
     w_out_ref,
     held_ref,
     inner_ref,
-    ada_attn,
-    w_kv,
     first_ref,
     second_ref,
     out_hbm,
@@ -384,9 +384,7 @@
     even = device_at % 2 == 0
     first, second = first_ref[...], second_ref[...]
     arrived = (jnp.where(even, second, first), jnp.where(even, first, second))
-    count = (samples + 1) * EDGE
-    normal = layer_norm(jnp.concatenate([rows[:count] for rows in arrived], 0))
-    normal = normal.reshape(2, samples + 1, EDGE, width)
+    count = 2 * samples * EDGE
     token = iota((tok_here, tok_here), 1)
     own_reach = bounds(counts_ref, device_at, token)
     sides = (
@@ -394,15 +392,9 @@
         (jnp.minimum(device_at + 1, blocks - 1), 0, inside, 0, atoms_here - inside),
     )
     for side, (block, offset, place, own_place, own_start) in enumerate(sides):
-        cond = normal[side, samples].astype(BF16)
-        normed = attn_norm(cond, normal[side, :samples], ada_attn[...])
-        both = dot(normed.reshape(-1, width), w_kv[...]).astype(BF16)
-        both = both.reshape(samples, EDGE, 2 * width)
-        for ref, own_ref, edge in (
-            (key_ref, own_key_ref, both[:, :, :width]),
-            (value_ref, own_value_ref, both[:, :, width:]),
-        ):
-            ref[side, :, place : place + EDGE, :] = edge
+        edges = arrived[side][:count].reshape(samples, 2, EDGE, width)
+        for i, (ref, own_ref) in enumerate(((key_ref, own_key_ref), (value_ref, own_value_ref))):
+            ref[side, :, place : place + EDGE, :] = edges[:, i]
             ref[side, :, own_place : own_place + inside, :] = own_ref[
                 :, own_start : own_start + inside, :
             ]
@@ -466,9 +458,10 @@
     heads = w_pair.shape[1]
     groups = tok_here // GROUP
     pairs = lax.axis_size("pair")
-    owners = pair_cond.shape[0] // tok_here
+    assert pair_cond.shape[0] == lax.axis_size("samp") * tok_here
     at = device_at.astype(jnp.int32).reshape(1)
     pair_at = lax.axis_index("pair").astype(jnp.int32).reshape(1)
+    core_at = lax.axis_index("samp").astype(jnp.int32).reshape(1)
     in_hbm = lambda array: pltpu.with_memory_space_constraint(array, pltpu.HBM)
     in_vmem = lambda array: pltpu.with_memory_space_constraint(array, pltpu.VMEM)
 
@@ -483,7 +476,7 @@
         (w_out,),
     )
     flat = [array for arrays in packing for array in arrays]
-    rows, cols, _ = pair_cond.shape
+    cols = pair_cond.shape[1]
     lanes = heads * GROUP
     wide = (samples, atoms_here, width)
     params = pltpu.CompilerParams(vmem_limit_bytes=VMEM_LIMIT)
@@ -491,11 +484,9 @@
     def cost(products):
         return pl.CostEstimate(flops=2 * products, bytes_accessed=4 << 20, transcendentals=0)
 
-    sent = pltpu.VMEM(((samples + 1) * EDGE + groups * cols, lanes), BF16)
+    sent = pltpu.VMEM((2 * samples * EDGE + groups * cols, lanes), BF16)
     shapes = [
-        pltpu.VMEM((owners, groups, cols, lanes), BF16),
-        sent,
-        sent,
+        pltpu.VMEM((groups, cols, lanes), BF16),
         pltpu.VMEM(wide, BF16),
         pltpu.VMEM(atom_cond.shape, BF16),
     ] + [
@@ -503,41 +494,45 @@
         for arrays in packing
     ]
     made = pl.pallas_call(
-        functools.partial(pair_kernel, tok_here, [len(arrays) for arrays in packing]),
+        functools.partial(pair_kernel, [len(arrays) for arrays in packing]),
         in_specs=[IN_SMEM] + [IN_HBM] * (4 + len(flat)),
         out_specs=[IN_VMEM] * len(shapes),
         out_shape=shapes,
         scratch_shapes=[
             pltpu.VMEM((heads, width), BF16),
-            pltpu.VMEM(pair_cond.shape, BF16),
-            pltpu.SemaphoreType.DMA((2 * rows // GROUP,)),
-            pltpu.SemaphoreType.DMA((3 + 2 * (samples + 1) + len(flat),)),
+            pltpu.VMEM((tok_here, cols, width), BF16),
+            pltpu.SemaphoreType.DMA((2 * groups,)),
+            pltpu.SemaphoreType.DMA((3 + len(flat),)),
         ],
         compiler_params=params,
-        cost_estimate=cost(rows * cols * width * width * 2),
-    )(at, *map(in_hbm, (w_pair.T, pair_cond, atom_single, atom_cond, *flat)))
-    own, near, far, single, cond, *packed = made
+        cost_estimate=cost(tok_here * cols * width * width * 2),
+    )(core_at, *map(in_hbm, (w_pair.T, pair_cond, atom_single, atom_cond, *flat)))
+    own, single, cond, *packed = made
     ada_attn, ada_trans, gates, w_kv, w_qg, w_up, w_down, w_out = packed
     if pairs == 2:
-        other = lax.ppermute(own, "pair", [(0, 1), (1, 0)])[None]
+        swapped = [(0, 1), (1, 0)]
+        across = lax.ppermute(own, "pair", swapped)
+        diagonal = lax.ppermute(own, ("pair", "samp"), [(0, 3), (1, 2), (2, 1), (3, 0)])
+        tiles = (own, lax.ppermute(own, "samp", swapped), across, diagonal)
     else:
-        other = lax.all_gather(own, "pair")
+        tiles = (lax.all_gather(own, ("pair", "samp")),)
 
     operands = (single, cond, ada_attn, ada_trans, gates, w_kv, w_qg, w_up, w_down)
-    query, keys, values, gate, opened, trans = pl.pallas_call(
+    query, keys, values, gate, opened, trans, near, far = pl.pallas_call(
         project_kernel,
-        in_specs=[IN_VMEM] * len(operands),
-        out_specs=[IN_VMEM] * 6,
+        in_specs=[IN_SMEM] + [IN_VMEM] * len(operands),
+        out_specs=[IN_VMEM] * 8,
         out_shape=[pltpu.VMEM(wide, BF16)] * 4
-        + [pltpu.VMEM((atoms_here, width), BF16), pltpu.VMEM(wide, BF16)],
+        + [pltpu.VMEM((atoms_here, width), BF16), pltpu.VMEM(wide, BF16), sent, sent],
         compiler_params=params,
         cost_estimate=cost(samples * atoms_here * width * width * 20),
-    )(*map(in_vmem, operands))
-
-    operands = (own, other, near, far, opened)
+    )(at, *map(in_vmem, operands))
+
+    operands = (*tiles, near, far, opened)
+    first = 3 + len(tiles)
     near, far, opened, held = pl.pallas_call(
         functools.partial(select_kernel, blocks),
-        in_specs=[IN_SMEM] * 2 + [IN_VMEM] * len(operands),
+        in_specs=[IN_SMEM] * 3 + [IN_VMEM] * len(operands),
         out_specs=[IN_VMEM] * 4,
         out_shape=[
             sent,
@@ -545,9 +540,9 @@
             pltpu.VMEM((atoms_here, width), BF16),
             pltpu.VMEM((groups * cols, lanes), BF16),
         ],
-        input_output_aliases={4: 0, 5: 1, 6: 2},
+        input_output_aliases={first: 0, first + 1: 1, first + 2: 2},
         compiler_params=params,
-    )(at, pair_at, *map(in_vmem, operands))
+    )(at, pair_at, core_at, *map(in_vmem, operands))
 
     def swap(value, start):
         sides = [(i, i + 1) for i in range(start, blocks - 1, 2)]
@@ -571,7 +566,7 @@
     )(at, atom_counts, *map(in_vmem, operands))
 
     reach = margin - Q_WIN + K_WIN
-    operands += (inner, ada_attn, w_kv, first, second)
+    operands += (inner, first, second)
     return pl.pallas_call(
         functools.partial(outer_kernel, heads, blocks),
         in_specs=[IN_SMEM] + [IN_VMEM] * (1 + len(operands)),

time: 19 us -> 18.2 us (0.958)
  the two profiles are of different devices: /device:TPU:18 before, /device:TPU:20 now
where the time goes in v7:
time: 18.2 us; the launch traced here: 18 us
  Pallas kernels  10 us (55%)
  starting transfers between devices  5.48 us (30%)
  waiting for transfers between devices  2.45 us (13%)
    ppermute x2, starting transfers between devices, swap(): return lax.ppermute(value, 'atoms', sides + [(j, i) for i, j in sides])  3.55 us
    pallas_call x1, Pallas kernels, shards(): pl.pallas_call(functools.partial(inner_kernel, heads), in_specs=[IN_SMEM]...  2.79 us
    pallas_call x1, Pallas kernels, shards(): pl.pallas_call(functools.partial(pair_kernel, [len(arrays) for arrays in...  2.75 us
    pallas_call x1, Pallas kernels, shards(): pl.pallas_call(project_kernel, in_specs=[IN_SMEM] + [IN_VMEM] * len(opera...  2.48 us
    pallas_call x1, Pallas kernels, shards(): pl.pallas_call(functools.partial(outer_kernel, heads, blocks), in_specs=[...  1.94 us
    ppermute x2, waiting for transfers between devices, swap(): return lax.ppermute(value, 'atoms', sides + [(j, i) for i, j in sides])  1.91 us
    ppermute x1, starting transfers between devices, shards(): across = lax.ppermute(own, 'pair', swapped)  1.56 us
    ppermute x1, waiting for transfers between devices, shards(): lax.ppermute(own, ('pair', 'samp'), [(0, 3), (1, 2), (2, 1), (3, 0)])  0.53 us
  transfers between devices with their start and end apart: 5, of which 2 were waited for; matrix products, arithmetic and copies ran while one was open for 0% of the time, Pallas kernels for 29%

profile of v7, /device:TPU:20, one launch (start us, length us, event | category | flops | bytes accessed | tf_op | source)
XLA Modules:
  0.0 18.0 jit_solution(10914556103135232682)
XLA Ops:
  0.0 2.7 %shard_map.181 = (bf16[2,64,128]{2,1,0:T(8,128)(2,1)S(1)}, bf16[3,512,128]{2,1,0:T(8,128)(2,1)S(1)}, bf16[512,128]{1,0:T(8,128)(2,1)S(1)}, bf16[128,256]{1,0:T(8...) custom-call(s32[1]{0:T(128)} %bitcast.1.core_ref, ...), custom_call_target="tpu_custom_call" | custom-call | flops 268435456 | bytes 4194304 | tf_op jit(solution)/shard_map/pallas_call | solution.py:496
  2.8 0.1 collective-permute-start
  2.8 1.6 %collective-permute-start.1 = (bf16[2,64,128]{2,1,0:T(8,128)(2,1)S(1)}, bf16[2,64,128]{2,1,0:T(8,128)(2,1)S(1)}, u32[]{:S(2)}, u32[]{:S(2)}) collective-permute-start(bf16[2,64,128]{2,1,0:T(8,128)(2,1)S(1)} %get-tuple-element.41.refs_0_), channel_id=1, source_target_pairs={{0,2},{2,0},{1,3},{3,1},{4,6},{6,4},{5,7},{7,5},{8,10},{10,8},{9,1... | collective-permute-start | bytes 98312 | tf_op jit(solution)/shard_map/ppermute | solution.py:514
  4.4 0.3 %collective-permute-start.2 = (bf16[2,64,128]{2,1,0:T(8,128)(2,1)S(1)}, bf16[2,64,128]{2,1,0:T(8,128)(2,1)S(1)}, u32[]{:S(2)}, u32[]{:S(2)}) collective-permute-start(bf16[2,64,128]{2,1,0:T(8,128)(2,1)S(1)} %get-tuple-element.41.refs_0_), channel_id=1, source_target_pairs={{0,3},{1,2},{2,1},{3,0},{4,7},{5,6},{6,5},{7,4},{8,11},{9,10},{10,... | collective-permute-start | bytes 98312 | tf_op jit(solution)/shard_map/ppermute | solution.py:515
  4.7 0.0 copy-start
  4.7 2.5 %shard_map.182 = (bf16[3,512,128]{2,1,0:T(8,128)(2,1)S(1)}, bf16[3,512,128]{2,1,0:T(8,128)(2,1)S(1)}, bf16[3,512,128]{2,1,0:T(8,128)(2,1)S(1)}, bf16[3,512,128]{...) custom-call(s32[1]{0:T(128)} %bitcast.at_ref, ...), custom_call_target="tpu_custom_call" | custom-call | flops 1006632960 | bytes 4194304 | tf_op jit(solution)/shard_map/pallas_call | solution.py:521
  7.2 0.0 collective-permute-done.refs_1_
  7.2 0.0 collective-permute-done.1.refs_2_
  7.2 0.5 %collective-permute-done.2.refs_3_ = bf16[2,64,128]{2,1,0:T(8,128)(2,1)S(1)} collective-permute-done((bf16[2,64,128]{2,1,0:T(8,128)(2,1)S(1)}, bf16[2,64,128]{2,1,0:T(8,128)(2,1)S(1)}, u32[]{:S(2)}, u32[]{:S(2)}) %collective-permute-start.2) | collective-permute-done | bytes 32800 | tf_op jit(solution)/shard_map/ppermute | solution.py:515
  7.8 1.6 %collective-permute-start.3 = (bf16[416,128]{1,0:T(8,128)(2,1)S(1)}, bf16[416,128]{1,0:T(8,128)(2,1)S(1)}, u32[]{:S(2)}, u32[]{:S(2)}) collective-permute-start(bf16[416,128]{1,0:T(8,128)(2,1)S(1)} %get-tuple-element.49), channel_id=1, source_target_pairs={{0,4},{8,12},{4,0},{12,8},{1,5},{9,13},{5,1},{13,9},{2,6},{10,14},... | collective-permute-start | bytes 319496 | tf_op jit(solution)/shard_map/ppermute | solution.py:549
  9.4 1.9 %collective-permute-start.4 = (bf16[416,128]{1,0:T(8,128)(2,1)S(1)}, bf16[416,128]{1,0:T(8,128)(2,1)S(1)}, u32[]{:S(2)}, u32[]{:S(2)}) collective-permute-start(bf16[416,128]{1,0:T(8,128)(2,1)S(1)} %get-tuple-element.50), channel_id=1, source_target_pairs={{4,8},{8,4},{5,9},{9,5},{6,10},{10,6},{7,11},{11,7},{20,24},{24,20... | collective-permute-start | bytes 319496 | tf_op jit(solution)/shard_map/ppermute | solution.py:549
  11.3 0.0 copy-done
  11.4 2.8 %shard_map.184.inner_ref = bf16[3,384,128]{2,1,0:T(8,128)(2,1)S(1)} custom-call(s32[1]{0:T(128)} %bitcast.at_ref, s32[4,64]{1,0:T(4,128)S(1)} %copy-done, bf16[3,512,128]{2,1,0:T(8,128)(2,1)S(1)} %get-tuple-element.37.query_ref, bf16[3,512,128]{2,1,0:T(8,128)(2,1)S(1)} %get-tuple-element.38.key_ref.own_key_ref, ...), custom_call_target="tpu_custom_call" | custom-call | flops 603979776 | bytes 4194304 | tf_op jit(solution)/shard_map/pallas_call | solution.py:555
  14.2 0.0 collective-permute-done.3.first_ref
  14.2 1.9 %collective-permute-done.4.second_ref = bf16[416,128]{1,0:T(8,128)(2,1)S(1)} collective-permute-done((bf16[416,128]{1,0:T(8,128)(2,1)S(1)}, bf16[416,128]{1,0:T(8,128)(2,1)S(1)}, u32[]{:S(2)}, u32[]{:S(2)}) %collective-permute-start.4) | collective-permute-done | bytes 106528 | tf_op jit(solution)/shard_map/ppermute | solution.py:549
  16.1 1.9 %shard_map.185 = bf16[3,512,128]{2,1,0:T(8,128)(2,1)} custom-call(s32[1]{0:T(128)} %bitcast.at_ref, s32[4,64]{1,0:T(4,128)S(1)} %copy-done, bf16[3,512,128]{2,1,0:T(8,128)(2,1)S(1)} %get-tuple-element.37.query_ref, bf16[3,512,128]{2,1,0:T(8,128)(2,1)S(1)} %get-tuple-element.38.key_ref.own_key_ref, ...), custom_call_target="tpu_custom_call" | custom-call | flops 201326592 | bytes 4194304 | tf_op jit(solution)/shard_map/pallas_call | solution.py:570
  (1 shorter events, 0.0 us)
Async XLA Ops:
  2.8 4.4 %collective-permute-start = (bf16[2,64,128]{2,1,0:T(8,128)(2,1)S(1)}, bf16[2,64,128]{2,1,0:T(8,128)(2,1)S(1)}, u32[]{:S(2)}, u32[]{:S(2)}) collective-permute-start(bf16[2,64,128]{2,1,0:T(8,128)(2,1)S(1)} %get-tuple-element.41.refs_0_), channel_id=1, source_target_pairs={{0,1},{1,0},{2,3},{3,2},{4,5},{5,4},{6,7},{7,6},{8,9},{9,8},{10,11... | collective-permute-start | bytes 98312 | tf_op jit(solution)/shard_map/ppermute | solution.py:516
  2.8 4.4 %collective-permute-start.1 = (bf16[2,64,128]{2,1,0:T(8,128)(2,1)S(1)}, bf16[2,64,128]{2,1,0:T(8,128)(2,1)S(1)}, u32[]{:S(2)}, u32[]{:S(2)}) collective-permute-start(bf16[2,64,128]{2,1,0:T(8,128)(2,1)S(1)} %get-tuple-element.41.refs_0_), channel_id=1, source_target_pairs={{0,2},{2,0},{1,3},{3,1},{4,6},{6,4},{5,7},{7,5},{8,10},{10,8},{9,1... | collective-permute-start | bytes 98312 | tf_op jit(solution)/shard_map/ppermute | solution.py:514
  4.4 3.3 %collective-permute-start.2 = (bf16[2,64,128]{2,1,0:T(8,128)(2,1)S(1)}, bf16[2,64,128]{2,1,0:T(8,128)(2,1)S(1)}, u32[]{:S(2)}, u32[]{:S(2)}) collective-permute-start(bf16[2,64,128]{2,1,0:T(8,128)(2,1)S(1)} %get-tuple-element.41.refs_0_), channel_id=1, source_target_pairs={{0,3},{1,2},{2,1},{3,0},{4,7},{5,6},{6,5},{7,4},{8,11},{9,10},{10,... | collective-permute-start | bytes 98312 | tf_op jit(solution)/shard_map/ppermute | solution.py:515
  4.7 6.6 %copy-start = (s32[4,64]{1,0:T(4,128)S(1)}, s32[4,64]{1,0:T(4,128)}, u32[]{:S(2)}) copy-start(s32[4,64]{1,0:T(4,128)} %counts_ref.3) | copy-start | bytes 3076
  7.8 6.4 %collective-permute-start.3 = (bf16[416,128]{1,0:T(8,128)(2,1)S(1)}, bf16[416,128]{1,0:T(8,128)(2,1)S(1)}, u32[]{:S(2)}, u32[]{:S(2)}) collective-permute-start(bf16[416,128]{1,0:T(8,128)(2,1)S(1)} %get-tuple-element.49), channel_id=1, source_target_pairs={{0,4},{8,12},{4,0},{12,8},{1,5},{9,13},{5,1},{13,9},{2,6},{10,14},... | collective-permute-start | bytes 319496 | tf_op jit(solution)/shard_map/ppermute | solution.py:549
  9.4 6.6 %collective-permute-start.4 = (bf16[416,128]{1,0:T(8,128)(2,1)S(1)}, bf16[416,128]{1,0:T(8,128)(2,1)S(1)}, u32[]{:S(2)}, u32[]{:S(2)}) collective-permute-start(bf16[416,128]{1,0:T(8,128)(2,1)S(1)} %get-tuple-element.50), channel_id=1, source_target_pairs={{4,8},{8,4},{5,9},{9,5},{6,10},{10,6},{7,11},{11,7},{20,24},{24,20... | collective-permute-start | bytes 319496 | tf_op jit(solution)/shard_map/ppermute | solution.py:549

commit v8 on v7

--- a/solution.py
+++ b/solution.py
@@ -178,7 +178,12 @@
         cond = layer_norm(cond_ref[at, :]).astype(BF16)
         single = layer_norm(single_ref[:, at, :].reshape(-1, width))
         single = single.reshape(samples, step, width)
-        normed = attn_norm(cond, single, ada_attn[...]).reshape(-1, width)
+        normed = attn_norm(cond, single, ada_attn[...])
+        if start == 0:
+            heads_of = [normed[sample, :EDGE] for sample in range(samples)]
+        if start + step == atoms_here:
+            tails_of = [normed[sample, step - EDGE :] for sample in range(samples)]
+        normed = normed.reshape(-1, width)
         both = dot(normed, w_kv[...]).astype(BF16).reshape(samples, step, 2 * width)
         key_ref[:, at, :] = both[:, :, :width]
         value_ref[:, at, :] = both[:, :, width:]
@@ -193,12 +198,10 @@
         down = dot(hidden, w_down[...]).reshape(samples, step, width)
         trans_ref[:, at, :] = (sigmoid(gates[:, width:])[None] * down).astype(BF16)
     even = at_ref[0] % 2 == 0
-    for i, ref in enumerate((key_ref, value_ref)):
-        for sample in range(samples):
-            head, tail = ref[sample, :EDGE, :], ref[sample, atoms_here - EDGE :, :]
-            place = (2 * sample + i) * EDGE
-            near_ref[place : place + EDGE, :] = jnp.where(even, tail, head)
-            far_ref[place : place + EDGE, :] = jnp.where(even, head, tail)
+    for sample, (head, tail) in enumerate(zip(heads_of, tails_of)):
+        cut = slice(sample * EDGE, (sample + 1) * EDGE)
+        near_ref[cut, :] = jnp.where(even, tail, head)
+        far_ref[cut, :] = jnp.where(even, head, tail)
 
 
 def tile_of(refs, place, row_block):
@@ -357,6 +360,7 @@
     w_out_ref,
     held_ref,
     inner_ref,
+    w_kv,
     first_ref,
     second_ref,
     out_hbm,
@@ -384,7 +388,9 @@
     even = device_at % 2 == 0
     first, second = first_ref[...], second_ref[...]
     arrived = (jnp.where(even, second, first), jnp.where(even, first, second))
-    count = 2 * samples * EDGE
+    count = samples * EDGE
+    edges = jnp.concatenate([rows[:count] for rows in arrived], 0)
+    edges = dot(edges, w_kv[...]).astype(BF16).reshape(2, samples, EDGE, 2 * width)
     token = iota((tok_here, tok_here), 1)
     own_reach = bounds(counts_ref, device_at, token)
     sides = (
@@ -392,9 +398,8 @@
         (jnp.minimum(device_at + 1, blocks - 1), 0, inside, 0, atoms_here - inside),
     )
     for side, (block, offset, place, own_place, own_start) in enumerate(sides):
-        edges = arrived[side][:count].reshape(samples, 2, EDGE, width)
         for i, (ref, own_ref) in enumerate(((key_ref, own_key_ref), (value_ref, own_value_ref))):
-            ref[side, :, place : place + EDGE, :] = edges[:, i]
+            ref[side, :, place : place + EDGE, :] = edges[side, :, :, i * width : (i + 1) * width]
             ref[side, :, own_place : own_place + inside, :] = own_ref[
                 :, own_start : own_start + inside, :
             ]
@@ -484,7 +489,7 @@
     def cost(products):
         return pl.CostEstimate(flops=2 * products, bytes_accessed=4 << 20, transcendentals=0)
 
-    sent = pltpu.VMEM((2 * samples * EDGE + groups * cols, lanes), BF16)
+    sent = pltpu.VMEM((samples * EDGE + groups * cols, lanes), BF16)
     shapes = [
         pltpu.VMEM((groups, cols, lanes), BF16),
         pltpu.VMEM(wide, BF16),
@@ -546,7 +551,9 @@
 
     def swap(value, start):
         sides = [(i, i + 1) for i in range(start, blocks - 1, 2)]
-        return lax.ppermute(value, "atoms", sides + [(j, i) for i, j in sides])
+        alone = set(range(blocks)) - {i for side in sides for i in side}
+        pairs_of = sides + [(j, i) for i, j in sides] + [(i, i) for i in sorted(alone)]
+        return lax.ppermute(value, "atoms", pairs_of)
 
     first, second = swap(near, 0), swap(far, 1)
 
@@ -566,7 +573,7 @@
     )(at, atom_counts, *map(in_vmem, operands))
 
     reach = margin - Q_WIN + K_WIN
-    operands += (inner, first, second)
+    operands += (inner, w_kv, first, second)
     return pl.pallas_call(
         functools.partial(outer_kernel, heads, blocks),
         in_specs=[IN_SMEM] + [IN_VMEM] * (1 + len(operands)),

time: 18.2 us -> 17.9 us (0.984)
  the two profiles are of different devices: /device:TPU:20 before, /device:TPU:8 now
where the time goes in v8:
time: 17.9 us; the launch traced here: 17.8 us
  Pallas kernels  10.1 us (56%)
  starting transfers between devices  7.05 us (39%)
  waiting for transfers between devices  0.54 us (3%)
    ppermute x2, starting transfers between devices, swap(): return lax.ppermute(value, 'atoms', pairs_of)  5.11 us
    pallas_call x1, Pallas kernels, shards(): pl.pallas_call(functools.partial(inner_kernel, heads), in_specs=[IN_SMEM]...  2.8 us
    pallas_call x1, Pallas kernels, shards(): pl.pallas_call(functools.partial(pair_kernel, [len(arrays) for arrays in...  2.75 us
    pallas_call x1, Pallas kernels, shards(): pl.pallas_call(project_kernel, in_specs=[IN_SMEM] + [IN_VMEM] * len(opera...  2.48 us
    pallas_call x1, Pallas kernels, shards(): pl.pallas_call(functools.partial(outer_kernel, heads, blocks), in_specs=[...  2.01 us
    ppermute x1, starting transfers between devices, shards(): across = lax.ppermute(own, 'pair', swapped)  1.56 us
    ppermute x1, waiting for transfers between devices, shards(): lax.ppermute(own, ('pair', 'samp'), [(0, 3), (1, 2), (2, 1), (3, 0)])  0.53 us
  transfers between devices with their start and end apart: 5, of which 1 were waited for; matrix products, arithmetic and copies ran while one was open for 0% of the time, Pallas kernels for 30%

profile of v8, /device:TPU:8, one launch (start us, length us, event | category | flops | bytes accessed | tf_op | source)
XLA Modules:
  0.0 17.8 jit_solution(9387224326137127955)
XLA Ops:
  0.0 2.7 %shard_map.181 = (bf16[2,64,128]{2,1,0:T(8,128)(2,1)S(1)}, bf16[3,512,128]{2,1,0:T(8,128)(2,1)S(1)}, bf16[512,128]{1,0:T(8,128)(2,1)S(1)}, bf16[128,256]{1,0:T(8...) custom-call(s32[1]{0:T(128)} %bitcast.1.core_ref, ...), custom_call_target="tpu_custom_call" | custom-call | flops 268435456 | bytes 4194304 | tf_op jit(solution)/shard_map/pallas_call | solution.py:501
  2.8 0.0 copy-start
  2.8 0.1 collective-permute-start
  2.8 1.6 %collective-permute-start.1 = (bf16[2,64,128]{2,1,0:T(8,128)(2,1)S(1)}, bf16[2,64,128]{2,1,0:T(8,128)(2,1)S(1)}, u32[]{:S(2)}, u32[]{:S(2)}) collective-permute-start(bf16[2,64,128]{2,1,0:T(8,128)(2,1)S(1)} %get-tuple-element.41.refs_0_), channel_id=1, source_target_pairs={{0,2},{2,0},{1,3},{3,1},{4,6},{6,4},{5,7},{7,5},{8,10},{10,8},{9,1... | collective-permute-start | bytes 98312 | tf_op jit(solution)/shard_map/ppermute | solution.py:519
  4.4 0.3 %collective-permute-start.2 = (bf16[2,64,128]{2,1,0:T(8,128)(2,1)S(1)}, bf16[2,64,128]{2,1,0:T(8,128)(2,1)S(1)}, u32[]{:S(2)}, u32[]{:S(2)}) collective-permute-start(bf16[2,64,128]{2,1,0:T(8,128)(2,1)S(1)} %get-tuple-element.41.refs_0_), channel_id=1, source_target_pairs={{0,3},{1,2},{2,1},{3,0},{4,7},{5,6},{6,5},{7,4},{8,11},{9,10},{10,... | collective-permute-start | bytes 98312 | tf_op jit(solution)/shard_map/ppermute | solution.py:520
  4.7 2.5 %shard_map.182 = (bf16[3,512,128]{2,1,0:T(8,128)(2,1)S(1)}, bf16[3,512,128]{2,1,0:T(8,128)(2,1)S(1)}, bf16[3,512,128]{2,1,0:T(8,128)(2,1)S(1)}, bf16[3,512,128]{...) custom-call(s32[1]{0:T(128)} %bitcast.at_ref, ...), custom_call_target="tpu_custom_call" | custom-call | flops 1006632960 | bytes 4194304 | tf_op jit(solution)/shard_map/pallas_call | solution.py:526
  7.2 0.0 collective-permute-done.refs_1_
  7.2 0.0 collective-permute-done.1.refs_2_
  7.2 0.5 %collective-permute-done.2.refs_3_ = bf16[2,64,128]{2,1,0:T(8,128)(2,1)S(1)} collective-permute-done((bf16[2,64,128]{2,1,0:T(8,128)(2,1)S(1)}, bf16[2,64,128]{2,1,0:T(8,128)(2,1)S(1)}, u32[]{:S(2)}, u32[]{:S(2)}) %collective-permute-start.2) | collective-permute-done | bytes 32800 | tf_op jit(solution)/shard_map/ppermute | solution.py:520
  7.8 0.5 %collective-permute-start.3 = (bf16[272,128]{1,0:T(8,128)(2,1)S(1)}, bf16[272,128]{1,0:T(8,128)(2,1)S(1)}, u32[]{:S(2)}, u32[]{:S(2)}) collective-permute-start(bf16[272,128]{1,0:T(8,128)(2,1)S(1)} %get-tuple-element.49), channel_id=1, source_target_pairs={{0,4},{8,12},{4,0},{12,8},{1,5},{9,13},{5,1},{13,9},{2,6},{10,14},... | collective-permute-start | bytes 208904 | tf_op jit(solution)/shard_map/ppermute | solution.py:556
  8.3 4.6 %collective-permute-start.4 = (bf16[272,128]{1,0:T(8,128)(2,1)S(1)}, bf16[272,128]{1,0:T(8,128)(2,1)S(1)}, u32[]{:S(2)}, u32[]{:S(2)}) collective-permute-start(bf16[272,128]{1,0:T(8,128)(2,1)S(1)} %get-tuple-element.50), channel_id=1, source_target_pairs={{4,8},{8,4},{0,0},{12,12},{5,9},{9,5},{1,1},{13,13},{6,10},{10,6},... | collective-permute-start | bytes 208904 | tf_op jit(solution)/shard_map/ppermute | solution.py:556
  12.9 0.0 copy-done
  12.9 2.8 %shard_map.184.inner_ref = bf16[3,384,128]{2,1,0:T(8,128)(2,1)S(1)} custom-call(s32[1]{0:T(128)} %bitcast.at_ref, s32[4,64]{1,0:T(4,128)S(1)} %copy-done, bf16[3,512,128]{2,1,0:T(8,128)(2,1)S(1)} %get-tuple-element.37.query_ref, bf16[3,512,128]{2,1,0:T(8,128)(2,1)S(1)} %get-tuple-element.38.key_ref.own_key_ref, ...), custom_call_target="tpu_custom_call" | custom-call | flops 603979776 | bytes 4194304 | tf_op jit(solution)/shard_map/pallas_call | solution.py:562
  15.7 0.0 collective-permute-done.3.first_ref
  15.7 0.0 collective-permute-done.4.second_ref
  15.8 2.0 %shard_map.185 = bf16[3,512,128]{2,1,0:T(8,128)(2,1)} custom-call(s32[1]{0:T(128)} %bitcast.at_ref, s32[4,64]{1,0:T(4,128)S(1)} %copy-done, bf16[3,512,128]{2,1,0:T(8,128)(2,1)S(1)} %get-tuple-element.37.query_ref, bf16[3,512,128]{2,1,0:T(8,128)(2,1)S(1)} %get-tuple-element.38.key_ref.own_key_ref, ...), custom_call_target="tpu_custom_call" | custom-call | flops 201326592 | bytes 4194304 | tf_op jit(solution)/shard_map/pallas_call | solution.py:577
  (1 shorter events, 0.0 us)
Async XLA Ops:
  2.8 10.2 %copy-start = (s32[4,64]{1,0:T(4,128)S(1)}, s32[4,64]{1,0:T(4,128)}, u32[]{:S(2)}) copy-start(s32[4,64]{1,0:T(4,128)} %counts_ref.3) | copy-start | bytes 3076
  2.8 4.4 %collective-permute-start = (bf16[2,64,128]{2,1,0:T(8,128)(2,1)S(1)}, bf16[2,64,128]{2,1,0:T(8,128)(2,1)S(1)}, u32[]{:S(2)}, u32[]{:S(2)}) collective-permute-start(bf16[2,64,128]{2,1,0:T(8,128)(2,1)S(1)} %get-tuple-element.41.refs_0_), channel_id=1, source_target_pairs={{0,1},{1,0},{2,3},{3,2},{4,5},{5,4},{6,7},{7,6},{8,9},{9,8},{10,11... | collective-permute-start | bytes 98312 | tf_op jit(solution)/shard_map/ppermute | solution.py:521
  2.8 4.4 %collective-permute-start.1 = (bf16[2,64,128]{2,1,0:T(8,128)(2,1)S(1)}, bf16[2,64,128]{2,1,0:T(8,128)(2,1)S(1)}, u32[]{:S(2)}, u32[]{:S(2)}) collective-permute-start(bf16[2,64,128]{2,1,0:T(8,128)(2,1)S(1)} %get-tuple-element.41.refs_0_), channel_id=1, source_target_pairs={{0,2},{2,0},{1,3},{3,1},{4,6},{6,4},{5,7},{7,5},{8,10},{10,8},{9,1... | collective-permute-start | bytes 98312 | tf_op jit(solution)/shard_map/ppermute | solution.py:519
  4.4 3.3 %collective-permute-start.2 = (bf16[2,64,128]{2,1,0:T(8,128)(2,1)S(1)}, bf16[2,64,128]{2,1,0:T(8,128)(2,1)S(1)}, u32[]{:S(2)}, u32[]{:S(2)}) collective-permute-start(bf16[2,64,128]{2,1,0:T(8,128)(2,1)S(1)} %get-tuple-element.41.refs_0_), channel_id=1, source_target_pairs={{0,3},{1,2},{2,1},{3,0},{4,7},{5,6},{6,5},{7,4},{8,11},{9,10},{10,... | collective-permute-start | bytes 98312 | tf_op jit(solution)/shard_map/ppermute | solution.py:520
  7.8 7.9 %collective-permute-start.3 = (bf16[272,128]{1,0:T(8,128)(2,1)S(1)}, bf16[272,128]{1,0:T(8,128)(2,1)S(1)}, u32[]{:S(2)}, u32[]{:S(2)}) collective-permute-start(bf16[272,128]{1,0:T(8,128)(2,1)S(1)} %get-tuple-element.49), channel_id=1, source_target_pairs={{0,4},{8,12},{4,0},{12,8},{1,5},{9,13},{5,1},{13,9},{2,6},{10,14},... | collective-permute-start | bytes 208904 | tf_op jit(solution)/shard_map/ppermute | solution.py:556
  8.3 7.4 %collective-permute-start.4 = (bf16[272,128]{1,0:T(8,128)(2,1)S(1)}, bf16[272,128]{1,0:T(8,128)(2,1)S(1)}, u32[]{:S(2)}, u32[]{:S(2)}) collective-permute-start(bf16[272,128]{1,0:T(8,128)(2,1)S(1)} %get-tuple-element.50), channel_id=1, source_target_pairs={{4,8},{8,4},{0,0},{12,12},{5,9},{9,5},{1,1},{13,13},{6,10},{10,6},... | collective-permute-start | bytes 208904 | tf_op jit(solution)/shard_map/ppermute | solution.py:556

commit v9 on v8

--- a/solution.py
+++ b/solution.py
@@ -361,8 +361,8 @@
     held_ref,
     inner_ref,
     w_kv,
+    second_ref,
     first_ref,
-    second_ref,
     out_hbm,
     key_ref,
     value_ref,
@@ -555,7 +555,8 @@
         pairs_of = sides + [(j, i) for i, j in sides] + [(i, i) for i in sorted(alone)]
         return lax.ppermute(value, "atoms", pairs_of)
 
-    first, second = swap(near, 0), swap(far, 1)
+    second = swap(far, 1)
+    first = swap(near, 0)
 
     margin = -(-EDGE // Q_WIN) * Q_WIN
     operands = (query, keys, values, gate, opened, trans, w_out, held)
@@ -573,7 +574,7 @@
     )(at, atom_counts, *map(in_vmem, operands))
 
     reach = margin - Q_WIN + K_WIN
-    operands += (inner, w_kv, first, second)
+    operands += (inner, w_kv, second, first)
     return pl.pallas_call(
         functools.partial(outer_kernel, heads, blocks),
         in_specs=[IN_SMEM] + [IN_VMEM] * (1 + len(operands)),

time: 17.9 us -> 19.4 us (1.084)
  the two profiles are of different devices: /device:TPU:8 before, /device:TPU:0 now
where the time goes in v9:
time: 19.4 us; the launch traced here: 19.2 us
  Pallas kernels  10.1 us (52%)
  starting transfers between devices  8.28 us (43%)
  waiting for transfers between devices  0.78 us (4%)
    ppermute x2, starting transfers between devices, swap(): return lax.ppermute(value, 'atoms', pairs_of)  5.13 us
    pallas_call x1, Pallas kernels, shards(): pl.pallas_call(functools.partial(inner_kernel, heads), in_specs=[IN_SMEM]...  2.78 us
    pallas_call x1, Pallas kernels, shards(): pl.pallas_call(functools.partial(pair_kernel, [len(arrays) for arrays in...  2.75 us
    ppermute x1, starting transfers between devices, shards(): across = lax.ppermute(own, 'pair', swapped)  2.67 us
    pallas_call x1, Pallas kernels, shards(): pl.pallas_call(project_kernel, in_specs=[IN_SMEM] + [IN_VMEM] * len(opera...  2.48 us
    pallas_call x1, Pallas kernels, shards(): pl.pallas_call(functools.partial(outer_kernel, heads, blocks), in_specs=[...  2.01 us
    ppermute x1, waiting for transfers between devices, shards(): lax.ppermute(own, ('pair', 'samp'), [(0, 3), (1, 2), (2, 1), (3, 0)])  0.77 us
    ppermute x1, starting transfers between devices, shards(): tiles = (own, lax.ppermute(own, 'samp', swapped), across, diagonal)  0.41 us
  transfers between devices with their start and end apart: 5, of which 1 were waited for; matrix products, arithmetic and copies ran while one was open for 0% of the time, Pallas kernels for 27%

profile of v9, /device:TPU:0, one launch (start us, length us, event | category | flops | bytes accessed | tf_op | source)
XLA Modules:
  0.0 19.2 jit_solution(13791717739721733852)
XLA Ops:
  0.0 2.8 %shard_map.181 = (bf16[2,64,128]{2,1,0:T(8,128)(2,1)S(1)}, bf16[3,512,128]{2,1,0:T(8,128)(2,1)S(1)}, bf16[512,128]{1,0:T(8,128)(2,1)S(1)}, bf16[128,256]{1,0:T(8...) custom-call(s32[1]{0:T(128)} %bitcast.1.core_ref, ...), custom_call_target="tpu_custom_call" | custom-call | flops 268435456 | bytes 4194304 | tf_op jit(solution)/shard_map/pallas_call | solution.py:501
  2.8 0.0 copy-start
  2.8 0.4 %collective-permute-start = (bf16[2,64,128]{2,1,0:T(8,128)(2,1)S(1)}, bf16[2,64,128]{2,1,0:T(8,128)(2,1)S(1)}, u32[]{:S(2)}, u32[]{:S(2)}) collective-permute-start(bf16[2,64,128]{2,1,0:T(8,128)(2,1)S(1)} %get-tuple-element.41.refs_0_), channel_id=1, source_target_pairs={{0,1},{1,0},{2,3},{3,2},{4,5},{5,4},{6,7},{7,6},{8,9},{9,8},{10,11... | collective-permute-start | bytes 98312 | tf_op jit(solution)/shard_map/ppermute | solution.py:521
  3.2 2.7 %collective-permute-start.1 = (bf16[2,64,128]{2,1,0:T(8,128)(2,1)S(1)}, bf16[2,64,128]{2,1,0:T(8,128)(2,1)S(1)}, u32[]{:S(2)}, u32[]{:S(2)}) collective-permute-start(bf16[2,64,128]{2,1,0:T(8,128)(2,1)S(1)} %get-tuple-element.41.refs_0_), channel_id=1, source_target_pairs={{0,2},{2,0},{1,3},{3,1},{4,6},{6,4},{5,7},{7,5},{8,10},{10,8},{9,1... | collective-permute-start | bytes 98312 | tf_op jit(solution)/shard_map/ppermute | solution.py:519
  5.9 0.1 collective-permute-start.2
  5.9 2.5 %shard_map.182 = (bf16[3,512,128]{2,1,0:T(8,128)(2,1)S(1)}, bf16[3,512,128]{2,1,0:T(8,128)(2,1)S(1)}, bf16[3,512,128]{2,1,0:T(8,128)(2,1)S(1)}, bf16[3,512,128]{...) custom-call(s32[1]{0:T(128)} %bitcast.at_ref, ...), custom_call_target="tpu_custom_call" | custom-call | flops 1006632960 | bytes 4194304 | tf_op jit(solution)/shard_map/pallas_call | solution.py:526
  8.4 0.0 collective-permute-done.refs_1_
  8.4 0.0 collective-permute-done.1.refs_2_
  8.4 0.8 %collective-permute-done.2.refs_3_ = bf16[2,64,128]{2,1,0:T(8,128)(2,1)S(1)} collective-permute-done((bf16[2,64,128]{2,1,0:T(8,128)(2,1)S(1)}, bf16[2,64,128]{2,1,0:T(8,128)(2,1)S(1)}, u32[]{:S(2)}, u32[]{:S(2)}) %collective-permute-start.2) | collective-permute-done | bytes 32800 | tf_op jit(solution)/shard_map/ppermute | solution.py:520
  9.2 0.7 %collective-permute-start.3 = (bf16[272,128]{1,0:T(8,128)(2,1)S(1)}, bf16[272,128]{1,0:T(8,128)(2,1)S(1)}, u32[]{:S(2)}, u32[]{:S(2)}) collective-permute-start(bf16[272,128]{1,0:T(8,128)(2,1)S(1)} %get-tuple-element.49), channel_id=1, source_target_pairs={{4,8},{8,4},{0,0},{12,12},{5,9},{9,5},{1,1},{13,13},{6,10},{10,6},... | collective-permute-start | bytes 208904 | tf_op jit(solution)/shard_map/ppermute | solution.py:556
  9.9 4.5 %collective-permute-start.4 = (bf16[272,128]{1,0:T(8,128)(2,1)S(1)}, bf16[272,128]{1,0:T(8,128)(2,1)S(1)}, u32[]{:S(2)}, u32[]{:S(2)}) collective-permute-start(bf16[272,128]{1,0:T(8,128)(2,1)S(1)} %get-tuple-element.50), channel_id=1, source_target_pairs={{0,4},{8,12},{4,0},{12,8},{1,5},{9,13},{5,1},{13,9},{2,6},{10,14},... | collective-permute-start | bytes 208904 | tf_op jit(solution)/shard_map/ppermute | solution.py:556
  14.4 0.0 copy-done
  14.4 2.8 %shard_map.184.inner_ref = bf16[3,384,128]{2,1,0:T(8,128)(2,1)S(1)} custom-call(s32[1]{0:T(128)} %bitcast.at_ref, s32[4,64]{1,0:T(4,128)S(1)} %copy-done, bf16[3,512,128]{2,1,0:T(8,128)(2,1)S(1)} %get-tuple-element.37.query_ref, bf16[3,512,128]{2,1,0:T(8,128)(2,1)S(1)} %get-tuple-element.38.key_ref.own_key_ref, ...), custom_call_target="tpu_custom_call" | custom-call | flops 603979776 | bytes 4194304 | tf_op jit(solution)/shard_map/pallas_call | solution.py:563
  17.2 0.0 collective-permute-done.3.second_ref
  17.2 0.0 collective-permute-done.4.first_ref
  17.2 2.0 %shard_map.185 = bf16[3,512,128]{2,1,0:T(8,128)(2,1)} custom-call(s32[1]{0:T(128)} %bitcast.at_ref, s32[4,64]{1,0:T(4,128)S(1)} %copy-done, bf16[3,512,128]{2,1,0:T(8,128)(2,1)S(1)} %get-tuple-element.37.query_ref, bf16[3,512,128]{2,1,0:T(8,128)(2,1)S(1)} %get-tuple-element.38.key_ref.own_key_ref, ...), custom_call_target="tpu_custom_call" | custom-call | flops 201326592 | bytes 4194304 | tf_op jit(solution)/shard_map/pallas_call | solution.py:578
  (1 shorter events, 0.0 us)
Async XLA Ops:
  2.8 11.6 %copy-start = (s32[4,64]{1,0:T(4,128)S(1)}, s32[4,64]{1,0:T(4,128)}, u32[]{:S(2)}) copy-start(s32[4,64]{1,0:T(4,128)} %counts_ref.3) | copy-start | bytes 3076
  2.8 5.6 %collective-permute-start = (bf16[2,64,128]{2,1,0:T(8,128)(2,1)S(1)}, bf16[2,64,128]{2,1,0:T(8,128)(2,1)S(1)}, u32[]{:S(2)}, u32[]{:S(2)}) collective-permute-start(bf16[2,64,128]{2,1,0:T(8,128)(2,1)S(1)} %get-tuple-element.41.refs_0_), channel_id=1, source_target_pairs={{0,1},{1,0},{2,3},{3,2},{4,5},{5,4},{6,7},{7,6},{8,9},{9,8},{10,11... | collective-permute-start | bytes 98312 | tf_op jit(solution)/shard_map/ppermute | solution.py:521
  3.2 5.2 %collective-permute-start.1 = (bf16[2,64,128]{2,1,0:T(8,128)(2,1)S(1)}, bf16[2,64,128]{2,1,0:T(8,128)(2,1)S(1)}, u32[]{:S(2)}, u32[]{:S(2)}) collective-permute-start(bf16[2,64,128]{2,1,0:T(8,128)(2,1)S(1)} %get-tuple-element.41.refs_0_), channel_id=1, source_target_pairs={{0,2},{2,0},{1,3},{3,1},{4,6},{6,4},{5,7},{7,5},{8,10},{10,8},{9,1... | collective-permute-start | bytes 98312 | tf_op jit(solution)/shard_map/ppermute | solution.py:519
  5.9 3.3 %collective-permute-start.2 = (bf16[2,64,128]{2,1,0:T(8,128)(2,1)S(1)}, bf16[2,64,128]{2,1,0:T(8,128)(2,1)S(1)}, u32[]{:S(2)}, u32[]{:S(2)}) collective-permute-start(bf16[2,64,128]{2,1,0:T(8,128)(2,1)S(1)} %get-tuple-element.41.refs_0_), channel_id=1, source_target_pairs={{0,3},{1,2},{2,1},{3,0},{4,7},{5,6},{6,5},{7,4},{8,11},{9,10},{10,... | collective-permute-start | bytes 98312 | tf_op jit(solution)/shard_map/ppermute | solution.py:520
  9.2 7.9 %collective-permute-start.3 = (bf16[272,128]{1,0:T(8,128)(2,1)S(1)}, bf16[272,128]{1,0:T(8,128)(2,1)S(1)}, u32[]{:S(2)}, u32[]{:S(2)}) collective-permute-start(bf16[272,128]{1,0:T(8,128)(2,1)S(1)} %get-tuple-element.49), channel_id=1, source_target_pairs={{4,8},{8,4},{0,0},{12,12},{5,9},{9,5},{1,1},{13,13},{6,10},{10,6},... | collective-permute-start | bytes 208904 | tf_op jit(solution)/shard_map/ppermute | solution.py:556
  9.9 7.3 %collective-permute-start.4 = (bf16[272,128]{1,0:T(8,128)(2,1)S(1)}, bf16[272,128]{1,0:T(8,128)(2,1)S(1)}, u32[]{:S(2)}, u32[]{:S(2)}) collective-permute-start(bf16[272,128]{1,0:T(8,128)(2,1)S(1)} %get-tuple-element.50), channel_id=1, source_target_pairs={{0,4},{8,12},{4,0},{12,8},{1,5},{9,13},{5,1},{13,9},{2,6},{10,14},... | collective-permute-start | bytes 208904 | tf_op jit(solution)/shard_map/ppermute | solution.py:556

commit v10 on v8

--- a/solution.py
+++ b/solution.py
@@ -45,21 +45,15 @@
     return jnp.concatenate([rows[:half], rows[half:]], 1)
 
 
-def centring(width):
-    same = iota((width, width), 0) == iota((width, width), 1)
-    return jnp.where(same, 1.0 - 1.0 / width, -1.0 / width).astype(BF16)
-
-
-def averaging(width):
-    return jnp.full((width, width), 1.0 / width, BF16)
+def centre(rows):
+    values = rows.astype(F32)
+    centred = values - jnp.mean(values, axis=-1, keepdims=True)
+    return centred, jnp.mean(centred * centred, axis=-1, keepdims=True)
 
 
 def layer_norm(rows):
-    width = rows.shape[1]
-    centred = dot(side_by_side(rows), twice(centring(width)))
-    variance = dot((centred * centred).astype(BF16), twice(averaging(width)))
-    normal = centred * lax.rsqrt(variance + EPSILON)
-    return jnp.concatenate([normal[:, :width], normal[:, width:]], 0)
+    centred, variance = centre(rows)
+    return centred * lax.rsqrt(variance + EPSILON)
 
 
 def sigmoid(values):
@@ -108,19 +102,13 @@
     for i in range(pieces):
         pair_copy(i).start()
 
-    centre = twice(centring(width))
     copies[0].wait()
     w_pair = w_pair_ref[...].astype(F32)
     spread = jnp.concatenate(
         [jnp.broadcast_to(w_pair[h : h + 1], (group, width)) for h in range(heads)], 0
     )
-    weight = spread.T.astype(BF16)
-    mean = jnp.full((width, lanes), 1.0 / width, BF16)
-    blank = jnp.zeros((width, lanes), BF16)
-    mix = jnp.concatenate(
-        [jnp.concatenate([weight, blank], 1), jnp.concatenate([blank, mean], 1)], 0
-    )
-    slot = iota((cols, 2 * lanes), 1) % group
+    mix = twice(spread.T.astype(BF16))
+    slot = iota((cols, lanes), 1) % group
 
     @pl.loop(0, rows // group)
     def _(chunk):
@@ -133,17 +121,16 @@
                 copy.start()
 
         pair = pair_ref[pl.ds(chunk * group, group)].reshape(group * cols, width)
-        centred = dot(side_by_side(pair), centre)
-        rounded = centred.astype(BF16)
-        squares = (centred * centred).astype(BF16)
-        total = jnp.zeros((cols, 2 * lanes), F32)
-        for part in range(2):
-            cut = slice(part * width, (part + 1) * width)
-            mixed = dot(jnp.concatenate([rounded[:, cut], squares[:, cut]], 1), mix)
-            mixed = mixed.reshape(half, cols, 2 * lanes)
-            for i in range(half):
-                total = jnp.where(slot == part * half + i, mixed[i], total)
-        bias = (total[:, :lanes] * lax.rsqrt(total[:, lanes:] + EPSILON)).astype(BF16)
+        centred, variance = centre(pair)
+        variance = variance.reshape(group, cols, 1)
+        mixed = dot(side_by_side(centred.astype(BF16)), mix).reshape(half, cols, 2 * lanes)
+        total = jnp.zeros((cols, lanes), F32)
+        spread_out = jnp.zeros((cols, lanes), F32)
+        for i in range(group):
+            side = slice(i // half * lanes, (i // half + 1) * lanes)
+            total = jnp.where(slot == i, mixed[i % half, :, side], total)
+            spread_out = jnp.where(slot == i, variance[i], spread_out)
+        bias = (total * lax.rsqrt(spread_out + EPSILON)).astype(BF16)
         tile_ref[chunk] = bias
 
     for copy in copies[1:]:
@@ -259,8 +246,7 @@
     same_head = (lane_head == row_head).astype(F32).astype(BF16)
     own_head = iota((rows, width), 1) // head_dim == iota((rows, width), 0) // Q_WIN
     own_head = own_head.astype(F32).astype(BF16)
-    channel_head = iota((Q_WIN, 2 * width), 1) % width // head_dim
-    ones = jnp.ones((K_WIN, width), BF16)
+    channel_head = iota((Q_WIN, width), 1) // head_dim
     scaling = LOG2E / math.sqrt(head_dim)
 
     biases = []
@@ -269,27 +255,49 @@
         bias = lax.dot_general(pick, near, LAST, preferred_element_type=F32) * LOG2E
         biases.append(bias if mask is None else jnp.where(mask, bias, MASKED))
     units = [(sample, i) for i in range(len(windows)) for sample in range(samples)]
+
+    def diagonal(parts):
+        if len(parts) == 1:
+            return parts[0]
+        blank = jnp.zeros_like(parts[0])
+        return jnp.concatenate(
+            [jnp.concatenate([parts[0], blank], 1), jnp.concatenate([blank, parts[1]], 1)], 0
+        )
+
     scores = []
-    for sample, i in units:
-        query = query_ref[sample, pl.ds(windows[i][0], Q_WIN), :]
-        query = jnp.concatenate([query] * heads, 0) * own_head
-        keys = windows[i][1](sample)[0]
-        product = lax.dot_general(query, keys, LAST, preferred_element_type=F32)
-        scores.append(product * scaling + biases[i])
+    for first in range(0, len(units), 2):
+        couple = units[first : first + 2]
+        queries, keys = [], []
+        for sample, i in couple:
+            query = query_ref[sample, pl.ds(windows[i][0], Q_WIN), :]
+            queries.append(jnp.concatenate([query] * heads, 0) * own_head)
+            keys.append(windows[i][1](sample)[0])
+        product = lax.dot_general(
+            jnp.concatenate(queries, 1), diagonal(keys), LAST, preferred_element_type=F32
+        )
+        for j, (_, i) in enumerate(couple):
+            cut = slice(j * K_WIN, (j + 1) * K_WIN)
+            scores.append(product[:, cut] * scaling + biases[i])
     tops = [jnp.max(score, axis=-1, keepdims=True) for score in scores]
-    raised = [jnp.exp2(score - top).astype(BF16) for score, top in zip(scores, tops)]
-    for (sample, i), weight in zip(units, raised):
-        values = windows[i][1](sample)[1]
-        mixed = dot(weight, jnp.concatenate([values, ones], 1))
-        picked = mixed[:Q_WIN]
-        for head in range(1, heads):
-            picked = jnp.where(
-                channel_head == head, mixed[head * Q_WIN : (head + 1) * Q_WIN], picked
-            )
-        attended = picked[:, :width] * pl.reciprocal(picked[:, width:], approx=True)
-        at = pl.ds(windows[i][0], Q_WIN)
-        gate = gate_ref[sample, at, :].astype(F32)
-        gated_ref[sample, at, :] = (gate * attended).astype(BF16)
+    raised = [jnp.exp2(score - top) for score, top in zip(scores, tops)]
+    sums = [jnp.sum(weight, axis=-1, keepdims=True) for weight in raised]
+    raised = [weight.astype(BF16) for weight in raised]
+    for first in range(0, len(units), 2):
+        couple = units[first : first + 2]
+        values = [windows[i][1](sample)[1] for sample, i in couple]
+        mixed = dot(jnp.concatenate(raised[first : first + 2], 1), diagonal(values))
+        for j, (sample, i) in enumerate(couple):
+            cut = slice(j * width, (j + 1) * width)
+            picked, total = mixed[:Q_WIN, cut], sums[first + j][:Q_WIN]
+            total = jnp.broadcast_to(total, picked.shape)
+            for head in range(1, heads):
+                rows_of = slice(head * Q_WIN, (head + 1) * Q_WIN)
+                picked = jnp.where(channel_head == head, mixed[rows_of, cut], picked)
+                total = jnp.where(channel_head == head, sums[first + j][rows_of], total)
+            attended = picked * pl.reciprocal(total, approx=True)
+            at = pl.ds(windows[i][0], Q_WIN)
+            gate = gate_ref[sample, at, :].astype(F32)
+            gated_ref[sample, at, :] = (gate * attended).astype(BF16)
 
 
 def close(sample, cut, gated_ref, open_ref, trans_ref, w_out_ref):

time: 17.9 us -> 18.3 us (1.022)
  Pallas kernels: 10.1 us -> 10.4 us
    pallas_call x1, Pallas kernels: 2.8 us -> 3.11 us  [shards(): pl.pallas_call(functools.partial(inner_kernel, heads), in_specs=[IN_SMEM]...]
  transfers between devices with their start and end apart: 5 -> 5, of which waited for: 1 -> 1; matrix products, arithmetic and copies ran while one was open for 0% -> 0% of each run, Pallas kernels for 30% -> 31%
where the time goes in v10:
time: 18.3 us; the launch traced here: 18.1 us
  Pallas kernels  10.4 us (57%)
  starting transfers between devices  7.05 us (39%)
  waiting for transfers between devices  0.57 us (3%)
    ppermute x2, starting transfers between devices, swap(): return lax.ppermute(value, 'atoms', pairs_of)  5.11 us
    pallas_call x1, Pallas kernels, shards(): pl.pallas_call(functools.partial(inner_kernel, heads), in_specs=[IN_SMEM]...  3.11 us
    pallas_call x1, Pallas kernels, shards(): pl.pallas_call(functools.partial(pair_kernel, [len(arrays) for arrays in...  2.64 us
    pallas_call x1, Pallas kernels, shards(): pl.pallas_call(project_kernel, in_specs=[IN_SMEM] + [IN_VMEM] * len(opera...  2.45 us
    pallas_call x1, Pallas kernels, shards(): pl.pallas_call(functools.partial(outer_kernel, heads, blocks), in_specs=[...  2.13 us
    ppermute x1, starting transfers between devices, shards(): across = lax.ppermute(own, 'pair', swapped)  1.56 us
    ppermute x1, waiting for transfers between devices, shards(): lax.ppermute(own, ('pair', 'samp'), [(0, 3), (1, 2), (2, 1), (3, 0)])  0.56 us
  transfers between devices with their start and end apart: 5, of which 1 were waited for; matrix products, arithmetic and copies ran while one was open for 0% of the time, Pallas kernels for 31%

profile of v10, /device:TPU:8, one launch (start us, length us, event | category | flops | bytes accessed | tf_op | source)
XLA Modules:
  0.0 18.1 jit_solution(1720188418075510739)
XLA Ops:
  0.0 2.6 %shard_map.181 = (bf16[2,64,128]{2,1,0:T(8,128)(2,1)S(1)}, bf16[3,512,128]{2,1,0:T(8,128)(2,1)S(1)}, bf16[512,128]{1,0:T(8,128)(2,1)S(1)}, bf16[128,256]{1,0:T(8...) custom-call(s32[1]{0:T(128)} %bitcast.1.core_ref, ...), custom_call_target="tpu_custom_call" | custom-call | flops 268435456 | bytes 4194304 | tf_op jit(solution)/shard_map/pallas_call | solution.py:509
  2.6 0.0 copy-start
  2.7 0.1 collective-permute-start
  2.7 1.6 %collective-permute-start.1 = (bf16[2,64,128]{2,1,0:T(8,128)(2,1)S(1)}, bf16[2,64,128]{2,1,0:T(8,128)(2,1)S(1)}, u32[]{:S(2)}, u32[]{:S(2)}) collective-permute-start(bf16[2,64,128]{2,1,0:T(8,128)(2,1)S(1)} %get-tuple-element.41.refs_0_), channel_id=1, source_target_pairs={{0,2},{2,0},{1,3},{3,1},{4,6},{6,4},{5,7},{7,5},{8,10},{10,8},{9,1... | collective-permute-start | bytes 98312 | tf_op jit(solution)/shard_map/ppermute | solution.py:527
  4.3 0.3 %collective-permute-start.2 = (bf16[2,64,128]{2,1,0:T(8,128)(2,1)S(1)}, bf16[2,64,128]{2,1,0:T(8,128)(2,1)S(1)}, u32[]{:S(2)}, u32[]{:S(2)}) collective-permute-start(bf16[2,64,128]{2,1,0:T(8,128)(2,1)S(1)} %get-tuple-element.41.refs_0_), channel_id=1, source_target_pairs={{0,3},{1,2},{2,1},{3,0},{4,7},{5,6},{6,5},{7,4},{8,11},{9,10},{10,... | collective-permute-start | bytes 98312 | tf_op jit(solution)/shard_map/ppermute | solution.py:528
  4.6 2.4 %shard_map.182 = (bf16[3,512,128]{2,1,0:T(8,128)(2,1)S(1)}, bf16[3,512,128]{2,1,0:T(8,128)(2,1)S(1)}, bf16[3,512,128]{2,1,0:T(8,128)(2,1)S(1)}, bf16[3,512,128]{...) custom-call(s32[1]{0:T(128)} %bitcast.at_ref, ...), custom_call_target="tpu_custom_call" | custom-call | flops 1006632960 | bytes 4194304 | tf_op jit(solution)/shard_map/pallas_call | solution.py:534
  7.1 0.0 collective-permute-done.refs_1_
  7.1 0.0 collective-permute-done.1.refs_2_
  7.1 0.6 %collective-permute-done.2.refs_3_ = bf16[2,64,128]{2,1,0:T(8,128)(2,1)S(1)} collective-permute-done((bf16[2,64,128]{2,1,0:T(8,128)(2,1)S(1)}, bf16[2,64,128]{2,1,0:T(8,128)(2,1)S(1)}, u32[]{:S(2)}, u32[]{:S(2)}) %collective-permute-start.2) | collective-permute-done | bytes 32800 | tf_op jit(solution)/shard_map/ppermute | solution.py:528
  7.7 0.5 %collective-permute-start.3 = (bf16[272,128]{1,0:T(8,128)(2,1)S(1)}, bf16[272,128]{1,0:T(8,128)(2,1)S(1)}, u32[]{:S(2)}, u32[]{:S(2)}) collective-permute-start(bf16[272,128]{1,0:T(8,128)(2,1)S(1)} %get-tuple-element.49), channel_id=1, source_target_pairs={{0,4},{8,12},{4,0},{12,8},{1,5},{9,13},{5,1},{13,9},{2,6},{10,14},... | collective-permute-start | bytes 208904 | tf_op jit(solution)/shard_map/ppermute | solution.py:564
  8.2 4.6 %collective-permute-start.4 = (bf16[272,128]{1,0:T(8,128)(2,1)S(1)}, bf16[272,128]{1,0:T(8,128)(2,1)S(1)}, u32[]{:S(2)}, u32[]{:S(2)}) collective-permute-start(bf16[272,128]{1,0:T(8,128)(2,1)S(1)} %get-tuple-element.50), channel_id=1, source_target_pairs={{4,8},{8,4},{0,0},{12,12},{5,9},{9,5},{1,1},{13,13},{6,10},{10,6},... | collective-permute-start | bytes 208904 | tf_op jit(solution)/shard_map/ppermute | solution.py:564
  12.8 0.0 copy-done
  12.8 3.1 %shard_map.184.inner_ref = bf16[3,384,128]{2,1,0:T(8,128)(2,1)S(1)} custom-call(s32[1]{0:T(128)} %bitcast.at_ref, s32[4,64]{1,0:T(4,128)S(1)} %copy-done, bf16[3,512,128]{2,1,0:T(8,128)(2,1)S(1)} %get-tuple-element.37.query_ref, bf16[3,512,128]{2,1,0:T(8,128)(2,1)S(1)} %get-tuple-element.38.key_ref.own_key_ref, ...), custom_call_target="tpu_custom_call" | custom-call | flops 603979776 | bytes 4194304 | tf_op jit(solution)/shard_map/pallas_call | solution.py:570
  15.9 0.0 collective-permute-done.3.first_ref
  16.0 0.0 collective-permute-done.4.second_ref
  16.0 2.1 %shard_map.185 = bf16[3,512,128]{2,1,0:T(8,128)(2,1)} custom-call(s32[1]{0:T(128)} %bitcast.at_ref, s32[4,64]{1,0:T(4,128)S(1)} %copy-done, bf16[3,512,128]{2,1,0:T(8,128)(2,1)S(1)} %get-tuple-element.37.query_ref, bf16[3,512,128]{2,1,0:T(8,128)(2,1)S(1)} %get-tuple-element.38.key_ref.own_key_ref, ...), custom_call_target="tpu_custom_call" | custom-call | flops 201326592 | bytes 4194304 | tf_op jit(solution)/shard_map/pallas_call | solution.py:585
  (1 shorter events, 0.0 us)
Async XLA Ops:
  2.6 10.2 %copy-start = (s32[4,64]{1,0:T(4,128)S(1)}, s32[4,64]{1,0:T(4,128)}, u32[]{:S(2)}) copy-start(s32[4,64]{1,0:T(4,128)} %counts_ref.3) | copy-start | bytes 3076
  2.7 4.4 %collective-permute-start = (bf16[2,64,128]{2,1,0:T(8,128)(2,1)S(1)}, bf16[2,64,128]{2,1,0:T(8,128)(2,1)S(1)}, u32[]{:S(2)}, u32[]{:S(2)}) collective-permute-start(bf16[2,64,128]{2,1,0:T(8,128)(2,1)S(1)} %get-tuple-element.41.refs_0_), channel_id=1, source_target_pairs={{0,1},{1,0},{2,3},{3,2},{4,5},{5,4},{6,7},{7,6},{8,9},{9,8},{10,11... | collective-permute-start | bytes 98312 | tf_op jit(solution)/shard_map/ppermute | solution.py:529
  2.7 4.3 %collective-permute-start.1 = (bf16[2,64,128]{2,1,0:T(8,128)(2,1)S(1)}, bf16[2,64,128]{2,1,0:T(8,128)(2,1)S(1)}, u32[]{:S(2)}, u32[]{:S(2)}) collective-permute-start(bf16[2,64,128]{2,1,0:T(8,128)(2,1)S(1)} %get-tuple-element.41.refs_0_), channel_id=1, source_target_pairs={{0,2},{2,0},{1,3},{3,1},{4,6},{6,4},{5,7},{7,5},{8,10},{10,8},{9,1... | collective-permute-start | bytes 98312 | tf_op jit(solution)/shard_map/ppermute | solution.py:527
  4.3 3.3 %collective-permute-start.2 = (bf16[2,64,128]{2,1,0:T(8,128)(2,1)S(1)}, bf16[2,64,128]{2,1,0:T(8,128)(2,1)S(1)}, u32[]{:S(2)}, u32[]{:S(2)}) collective-permute-start(bf16[2,64,128]{2,1,0:T(8,128)(2,1)S(1)} %get-tuple-element.41.refs_0_), channel_id=1, source_target_pairs={{0,3},{1,2},{2,1},{3,0},{4,7},{5,6},{6,5},{7,4},{8,11},{9,10},{10,... | collective-permute-start | bytes 98312 | tf_op jit(solution)/shard_map/ppermute | solution.py:528
  7.7 8.3 %collective-permute-start.3 = (bf16[272,128]{1,0:T(8,128)(2,1)S(1)}, bf16[272,128]{1,0:T(8,128)(2,1)S(1)}, u32[]{:S(2)}, u32[]{:S(2)}) collective-permute-start(bf16[272,128]{1,0:T(8,128)(2,1)S(1)} %get-tuple-element.49), channel_id=1, source_target_pairs={{0,4},{8,12},{4,0},{12,8},{1,5},{9,13},{5,1},{13,9},{2,6},{10,14},... | collective-permute-start | bytes 208904 | tf_op jit(solution)/shard_map/ppermute | solution.py:564
  8.2 7.7 %collective-permute-start.4 = (bf16[272,128]{1,0:T(8,128)(2,1)S(1)}, bf16[272,128]{1,0:T(8,128)(2,1)S(1)}, u32[]{:S(2)}, u32[]{:S(2)}) collective-permute-start(bf16[272,128]{1,0:T(8,128)(2,1)S(1)} %get-tuple-element.50), channel_id=1, source_target_pairs={{4,8},{8,4},{0,0},{12,12},{5,9},{9,5},{1,1},{13,13},{6,10},{10,6},... | collective-permute-start | bytes 208904 | tf_op jit(solution)/shard_map/ppermute | solution.py:564

commit v11 on v8

--- a/solution.py
+++ b/solution.py
@@ -45,25 +45,19 @@
     return jnp.concatenate([rows[:half], rows[half:]], 1)
 
 
-def centring(width):
-    same = iota((width, width), 0) == iota((width, width), 1)
-    return jnp.where(same, 1.0 - 1.0 / width, -1.0 / width).astype(BF16)
-
-
-def averaging(width):
-    return jnp.full((width, width), 1.0 / width, BF16)
+def centre(rows):
+    values = rows.astype(F32)
+    centred = values - jnp.mean(values, axis=-1, keepdims=True)
+    return centred, jnp.mean(centred * centred, axis=-1, keepdims=True)
 
 
 def layer_norm(rows):
-    width = rows.shape[1]
-    centred = dot(side_by_side(rows), twice(centring(width)))
-    variance = dot((centred * centred).astype(BF16), twice(averaging(width)))
-    normal = centred * lax.rsqrt(variance + EPSILON)
-    return jnp.concatenate([normal[:, :width], normal[:, width:]], 0)
+    centred, variance = centre(rows)
+    return centred * lax.rsqrt(variance + EPSILON)
 
 
 def sigmoid(values):
-    return pl.reciprocal(1.0 + jnp.exp2(values * -LOG2E), approx=True)
+    return 0.5 * jnp.tanh(0.5 * values) + 0.5
 
 
 def attn_norm(cond, single, ada):
@@ -107,43 +101,33 @@
     copies[0].start()
     for i in range(pieces):
         pair_copy(i).start()
-
-    centre = twice(centring(width))
+    for copy in copies[1:]:
+        copy.start()
+
     copies[0].wait()
     w_pair = w_pair_ref[...].astype(F32)
     spread = jnp.concatenate(
         [jnp.broadcast_to(w_pair[h : h + 1], (group, width)) for h in range(heads)], 0
     )
-    weight = spread.T.astype(BF16)
-    mean = jnp.full((width, lanes), 1.0 / width, BF16)
-    blank = jnp.zeros((width, lanes), BF16)
-    mix = jnp.concatenate(
-        [jnp.concatenate([weight, blank], 1), jnp.concatenate([blank, mean], 1)], 0
-    )
-    slot = iota((cols, 2 * lanes), 1) % group
+    mix = twice(spread.T.astype(BF16))
+    slot = iota((cols, lanes), 1) % group
 
     @pl.loop(0, rows // group)
     def _(chunk):
         for part in range(2):
             pair_copy(chunk * 2 + part).wait()
 
-        @pl.when(chunk == 0)
-        def _():
-            for copy in copies[1:]:
-                copy.start()
-
         pair = pair_ref[pl.ds(chunk * group, group)].reshape(group * cols, width)
-        centred = dot(side_by_side(pair), centre)
-        rounded = centred.astype(BF16)
-        squares = (centred * centred).astype(BF16)
-        total = jnp.zeros((cols, 2 * lanes), F32)
-        for part in range(2):
-            cut = slice(part * width, (part + 1) * width)
-            mixed = dot(jnp.concatenate([rounded[:, cut], squares[:, cut]], 1), mix)
-            mixed = mixed.reshape(half, cols, 2 * lanes)
-            for i in range(half):
-                total = jnp.where(slot == part * half + i, mixed[i], total)
-        bias = (total[:, :lanes] * lax.rsqrt(total[:, lanes:] + EPSILON)).astype(BF16)
+        centred, variance = centre(pair)
+        variance = variance.reshape(group, cols, 1)
+        mixed = dot(side_by_side(centred.astype(BF16)), mix).reshape(half, cols, 2 * lanes)
+        total = jnp.zeros((cols, lanes), F32)
+        spread_out = jnp.zeros((cols, lanes), F32)
+        for i in range(group):
+            side = slice(i // half * lanes, (i // half + 1) * lanes)
+            total = jnp.where(slot == i, mixed[i % half, :, side], total)
+            spread_out = jnp.where(slot == i, variance[i], spread_out)
+        bias = (total * lax.rsqrt(spread_out + EPSILON)).astype(BF16)
         tile_ref[chunk] = bias
 
     for copy in copies[1:]:
@@ -329,7 +313,7 @@
     reach = bounds(counts_ref, device_at, row_tokens(heads, tok_here))
     skip = -(-EDGE // Q_WIN)
     inner = atoms_here // Q_WIN - 2 * skip
-    batch = math.gcd(inner, 4)
+    batch = math.gcd(inner, 12)
 
     @pl.loop(0, inner // batch)
     def _(turn):

time: 17.9 us -> 17.9 us (level)
  the two profiles are of different devices: /device:TPU:8 before, /device:TPU:16 now
where the time goes in v11:
time: 17.9 us; the launch traced here: 17.7 us
  Pallas kernels  9.51 us (53%)
  starting transfers between devices  5.48 us (31%)
  waiting for transfers between devices  2.65 us (15%)
    ppermute x2, starting transfers between devices, swap(): return lax.ppermute(value, 'atoms', pairs_of)  3.55 us
    pallas_call x1, Pallas kernels, shards(): pl.pallas_call(functools.partial(pair_kernel, [len(arrays) for arrays in...  2.84 us
    pallas_call x1, Pallas kernels, shards(): pl.pallas_call(project_kernel, in_specs=[IN_SMEM] + [IN_VMEM] * len(opera...  2.4 us
    pallas_call x1, Pallas kernels, shards(): pl.pallas_call(functools.partial(inner_kernel, heads), in_specs=[IN_SMEM]...  2.21 us
    ppermute x2, waiting for transfers between devices, swap(): return lax.ppermute(value, 'atoms', pairs_of)  2.03 us
    pallas_call x1, Pallas kernels, shards(): pl.pallas_call(functools.partial(outer_kernel, heads, blocks), in_specs=[...  2.01 us
    ppermute x1, starting transfers between devices, shards(): across = lax.ppermute(own, 'pair', swapped)  1.56 us
    ppermute x1, waiting for transfers between devices, shards(): lax.ppermute(own, ('pair', 'samp'), [(0, 3), (1, 2), (2, 1), (3, 0)])  0.61 us
  transfers between devices with their start and end apart: 5, of which 2 were waited for; matrix products, arithmetic and copies ran while one was open for 0% of the time, Pallas kernels for 26%

profile of v11, /device:TPU:16, one launch (start us, length us, event | category | flops | bytes accessed | tf_op | source)
XLA Modules:
  0.0 17.7 jit_solution(9729284758900622115)
XLA Ops:
  0.0 2.8 %shard_map.181 = (bf16[2,64,128]{2,1,0:T(8,128)(2,1)S(1)}, bf16[3,512,128]{2,1,0:T(8,128)(2,1)S(1)}, bf16[512,128]{1,0:T(8,128)(2,1)S(1)}, bf16[128,256]{1,0:T(8...) custom-call(s32[1]{0:T(128)} %bitcast.1.core_ref, ...), custom_call_target="tpu_custom_call" | custom-call | flops 268435456 | bytes 4194304 | tf_op jit(solution)/shard_map/pallas_call | solution.py:485
  2.9 0.0 copy-start
  2.9 0.1 collective-permute-start
  2.9 1.6 %collective-permute-start.1 = (bf16[2,64,128]{2,1,0:T(8,128)(2,1)S(1)}, bf16[2,64,128]{2,1,0:T(8,128)(2,1)S(1)}, u32[]{:S(2)}, u32[]{:S(2)}) collective-permute-start(bf16[2,64,128]{2,1,0:T(8,128)(2,1)S(1)} %get-tuple-element.41.refs_0_), channel_id=1, source_target_pairs={{0,2},{2,0},{1,3},{3,1},{4,6},{6,4},{5,7},{7,5},{8,10},{10,8},{9,1... | collective-permute-start | bytes 98312 | tf_op jit(solution)/shard_map/ppermute | solution.py:503
  4.5 0.3 %collective-permute-start.2 = (bf16[2,64,128]{2,1,0:T(8,128)(2,1)S(1)}, bf16[2,64,128]{2,1,0:T(8,128)(2,1)S(1)}, u32[]{:S(2)}, u32[]{:S(2)}) collective-permute-start(bf16[2,64,128]{2,1,0:T(8,128)(2,1)S(1)} %get-tuple-element.41.refs_0_), channel_id=1, source_target_pairs={{0,3},{1,2},{2,1},{3,0},{4,7},{5,6},{6,5},{7,4},{8,11},{9,10},{10,... | collective-permute-start | bytes 98312 | tf_op jit(solution)/shard_map/ppermute | solution.py:504
  4.8 2.4 %shard_map.182 = (bf16[3,512,128]{2,1,0:T(8,128)(2,1)S(1)}, bf16[3,512,128]{2,1,0:T(8,128)(2,1)S(1)}, bf16[3,512,128]{2,1,0:T(8,128)(2,1)S(1)}, bf16[3,512,128]{...) custom-call(s32[1]{0:T(128)} %bitcast.at_ref, ...), custom_call_target="tpu_custom_call" | custom-call | flops 1006632960 | bytes 4194304 | tf_op jit(solution)/shard_map/pallas_call | solution.py:510
  7.2 0.0 collective-permute-done.refs_1_
  7.2 0.0 collective-permute-done.1.refs_2_
  7.2 0.6 %collective-permute-done.2.refs_3_ = bf16[2,64,128]{2,1,0:T(8,128)(2,1)S(1)} collective-permute-done((bf16[2,64,128]{2,1,0:T(8,128)(2,1)S(1)}, bf16[2,64,128]{2,1,0:T(8,128)(2,1)S(1)}, u32[]{:S(2)}, u32[]{:S(2)}) %collective-permute-start.2) | collective-permute-done | bytes 32800 | tf_op jit(solution)/shard_map/ppermute | solution.py:504
  7.9 1.6 %collective-permute-start.3 = (bf16[272,128]{1,0:T(8,128)(2,1)S(1)}, bf16[272,128]{1,0:T(8,128)(2,1)S(1)}, u32[]{:S(2)}, u32[]{:S(2)}) collective-permute-start(bf16[272,128]{1,0:T(8,128)(2,1)S(1)} %get-tuple-element.49), channel_id=1, source_target_pairs={{0,4},{8,12},{4,0},{12,8},{1,5},{9,13},{5,1},{13,9},{2,6},{10,14},... | collective-permute-start | bytes 208904 | tf_op jit(solution)/shard_map/ppermute | solution.py:540
  9.5 1.9 %collective-permute-start.4 = (bf16[272,128]{1,0:T(8,128)(2,1)S(1)}, bf16[272,128]{1,0:T(8,128)(2,1)S(1)}, u32[]{:S(2)}, u32[]{:S(2)}) collective-permute-start(bf16[272,128]{1,0:T(8,128)(2,1)S(1)} %get-tuple-element.50), channel_id=1, source_target_pairs={{4,8},{8,4},{0,0},{12,12},{5,9},{9,5},{1,1},{13,13},{6,10},{10,6},... | collective-permute-start | bytes 208904 | tf_op jit(solution)/shard_map/ppermute | solution.py:540
  11.4 0.0 copy-done
  11.5 2.2 %shard_map.184.inner_ref = bf16[3,384,128]{2,1,0:T(8,128)(2,1)S(1)} custom-call(s32[1]{0:T(128)} %bitcast.at_ref, s32[4,64]{1,0:T(4,128)S(1)} %copy-done, bf16[3,512,128]{2,1,0:T(8,128)(2,1)S(1)} %get-tuple-element.37.query_ref, bf16[3,512,128]{2,1,0:T(8,128)(2,1)S(1)} %get-tuple-element.38.key_ref.own_key_ref, ...), custom_call_target="tpu_custom_call" | custom-call | flops 603979776 | bytes 4194304 | tf_op jit(solution)/shard_map/pallas_call | solution.py:546
  13.7 0.0 collective-permute-done.3.first_ref
  13.7 2.0 %collective-permute-done.4.second_ref = bf16[272,128]{1,0:T(8,128)(2,1)S(1)} collective-permute-done((bf16[272,128]{1,0:T(8,128)(2,1)S(1)}, bf16[272,128]{1,0:T(8,128)(2,1)S(1)}, u32[]{:S(2)}, u32[]{:S(2)}) %collective-permute-start.4) | collective-permute-done | bytes 69664 | tf_op jit(solution)/shard_map/ppermute | solution.py:540
  15.7 2.0 %shard_map.185 = bf16[3,512,128]{2,1,0:T(8,128)(2,1)} custom-call(s32[1]{0:T(128)} %bitcast.at_ref, s32[4,64]{1,0:T(4,128)S(1)} %copy-done, bf16[3,512,128]{2,1,0:T(8,128)(2,1)S(1)} %get-tuple-element.37.query_ref, bf16[3,512,128]{2,1,0:T(8,128)(2,1)S(1)} %get-tuple-element.38.key_ref.own_key_ref, ...), custom_call_target="tpu_custom_call" | custom-call | flops 201326592 | bytes 4194304 | tf_op jit(solution)/shard_map/pallas_call | solution.py:561
  (1 shorter events, 0.0 us)
Async XLA Ops:
  2.9 8.6 %copy-start = (s32[4,64]{1,0:T(4,128)S(1)}, s32[4,64]{1,0:T(4,128)}, u32[]{:S(2)}) copy-start(s32[4,64]{1,0:T(4,128)} %counts_ref.3) | copy-start | bytes 3076
  2.9 4.4 %collective-permute-start = (bf16[2,64,128]{2,1,0:T(8,128)(2,1)S(1)}, bf16[2,64,128]{2,1,0:T(8,128)(2,1)S(1)}, u32[]{:S(2)}, u32[]{:S(2)}) collective-permute-start(bf16[2,64,128]{2,1,0:T(8,128)(2,1)S(1)} %get-tuple-element.41.refs_0_), channel_id=1, source_target_pairs={{0,1},{1,0},{2,3},{3,2},{4,5},{5,4},{6,7},{7,6},{8,9},{9,8},{10,11... | collective-permute-start | bytes 98312 | tf_op jit(solution)/shard_map/ppermute | solution.py:505
  2.9 4.3 %collective-permute-start.1 = (bf16[2,64,128]{2,1,0:T(8,128)(2,1)S(1)}, bf16[2,64,128]{2,1,0:T(8,128)(2,1)S(1)}, u32[]{:S(2)}, u32[]{:S(2)}) collective-permute-start(bf16[2,64,128]{2,1,0:T(8,128)(2,1)S(1)} %get-tuple-element.41.refs_0_), channel_id=1, source_target_pairs={{0,2},{2,0},{1,3},{3,1},{4,6},{6,4},{5,7},{7,5},{8,10},{10,8},{9,1... | collective-permute-start | bytes 98312 | tf_op jit(solution)/shard_map/ppermute | solution.py:503
  4.5 3.3 %collective-permute-start.2 = (bf16[2,64,128]{2,1,0:T(8,128)(2,1)S(1)}, bf16[2,64,128]{2,1,0:T(8,128)(2,1)S(1)}, u32[]{:S(2)}, u32[]{:S(2)}) collective-permute-start(bf16[2,64,128]{2,1,0:T(8,128)(2,1)S(1)} %get-tuple-element.41.refs_0_), channel_id=1, source_target_pairs={{0,3},{1,2},{2,1},{3,0},{4,7},{5,6},{6,5},{7,4},{8,11},{9,10},{10,... | collective-permute-start | bytes 98312 | tf_op jit(solution)/shard_map/ppermute | solution.py:504
  7.9 5.8 %collective-permute-start.3 = (bf16[272,128]{1,0:T(8,128)(2,1)S(1)}, bf16[272,128]{1,0:T(8,128)(2,1)S(1)}, u32[]{:S(2)}, u32[]{:S(2)}) collective-permute-start(bf16[272,128]{1,0:T(8,128)(2,1)S(1)} %get-tuple-element.49), channel_id=1, source_target_pairs={{0,4},{8,12},{4,0},{12,8},{1,5},{9,13},{5,1},{13,9},{2,6},{10,14},... | collective-permute-start | bytes 208904 | tf_op jit(solution)/shard_map/ppermute | solution.py:540
  9.5 6.2 %collective-permute-start.4 = (bf16[272,128]{1,0:T(8,128)(2,1)S(1)}, bf16[272,128]{1,0:T(8,128)(2,1)S(1)}, u32[]{:S(2)}, u32[]{:S(2)}) collective-permute-start(bf16[272,128]{1,0:T(8,128)(2,1)S(1)} %get-tuple-element.50), channel_id=1, source_target_pairs={{4,8},{8,4},{0,0},{12,12},{5,9},{9,5},{1,1},{13,13},{6,10},{10,6},... | collective-permute-start | bytes 208904 | tf_op jit(solution)/shard_map/ppermute | solution.py:540

commit v12 on v11

--- a/solution.py
+++ b/solution.py
@@ -66,7 +66,7 @@
     return (sigmoid(mixed[:, :width])[None] * single + mixed[None, :, width:]).astype(BF16)
 
 
-def pair_kernel(packing, core_ref, w_pair_hbm, pair_hbm, single_hbm, cond_hbm, *refs):
+def pair_kernel(packing, w_pair_hbm, pair_hbm, single_hbm, cond_hbm, *refs):
     count = sum(packing)
     weights_hbm, refs = refs[:count], refs[count:]
     tile_ref, single_ref, cond_ref = refs[:3]
@@ -78,11 +78,10 @@
     lanes = heads * group
     half = group // 2
     pieces = rows // half
-    row_start = core_ref[0] * rows
 
     def pair_copy(i):
-        source = pair_hbm.at[pl.ds(row_start + i * half, half)]
-        return pltpu.make_async_copy(source, pair_ref.at[pl.ds(i * half, half)], pair_sem.at[i])
+        at = pl.ds(i * half, half)
+        return pltpu.make_async_copy(pair_hbm.at[at], pair_ref.at[at], pair_sem.at[i])
 
     moves = [(w_pair_hbm, w_pair_ref), (single_hbm, single_ref), (cond_hbm, cond_ref)]
     index = 0
@@ -101,9 +100,6 @@
     copies[0].start()
     for i in range(pieces):
         pair_copy(i).start()
-    for copy in copies[1:]:
-        copy.start()
-
     copies[0].wait()
     w_pair = w_pair_ref[...].astype(F32)
     spread = jnp.concatenate(
@@ -111,11 +107,17 @@
     )
     mix = twice(spread.T.astype(BF16))
     slot = iota((cols, lanes), 1) % group
+    per_block = tile_ref.shape[1]
 
     @pl.loop(0, rows // group)
     def _(chunk):
         for part in range(2):
             pair_copy(chunk * 2 + part).wait()
+
+        @pl.when(chunk == 1)
+        def _():
+            for copy in copies[1:]:
+                copy.start()
 
         pair = pair_ref[pl.ds(chunk * group, group)].reshape(group * cols, width)
         centred, variance = centre(pair)
@@ -128,7 +130,7 @@
             total = jnp.where(slot == i, mixed[i % half, :, side], total)
             spread_out = jnp.where(slot == i, variance[i], spread_out)
         bias = (total * lax.rsqrt(spread_out + EPSILON)).astype(BF16)
-        tile_ref[chunk] = bias
+        tile_ref[chunk // per_block, chunk % per_block] = bias
 
     for copy in copies[1:]:
         copy.wait()
@@ -139,23 +141,26 @@
     single_ref,
     cond_ref,
     ada_attn,
-    ada_trans,
-    gates_ref,
     w_kv,
     w_qg,
-    w_up,
-    w_down,
-    query_ref,
-    key_ref,
-    value_ref,
-    gate_ref,
-    open_ref,
-    trans_ref,
-    near_ref,
-    far_ref,
+    *refs,
 ):
+    late_hbm, refs = refs[:8], refs[8:]
+    query_ref, key_ref, value_ref, gate_ref, open_ref, trans_ref, near_ref, far_ref, w_out = refs[:9]
+    ada_trans, gates_ref, w_up, w_down, sem = refs[9:]
     samples, atoms_here, width = single_ref.shape
     hidden_width = w_down.shape[0]
+    targets = [w_out, w_down]
+    for ref in (ada_trans, gates_ref, w_up):
+        middle = ref.shape[1] // 2
+        targets += [ref.at[:, pl.ds(0, middle)], ref.at[:, pl.ds(middle, middle)]]
+    copies = [
+        pltpu.make_async_copy(source, target, sem.at[i])
+        for i, (source, target) in enumerate(zip(late_hbm, targets))
+    ]
+    for copy in copies:
+        copy.start()
+    transitions = []
     step = math.gcd(atoms_here, 256)
     for start in range(0, atoms_here, step):
         at = slice(start, start + step)
@@ -174,6 +179,11 @@
         both = dot(normed, w_qg[...]).reshape(samples, step, 2 * width)
         query_ref[:, at, :] = both[:, :, :width].astype(BF16)
         gate_ref[:, at, :] = sigmoid(both[:, :, width:]).astype(BF16)
+        transitions.append((at, cond, single))
+
+    for copy in copies:
+        copy.wait()
+    for at, cond, single in transitions:
         gates = dot(cond, gates_ref[...])
         open_ref[at, :] = sigmoid(gates[:, :width]).astype(BF16)
         normed = attn_norm(cond, single, ada_trans[...]).reshape(-1, width)
@@ -188,27 +198,24 @@
         far_ref[cut, :] = jnp.where(even, head, tail)
 
 
-def tile_of(refs, place, row_block):
-    if len(refs) == 1:
-        return refs[0][row_block]
-    pair_at, core_at = place
-    owners = 2
-    mine, theirs, across, diagonal = [ref[...] for ref in refs]
-    near = jnp.where(row_block % owners == core_at, mine, theirs)
-    far = jnp.where(row_block % owners == core_at, across, diagonal)
-    return jnp.where(row_block // owners == pair_at, near, far)
-
-
-def select_kernel(blocks, at_ref, pair_ref, core_ref, *refs):
-    *tile_refs, _, __, ___, near_ref, far_ref, ____, held_ref = refs
-    groups, cols, lanes = tile_refs[0].shape[-3:]
+def tile_of(own_ref, other_ref, pair_at, row_block):
+    owners, groups, cols, lanes = own_ref.shape
+    place, part = row_block // owners, row_block % owners
+    other = other_ref[0, part] if other_ref.shape[0] == 1 else other_ref[place, part]
+    return jnp.where(place == pair_at, own_ref[part], other)
+
+
+def select_kernel(blocks, at_ref, pair_ref, own_ref, other_ref, *refs):
+    near_ref, far_ref, _, held_ref, again_ref = refs[3:]
+    groups, cols, lanes = own_ref.shape[1:]
     rows = groups * cols
-    device_at, place = at_ref[0], (pair_ref[0], core_ref[0])
+    device_at, pair_at = at_ref[0], pair_ref[0]
     for send_ref, parity in ((near_ref, 0), (far_ref, 1)):
         beside = jnp.where(device_at % 2 == parity, device_at + 1, device_at - 1)
-        tile = tile_of(tile_refs, place, jnp.clip(beside, 0, blocks - 1))
+        tile = tile_of(own_ref, other_ref, pair_at, jnp.clip(beside, 0, blocks - 1))
         send_ref[send_ref.shape[0] - rows :, :] = tile.reshape(rows, lanes)
-    held_ref[...] = tile_of(tile_refs, place, device_at).reshape(rows, lanes)
+    held_ref[...] = tile_of(own_ref, other_ref, pair_at, device_at).reshape(rows, lanes)
+    again_ref[...] = near_ref[...]
 
 
 def bounds(counts_ref, block, token):
@@ -345,8 +352,9 @@
     held_ref,
     inner_ref,
     w_kv,
-    first_ref,
+    early_ref,
     second_ref,
+    late_ref,
     out_hbm,
     key_ref,
     value_ref,
@@ -370,7 +378,8 @@
     whole.start()
 
     even = device_at % 2 == 0
-    first, second = first_ref[...], second_ref[...]
+    first = jnp.where(device_at % 4 < 2, early_ref[...], late_ref[...])
+    second = second_ref[...]
     arrived = (jnp.where(even, second, first), jnp.where(even, first, second))
     count = samples * EDGE
     edges = jnp.concatenate([rows[:count] for rows in arrived], 0)
@@ -447,25 +456,16 @@
     heads = w_pair.shape[1]
     groups = tok_here // GROUP
     pairs = lax.axis_size("pair")
-    assert pair_cond.shape[0] == lax.axis_size("samp") * tok_here
+    owners = pair_cond.shape[0] // tok_here
     at = device_at.astype(jnp.int32).reshape(1)
     pair_at = lax.axis_index("pair").astype(jnp.int32).reshape(1)
-    core_at = lax.axis_index("samp").astype(jnp.int32).reshape(1)
     in_hbm = lambda array: pltpu.with_memory_space_constraint(array, pltpu.HBM)
     in_vmem = lambda array: pltpu.with_memory_space_constraint(array, pltpu.VMEM)
 
-    packing = (
-        (ada_attn_scale, ada_attn_shift),
-        (ada_trans_scale, ada_trans_shift),
-        (attn_gate, trans_gate),
-        (w_key, w_value),
-        (w_query, w_gate),
-        (w_swish, w_linear),
-        (w_down,),
-        (w_out,),
-    )
+    packing = ((ada_attn_scale, ada_attn_shift), (w_key, w_value), (w_query, w_gate))
+    late = (w_out, w_down, ada_trans_scale, ada_trans_shift, attn_gate, trans_gate, w_swish, w_linear)
     flat = [array for arrays in packing for array in arrays]
-    cols = pair_cond.shape[1]
+    rows, cols, _ = pair_cond.shape
     lanes = heads * GROUP
     wide = (samples, atoms_here, width)
     params = pltpu.CompilerParams(vmem_limit_bytes=VMEM_LIMIT)
@@ -475,7 +475,7 @@
 
     sent = pltpu.VMEM((samples * EDGE + groups * cols, lanes), BF16)
     shapes = [
-        pltpu.VMEM((groups, cols, lanes), BF16),
+        pltpu.VMEM((owners, groups, cols, lanes), BF16),
         pltpu.VMEM(wide, BF16),
         pltpu.VMEM(atom_cond.shape, BF16),
     ] + [
@@ -484,62 +484,65 @@
     ]
     made = pl.pallas_call(
         functools.partial(pair_kernel, [len(arrays) for arrays in packing]),
-        in_specs=[IN_SMEM] + [IN_HBM] * (4 + len(flat)),
+        in_specs=[IN_HBM] * (4 + len(flat)),
         out_specs=[IN_VMEM] * len(shapes),
         out_shape=shapes,
         scratch_shapes=[
             pltpu.VMEM((heads, width), BF16),
-            pltpu.VMEM((tok_here, cols, width), BF16),
-            pltpu.SemaphoreType.DMA((2 * groups,)),
+            pltpu.VMEM(pair_cond.shape, BF16),
+            pltpu.SemaphoreType.DMA((2 * rows // GROUP,)),
             pltpu.SemaphoreType.DMA((3 + len(flat),)),
         ],
         compiler_params=params,
-        cost_estimate=cost(tok_here * cols * width * width * 2),
-    )(core_at, *map(in_hbm, (w_pair.T, pair_cond, atom_single, atom_cond, *flat)))
+        cost_estimate=cost(rows * cols * width * width * 2),
+    )(*map(in_hbm, (w_pair.T, pair_cond, atom_single, atom_cond, *flat)))
     own, single, cond, *packed = made
-    ada_attn, ada_trans, gates, w_kv, w_qg, w_up, w_down, w_out = packed
+    ada_attn, w_kv, w_qg = packed
     if pairs == 2:
-        swapped = [(0, 1), (1, 0)]
-        across = lax.ppermute(own, "pair", swapped)
-        diagonal = lax.ppermute(own, ("pair", "samp"), [(0, 3), (1, 2), (2, 1), (3, 0)])
-        tiles = (own, lax.ppermute(own, "samp", swapped), across, diagonal)
+        other = lax.ppermute(own, "pair", [(0, 1), (1, 0)])[None]
     else:
-        tiles = (lax.all_gather(own, ("pair", "samp")),)
-
-    operands = (single, cond, ada_attn, ada_trans, gates, w_kv, w_qg, w_up, w_down)
-    query, keys, values, gate, opened, trans, near, far = pl.pallas_call(
+        other = lax.all_gather(own, "pair")
+
+    operands = (single, cond, ada_attn, w_kv, w_qg)
+    query, keys, values, gate, opened, trans, near, far, w_out = pl.pallas_call(
         project_kernel,
-        in_specs=[IN_SMEM] + [IN_VMEM] * len(operands),
-        out_specs=[IN_VMEM] * 8,
+        in_specs=[IN_SMEM] + [IN_VMEM] * len(operands) + [IN_HBM] * len(late),
+        out_specs=[IN_VMEM] * 9,
         out_shape=[pltpu.VMEM(wide, BF16)] * 4
-        + [pltpu.VMEM((atoms_here, width), BF16), pltpu.VMEM(wide, BF16), sent, sent],
+        + [pltpu.VMEM((atoms_here, width), BF16), pltpu.VMEM(wide, BF16), sent, sent]
+        + [pltpu.VMEM(w_out.shape, BF16)],
+        scratch_shapes=[
+            pltpu.VMEM((width, 2 * width), BF16),
+            pltpu.VMEM((width, 2 * width), BF16),
+            pltpu.VMEM((width, 2 * w_swish.shape[1]), BF16),
+            pltpu.VMEM(w_down.shape, BF16),
+            pltpu.SemaphoreType.DMA((len(late),)),
+        ],
         compiler_params=params,
         cost_estimate=cost(samples * atoms_here * width * width * 20),
-    )(at, *map(in_vmem, operands))
-
-    operands = (*tiles, near, far, opened)
-    first = 3 + len(tiles)
-    near, far, opened, held = pl.pallas_call(
+    )(at, *map(in_vmem, operands), *map(in_hbm, late))
+
+    operands = (own, other, near, far, opened)
+    near, far, opened, held, again = pl.pallas_call(
         functools.partial(select_kernel, blocks),
-        in_specs=[IN_SMEM] * 3 + [IN_VMEM] * len(operands),
-        out_specs=[IN_VMEM] * 4,
+        in_specs=[IN_SMEM] * 2 + [IN_VMEM] * len(operands),
+        out_specs=[IN_VMEM] * 5,
         out_shape=[
             sent,
             sent,
             pltpu.VMEM((atoms_here, width), BF16),
             pltpu.VMEM((groups * cols, lanes), BF16),
+            sent,
         ],
-        input_output_aliases={first: 0, first + 1: 1, first + 2: 2},
+        input_output_aliases={4: 0, 5: 1, 6: 2},
         compiler_params=params,
-    )(at, pair_at, core_at, *map(in_vmem, operands))
-
-    def swap(value, start):
-        sides = [(i, i + 1) for i in range(start, blocks - 1, 2)]
-        alone = set(range(blocks)) - {i for side in sides for i in side}
-        pairs_of = sides + [(j, i) for i, j in sides] + [(i, i) for i in sorted(alone)]
-        return lax.ppermute(value, "atoms", pairs_of)
-
-    first, second = swap(near, 0), swap(far, 1)
+    )(at, pair_at, *map(in_vmem, operands))
+
+    def swap(value, start, step):
+        sides = [(i, i + 1) for i in range(start, blocks - 1, step)]
+        return lax.ppermute(value, "atoms", sides + [(j, i) for i, j in sides])
+
+    early, second, later = swap(near, 0, 4), swap(far, 1, 2), swap(again, 2, 4)
 
     margin = -(-EDGE // Q_WIN) * Q_WIN
     operands = (query, keys, values, gate, opened, trans, w_out, held)
@@ -557,7 +560,7 @@
     )(at, atom_counts, *map(in_vmem, operands))
 
     reach = margin - Q_WIN + K_WIN
-    operands += (inner, w_kv, first, second)
+    operands += (inner, w_kv, early, second, later)
     return pl.pallas_call(
         functools.partial(outer_kernel, heads, blocks),
         in_specs=[IN_SMEM] + [IN_VMEM] * (1 + len(operands)),

time: 17.9 us -> 22.2 us (1.24)
  starting transfers between devices: 5.48 us -> 8.19 us
  Pallas kernels: 9.51 us -> 11.6 us
  waiting for transfers between devices: 2.65 us -> 2 us
    ppermute x5 -> x4, starting transfers between devices: 5.48 us -> 8.19 us  [the longest x3 6.63 us: swap(): return lax.ppermute(value, 'atoms', sides + [(j, i) for i, j in sides])]
    pallas_call x1, Pallas kernels: 2.84 us -> 4.24 us  [shards(): pl.pallas_call(functools.partial(pair_kernel, [len(arrays) for arrays in...]
    pallas_call x1, Pallas kernels: 2.4 us -> 3.1 us  [shards(): pl.pallas_call(project_kernel, in_specs=[IN_SMEM] + [IN_VMEM] * len(opera...]
    ppermute x5 -> x4, waiting for transfers between devices: 2.65 us -> 2 us  [the longest x3 2 us: swap(): return lax.ppermute(value, 'atoms', sides + [(j, i) for i, j in sides])]
  transfers between devices with their start and end apart: 5 -> 4, of which waited for: 2 -> 1; matrix products, arithmetic and copies ran while one was open for 0% -> 0% of each run, Pallas kernels for 26% -> 24%
where the time goes in v12:
time: 22.2 us; the launch traced here: 21.9 us
  Pallas kernels  11.6 us (52%)
  starting transfers between devices  8.19 us (37%)
  waiting for transfers between devices  2 us (9%)
    ppermute x3, starting transfers between devices, swap(): return lax.ppermute(value, 'atoms', sides + [(j, i) for i, j in sides])  6.63 us
    pallas_call x1, Pallas kernels, shards(): pl.pallas_call(functools.partial(pair_kernel, [len(arrays) for arrays in...  4.24 us
    pallas_call x1, Pallas kernels, shards(): pl.pallas_call(project_kernel, in_specs=[IN_SMEM] + [IN_VMEM] * len(opera...  3.1 us
    pallas_call x1, Pallas kernels, shards(): pl.pallas_call(functools.partial(inner_kernel, heads), in_specs=[IN_SMEM]...  2.24 us
    pallas_call x1, Pallas kernels, shards(): pl.pallas_call(functools.partial(outer_kernel, heads, blocks), in_specs=[...  2.02 us
    ppermute x3, waiting for transfers between devices, swap(): return lax.ppermute(value, 'atoms', sides + [(j, i) for i, j in sides])  2 us
    ppermute x1, starting transfers between devices, shards(): other = lax.ppermute(own, 'pair', [(0, 1), (1, 0)])[None]  1.56 us
  transfers between devices with their start and end apart: 4, of which 1 were waited for; matrix products, arithmetic and copies ran while one was open for 0% of the time, Pallas kernels for 24%

profile of v12, /device:TPU:16, one launch (start us, length us, event | category | flops | bytes accessed | tf_op | source)
XLA Modules:
  0.0 21.9 jit_solution(3718215160291612202)
XLA Ops:
  0.0 4.2 %shard_map.181 = (bf16[2,2,64,128]{3,2,1,0:T(8,128)(2,1)S(1)}, bf16[3,512,128]{2,1,0:T(8,128)(2,1)S(1)}, bf16[512,128]{1,0:T(8,128)(2,1)S(1)}, bf16[128,256]{1,0...) custom-call(bf16[4,128]{1,0:T(4,128)(2,1)} %bitcast.5, bf16[128,64,128]{2,1,0:T(8,128)(2,1)} %pair_hbm.1, ...), custom_call_target="tpu_custom_call" | custom-call | flops 536870912 | bytes 4194304 | tf_op jit(solution)/shard_map/pallas_call | solution.py:485
  4.2 0.0 copy-start
  4.3 1.6 %collective-permute-start = (bf16[2,2,64,128]{3,2,1,0:T(8,128)(2,1)S(1)}, bf16[2,2,64,128]{3,2,1,0:T(8,128)(2,1)S(1)}, u32[]{:S(2)}, u32[]{:S(2)}) collective-permute-start(bf16[2,2,64,128]{3,2,1,0:T(8,128)(2,1)S(1)} %get-tuple-element.34.own_ref), channel_id=1, source_target_pairs={{0,2},{2,0},{1,3},{3,1},{4,6},{6,4},{5,7},{7,5},{8,10},{10,8},{9,1... | collective-permute-start | bytes 196616 | tf_op jit(solution)/shard_map/ppermute | solution.py:502
  5.8 3.1 %shard_map.182 = (bf16[3,512,128]{2,1,0:T(8,128)(2,1)S(1)}, bf16[3,512,128]{2,1,0:T(8,128)(2,1)S(1)}, bf16[3,512,128]{2,1,0:T(8,128)(2,1)S(1)}, bf16[3,512,128]{...) custom-call(s32[1]{0:T(128)} %bitcast.at_ref, ...), custom_call_target="tpu_custom_call" | custom-call | flops 1006632960 | bytes 4194304 | tf_op jit(solution)/shard_map/pallas_call | solution.py:507
  8.9 0.0 collective-permute-done
  8.9 0.1 shard_map.183
  9.0 0.7 %collective-permute-start.1 = (bf16[272,128]{1,0:T(8,128)(2,1)S(1)}, bf16[272,128]{1,0:T(8,128)(2,1)S(1)}, u32[]{:S(2)}, u32[]{:S(2)}) collective-permute-start(bf16[272,128]{1,0:T(8,128)(2,1)S(1)} %get-tuple-element.42), channel_id=1, source_target_pairs={{0,4},{4,0},{1,5},{5,1},{2,6},{6,2},{3,7},{7,3},{16,20},{20,16},{1... | collective-permute-start | bytes 208904 | tf_op jit(solution)/shard_map/ppermute | solution.py:543
  9.7 4.0 %collective-permute-start.2 = (bf16[272,128]{1,0:T(8,128)(2,1)S(1)}, bf16[272,128]{1,0:T(8,128)(2,1)S(1)}, u32[]{:S(2)}, u32[]{:S(2)}) collective-permute-start(bf16[272,128]{1,0:T(8,128)(2,1)S(1)} %get-tuple-element.43), channel_id=1, source_target_pairs={{4,8},{8,4},{5,9},{9,5},{6,10},{10,6},{7,11},{11,7},{20,24},{24,20... | collective-permute-start | bytes 208904 | tf_op jit(solution)/shard_map/ppermute | solution.py:543
  13.7 1.9 %collective-permute-start.3 = (bf16[272,128]{1,0:T(8,128)(2,1)S(1)}, bf16[272,128]{1,0:T(8,128)(2,1)S(1)}, u32[]{:S(2)}, u32[]{:S(2)}) collective-permute-start(bf16[272,128]{1,0:T(8,128)(2,1)S(1)} %get-tuple-element.44), channel_id=1, source_target_pairs={{8,12},{12,8},{9,13},{13,9},{10,14},{14,10},{11,15},{15,11},{24,28... | collective-permute-start | bytes 208904 | tf_op jit(solution)/shard_map/ppermute | solution.py:543
  15.7 0.0 copy-done
  15.7 2.2 %shard_map.184.inner_ref = bf16[3,384,128]{2,1,0:T(8,128)(2,1)S(1)} custom-call(s32[1]{0:T(128)} %bitcast.at_ref, s32[4,64]{1,0:T(4,128)S(1)} %copy-done, bf16[3,512,128]{2,1,0:T(8,128)(2,1)S(1)} %get-tuple-element.30.query_ref, bf16[3,512,128]{2,1,0:T(8,128)(2,1)S(1)} %get-tuple-element.31.key_ref.own_key_ref, ...), custom_call_target="tpu_custom_call" | custom-call | flops 603979776 | bytes 4194304 | tf_op jit(solution)/shard_map/pallas_call | solution.py:549
  17.9 0.0 collective-permute-done.1.early_ref
  17.9 0.0 collective-permute-done.2.second_ref
  17.9 2.0 %collective-permute-done.3.late_ref = bf16[272,128]{1,0:T(8,128)(2,1)S(1)} collective-permute-done((bf16[272,128]{1,0:T(8,128)(2,1)S(1)}, bf16[272,128]{1,0:T(8,128)(2,1)S(1)}, u32[]{:S(2)}, u32[]{:S(2)}) %collective-permute-start.3) | collective-permute-done | bytes 69664 | tf_op jit(solution)/shard_map/ppermute | solution.py:543
  19.9 2.0 %shard_map.185 = bf16[3,512,128]{2,1,0:T(8,128)(2,1)} custom-call(s32[1]{0:T(128)} %bitcast.at_ref, s32[4,64]{1,0:T(4,128)S(1)} %copy-done, bf16[3,512,128]{2,1,0:T(8,128)(2,1)S(1)} %get-tuple-element.30.query_ref, bf16[3,512,128]{2,1,0:T(8,128)(2,1)S(1)} %get-tuple-element.31.key_ref.own_key_ref, ...), custom_call_target="tpu_custom_call" | custom-call | flops 201326592 | bytes 4194304 | tf_op jit(solution)/shard_map/pallas_call | solution.py:564
Async XLA Ops:
  4.2 11.4 %copy-start = (s32[4,64]{1,0:T(4,128)S(1)}, s32[4,64]{1,0:T(4,128)}, u32[]{:S(2)}) copy-start(s32[4,64]{1,0:T(4,128)} %counts_ref.3) | copy-start | bytes 3076
  4.3 4.7 %collective-permute-start = (bf16[2,2,64,128]{3,2,1,0:T(8,128)(2,1)S(1)}, bf16[2,2,64,128]{3,2,1,0:T(8,128)(2,1)S(1)}, u32[]{:S(2)}, u32[]{:S(2)}) collective-permute-start(bf16[2,2,64,128]{3,2,1,0:T(8,128)(2,1)S(1)} %get-tuple-element.34.own_ref), channel_id=1, source_target_pairs={{0,2},{2,0},{1,3},{3,1},{4,6},{6,4},{5,7},{7,5},{8,10},{10,8},{9,1... | collective-permute-start | bytes 196616 | tf_op jit(solution)/shard_map/ppermute | solution.py:502
  9.0 8.9 %collective-permute-start.1 = (bf16[272,128]{1,0:T(8,128)(2,1)S(1)}, bf16[272,128]{1,0:T(8,128)(2,1)S(1)}, u32[]{:S(2)}, u32[]{:S(2)}) collective-permute-start(bf16[272,128]{1,0:T(8,128)(2,1)S(1)} %get-tuple-element.42), channel_id=1, source_target_pairs={{0,4},{4,0},{1,5},{5,1},{2,6},{6,2},{3,7},{7,3},{16,20},{20,16},{1... | collective-permute-start | bytes 208904 | tf_op jit(solution)/shard_map/ppermute | solution.py:543
  9.7 8.3 %collective-permute-start.2 = (bf16[272,128]{1,0:T(8,128)(2,1)S(1)}, bf16[272,128]{1,0:T(8,128)(2,1)S(1)}, u32[]{:S(2)}, u32[]{:S(2)}) collective-permute-start(bf16[272,128]{1,0:T(8,128)(2,1)S(1)} %get-tuple-element.43), channel_id=1, source_target_pairs={{4,8},{8,4},{5,9},{9,5},{6,10},{10,6},{7,11},{11,7},{20,24},{24,20... | collective-permute-start | bytes 208904 | tf_op jit(solution)/shard_map/ppermute | solution.py:543
  13.7 6.2 %collective-permute-start.3 = (bf16[272,128]{1,0:T(8,128)(2,1)S(1)}, bf16[272,128]{1,0:T(8,128)(2,1)S(1)}, u32[]{:S(2)}, u32[]{:S(2)}) collective-permute-start(bf16[272,128]{1,0:T(8,128)(2,1)S(1)} %get-tuple-element.44), channel_id=1, source_target_pairs={{8,12},{12,8},{9,13},{13,9},{10,14},{14,10},{11,15},{15,11},{24,28... | collective-permute-start | bytes 208904 | tf_op jit(solution)/shard_map/ppermute | solution.py:543

commit v13 on v11

--- a/solution.py
+++ b/solution.py
@@ -101,9 +101,6 @@
     copies[0].start()
     for i in range(pieces):
         pair_copy(i).start()
-    for copy in copies[1:]:
-        copy.start()
-
     copies[0].wait()
     w_pair = w_pair_ref[...].astype(F32)
     spread = jnp.concatenate(
@@ -116,6 +113,11 @@
     def _(chunk):
         for part in range(2):
             pair_copy(chunk * 2 + part).wait()
+
+        @pl.when(chunk == 0)
+        def _():
+            for copy in copies[1:]:
+                copy.start()
 
         pair = pair_ref[pl.ds(chunk * group, group)].reshape(group * cols, width)
         centred, variance = centre(pair)
@@ -534,10 +536,16 @@
     )(at, pair_at, core_at, *map(in_vmem, operands))
 
     def swap(value, start):
-        sides = [(i, i + 1) for i in range(start, blocks - 1, 2)]
-        alone = set(range(blocks)) - {i for side in sides for i in side}
-        pairs_of = sides + [(j, i) for i, j in sides] + [(i, i) for i in sorted(alone)]
-        return lax.ppermute(value, "atoms", pairs_of)
+        cores = lax.axis_size("samp")
+        other_of = {}
+        for i in range(start, blocks - 1, 2):
+            other_of[i], other_of[i + 1] = i + 1, i
+        sides = []
+        for i in range(blocks):
+            for core in range(cores):
+                target = (other_of[i], core) if i in other_of else (i, (core + 1) % cores)
+                sides.append((i * cores + core, target[0] * cores + target[1]))
+        return lax.ppermute(value, ("atoms", "samp"), sides)
 
     first, second = swap(near, 0), swap(far, 1)
 

time: 17.9 us -> 15.8 us (0.88)
  the two profiles are of different devices: /device:TPU:16 before, /device:TPU:0 now
where the time goes in v13:
time: 15.8 us; the launch traced here: 15.5 us
  Pallas kernels  9.32 us (59%)
  starting transfers between devices  4.8 us (30%)
  waiting for transfers between devices  1.35 us (9%)
    pallas_call x1, Pallas kernels, shards(): pl.pallas_call(functools.partial(pair_kernel, [len(arrays) for arrays in...  2.64 us
    ppermute x1, starting transfers between devices, shards(): across = lax.ppermute(own, 'pair', swapped)  2.62 us
    pallas_call x1, Pallas kernels, shards(): pl.pallas_call(project_kernel, in_specs=[IN_SMEM] + [IN_VMEM] * len(opera...  2.41 us
    pallas_call x1, Pallas kernels, shards(): pl.pallas_call(functools.partial(inner_kernel, heads), in_specs=[IN_SMEM]...  2.21 us
    pallas_call x1, Pallas kernels, shards(): pl.pallas_call(functools.partial(outer_kernel, heads, blocks), in_specs=[...  2.01 us
    ppermute x2, starting transfers between devices, swap(): return lax.ppermute(value, ('atoms', 'samp'), sides)  1.64 us
    ppermute x1, waiting for transfers between devices, shards(): lax.ppermute(own, ('pair', 'samp'), [(0, 3), (1, 2), (2, 1), (3, 0)])  0.83 us
    ppermute x2, waiting for transfers between devices, swap(): return lax.ppermute(value, ('atoms', 'samp'), sides)  0.51 us
  transfers between devices with their start and end apart: 5, of which 2 were waited for; matrix products, arithmetic and copies ran while one was open for 0% of the time, Pallas kernels for 30%

profile of v13, /device:TPU:0, one launch (start us, length us, event | category | flops | bytes accessed | tf_op | source)
XLA Modules:
  0.0 15.5 jit_solution(3849555444088773673)
XLA Ops:
  0.0 2.6 %shard_map.181 = (bf16[2,64,128]{2,1,0:T(8,128)(2,1)S(1)}, bf16[3,512,128]{2,1,0:T(8,128)(2,1)S(1)}, bf16[512,128]{1,0:T(8,128)(2,1)S(1)}, bf16[128,256]{1,0:T(8...) custom-call(s32[1]{0:T(128)} %bitcast.1.core_ref, ...), custom_call_target="tpu_custom_call" | custom-call | flops 268435456 | bytes 4194304 | tf_op jit(solution)/shard_map/pallas_call | solution.py:487
  2.6 0.0 copy-start
  2.7 0.5 %collective-permute-start = (bf16[2,64,128]{2,1,0:T(8,128)(2,1)S(1)}, bf16[2,64,128]{2,1,0:T(8,128)(2,1)S(1)}, u32[]{:S(2)}, u32[]{:S(2)}) collective-permute-start(bf16[2,64,128]{2,1,0:T(8,128)(2,1)S(1)} %get-tuple-element.41.refs_0_), channel_id=1, source_target_pairs={{0,1},{1,0},{2,3},{3,2},{4,5},{5,4},{6,7},{7,6},{8,9},{9,8},{10,11... | collective-permute-start | bytes 98312 | tf_op jit(solution)/shard_map/ppermute | solution.py:507
  3.1 2.6 %collective-permute-start.1 = (bf16[2,64,128]{2,1,0:T(8,128)(2,1)S(1)}, bf16[2,64,128]{2,1,0:T(8,128)(2,1)S(1)}, u32[]{:S(2)}, u32[]{:S(2)}) collective-permute-start(bf16[2,64,128]{2,1,0:T(8,128)(2,1)S(1)} %get-tuple-element.41.refs_0_), channel_id=1, source_target_pairs={{0,2},{2,0},{1,3},{3,1},{4,6},{6,4},{5,7},{7,5},{8,10},{10,8},{9,1... | collective-permute-start | bytes 98312 | tf_op jit(solution)/shard_map/ppermute | solution.py:505
  5.7 0.1 collective-permute-start.2
  5.8 2.4 %shard_map.182 = (bf16[3,512,128]{2,1,0:T(8,128)(2,1)S(1)}, bf16[3,512,128]{2,1,0:T(8,128)(2,1)S(1)}, bf16[3,512,128]{2,1,0:T(8,128)(2,1)S(1)}, bf16[3,512,128]{...) custom-call(s32[1]{0:T(128)} %bitcast.at_ref, ...), custom_call_target="tpu_custom_call" | custom-call | flops 1006632960 | bytes 4194304 | tf_op jit(solution)/shard_map/pallas_call | solution.py:512
  8.2 0.0 collective-permute-done.refs_1_
  8.2 0.0 collective-permute-done.1.refs_2_
  8.3 0.8 %collective-permute-done.2.refs_3_ = bf16[2,64,128]{2,1,0:T(8,128)(2,1)S(1)} collective-permute-done((bf16[2,64,128]{2,1,0:T(8,128)(2,1)S(1)}, bf16[2,64,128]{2,1,0:T(8,128)(2,1)S(1)}, u32[]{:S(2)}, u32[]{:S(2)}) %collective-permute-start.2) | collective-permute-done | bytes 32800 | tf_op jit(solution)/shard_map/ppermute | solution.py:506
  9.1 1.6 %collective-permute-start.3 = (bf16[272,128]{1,0:T(8,128)(2,1)S(1)}, bf16[272,128]{1,0:T(8,128)(2,1)S(1)}, u32[]{:S(2)}, u32[]{:S(2)}) collective-permute-start(bf16[272,128]{1,0:T(8,128)(2,1)S(1)} %get-tuple-element.49), channel_id=1, source_target_pairs={{0,4},{1,5},{4,0},{5,1},{8,12},{9,13},{12,8},{13,9},{2,6},{3,7},{6... | collective-permute-start | bytes 208904 | tf_op jit(solution)/shard_map/ppermute | solution.py:548
  10.8 0.0 collective-permute-start.4
  10.8 0.0 copy-done
  10.8 2.2 %shard_map.184.inner_ref = bf16[3,384,128]{2,1,0:T(8,128)(2,1)S(1)} custom-call(s32[1]{0:T(128)} %bitcast.at_ref, s32[4,64]{1,0:T(4,128)S(1)} %copy-done, bf16[3,512,128]{2,1,0:T(8,128)(2,1)S(1)} %get-tuple-element.37.query_ref, bf16[3,512,128]{2,1,0:T(8,128)(2,1)S(1)} %get-tuple-element.38.key_ref.own_key_ref, ...), custom_call_target="tpu_custom_call" | custom-call | flops 603979776 | bytes 4194304 | tf_op jit(solution)/shard_map/pallas_call | solution.py:554
  13.0 0.5 %collective-permute-done.3.first_ref = bf16[272,128]{1,0:T(8,128)(2,1)S(1)} collective-permute-done((bf16[272,128]{1,0:T(8,128)(2,1)S(1)}, bf16[272,128]{1,0:T(8,128)(2,1)S(1)}, u32[]{:S(2)}, u32[]{:S(2)}) %collective-permute-start.3) | collective-permute-done | bytes 69664 | tf_op jit(solution)/shard_map/ppermute | solution.py:548
  13.5 0.0 collective-permute-done.4.second_ref
  13.5 2.0 %shard_map.185 = bf16[3,512,128]{2,1,0:T(8,128)(2,1)} custom-call(s32[1]{0:T(128)} %bitcast.at_ref, s32[4,64]{1,0:T(4,128)S(1)} %copy-done, bf16[3,512,128]{2,1,0:T(8,128)(2,1)S(1)} %get-tuple-element.37.query_ref, bf16[3,512,128]{2,1,0:T(8,128)(2,1)S(1)} %get-tuple-element.38.key_ref.own_key_ref, ...), custom_call_target="tpu_custom_call" | custom-call | flops 201326592 | bytes 4194304 | tf_op jit(solution)/shard_map/pallas_call | solution.py:569
  (1 shorter events, 0.0 us)
Async XLA Ops:
  2.6 8.1 %copy-start = (s32[4,64]{1,0:T(4,128)S(1)}, s32[4,64]{1,0:T(4,128)}, u32[]{:S(2)}) copy-start(s32[4,64]{1,0:T(4,128)} %counts_ref.3) | copy-start | bytes 3076
  2.7 5.6 %collective-permute-start = (bf16[2,64,128]{2,1,0:T(8,128)(2,1)S(1)}, bf16[2,64,128]{2,1,0:T(8,128)(2,1)S(1)}, u32[]{:S(2)}, u32[]{:S(2)}) collective-permute-start(bf16[2,64,128]{2,1,0:T(8,128)(2,1)S(1)} %get-tuple-element.41.refs_0_), channel_id=1, source_target_pairs={{0,1},{1,0},{2,3},{3,2},{4,5},{5,4},{6,7},{7,6},{8,9},{9,8},{10,11... | collective-permute-start | bytes 98312 | tf_op jit(solution)/shard_map/ppermute | solution.py:507
  3.1 5.1 %collective-permute-start.1 = (bf16[2,64,128]{2,1,0:T(8,128)(2,1)S(1)}, bf16[2,64,128]{2,1,0:T(8,128)(2,1)S(1)}, u32[]{:S(2)}, u32[]{:S(2)}) collective-permute-start(bf16[2,64,128]{2,1,0:T(8,128)(2,1)S(1)} %get-tuple-element.41.refs_0_), channel_id=1, source_target_pairs={{0,2},{2,0},{1,3},{3,1},{4,6},{6,4},{5,7},{7,5},{8,10},{10,8},{9,1... | collective-permute-start | bytes 98312 | tf_op jit(solution)/shard_map/ppermute | solution.py:505
  5.7 3.3 %collective-permute-start.2 = (bf16[2,64,128]{2,1,0:T(8,128)(2,1)S(1)}, bf16[2,64,128]{2,1,0:T(8,128)(2,1)S(1)}, u32[]{:S(2)}, u32[]{:S(2)}) collective-permute-start(bf16[2,64,128]{2,1,0:T(8,128)(2,1)S(1)} %get-tuple-element.41.refs_0_), channel_id=1, source_target_pairs={{0,3},{1,2},{2,1},{3,0},{4,7},{5,6},{6,5},{7,4},{8,11},{9,10},{10,... | collective-permute-start | bytes 98312 | tf_op jit(solution)/shard_map/ppermute | solution.py:506
  9.1 4.4 %collective-permute-start.3 = (bf16[272,128]{1,0:T(8,128)(2,1)S(1)}, bf16[272,128]{1,0:T(8,128)(2,1)S(1)}, u32[]{:S(2)}, u32[]{:S(2)}) collective-permute-start(bf16[272,128]{1,0:T(8,128)(2,1)S(1)} %get-tuple-element.49), channel_id=1, source_target_pairs={{0,4},{1,5},{4,0},{5,1},{8,12},{9,13},{12,8},{13,9},{2,6},{3,7},{6... | collective-permute-start | bytes 208904 | tf_op jit(solution)/shard_map/ppermute | solution.py:548
  10.8 2.7 %collective-permute-start.4 = (bf16[272,128]{1,0:T(8,128)(2,1)S(1)}, bf16[272,128]{1,0:T(8,128)(2,1)S(1)}, u32[]{:S(2)}, u32[]{:S(2)}) collective-permute-start(bf16[272,128]{1,0:T(8,128)(2,1)S(1)} %get-tuple-element.50), channel_id=1, source_target_pairs={{0,1},{1,0},{4,8},{5,9},{8,4},{9,5},{12,13},{13,12},{2,3},{3,2},{6... | collective-permute-start | bytes 208904 | tf_op jit(solution)/shard_map/ppermute | solution.py:548

commit v14 on v13

--- a/solution.py
+++ b/solution.py
@@ -202,15 +202,18 @@
 
 
 def select_kernel(blocks, at_ref, pair_ref, core_ref, *refs):
-    *tile_refs, _, __, ___, near_ref, far_ref, ____, held_ref = refs
+    *tile_refs, _, __, ___, near_ref, far_ref, ____, held_ref, again_ref = refs
     groups, cols, lanes = tile_refs[0].shape[-3:]
-    rows = groups * cols
+    rows = groups * EDGE
     device_at, place = at_ref[0], (pair_ref[0], core_ref[0])
     for send_ref, parity in ((near_ref, 0), (far_ref, 1)):
-        beside = jnp.where(device_at % 2 == parity, device_at + 1, device_at - 1)
+        above = device_at % 2 == parity
+        beside = jnp.where(above, device_at + 1, device_at - 1)
         tile = tile_of(tile_refs, place, jnp.clip(beside, 0, blocks - 1))
+        tile = jnp.where(above, tile[:, cols - EDGE :], tile[:, :EDGE])
         send_ref[send_ref.shape[0] - rows :, :] = tile.reshape(rows, lanes)
-    held_ref[...] = tile_of(tile_refs, place, device_at).reshape(rows, lanes)
+    again_ref[...] = near_ref[...]
+    held_ref[...] = tile_of(tile_refs, place, device_at).reshape(groups * cols, lanes)
 
 
 def bounds(counts_ref, block, token):
@@ -229,9 +232,9 @@
     return ((first <= position) & (position < last)).astype(F32).astype(BF16)
 
 
-def expand(hot, tile, tok_here):
-    tile = tile.reshape(tok_here // GROUP, tok_here, tile.shape[-1])
-    tile = jnp.concatenate([tile[part] for part in range(tok_here // GROUP)], 1)
+def expand(hot, tile, groups):
+    tile = tile.reshape(groups, -1, tile.shape[-1])
+    tile = jnp.concatenate([tile[part] for part in range(groups)], 1)
     return dot(hot, tile).astype(BF16)
 
 
@@ -311,7 +314,7 @@
     hot = one_hot(
         bounds(counts_ref, device_at, iota((tok_here, tok_here), 1)), 0, atoms_here
     )
-    near_ref[...] = expand(hot, held_ref[...], tok_here)
+    near_ref[...] = expand(hot, held_ref[...], tok_here // GROUP)
     reach = bounds(counts_ref, device_at, row_tokens(heads, tok_here))
     skip = -(-EDGE // Q_WIN)
     inner = atoms_here // Q_WIN - 2 * skip
@@ -347,8 +350,9 @@
     held_ref,
     inner_ref,
     w_kv,
-    first_ref,
+    early_ref,
     second_ref,
+    late_ref,
     out_hbm,
     key_ref,
     value_ref,
@@ -372,11 +376,13 @@
     whole.start()
 
     even = device_at % 2 == 0
-    first, second = first_ref[...], second_ref[...]
+    first = jnp.where(device_at % 4 < 2, early_ref[...], late_ref[...])
+    second = second_ref[...]
     arrived = (jnp.where(even, second, first), jnp.where(even, first, second))
     count = samples * EDGE
     edges = jnp.concatenate([rows[:count] for rows in arrived], 0)
     edges = dot(edges, w_kv[...]).astype(BF16).reshape(2, samples, EDGE, 2 * width)
+    groups = tok_here // GROUP
     token = iota((tok_here, tok_here), 1)
     own_reach = bounds(counts_ref, device_at, token)
     sides = (
@@ -389,10 +395,11 @@
             ref[side, :, own_place : own_place + inside, :] = own_ref[
                 :, own_start : own_start + inside, :
             ]
-        hot = one_hot(bounds(counts_ref, block, token), offset, EDGE)
-        near_ref[side, place : place + EDGE, :] = expand(hot, arrived[side][count:], tok_here)
+        nearest = iota((tok_here, EDGE), 1) + (tok_here - EDGE if side == 0 else 0)
+        hot = one_hot(bounds(counts_ref, block, nearest), offset, EDGE)
+        near_ref[side, place : place + EDGE, :] = expand(hot, arrived[side][count:], groups)
         hot = one_hot(own_reach, own_start, inside)
-        near_ref[side, own_place : own_place + inside, :] = expand(hot, held_ref[...], tok_here)
+        near_ref[side, own_place : own_place + inside, :] = expand(hot, held_ref[...], groups)
 
     reach = bounds(counts_ref, device_at, row_tokens(heads, tok_here))
     windows = []
@@ -475,7 +482,7 @@
     def cost(products):
         return pl.CostEstimate(flops=2 * products, bytes_accessed=4 << 20, transcendentals=0)
 
-    sent = pltpu.VMEM((samples * EDGE + groups * cols, lanes), BF16)
+    sent = pltpu.VMEM((samples * EDGE + groups * EDGE, lanes), BF16)
     shapes = [
         pltpu.VMEM((groups, cols, lanes), BF16),
         pltpu.VMEM(wide, BF16),
@@ -521,24 +528,25 @@
 
     operands = (*tiles, near, far, opened)
     first = 3 + len(tiles)
-    near, far, opened, held = pl.pallas_call(
+    near, far, opened, held, again = pl.pallas_call(
         functools.partial(select_kernel, blocks),
         in_specs=[IN_SMEM] * 3 + [IN_VMEM] * len(operands),
-        out_specs=[IN_VMEM] * 4,
+        out_specs=[IN_VMEM] * 5,
         out_shape=[
             sent,
             sent,
             pltpu.VMEM((atoms_here, width), BF16),
             pltpu.VMEM((groups * cols, lanes), BF16),
+            sent,
         ],
         input_output_aliases={first: 0, first + 1: 1, first + 2: 2},
         compiler_params=params,
     )(at, pair_at, core_at, *map(in_vmem, operands))
 
-    def swap(value, start):
+    def swap(value, start, step):
         cores = lax.axis_size("samp")
         other_of = {}
-        for i in range(start, blocks - 1, 2):
+        for i in range(start, blocks - 1, step):
             other_of[i], other_of[i + 1] = i + 1, i
         sides = []
         for i in range(blocks):
@@ -547,7 +555,7 @@
                 sides.append((i * cores + core, target[0] * cores + target[1]))
         return lax.ppermute(value, ("atoms", "samp"), sides)
 
-    first, second = swap(near, 0), swap(far, 1)
+    early, second, later = swap(near, 0, 4), swap(far, 1, 2), swap(again, 2, 4)
 
     margin = -(-EDGE // Q_WIN) * Q_WIN
     operands = (query, keys, values, gate, opened, trans, w_out, held)
@@ -565,7 +573,7 @@
     )(at, atom_counts, *map(in_vmem, operands))
 
     reach = margin - Q_WIN + K_WIN
-    operands += (inner, w_kv, first, second)
+    operands += (inner, w_kv, early, second, later)
     return pl.pallas_call(
         functools.partial(outer_kernel, heads, blocks),
         in_specs=[IN_SMEM] + [IN_VMEM] * (1 + len(operands)),

time: 15.8 us -> 15.7 us (level)
  waiting for transfers between devices: 1.35 us -> 0.85 us
  starting transfers between devices: 4.8 us -> 5.3 us
    ppermute x2 -> x3, starting transfers between devices: 1.64 us -> 2.15 us  [swap(): return lax.ppermute(value, ('atoms', 'samp'), sides)]
    ppermute x2 -> x3, waiting for transfers between devices: 0.51 us -> 0.01 us  [swap(): return lax.ppermute(value, ('atoms', 'samp'), sides)]
  transfers between devices with their start and end apart: 5 -> 6, of which waited for: 2 -> 1; matrix products, arithmetic and copies ran while one was open for 0% -> 0% of each run, Pallas kernels for 30% -> 30%
where the time goes in v14:
time: 15.7 us; the launch traced here: 15.5 us
  Pallas kernels  9.26 us (59%)
  starting transfers between devices  5.3 us (34%)
  waiting for transfers between devices  0.85 us (5%)
    pallas_call x1, Pallas kernels, shards(): pl.pallas_call(functools.partial(pair_kernel, [len(arrays) for arrays in...  2.64 us
    ppermute x1, starting transfers between devices, shards(): across = lax.ppermute(own, 'pair', swapped)  2.62 us
    pallas_call x1, Pallas kernels, shards(): pl.pallas_call(project_kernel, in_specs=[IN_SMEM] + [IN_VMEM] * len(opera...  2.41 us
    pallas_call x1, Pallas kernels, shards(): pl.pallas_call(functools.partial(inner_kernel, heads), in_specs=[IN_SMEM]...  2.21 us
    ppermute x3, starting transfers between devices, swap(): return lax.ppermute(value, ('atoms', 'samp'), sides)  2.15 us
    pallas_call x1, Pallas kernels, shards(): pl.pallas_call(functools.partial(outer_kernel, heads, blocks), in_specs=[...  1.95 us
    ppermute x1, waiting for transfers between devices, shards(): lax.ppermute(own, ('pair', 'samp'), [(0, 3), (1, 2), (2, 1), (3, 0)])  0.84 us
    ppermute x1, starting transfers between devices, shards(): tiles = (own, lax.ppermute(own, 'samp', swapped), across, diagonal)  0.46 us
  transfers between devices with their start and end apart: 6, of which 1 were waited for; matrix products, arithmetic and copies ran while one was open for 0% of the time, Pallas kernels for 30%

profile of v14, /device:TPU:0, one launch (start us, length us, event | category | flops | bytes accessed | tf_op | source)
XLA Modules:
  0.0 15.5 jit_solution(2417593695284375277)
XLA Ops:
  0.0 2.6 %shard_map.181 = (bf16[2,64,128]{2,1,0:T(8,128)(2,1)S(1)}, bf16[3,512,128]{2,1,0:T(8,128)(2,1)S(1)}, bf16[512,128]{1,0:T(8,128)(2,1)S(1)}, bf16[128,256]{1,0:T(8...) custom-call(s32[1]{0:T(128)} %bitcast.1.core_ref, ...), custom_call_target="tpu_custom_call" | custom-call | flops 268435456 | bytes 4194304 | tf_op jit(solution)/shard_map/pallas_call | solution.py:494
  2.6 0.0 copy-start
  2.7 0.5 %collective-permute-start = (bf16[2,64,128]{2,1,0:T(8,128)(2,1)S(1)}, bf16[2,64,128]{2,1,0:T(8,128)(2,1)S(1)}, u32[]{:S(2)}, u32[]{:S(2)}) collective-permute-start(bf16[2,64,128]{2,1,0:T(8,128)(2,1)S(1)} %get-tuple-element.42.refs_0_), channel_id=1, source_target_pairs={{0,1},{1,0},{2,3},{3,2},{4,5},{5,4},{6,7},{7,6},{8,9},{9,8},{10,11... | collective-permute-start | bytes 98312 | tf_op jit(solution)/shard_map/ppermute | solution.py:514
  3.1 2.6 %collective-permute-start.1 = (bf16[2,64,128]{2,1,0:T(8,128)(2,1)S(1)}, bf16[2,64,128]{2,1,0:T(8,128)(2,1)S(1)}, u32[]{:S(2)}, u32[]{:S(2)}) collective-permute-start(bf16[2,64,128]{2,1,0:T(8,128)(2,1)S(1)} %get-tuple-element.42.refs_0_), channel_id=1, source_target_pairs={{0,2},{2,0},{1,3},{3,1},{4,6},{6,4},{5,7},{7,5},{8,10},{10,8},{9,1... | collective-permute-start | bytes 98312 | tf_op jit(solution)/shard_map/ppermute | solution.py:512
  5.7 0.1 collective-permute-start.2
  5.8 2.4 %shard_map.182 = (bf16[3,512,128]{2,1,0:T(8,128)(2,1)S(1)}, bf16[3,512,128]{2,1,0:T(8,128)(2,1)S(1)}, bf16[3,512,128]{2,1,0:T(8,128)(2,1)S(1)}, bf16[3,512,128]{...) custom-call(s32[1]{0:T(128)} %bitcast.at_ref, ...), custom_call_target="tpu_custom_call" | custom-call | flops 1006632960 | bytes 4194304 | tf_op jit(solution)/shard_map/pallas_call | solution.py:519
  8.2 0.0 collective-permute-done.refs_1_
  8.2 0.0 collective-permute-done.1.refs_2_
  8.3 0.8 %collective-permute-done.2.refs_3_ = bf16[2,64,128]{2,1,0:T(8,128)(2,1)S(1)} collective-permute-done((bf16[2,64,128]{2,1,0:T(8,128)(2,1)S(1)}, bf16[2,64,128]{2,1,0:T(8,128)(2,1)S(1)}, u32[]{:S(2)}, u32[]{:S(2)}) %collective-permute-start.2) | collective-permute-done | bytes 32800 | tf_op jit(solution)/shard_map/ppermute | solution.py:513
  9.1 1.6 %collective-permute-start.3 = (bf16[240,128]{1,0:T(8,128)(2,1)S(1)}, bf16[240,128]{1,0:T(8,128)(2,1)S(1)}, u32[]{:S(2)}, u32[]{:S(2)}) collective-permute-start(bf16[240,128]{1,0:T(8,128)(2,1)S(1)} %get-tuple-element.50), channel_id=1, source_target_pairs={{0,4},{1,5},{4,0},{5,1},{8,9},{9,8},{12,13},{13,12},{2,6},{3,7},{6... | collective-permute-start | bytes 184328 | tf_op jit(solution)/shard_map/ppermute | solution.py:556
  10.8 0.0 collective-permute-start.4
  10.8 0.5 %collective-permute-start.5 = (bf16[240,128]{1,0:T(8,128)(2,1)S(1)}, bf16[240,128]{1,0:T(8,128)(2,1)S(1)}, u32[]{:S(2)}, u32[]{:S(2)}) collective-permute-start(bf16[240,128]{1,0:T(8,128)(2,1)S(1)} %get-tuple-element.52), channel_id=1, source_target_pairs={{0,1},{1,0},{4,5},{5,4},{8,12},{9,13},{12,8},{13,9},{2,3},{3,2},{6... | collective-permute-start | bytes 184328 | tf_op jit(solution)/shard_map/ppermute | solution.py:556
  11.3 0.0 copy-done
  11.3 2.2 %shard_map.184.inner_ref = bf16[3,384,128]{2,1,0:T(8,128)(2,1)S(1)} custom-call(s32[1]{0:T(128)} %bitcast.at_ref, s32[4,64]{1,0:T(4,128)S(1)} %copy-done, bf16[3,512,128]{2,1,0:T(8,128)(2,1)S(1)} %get-tuple-element.38.query_ref, bf16[3,512,128]{2,1,0:T(8,128)(2,1)S(1)} %get-tuple-element.39.key_ref.own_key_ref, ...), custom_call_target="tpu_custom_call" | custom-call | flops 603979776 | bytes 4194304 | tf_op jit(solution)/shard_map/pallas_call | solution.py:562
  13.5 0.0 collective-permute-done.3.early_ref
  13.5 0.0 collective-permute-done.4.second_ref
  13.5 0.0 collective-permute-done.5.late_ref
  13.5 2.0 %shard_map.185 = bf16[3,512,128]{2,1,0:T(8,128)(2,1)} custom-call(s32[1]{0:T(128)} %bitcast.at_ref, s32[4,64]{1,0:T(4,128)S(1)} %copy-done, bf16[3,512,128]{2,1,0:T(8,128)(2,1)S(1)} %get-tuple-element.38.query_ref, bf16[3,512,128]{2,1,0:T(8,128)(2,1)S(1)} %get-tuple-element.39.key_ref.own_key_ref, ...), custom_call_target="tpu_custom_call" | custom-call | flops 201326592 | bytes 4194304 | tf_op jit(solution)/shard_map/pallas_call | solution.py:577
  (1 shorter events, 0.0 us)
Async XLA Ops:
  2.6 8.6 %copy-start = (s32[4,64]{1,0:T(4,128)S(1)}, s32[4,64]{1,0:T(4,128)}, u32[]{:S(2)}) copy-start(s32[4,64]{1,0:T(4,128)} %counts_ref.3) | copy-start | bytes 3076
  2.7 5.6 %collective-permute-start = (bf16[2,64,128]{2,1,0:T(8,128)(2,1)S(1)}, bf16[2,64,128]{2,1,0:T(8,128)(2,1)S(1)}, u32[]{:S(2)}, u32[]{:S(2)}) collective-permute-start(bf16[2,64,128]{2,1,0:T(8,128)(2,1)S(1)} %get-tuple-element.42.refs_0_), channel_id=1, source_target_pairs={{0,1},{1,0},{2,3},{3,2},{4,5},{5,4},{6,7},{7,6},{8,9},{9,8},{10,11... | collective-permute-start | bytes 98312 | tf_op jit(solution)/shard_map/ppermute | solution.py:514
  3.1 5.1 %collective-permute-start.1 = (bf16[2,64,128]{2,1,0:T(8,128)(2,1)S(1)}, bf16[2,64,128]{2,1,0:T(8,128)(2,1)S(1)}, u32[]{:S(2)}, u32[]{:S(2)}) collective-permute-start(bf16[2,64,128]{2,1,0:T(8,128)(2,1)S(1)} %get-tuple-element.42.refs_0_), channel_id=1, source_target_pairs={{0,2},{2,0},{1,3},{3,1},{4,6},{6,4},{5,7},{7,5},{8,10},{10,8},{9,1... | collective-permute-start | bytes 98312 | tf_op jit(solution)/shard_map/ppermute | solution.py:512
  5.7 3.3 %collective-permute-start.2 = (bf16[2,64,128]{2,1,0:T(8,128)(2,1)S(1)}, bf16[2,64,128]{2,1,0:T(8,128)(2,1)S(1)}, u32[]{:S(2)}, u32[]{:S(2)}) collective-permute-start(bf16[2,64,128]{2,1,0:T(8,128)(2,1)S(1)} %get-tuple-element.42.refs_0_), channel_id=1, source_target_pairs={{0,3},{1,2},{2,1},{3,0},{4,7},{5,6},{6,5},{7,4},{8,11},{9,10},{10,... | collective-permute-start | bytes 98312 | tf_op jit(solution)/shard_map/ppermute | solution.py:513
  9.1 4.4 %collective-permute-start.3 = (bf16[240,128]{1,0:T(8,128)(2,1)S(1)}, bf16[240,128]{1,0:T(8,128)(2,1)S(1)}, u32[]{:S(2)}, u32[]{:S(2)}) collective-permute-start(bf16[240,128]{1,0:T(8,128)(2,1)S(1)} %get-tuple-element.50), channel_id=1, source_target_pairs={{0,4},{1,5},{4,0},{5,1},{8,9},{9,8},{12,13},{13,12},{2,6},{3,7},{6... | collective-permute-start | bytes 184328 | tf_op jit(solution)/shard_map/ppermute | solution.py:556
  10.8 2.7 %collective-permute-start.4 = (bf16[240,128]{1,0:T(8,128)(2,1)S(1)}, bf16[240,128]{1,0:T(8,128)(2,1)S(1)}, u32[]{:S(2)}, u32[]{:S(2)}) collective-permute-start(bf16[240,128]{1,0:T(8,128)(2,1)S(1)} %get-tuple-element.51), channel_id=1, source_target_pairs={{0,1},{1,0},{4,8},{5,9},{8,4},{9,5},{12,13},{13,12},{2,3},{3,2},{6... | collective-permute-start | bytes 184328 | tf_op jit(solution)/shard_map/ppermute | solution.py:556
  10.8 2.8 %collective-permute-start.5 = (bf16[240,128]{1,0:T(8,128)(2,1)S(1)}, bf16[240,128]{1,0:T(8,128)(2,1)S(1)}, u32[]{:S(2)}, u32[]{:S(2)}) collective-permute-start(bf16[240,128]{1,0:T(8,128)(2,1)S(1)} %get-tuple-element.52), channel_id=1, source_target_pairs={{0,1},{1,0},{4,5},{5,4},{8,12},{9,13},{12,8},{13,9},{2,3},{3,2},{6... | collective-permute-start | bytes 184328 | tf_op jit(solution)/shard_map/ppermute | solution.py:556

commit v15 on v14

--- a/solution.py
+++ b/solution.py
@@ -66,12 +66,7 @@
     return (sigmoid(mixed[:, :width])[None] * single + mixed[None, :, width:]).astype(BF16)
 
 
-def pair_kernel(packing, core_ref, w_pair_hbm, pair_hbm, single_hbm, cond_hbm, *refs):
-    count = sum(packing)
-    weights_hbm, refs = refs[:count], refs[count:]
-    tile_ref, single_ref, cond_ref = refs[:3]
-    packed_refs, refs = refs[3 : 3 + len(packing)], refs[3 + len(packing) :]
-    w_pair_ref, pair_ref, pair_sem, sem = refs
+def pair_kernel(core_ref, w_pair_hbm, pair_hbm, tile_ref, w_pair_ref, pair_ref, pair_sem, sem):
     rows, cols, width = pair_ref.shape
     heads = w_pair_ref.shape[0]
     group = GROUP
@@ -84,24 +79,11 @@
         source = pair_hbm.at[pl.ds(row_start + i * half, half)]
         return pltpu.make_async_copy(source, pair_ref.at[pl.ds(i * half, half)], pair_sem.at[i])
 
-    moves = [(w_pair_hbm, w_pair_ref), (single_hbm, single_ref), (cond_hbm, cond_ref)]
-    index = 0
-    for number, packed in zip(packing, packed_refs):
-        offset = 0
-        for _ in range(number):
-            source = weights_hbm[index]
-            span = source.shape[1]
-            moves.append((source, packed.at[:, pl.ds(offset, span)]))
-            offset += span
-            index += 1
-    copies = [
-        pltpu.make_async_copy(source, target, sem.at[i])
-        for i, (source, target) in enumerate(moves)
-    ]
-    copies[0].start()
+    w_pair_copy = pltpu.make_async_copy(w_pair_hbm, w_pair_ref, sem)
+    w_pair_copy.start()
     for i in range(pieces):
         pair_copy(i).start()
-    copies[0].wait()
+    w_pair_copy.wait()
     w_pair = w_pair_ref[...].astype(F32)
     spread = jnp.concatenate(
         [jnp.broadcast_to(w_pair[h : h + 1], (group, width)) for h in range(heads)], 0
@@ -113,11 +95,6 @@
     def _(chunk):
         for part in range(2):
             pair_copy(chunk * 2 + part).wait()
-
-        @pl.when(chunk == 0)
-        def _():
-            for copy in copies[1:]:
-                copy.start()
 
         pair = pair_ref[pl.ds(chunk * group, group)].reshape(group * cols, width)
         centred, variance = centre(pair)
@@ -132,8 +109,9 @@
         bias = (total * lax.rsqrt(spread_out + EPSILON)).astype(BF16)
         tile_ref[chunk] = bias
 
-    for copy in copies[1:]:
-        copy.wait()
+
+def beside(first, second):
+    return jnp.concatenate([first[...], second[...]], 1)
 
 
 def project_kernel(
@@ -141,11 +119,17 @@
     single_ref,
     cond_ref,
     ada_attn,
+    ada_attn_shift,
     ada_trans,
-    gates_ref,
-    w_kv,
-    w_qg,
-    w_up,
+    ada_trans_shift,
+    attn_gate,
+    trans_gate,
+    w_key,
+    w_value,
+    w_query,
+    w_gate,
+    w_swish,
+    w_linear,
     w_down,
     query_ref,
     key_ref,
@@ -157,30 +141,29 @@
     far_ref,
 ):
     samples, atoms_here, width = single_ref.shape
-    hidden_width = w_down.shape[0]
     step = math.gcd(atoms_here, 256)
     for start in range(0, atoms_here, step):
         at = slice(start, start + step)
         cond = layer_norm(cond_ref[at, :]).astype(BF16)
         single = layer_norm(single_ref[:, at, :].reshape(-1, width))
         single = single.reshape(samples, step, width)
-        normed = attn_norm(cond, single, ada_attn[...])
+        normed = attn_norm(cond, single, beside(ada_attn, ada_attn_shift))
         if start == 0:
             heads_of = [normed[sample, :EDGE] for sample in range(samples)]
         if start + step == atoms_here:
             tails_of = [normed[sample, step - EDGE :] for sample in range(samples)]
         normed = normed.reshape(-1, width)
-        both = dot(normed, w_kv[...]).astype(BF16).reshape(samples, step, 2 * width)
+        both = dot(normed, beside(w_key, w_value)).astype(BF16).reshape(samples, step, 2 * width)
         key_ref[:, at, :] = both[:, :, :width]
         value_ref[:, at, :] = both[:, :, width:]
-        both = dot(normed, w_qg[...]).reshape(samples, step, 2 * width)
+        both = dot(normed, beside(w_query, w_gate)).reshape(samples, step, 2 * width)
         query_ref[:, at, :] = both[:, :, :width].astype(BF16)
         gate_ref[:, at, :] = sigmoid(both[:, :, width:]).astype(BF16)
-        gates = dot(cond, gates_ref[...])
+        gates = dot(cond, beside(attn_gate, trans_gate))
         open_ref[at, :] = sigmoid(gates[:, :width]).astype(BF16)
-        normed = attn_norm(cond, single, ada_trans[...]).reshape(-1, width)
-        swish = dot(normed, w_up[:, :hidden_width])
-        hidden = (swish * sigmoid(swish) * dot(normed, w_up[:, hidden_width:])).astype(BF16)
+        normed = attn_norm(cond, single, beside(ada_trans, ada_trans_shift)).reshape(-1, width)
+        swish = dot(normed, w_swish[...])
+        hidden = (swish * sigmoid(swish) * dot(normed, w_linear[...])).astype(BF16)
         down = dot(hidden, w_down[...]).reshape(samples, step, width)
         trans_ref[:, at, :] = (sigmoid(gates[:, width:])[None] * down).astype(BF16)
     even = at_ref[0] % 2 == 0
@@ -349,7 +332,8 @@
     w_out_ref,
     held_ref,
     inner_ref,
-    w_kv,
+    w_key,
+    w_value,
     early_ref,
     second_ref,
     late_ref,
@@ -381,7 +365,7 @@
     arrived = (jnp.where(even, second, first), jnp.where(even, first, second))
     count = samples * EDGE
     edges = jnp.concatenate([rows[:count] for rows in arrived], 0)
-    edges = dot(edges, w_kv[...]).astype(BF16).reshape(2, samples, EDGE, 2 * width)
+    edges = dot(edges, beside(w_key, w_value)).astype(BF16).reshape(2, samples, EDGE, 2 * width)
     groups = tok_here // GROUP
     token = iota((tok_here, tok_here), 1)
     own_reach = bounds(counts_ref, device_at, token)
@@ -463,17 +447,6 @@
     in_hbm = lambda array: pltpu.with_memory_space_constraint(array, pltpu.HBM)
     in_vmem = lambda array: pltpu.with_memory_space_constraint(array, pltpu.VMEM)
 
-    packing = (
-        (ada_attn_scale, ada_attn_shift),
-        (ada_trans_scale, ada_trans_shift),
-        (attn_gate, trans_gate),
-        (w_key, w_value),
-        (w_query, w_gate),
-        (w_swish, w_linear),
-        (w_down,),
-        (w_out,),
-    )
-    flat = [array for arrays in packing for array in arrays]
     cols = pair_cond.shape[1]
     lanes = heads * GROUP
     wide = (samples, atoms_here, width)
@@ -483,30 +456,20 @@
         return pl.CostEstimate(flops=2 * products, bytes_accessed=4 << 20, transcendentals=0)
 
     sent = pltpu.VMEM((samples * EDGE + groups * EDGE, lanes), BF16)
-    shapes = [
-        pltpu.VMEM((groups, cols, lanes), BF16),
-        pltpu.VMEM(wide, BF16),
-        pltpu.VMEM(atom_cond.shape, BF16),
-    ] + [
-        pltpu.VMEM((arrays[0].shape[0], sum(a.shape[1] for a in arrays)), BF16)
-        for arrays in packing
-    ]
-    made = pl.pallas_call(
-        functools.partial(pair_kernel, [len(arrays) for arrays in packing]),
-        in_specs=[IN_SMEM] + [IN_HBM] * (4 + len(flat)),
-        out_specs=[IN_VMEM] * len(shapes),
-        out_shape=shapes,
+    own = pl.pallas_call(
+        pair_kernel,
+        in_specs=[IN_SMEM] + [IN_HBM] * 2,
+        out_specs=IN_VMEM,
+        out_shape=pltpu.VMEM((groups, cols, lanes), BF16),
         scratch_shapes=[
             pltpu.VMEM((heads, width), BF16),
             pltpu.VMEM((tok_here, cols, width), BF16),
             pltpu.SemaphoreType.DMA((2 * groups,)),
-            pltpu.SemaphoreType.DMA((3 + len(flat),)),
+            pltpu.SemaphoreType.DMA,
         ],
         compiler_params=params,
         cost_estimate=cost(tok_here * cols * width * width * 2),
-    )(core_at, *map(in_hbm, (w_pair.T, pair_cond, atom_single, atom_cond, *flat)))
-    own, single, cond, *packed = made
-    ada_attn, ada_trans, gates, w_kv, w_qg, w_up, w_down, w_out = packed
+    )(core_at, *map(in_hbm, (w_pair.T, pair_cond)))
     if pairs == 2:
         swapped = [(0, 1), (1, 0)]
         across = lax.ppermute(own, "pair", swapped)
@@ -515,7 +478,23 @@
     else:
         tiles = (lax.all_gather(own, ("pair", "samp")),)
 
-    operands = (single, cond, ada_attn, ada_trans, gates, w_kv, w_qg, w_up, w_down)
+    operands = (
+        atom_single,
+        atom_cond,
+        ada_attn_scale,
+        ada_attn_shift,
+        ada_trans_scale,
+        ada_trans_shift,
+        attn_gate,
+        trans_gate,
+        w_key,
+        w_value,
+        w_query,
+        w_gate,
+        w_swish,
+        w_linear,
+        w_down,
+    )
     query, keys, values, gate, opened, trans, near, far = pl.pallas_call(
         project_kernel,
         in_specs=[IN_SMEM] + [IN_VMEM] * len(operands),
@@ -573,7 +552,7 @@
     )(at, atom_counts, *map(in_vmem, operands))
 
     reach = margin - Q_WIN + K_WIN
-    operands += (inner, w_kv, early, second, later)
+    operands += (inner, w_key, w_value, early, second, later)
     return pl.pallas_call(
         functools.partial(outer_kernel, heads, blocks),
         in_specs=[IN_SMEM] + [IN_VMEM] * (1 + len(operands)),

time: 15.7 us -> 15.6 us (level)
  between operations: 0.08 us -> 0.26 us
    ppermute x1, starting transfers between devices: 0.07 us -> 2.46 us  [shards(): lax.ppermute(own, ('pair', 'samp'), [(0, 3), (1, 2), (2, 1), (3, 0)])]
    ppermute x1, starting transfers between devices: 2.62 us -> 0.64 us  [shards(): across = lax.ppermute(own, 'pair', swapped)]
    ppermute x1, waiting for transfers between devices: 0.84 us -> 0.01 us  [shards(): lax.ppermute(own, ('pair', 'samp'), [(0, 3), (1, 2), (2, 1), (3, 0)])]
    ppermute x1, waiting for transfers between devices: 0.01 us -> 0.74 us  [shards(): across = lax.ppermute(own, 'pair', swapped)]
    ppermute x1, starting transfers between devices: 0.46 us -> 0.04 us  [shards(): tiles = (own, lax.ppermute(own, 'samp', swapped), across, diagonal)]
where the time goes in v15:
time: 15.6 us; the launch traced here: 15.5 us
  Pallas kernels  9.11 us (58%)
  starting transfers between devices  5.29 us (34%)
  waiting for transfers between devices  0.76 us (5%)
  between operations  0.26 us (2%)
    pallas_call x1, Pallas kernels, shards(): pl.pallas_call(pair_kernel, in_specs=[IN_SMEM] + [IN_HBM] * 2, out_specs=...  2.5 us
    ppermute x1, starting transfers between devices, shards(): lax.ppermute(own, ('pair', 'samp'), [(0, 3), (1, 2), (2, 1), (3, 0)])  2.46 us
    pallas_call x1, Pallas kernels, shards(): pl.pallas_call(project_kernel, in_specs=[IN_SMEM] + [IN_VMEM] * len(opera...  2.41 us
    pallas_call x1, Pallas kernels, shards(): pl.pallas_call(functools.partial(inner_kernel, heads), in_specs=[IN_SMEM]...  2.21 us
    ppermute x3, starting transfers between devices, swap(): return lax.ppermute(value, ('atoms', 'samp'), sides)  2.15 us
    pallas_call x1, Pallas kernels, shards(): pl.pallas_call(functools.partial(outer_kernel, heads, blocks), in_specs=[...  1.95 us
    ppermute x1, waiting for transfers between devices, shards(): across = lax.ppermute(own, 'pair', swapped)  0.74 us
    ppermute x1, starting transfers between devices, shards(): across = lax.ppermute(own, 'pair', swapped)  0.64 us
  transfers between devices with their start and end apart: 6, of which 1 were waited for; matrix products, arithmetic and copies ran while one was open for 0% of the time, Pallas kernels for 30%

profile of v15, /device:TPU:0, one launch (start us, length us, event | category | flops | bytes accessed | tf_op | source)
XLA Modules:
  0.0 15.5 jit_solution(2942992237887214962)
XLA Ops:
  0.0 0.0 copy-start.2
  0.0 0.0 copy-start.1
  0.0 0.0 copy-start.14
  0.0 0.0 copy-start.6
  0.0 0.0 copy-start.12
  0.0 0.0 copy-start.11
  0.0 0.0 copy-start.13
  0.1 0.0 copy-start.16
  0.1 0.0 copy-start.15
  0.1 0.0 copy-start.10
  0.1 0.0 copy-start.9
  0.1 0.0 copy-start.5
  0.1 0.0 copy-start.4
  0.1 2.5 %shard_map.182.refs_0_ = bf16[2,64,128]{2,1,0:T(8,128)(2,1)S(1)} custom-call(s32[1]{0:T(128)} %bitcast.2.core_ref, bf16[4,128]{1,0:T(4,128)(2,1)} %bitcast.4, bf16[128,64,128]{2,1,0:T(8,128)(2,1)} %pair_hbm.1), custom_call_target="tpu_custom_call" | custom-call | flops 268435456 | bytes 4194304 | tf_op jit(solution)/shard_map/pallas_call | solution.py:459
  2.6 0.0 copy-start
  2.6 0.0 copy-start.3
  2.7 2.5 %collective-permute-start.2 = (bf16[2,64,128]{2,1,0:T(8,128)(2,1)S(1)}, bf16[2,64,128]{2,1,0:T(8,128)(2,1)S(1)}, u32[]{:S(2)}, u32[]{:S(2)}) collective-permute-start(bf16[2,64,128]{2,1,0:T(8,128)(2,1)S(1)} %shard_map.182.refs_0_), channel_id=1, source_target_pairs={{0,3},{1,2},{2,1},{3,0},{4,7},{5,6},{6,5},{7,4},{8,11},{9,10},{10,... | collective-permute-start | bytes 98312 | tf_op jit(solution)/shard_map/ppermute | solution.py:476
  5.1 0.6 %collective-permute-start.1 = (bf16[2,64,128]{2,1,0:T(8,128)(2,1)S(1)}, bf16[2,64,128]{2,1,0:T(8,128)(2,1)S(1)}, u32[]{:S(2)}, u32[]{:S(2)}) collective-permute-start(bf16[2,64,128]{2,1,0:T(8,128)(2,1)S(1)} %shard_map.182.refs_0_), channel_id=1, source_target_pairs={{0,2},{2,0},{1,3},{3,1},{4,6},{6,4},{5,7},{7,5},{8,10},{10,8},{9,1... | collective-permute-start | bytes 98312 | tf_op jit(solution)/shard_map/ppermute | solution.py:475
  5.8 0.0 collective-permute-start
  5.8 0.0 copy-done.2
  5.8 0.0 copy-done.1
  5.8 0.0 copy-done.14
  5.8 0.0 copy-done.8
  5.8 0.0 copy-done.7
  5.8 0.0 copy-done.6
  5.8 0.0 copy-done.12
  5.8 0.0 copy-done.11
  5.8 0.0 copy-done.13
  5.9 0.0 copy-done.16
  5.9 0.0 copy-done.15
  5.9 0.0 copy-done.10
  5.9 0.0 copy-done.9
  5.9 0.0 copy-done.5
  5.9 0.0 copy-done.4
  5.9 2.4 %shard_map.181 = (bf16[3,512,128]{2,1,0:T(8,128)(2,1)S(1)}, bf16[3,512,128]{2,1,0:T(8,128)(2,1)S(1)}, bf16[3,512,128]{2,1,0:T(8,128)(2,1)S(1)}, bf16[3,512,128]{...) custom-call(s32[1]{0:T(128)} %bitcast.at_ref, ...), custom_call_target="tpu_custom_call" | custom-call | flops 1006632960 | bytes 4194304 | tf_op jit(solution)/shard_map/pallas_call | solution.py:498
  8.3 0.0 collective-permute-done.2.refs_3_
  8.3 0.7 %collective-permute-done.1.refs_2_ = bf16[2,64,128]{2,1,0:T(8,128)(2,1)S(1)} collective-permute-done((bf16[2,64,128]{2,1,0:T(8,128)(2,1)S(1)}, bf16[2,64,128]{2,1,0:T(8,128)(2,1)S(1)}, u32[]{:S(2)}, u32[]{:S(2)}) %collective-permute-start.1) | collective-permute-done | bytes 32800 | tf_op jit(solution)/shard_map/ppermute | solution.py:475
  9.1 0.0 collective-permute-done.refs_1_
  9.1 1.6 %collective-permute-start.3 = (bf16[240,128]{1,0:T(8,128)(2,1)S(1)}, bf16[240,128]{1,0:T(8,128)(2,1)S(1)}, u32[]{:S(2)}, u32[]{:S(2)}) collective-permute-start(bf16[240,128]{1,0:T(8,128)(2,1)S(1)} %get-tuple-element.28), channel_id=1, source_target_pairs={{0,4},{1,5},{4,0},{5,1},{8,9},{9,8},{12,13},{13,12},{2,6},{3,7},{6... | collective-permute-start | bytes 184328 | tf_op jit(solution)/shard_map/ppermute | solution.py:535
  10.8 0.0 collective-permute-start.4
  10.8 0.5 %collective-permute-start.5 = (bf16[240,128]{1,0:T(8,128)(2,1)S(1)}, bf16[240,128]{1,0:T(8,128)(2,1)S(1)}, u32[]{:S(2)}, u32[]{:S(2)}) collective-permute-start(bf16[240,128]{1,0:T(8,128)(2,1)S(1)} %get-tuple-element.30), channel_id=1, source_target_pairs={{0,1},{1,0},{4,5},{5,4},{8,12},{9,13},{12,8},{13,9},{2,3},{3,2},{6... | collective-permute-start | bytes 184328 | tf_op jit(solution)/shard_map/ppermute | solution.py:535
  11.3 0.0 copy-done
  11.3 0.0 copy-done.3
  11.3 2.2 %shard_map.184.inner_ref = bf16[3,384,128]{2,1,0:T(8,128)(2,1)S(1)} custom-call(s32[1]{0:T(128)} %bitcast.at_ref, s32[4,64]{1,0:T(4,128)S(1)} %copy-done.3, bf16[3,512,128]{2,1,0:T(8,128)(2,1)S(1)} %get-tuple-element.18.query_ref, bf16[3,512,128]{2,1,0:T(8,128)(2,1)S(1)} %get-tuple-element.19.key_ref.own_key_ref, ...), custom_call_target="tpu_custom_call" | custom-call | flops 603979776 | bytes 4194304 | tf_op jit(solution)/shard_map/pallas_call | solution.py:541
  13.5 0.0 collective-permute-done.3.early_ref
  13.5 0.0 collective-permute-done.4.second_ref
  13.5 0.0 collective-permute-done.5.late_ref
  13.5 1.9 %shard_map.185 = bf16[3,512,128]{2,1,0:T(8,128)(2,1)} custom-call(s32[1]{0:T(128)} %bitcast.at_ref, s32[4,64]{1,0:T(4,128)S(1)} %copy-done.3, bf16[3,512,128]{2,1,0:T(8,128)(2,1)S(1)} %get-tuple-element.18.query_ref, bf16[3,512,128]{2,1,0:T(8,128)(2,1)S(1)} %get-tuple-element.19.key_ref.own_key_ref, ...), custom_call_target="tpu_custom_call" | custom-call | flops 201326592 | bytes 4194304 | tf_op jit(solution)/shard_map/pallas_call | solution.py:556
  (3 shorter events, 0.1 us)
Async XLA Ops:
  0.0 5.8 %copy-start.2 = (bf16[128,128]{1,0:T(8,128)(2,1)S(1)}, bf16[128,128]{1,0:T(8,128)(2,1)}, u32[]{:S(2)}) copy-start(bf16[128,128]{1,0:T(8,128)(2,1)} %w_value.3) | copy-start | bytes 98308
  0.0 5.8 %copy-start.1 = (bf16[128,128]{1,0:T(8,128)(2,1)S(1)}, bf16[128,128]{1,0:T(8,128)(2,1)}, u32[]{:S(2)}) copy-start(bf16[128,128]{1,0:T(8,128)(2,1)} %w_key.3) | copy-start | bytes 98308
  0.0 5.8 %copy-start.14 = (bf16[128,128]{1,0:T(8,128)(2,1)S(1)}, bf16[128,128]{1,0:T(8,128)(2,1)}, u32[]{:S(2)}) copy-start(bf16[128,128]{1,0:T(8,128)(2,1)} %trans_gate.1) | copy-start | bytes 98308
  0.0 5.8 %copy-start.8 = (bf16[256,128]{1,0:T(8,128)(2,1)S(1)}, bf16[256,128]{1,0:T(8,128)(2,1)}, u32[]{:S(2)}) copy-start(bf16[256,128]{1,0:T(8,128)(2,1)} %w_down.1) | copy-start | bytes 196612
  0.0 5.8 %copy-start.7 = (bf16[128,256]{1,0:T(8,128)(2,1)S(1)}, bf16[128,256]{1,0:T(8,128)(2,1)}, u32[]{:S(2)}) copy-start(bf16[128,256]{1,0:T(8,128)(2,1)} %w_linear.1) | copy-start | bytes 196612
  0.0 5.8 %copy-start.6 = (bf16[128,256]{1,0:T(8,128)(2,1)S(1)}, bf16[128,256]{1,0:T(8,128)(2,1)}, u32[]{:S(2)}) copy-start(bf16[128,256]{1,0:T(8,128)(2,1)} %w_swish.1) | copy-start | bytes 196612
  0.0 5.8 %copy-start.12 = (bf16[128,128]{1,0:T(8,128)(2,1)S(1)}, bf16[128,128]{1,0:T(8,128)(2,1)}, u32[]{:S(2)}) copy-start(bf16[128,128]{1,0:T(8,128)(2,1)} %ada_trans_shift.1) | copy-start | bytes 98308
  0.0 5.8 %copy-start.11 = (bf16[128,128]{1,0:T(8,128)(2,1)S(1)}, bf16[128,128]{1,0:T(8,128)(2,1)}, u32[]{:S(2)}) copy-start(bf16[128,128]{1,0:T(8,128)(2,1)} %ada_trans.1) | copy-start | bytes 98308
  0.0 5.8 %copy-start.13 = (bf16[128,128]{1,0:T(8,128)(2,1)S(1)}, bf16[128,128]{1,0:T(8,128)(2,1)}, u32[]{:S(2)}) copy-start(bf16[128,128]{1,0:T(8,128)(2,1)} %attn_gate.1) | copy-start | bytes 98308
  0.1 5.8 %copy-start.16 = (bf16[128,128]{1,0:T(8,128)(2,1)S(1)}, bf16[128,128]{1,0:T(8,128)(2,1)}, u32[]{:S(2)}) copy-start(bf16[128,128]{1,0:T(8,128)(2,1)} %w_gate.1) | copy-start | bytes 98308
  0.1 5.8 %copy-start.15 = (bf16[128,128]{1,0:T(8,128)(2,1)S(1)}, bf16[128,128]{1,0:T(8,128)(2,1)}, u32[]{:S(2)}) copy-start(bf16[128,128]{1,0:T(8,128)(2,1)} %w_query.1) | copy-start | bytes 98308
  0.1 5.8 %copy-start.10 = (bf16[128,128]{1,0:T(8,128)(2,1)S(1)}, bf16[128,128]{1,0:T(8,128)(2,1)}, u32[]{:S(2)}) copy-start(bf16[128,128]{1,0:T(8,128)(2,1)} %ada_attn_shift.1) | copy-start | bytes 98308
  0.1 5.8 %copy-start.9 = (bf16[128,128]{1,0:T(8,128)(2,1)S(1)}, bf16[128,128]{1,0:T(8,128)(2,1)}, u32[]{:S(2)}) copy-start(bf16[128,128]{1,0:T(8,128)(2,1)} %ada_attn.1) | copy-start | bytes 98308
  0.1 5.8 %copy-start.5 = (bf16[512,128]{1,0:T(8,128)(2,1)S(1)}, bf16[512,128]{1,0:T(8,128)(2,1)}, u32[]{:S(2)}) copy-start(bf16[512,128]{1,0:T(8,128)(2,1)} %cond_ref.1) | copy-start | bytes 393220
  0.1 5.8 %copy-start.4 = (bf16[3,512,128]{2,1,0:T(8,128)(2,1)S(1)}, bf16[3,512,128]{2,1,0:T(8,128)(2,1)}, u32[]{:S(2)}) copy-start(bf16[3,512,128]{2,1,0:T(8,128)(2,1)} %single_ref.1) | copy-start | bytes 1179652
  2.6 8.7 %copy-start = (bf16[128,128]{1,0:T(8,128)(2,1)S(1)}, bf16[128,128]{1,0:T(8,128)(2,1)}, u32[]{:S(2)}) copy-start(bf16[128,128]{1,0:T(8,128)(2,1)} %w_out_ref.3) | copy-start | bytes 98308
  2.6 8.7 %copy-start.3 = (s32[4,64]{1,0:T(4,128)S(1)}, s32[4,64]{1,0:T(4,128)}, u32[]{:S(2)}) copy-start(s32[4,64]{1,0:T(4,128)} %counts_ref.3) | copy-start | bytes 3076
  2.7 5.7 %collective-permute-start.2 = (bf16[2,64,128]{2,1,0:T(8,128)(2,1)S(1)}, bf16[2,64,128]{2,1,0:T(8,128)(2,1)S(1)}, u32[]{:S(2)}, u32[]{:S(2)}) collective-permute-start(bf16[2,64,128]{2,1,0:T(8,128)(2,1)S(1)} %shard_map.182.refs_0_), channel_id=1, source_target_pairs={{0,3},{1,2},{2,1},{3,0},{4,7},{5,6},{6,5},{7,4},{8,11},{9,10},{10,... | collective-permute-start | bytes 98312 | tf_op jit(solution)/shard_map/ppermute | solution.py:476
  5.1 4.0 %collective-permute-start.1 = (bf16[2,64,128]{2,1,0:T(8,128)(2,1)S(1)}, bf16[2,64,128]{2,1,0:T(8,128)(2,1)S(1)}, u32[]{:S(2)}, u32[]{:S(2)}) collective-permute-start(bf16[2,64,128]{2,1,0:T(8,128)(2,1)S(1)} %shard_map.182.refs_0_), channel_id=1, source_target_pairs={{0,2},{2,0},{1,3},{3,1},{4,6},{6,4},{5,7},{7,5},{8,10},{10,8},{9,1... | collective-permute-start | bytes 98312 | tf_op jit(solution)/shard_map/ppermute | solution.py:475
  5.8 3.3 %collective-permute-start = (bf16[2,64,128]{2,1,0:T(8,128)(2,1)S(1)}, bf16[2,64,128]{2,1,0:T(8,128)(2,1)S(1)}, u32[]{:S(2)}, u32[]{:S(2)}) collective-permute-start(bf16[2,64,128]{2,1,0:T(8,128)(2,1)S(1)} %shard_map.182.refs_0_), channel_id=1, source_target_pairs={{0,1},{1,0},{2,3},{3,2},{4,5},{5,4},{6,7},{7,6},{8,9},{9,8},{10,11... | collective-permute-start | bytes 98312 | tf_op jit(solution)/shard_map/ppermute | solution.py:477
  9.1 4.4 %collective-permute-start.3 = (bf16[240,128]{1,0:T(8,128)(2,1)S(1)}, bf16[240,128]{1,0:T(8,128)(2,1)S(1)}, u32[]{:S(2)}, u32[]{:S(2)}) collective-permute-start(bf16[240,128]{1,0:T(8,128)(2,1)S(1)} %get-tuple-element.28), channel_id=1, source_target_pairs={{0,4},{1,5},{4,0},{5,1},{8,9},{9,8},{12,13},{13,12},{2,6},{3,7},{6... | collective-permute-start | bytes 184328 | tf_op jit(solution)/shard_map/ppermute | solution.py:535
  10.8 2.7 %collective-permute-start.4 = (bf16[240,128]{1,0:T(8,128)(2,1)S(1)}, bf16[240,128]{1,0:T(8,128)(2,1)S(1)}, u32[]{:S(2)}, u32[]{:S(2)}) collective-permute-start(bf16[240,128]{1,0:T(8,128)(2,1)S(1)} %get-tuple-element.29), channel_id=1, source_target_pairs={{0,1},{1,0},{4,8},{5,9},{8,4},{9,5},{12,13},{13,12},{2,3},{3,2},{6... | collective-permute-start | bytes 184328 | tf_op jit(solution)/shard_map/ppermute | solution.py:535
  10.8 2.8 %collective-permute-start.5 = (bf16[240,128]{1,0:T(8,128)(2,1)S(1)}, bf16[240,128]{1,0:T(8,128)(2,1)S(1)}, u32[]{:S(2)}, u32[]{:S(2)}) collective-permute-start(bf16[240,128]{1,0:T(8,128)(2,1)S(1)} %get-tuple-element.30), channel_id=1, source_target_pairs={{0,1},{1,0},{4,5},{5,4},{8,12},{9,13},{12,8},{13,9},{2,3},{3,2},{6... | collective-permute-start | bytes 184328 | tf_op jit(solution)/shard_map/ppermute | solution.py:535

commit v16 on v15

--- a/solution.py
+++ b/solution.py
@@ -45,15 +45,20 @@
     return jnp.concatenate([rows[:half], rows[half:]], 1)
 
 
-def centre(rows):
-    values = rows.astype(F32)
-    centred = values - jnp.mean(values, axis=-1, keepdims=True)
-    return centred, jnp.mean(centred * centred, axis=-1, keepdims=True)
+def centring(width):
+    same = iota((width, width), 0) == iota((width, width), 1)
+    return jnp.where(same, 1.0 - 1.0 / width, -1.0 / width).astype(BF16)
+
+
+def mean_square(centred):
+    return jnp.mean(centred * centred, axis=-1, keepdims=True)
 
 
 def layer_norm(rows):
-    centred, variance = centre(rows)
-    return centred * lax.rsqrt(variance + EPSILON)
+    width = rows.shape[1]
+    both = dot(side_by_side(rows), twice(centring(width)))
+    centred = jnp.concatenate([both[:, :width], both[:, width:]], 0)
+    return centred * lax.rsqrt(mean_square(centred) + EPSILON)
 
 
 def sigmoid(values):
@@ -89,6 +94,7 @@
         [jnp.broadcast_to(w_pair[h : h + 1], (group, width)) for h in range(heads)], 0
     )
     mix = twice(spread.T.astype(BF16))
+    centre = twice(centring(width))
     slot = iota((cols, lanes), 1) % group
 
     @pl.loop(0, rows // group)
@@ -97,15 +103,18 @@
             pair_copy(chunk * 2 + part).wait()
 
         pair = pair_ref[pl.ds(chunk * group, group)].reshape(group * cols, width)
-        centred, variance = centre(pair)
-        variance = variance.reshape(group, cols, 1)
-        mixed = dot(side_by_side(centred.astype(BF16)), mix).reshape(half, cols, 2 * lanes)
+        centred = dot(side_by_side(pair), centre)
+        mixed = dot(centred.astype(BF16), mix).reshape(half, cols, 2 * lanes)
+        variances = [
+            mean_square(centred[:, part * width : (part + 1) * width]).reshape(half, cols, 1)
+            for part in range(2)
+        ]
         total = jnp.zeros((cols, lanes), F32)
         spread_out = jnp.zeros((cols, lanes), F32)
         for i in range(group):
             side = slice(i // half * lanes, (i // half + 1) * lanes)
             total = jnp.where(slot == i, mixed[i % half, :, side], total)
-            spread_out = jnp.where(slot == i, variance[i], spread_out)
+            spread_out = jnp.where(slot == i, variances[i // half][i % half], spread_out)
         bias = (total * lax.rsqrt(spread_out + EPSILON)).astype(BF16)
         tile_ref[chunk] = bias
 
@@ -242,12 +251,24 @@
         biases.append(bias if mask is None else jnp.where(mask, bias, MASKED))
     units = [(sample, i) for i in range(len(windows)) for sample in range(samples)]
     scores = []
-    for sample, i in units:
-        query = query_ref[sample, pl.ds(windows[i][0], Q_WIN), :]
-        query = jnp.concatenate([query] * heads, 0) * own_head
-        keys = windows[i][1](sample)[0]
-        product = lax.dot_general(query, keys, LAST, preferred_element_type=F32)
-        scores.append(product * scaling + biases[i])
+    for first in range(0, len(units), 2):
+        couple = units[first : first + 2]
+        queries, keys = [], []
+        for sample, i in couple:
+            query = query_ref[sample, pl.ds(windows[i][0], Q_WIN), :]
+            queries.append(jnp.concatenate([query] * heads, 0) * own_head)
+            keys.append(windows[i][1](sample)[0])
+        if len(couple) == 2:
+            blank = jnp.zeros_like(keys[0])
+            keys = [jnp.concatenate([keys[0], blank], 1), jnp.concatenate([blank, keys[1]], 1)]
+        product = lax.dot_general(
+            jnp.concatenate(queries, 1),
+            jnp.concatenate(keys, 0),
+            LAST,
+            preferred_element_type=F32,
+        )
+        for j, (_, i) in enumerate(couple):
+            scores.append(product[:, j * K_WIN : (j + 1) * K_WIN] * scaling + biases[i])
     tops = [jnp.max(score, axis=-1, keepdims=True) for score in scores]
     raised = [jnp.exp2(score - top).astype(BF16) for score, top in zip(scores, tops)]
     for (sample, i), weight in zip(units, raised):

time: 15.6 us -> 15.4 us (0.987)
  Pallas kernels: 9.11 us -> 8.87 us
  transfers between devices with their start and end apart: 6 -> 6, of which waited for: 1 -> 1; matrix products, arithmetic and copies ran while one was open for 0% -> 0% of each run, Pallas kernels for 30% -> 29%
where the time goes in v16:
time: 15.4 us; the launch traced here: 15.3 us
  Pallas kernels  8.87 us (58%)
  starting transfers between devices  5.29 us (34%)
  waiting for transfers between devices  0.81 us (5%)
  between operations  0.25 us (2%)
    ppermute x1, starting transfers between devices, shards(): lax.ppermute(own, ('pair', 'samp'), [(0, 3), (1, 2), (2, 1), (3, 0)])  2.46 us
    pallas_call x1, Pallas kernels, shards(): pl.pallas_call(project_kernel, in_specs=[IN_SMEM] + [IN_VMEM] * len(opera...  2.37 us
    pallas_call x1, Pallas kernels, shards(): pl.pallas_call(pair_kernel, in_specs=[IN_SMEM] + [IN_HBM] * 2, out_specs=...  2.35 us
    ppermute x3, starting transfers between devices, swap(): return lax.ppermute(value, ('atoms', 'samp'), sides)  2.15 us
    pallas_call x1, Pallas kernels, shards(): pl.pallas_call(functools.partial(inner_kernel, heads), in_specs=[IN_SMEM]...  2.1 us
    pallas_call x1, Pallas kernels, shards(): pl.pallas_call(functools.partial(outer_kernel, heads, blocks), in_specs=[...  2 us
    ppermute x1, waiting for transfers between devices, shards(): across = lax.ppermute(own, 'pair', swapped)  0.78 us
    ppermute x1, starting transfers between devices, shards(): across = lax.ppermute(own, 'pair', swapped)  0.64 us
  transfers between devices with their start and end apart: 6, of which 1 were waited for; matrix products, arithmetic and copies ran while one was open for 0% of the time, Pallas kernels for 29%

profile of v16, /device:TPU:0, one launch (start us, length us, event | category | flops | bytes accessed | tf_op | source)
XLA Modules:
  0.0 15.3 jit_solution(13604436586114176334)
XLA Ops:
  0.0 0.0 copy-start.2
  0.0 0.0 copy-start.1
  0.0 0.0 copy-start.14
  0.0 0.0 copy-start.6
  0.0 0.0 copy-start.12
  0.0 0.0 copy-start.11
  0.0 0.0 copy-start.13
  0.1 0.0 copy-start.16
  0.1 0.0 copy-start.15
  0.1 0.0 copy-start.10
  0.1 0.0 copy-start.9
  0.1 0.0 copy-start.5
  0.1 0.0 copy-start.4
  0.1 2.4 %shard_map.182.refs_0_ = bf16[2,64,128]{2,1,0:T(8,128)(2,1)S(1)} custom-call(s32[1]{0:T(128)} %bitcast.2.core_ref, bf16[4,128]{1,0:T(4,128)(2,1)} %bitcast.4, bf16[128,64,128]{2,1,0:T(8,128)(2,1)} %pair_hbm.1), custom_call_target="tpu_custom_call" | custom-call | flops 268435456 | bytes 4194304 | tf_op jit(solution)/shard_map/pallas_call | solution.py:480
  2.5 0.0 copy-start
  2.5 0.0 copy-start.3
  2.5 2.5 %collective-permute-start.2 = (bf16[2,64,128]{2,1,0:T(8,128)(2,1)S(1)}, bf16[2,64,128]{2,1,0:T(8,128)(2,1)S(1)}, u32[]{:S(2)}, u32[]{:S(2)}) collective-permute-start(bf16[2,64,128]{2,1,0:T(8,128)(2,1)S(1)} %shard_map.182.refs_0_), channel_id=1, source_target_pairs={{0,3},{1,2},{2,1},{3,0},{4,7},{5,6},{6,5},{7,4},{8,11},{9,10},{10,... | collective-permute-start | bytes 98312 | tf_op jit(solution)/shard_map/ppermute | solution.py:497
  5.0 0.6 %collective-permute-start.1 = (bf16[2,64,128]{2,1,0:T(8,128)(2,1)S(1)}, bf16[2,64,128]{2,1,0:T(8,128)(2,1)S(1)}, u32[]{:S(2)}, u32[]{:S(2)}) collective-permute-start(bf16[2,64,128]{2,1,0:T(8,128)(2,1)S(1)} %shard_map.182.refs_0_), channel_id=1, source_target_pairs={{0,2},{2,0},{1,3},{3,1},{4,6},{6,4},{5,7},{7,5},{8,10},{10,8},{9,1... | collective-permute-start | bytes 98312 | tf_op jit(solution)/shard_map/ppermute | solution.py:496
  5.6 0.0 collective-permute-start
  5.6 0.0 copy-done.2
  5.6 0.0 copy-done.1
  5.6 0.0 copy-done.14
  5.6 0.0 copy-done.8
  5.7 0.0 copy-done.7
  5.7 0.0 copy-done.6
  5.7 0.0 copy-done.12
  5.7 0.0 copy-done.11
  5.7 0.0 copy-done.13
  5.7 0.0 copy-done.16
  5.7 0.0 copy-done.15
  5.7 0.0 copy-done.10
  5.7 0.0 copy-done.9
  5.7 0.0 copy-done.5
  5.8 0.0 copy-done.4
  5.8 2.4 %shard_map.181 = (bf16[3,512,128]{2,1,0:T(8,128)(2,1)S(1)}, bf16[3,512,128]{2,1,0:T(8,128)(2,1)S(1)}, bf16[3,512,128]{2,1,0:T(8,128)(2,1)S(1)}, bf16[3,512,128]{...) custom-call(s32[1]{0:T(128)} %bitcast.at_ref, ...), custom_call_target="tpu_custom_call" | custom-call | flops 1006632960 | bytes 4194304 | tf_op jit(solution)/shard_map/pallas_call | solution.py:519
  8.1 0.0 collective-permute-done.2.refs_3_
  8.2 0.8 %collective-permute-done.1.refs_2_ = bf16[2,64,128]{2,1,0:T(8,128)(2,1)S(1)} collective-permute-done((bf16[2,64,128]{2,1,0:T(8,128)(2,1)S(1)}, bf16[2,64,128]{2,1,0:T(8,128)(2,1)S(1)}, u32[]{:S(2)}, u32[]{:S(2)}) %collective-permute-start.1) | collective-permute-done | bytes 32800 | tf_op jit(solution)/shard_map/ppermute | solution.py:496
  8.9 0.0 collective-permute-done.refs_1_
  9.0 1.6 %collective-permute-start.3 = (bf16[240,128]{1,0:T(8,128)(2,1)S(1)}, bf16[240,128]{1,0:T(8,128)(2,1)S(1)}, u32[]{:S(2)}, u32[]{:S(2)}) collective-permute-start(bf16[240,128]{1,0:T(8,128)(2,1)S(1)} %get-tuple-element.28), channel_id=1, source_target_pairs={{0,4},{1,5},{4,0},{5,1},{8,9},{9,8},{12,13},{13,12},{2,6},{3,7},{6... | collective-permute-start | bytes 184328 | tf_op jit(solution)/shard_map/ppermute | solution.py:556
  10.6 0.0 collective-permute-start.4
  10.6 0.5 %collective-permute-start.5 = (bf16[240,128]{1,0:T(8,128)(2,1)S(1)}, bf16[240,128]{1,0:T(8,128)(2,1)S(1)}, u32[]{:S(2)}, u32[]{:S(2)}) collective-permute-start(bf16[240,128]{1,0:T(8,128)(2,1)S(1)} %get-tuple-element.30), channel_id=1, source_target_pairs={{0,1},{1,0},{4,5},{5,4},{8,12},{9,13},{12,8},{13,9},{2,3},{3,2},{6... | collective-permute-start | bytes 184328 | tf_op jit(solution)/shard_map/ppermute | solution.py:556
  11.1 0.0 copy-done
  11.1 0.0 copy-done.3
  11.1 2.1 %shard_map.184.inner_ref = bf16[3,384,128]{2,1,0:T(8,128)(2,1)S(1)} custom-call(s32[1]{0:T(128)} %bitcast.at_ref, s32[4,64]{1,0:T(4,128)S(1)} %copy-done.3, bf16[3,512,128]{2,1,0:T(8,128)(2,1)S(1)} %get-tuple-element.18.query_ref, bf16[3,512,128]{2,1,0:T(8,128)(2,1)S(1)} %get-tuple-element.19.key_ref.own_key_ref, ...), custom_call_target="tpu_custom_call" | custom-call | flops 603979776 | bytes 4194304 | tf_op jit(solution)/shard_map/pallas_call | solution.py:562
  13.3 0.0 collective-permute-done.3.early_ref
  13.3 0.0 collective-permute-done.4.second_ref
  13.3 0.0 collective-permute-done.5.late_ref
  13.3 2.0 %shard_map.185 = bf16[3,512,128]{2,1,0:T(8,128)(2,1)} custom-call(s32[1]{0:T(128)} %bitcast.at_ref, s32[4,64]{1,0:T(4,128)S(1)} %copy-done.3, bf16[3,512,128]{2,1,0:T(8,128)(2,1)S(1)} %get-tuple-element.18.query_ref, bf16[3,512,128]{2,1,0:T(8,128)(2,1)S(1)} %get-tuple-element.19.key_ref.own_key_ref, ...), custom_call_target="tpu_custom_call" | custom-call | flops 201326592 | bytes 4194304 | tf_op jit(solution)/shard_map/pallas_call | solution.py:577
  (3 shorter events, 0.1 us)
Async XLA Ops:
  0.0 5.6 %copy-start.2 = (bf16[128,128]{1,0:T(8,128)(2,1)S(1)}, bf16[128,128]{1,0:T(8,128)(2,1)}, u32[]{:S(2)}) copy-start(bf16[128,128]{1,0:T(8,128)(2,1)} %w_value.3) | copy-start | bytes 98308
  0.0 5.6 %copy-start.1 = (bf16[128,128]{1,0:T(8,128)(2,1)S(1)}, bf16[128,128]{1,0:T(8,128)(2,1)}, u32[]{:S(2)}) copy-start(bf16[128,128]{1,0:T(8,128)(2,1)} %w_key.3) | copy-start | bytes 98308
  0.0 5.6 %copy-start.14 = (bf16[128,128]{1,0:T(8,128)(2,1)S(1)}, bf16[128,128]{1,0:T(8,128)(2,1)}, u32[]{:S(2)}) copy-start(bf16[128,128]{1,0:T(8,128)(2,1)} %trans_gate.1) | copy-start | bytes 98308
  0.0 5.6 %copy-start.8 = (bf16[256,128]{1,0:T(8,128)(2,1)S(1)}, bf16[256,128]{1,0:T(8,128)(2,1)}, u32[]{:S(2)}) copy-start(bf16[256,128]{1,0:T(8,128)(2,1)} %w_down.1) | copy-start | bytes 196612
  0.0 5.6 %copy-start.7 = (bf16[128,256]{1,0:T(8,128)(2,1)S(1)}, bf16[128,256]{1,0:T(8,128)(2,1)}, u32[]{:S(2)}) copy-start(bf16[128,256]{1,0:T(8,128)(2,1)} %w_linear.1) | copy-start | bytes 196612
  0.0 5.7 %copy-start.6 = (bf16[128,256]{1,0:T(8,128)(2,1)S(1)}, bf16[128,256]{1,0:T(8,128)(2,1)}, u32[]{:S(2)}) copy-start(bf16[128,256]{1,0:T(8,128)(2,1)} %w_swish.1) | copy-start | bytes 196612
  0.0 5.7 %copy-start.12 = (bf16[128,128]{1,0:T(8,128)(2,1)S(1)}, bf16[128,128]{1,0:T(8,128)(2,1)}, u32[]{:S(2)}) copy-start(bf16[128,128]{1,0:T(8,128)(2,1)} %ada_trans_shift.1) | copy-start | bytes 98308
  0.0 5.7 %copy-start.11 = (bf16[128,128]{1,0:T(8,128)(2,1)S(1)}, bf16[128,128]{1,0:T(8,128)(2,1)}, u32[]{:S(2)}) copy-start(bf16[128,128]{1,0:T(8,128)(2,1)} %ada_trans.1) | copy-start | bytes 98308
  0.0 5.7 %copy-start.13 = (bf16[128,128]{1,0:T(8,128)(2,1)S(1)}, bf16[128,128]{1,0:T(8,128)(2,1)}, u32[]{:S(2)}) copy-start(bf16[128,128]{1,0:T(8,128)(2,1)} %attn_gate.1) | copy-start | bytes 98308
  0.1 5.7 %copy-start.16 = (bf16[128,128]{1,0:T(8,128)(2,1)S(1)}, bf16[128,128]{1,0:T(8,128)(2,1)}, u32[]{:S(2)}) copy-start(bf16[128,128]{1,0:T(8,128)(2,1)} %w_gate.1) | copy-start | bytes 98308
  0.1 5.7 %copy-start.15 = (bf16[128,128]{1,0:T(8,128)(2,1)S(1)}, bf16[128,128]{1,0:T(8,128)(2,1)}, u32[]{:S(2)}) copy-start(bf16[128,128]{1,0:T(8,128)(2,1)} %w_query.1) | copy-start | bytes 98308
  0.1 5.7 %copy-start.10 = (bf16[128,128]{1,0:T(8,128)(2,1)S(1)}, bf16[128,128]{1,0:T(8,128)(2,1)}, u32[]{:S(2)}) copy-start(bf16[128,128]{1,0:T(8,128)(2,1)} %ada_attn_shift.1) | copy-start | bytes 98308
  0.1 5.7 %copy-start.9 = (bf16[128,128]{1,0:T(8,128)(2,1)S(1)}, bf16[128,128]{1,0:T(8,128)(2,1)}, u32[]{:S(2)}) copy-start(bf16[128,128]{1,0:T(8,128)(2,1)} %ada_attn.1) | copy-start | bytes 98308
  0.1 5.7 %copy-start.5 = (bf16[512,128]{1,0:T(8,128)(2,1)S(1)}, bf16[512,128]{1,0:T(8,128)(2,1)}, u32[]{:S(2)}) copy-start(bf16[512,128]{1,0:T(8,128)(2,1)} %cond_ref.1) | copy-start | bytes 393220
  0.1 5.7 %copy-start.4 = (bf16[3,512,128]{2,1,0:T(8,128)(2,1)S(1)}, bf16[3,512,128]{2,1,0:T(8,128)(2,1)}, u32[]{:S(2)}) copy-start(bf16[3,512,128]{2,1,0:T(8,128)(2,1)} %single_ref.1) | copy-start | bytes 1179652
  2.5 8.7 %copy-start = (bf16[128,128]{1,0:T(8,128)(2,1)S(1)}, bf16[128,128]{1,0:T(8,128)(2,1)}, u32[]{:S(2)}) copy-start(bf16[128,128]{1,0:T(8,128)(2,1)} %w_out_ref.3) | copy-start | bytes 98308
  2.5 8.7 %copy-start.3 = (s32[4,64]{1,0:T(4,128)S(1)}, s32[4,64]{1,0:T(4,128)}, u32[]{:S(2)}) copy-start(s32[4,64]{1,0:T(4,128)} %counts_ref.3) | copy-start | bytes 3076
  2.5 5.6 %collective-permute-start.2 = (bf16[2,64,128]{2,1,0:T(8,128)(2,1)S(1)}, bf16[2,64,128]{2,1,0:T(8,128)(2,1)S(1)}, u32[]{:S(2)}, u32[]{:S(2)}) collective-permute-start(bf16[2,64,128]{2,1,0:T(8,128)(2,1)S(1)} %shard_map.182.refs_0_), channel_id=1, source_target_pairs={{0,3},{1,2},{2,1},{3,0},{4,7},{5,6},{6,5},{7,4},{8,11},{9,10},{10,... | collective-permute-start | bytes 98312 | tf_op jit(solution)/shard_map/ppermute | solution.py:497
  5.0 4.0 %collective-permute-start.1 = (bf16[2,64,128]{2,1,0:T(8,128)(2,1)S(1)}, bf16[2,64,128]{2,1,0:T(8,128)(2,1)S(1)}, u32[]{:S(2)}, u32[]{:S(2)}) collective-permute-start(bf16[2,64,128]{2,1,0:T(8,128)(2,1)S(1)} %shard_map.182.refs_0_), channel_id=1, source_target_pairs={{0,2},{2,0},{1,3},{3,1},{4,6},{6,4},{5,7},{7,5},{8,10},{10,8},{9,1... | collective-permute-start | bytes 98312 | tf_op jit(solution)/shard_map/ppermute | solution.py:496
  5.6 3.3 %collective-permute-start = (bf16[2,64,128]{2,1,0:T(8,128)(2,1)S(1)}, bf16[2,64,128]{2,1,0:T(8,128)(2,1)S(1)}, u32[]{:S(2)}, u32[]{:S(2)}) collective-permute-start(bf16[2,64,128]{2,1,0:T(8,128)(2,1)S(1)} %shard_map.182.refs_0_), channel_id=1, source_target_pairs={{0,1},{1,0},{2,3},{3,2},{4,5},{5,4},{6,7},{7,6},{8,9},{9,8},{10,11... | collective-permute-start | bytes 98312 | tf_op jit(solution)/shard_map/ppermute | solution.py:498
  9.0 4.3 %collective-permute-start.3 = (bf16[240,128]{1,0:T(8,128)(2,1)S(1)}, bf16[240,128]{1,0:T(8,128)(2,1)S(1)}, u32[]{:S(2)}, u32[]{:S(2)}) collective-permute-start(bf16[240,128]{1,0:T(8,128)(2,1)S(1)} %get-tuple-element.28), channel_id=1, source_target_pairs={{0,4},{1,5},{4,0},{5,1},{8,9},{9,8},{12,13},{13,12},{2,6},{3,7},{6... | collective-permute-start | bytes 184328 | tf_op jit(solution)/shard_map/ppermute | solution.py:556
  10.6 2.6 %collective-permute-start.4 = (bf16[240,128]{1,0:T(8,128)(2,1)S(1)}, bf16[240,128]{1,0:T(8,128)(2,1)S(1)}, u32[]{:S(2)}, u32[]{:S(2)}) collective-permute-start(bf16[240,128]{1,0:T(8,128)(2,1)S(1)} %get-tuple-element.29), channel_id=1, source_target_pairs={{0,1},{1,0},{4,8},{5,9},{8,4},{9,5},{12,13},{13,12},{2,3},{3,2},{6... | collective-permute-start | bytes 184328 | tf_op jit(solution)/shard_map/ppermute | solution.py:556
  10.6 2.6 %collective-permute-start.5 = (bf16[240,128]{1,0:T(8,128)(2,1)S(1)}, bf16[240,128]{1,0:T(8,128)(2,1)S(1)}, u32[]{:S(2)}, u32[]{:S(2)}) collective-permute-start(bf16[240,128]{1,0:T(8,128)(2,1)S(1)} %get-tuple-element.30), channel_id=1, source_target_pairs={{0,1},{1,0},{4,5},{5,4},{8,12},{9,13},{12,8},{13,9},{2,3},{3,2},{6... | collective-permute-start | bytes 184328 | tf_op jit(solution)/shard_map/ppermute | solution.py:556

commit v17 on v16

--- a/solution.py
+++ b/solution.py
@@ -87,7 +87,7 @@
     w_pair_copy = pltpu.make_async_copy(w_pair_hbm, w_pair_ref, sem)
     w_pair_copy.start()
     for i in range(pieces):
-        pair_copy(i).start()
+        pair_copy(i).start(priority=i % 2)
     w_pair_copy.wait()
     w_pair = w_pair_ref[...].astype(F32)
     spread = jnp.concatenate(
@@ -127,25 +127,20 @@
     at_ref,
     single_ref,
     cond_ref,
-    ada_attn,
+    ada_attn_scale,
     ada_attn_shift,
-    ada_trans,
+    ada_trans_scale,
     ada_trans_shift,
-    attn_gate,
-    trans_gate,
     w_key,
     w_value,
     w_query,
     w_gate,
-    w_swish,
-    w_linear,
-    w_down,
     query_ref,
     key_ref,
     value_ref,
     gate_ref,
-    open_ref,
-    trans_ref,
+    cond_norm_ref,
+    trans_norm_ref,
     near_ref,
     far_ref,
 ):
@@ -154,27 +149,25 @@
     for start in range(0, atoms_here, step):
         at = slice(start, start + step)
         cond = layer_norm(cond_ref[at, :]).astype(BF16)
+        cond_norm_ref[at, :] = cond
         single = layer_norm(single_ref[:, at, :].reshape(-1, width))
         single = single.reshape(samples, step, width)
-        normed = attn_norm(cond, single, beside(ada_attn, ada_attn_shift))
+        normed = attn_norm(cond, single, beside(ada_attn_scale, ada_attn_shift))
         if start == 0:
             heads_of = [normed[sample, :EDGE] for sample in range(samples)]
         if start + step == atoms_here:
             tails_of = [normed[sample, step - EDGE :] for sample in range(samples)]
         normed = normed.reshape(-1, width)
-        both = dot(normed, beside(w_key, w_value)).astype(BF16).reshape(samples, step, 2 * width)
+        both = dot(normed, beside(w_key, w_value)).astype(BF16)
+        both = both.reshape(samples, step, 2 * width)
         key_ref[:, at, :] = both[:, :, :width]
         value_ref[:, at, :] = both[:, :, width:]
         both = dot(normed, beside(w_query, w_gate)).reshape(samples, step, 2 * width)
         query_ref[:, at, :] = both[:, :, :width].astype(BF16)
         gate_ref[:, at, :] = sigmoid(both[:, :, width:]).astype(BF16)
-        gates = dot(cond, beside(attn_gate, trans_gate))
-        open_ref[at, :] = sigmoid(gates[:, :width]).astype(BF16)
-        normed = attn_norm(cond, single, beside(ada_trans, ada_trans_shift)).reshape(-1, width)
-        swish = dot(normed, w_swish[...])
-        hidden = (swish * sigmoid(swish) * dot(normed, w_linear[...])).astype(BF16)
-        down = dot(hidden, w_down[...]).reshape(samples, step, width)
-        trans_ref[:, at, :] = (sigmoid(gates[:, width:])[None] * down).astype(BF16)
+        ada = beside(ada_trans_scale, ada_trans_shift)
+        trans_norm_ref[:, at, :] = attn_norm(cond, single, ada)
+
     even = at_ref[0] % 2 == 0
     for sample, (head, tail) in enumerate(zip(heads_of, tails_of)):
         cut = slice(sample * EDGE, (sample + 1) * EDGE)
@@ -182,15 +175,42 @@
         far_ref[cut, :] = jnp.where(even, head, tail)
 
 
+def transition_kernel(
+    cond_norm_ref,
+    trans_norm_ref,
+    attn_gate,
+    trans_gate,
+    w_swish,
+    w_linear,
+    w_down,
+    open_ref,
+    trans_ref,
+):
+    samples, atoms_here, width = trans_norm_ref.shape
+    step = math.gcd(atoms_here, 256)
+    for start in range(0, atoms_here, step):
+        at = slice(start, start + step)
+        gates = sigmoid(dot(cond_norm_ref[at, :], beside(attn_gate, trans_gate)))
+        open_ref[at, :] = gates[:, :width].astype(BF16)
+        normed = trans_norm_ref[:, at, :].reshape(-1, width)
+        swish = dot(normed, w_swish[...])
+        hidden = (swish * sigmoid(swish) * dot(normed, w_linear[...])).astype(BF16)
+        down = dot(hidden, w_down[...]).reshape(samples, step, width)
+        trans_ref[:, at, :] = (gates[None, :, width:] * down).astype(BF16)
+
+
+def gather_kernel(own_ref, across_ref, _, both_ref, __):
+    both_ref[0] = own_ref[...]
+    both_ref[1] = across_ref[...]
+
+
 def tile_of(refs, place, row_block):
     if len(refs) == 1:
         return refs[0][row_block]
     pair_at, core_at = place
     owners = 2
-    mine, theirs, across, diagonal = [ref[...] for ref in refs]
-    near = jnp.where(row_block % owners == core_at, mine, theirs)
-    far = jnp.where(row_block % owners == core_at, across, diagonal)
-    return jnp.where(row_block // owners == pair_at, near, far)
+    mine, theirs = [jnp.where(row_block // owners == pair_at, ref[0], ref[1]) for ref in refs]
+    return jnp.where(row_block % owners == core_at, mine, theirs)
 
 
 def select_kernel(blocks, at_ref, pair_ref, core_ref, *refs):
@@ -491,11 +511,9 @@
         compiler_params=params,
         cost_estimate=cost(tok_here * cols * width * width * 2),
     )(core_at, *map(in_hbm, (w_pair.T, pair_cond)))
+    swapped = [(0, 1), (1, 0)]
     if pairs == 2:
-        swapped = [(0, 1), (1, 0)]
         across = lax.ppermute(own, "pair", swapped)
-        diagonal = lax.ppermute(own, ("pair", "samp"), [(0, 3), (1, 2), (2, 1), (3, 0)])
-        tiles = (own, lax.ppermute(own, "samp", swapped), across, diagonal)
     else:
         tiles = (lax.all_gather(own, ("pair", "samp")),)
 
@@ -506,25 +524,42 @@
         ada_attn_shift,
         ada_trans_scale,
         ada_trans_shift,
-        attn_gate,
-        trans_gate,
         w_key,
         w_value,
         w_query,
         w_gate,
-        w_swish,
-        w_linear,
-        w_down,
     )
-    query, keys, values, gate, opened, trans, near, far = pl.pallas_call(
+    query, keys, values, gate, cond_norm, trans_norm, near, far = pl.pallas_call(
         project_kernel,
         in_specs=[IN_SMEM] + [IN_VMEM] * len(operands),
         out_specs=[IN_VMEM] * 8,
         out_shape=[pltpu.VMEM(wide, BF16)] * 4
         + [pltpu.VMEM((atoms_here, width), BF16), pltpu.VMEM(wide, BF16), sent, sent],
         compiler_params=params,
-        cost_estimate=cost(samples * atoms_here * width * width * 20),
+        cost_estimate=cost(samples * atoms_here * width * width * 10),
     )(at, *map(in_vmem, operands))
+
+    if pairs == 2:
+        operands = (own, across, trans_norm)
+        both, trans_norm = pl.pallas_call(
+            gather_kernel,
+            in_specs=[IN_VMEM] * 3,
+            out_specs=[IN_VMEM] * 2,
+            out_shape=[pltpu.VMEM((2, groups, cols, lanes), BF16), pltpu.VMEM(wide, BF16)],
+            input_output_aliases={2: 1},
+            compiler_params=params,
+        )(*map(in_vmem, operands))
+        tiles = (both, lax.ppermute(both, "samp", swapped))
+
+    operands = (cond_norm, trans_norm, attn_gate, trans_gate, w_swish, w_linear, w_down)
+    opened, trans = pl.pallas_call(
+        transition_kernel,
+        in_specs=[IN_VMEM] * len(operands),
+        out_specs=[IN_VMEM] * 2,
+        out_shape=[pltpu.VMEM((atoms_here, width), BF16), pltpu.VMEM(wide, BF16)],
+        compiler_params=params,
+        cost_estimate=cost(samples * atoms_here * width * width * 10),
+    )(*map(in_vmem, operands))
 
     operands = (*tiles, near, far, opened)
     first = 3 + len(tiles)

time: 15.4 us -> 15.7 us (1.019)
  starting transfers between devices: 5.29 us -> 5.7 us
  waiting for transfers between devices: 0.81 us -> 0.64 us
    ppermute x2 -> x1, starting transfers between devices: 2.5 us -> 0.01 us  [shards(): tiles = (both, lax.ppermute(both, 'samp', swapped))]
    ppermute x1, starting transfers between devices: 0.64 us -> 3.02 us  [shards(): across = lax.ppermute(own, 'pair', swapped)]
    pallas_call x1, Pallas kernels: 2.37 us -> 1.39 us  [shards(): pl.pallas_call(project_kernel, in_specs=[IN_SMEM] + [IN_VMEM] * len(opera...]
    pallas_call x0 -> x2, Pallas kernels: none -> 0.96 us  [the longest x1 0.96 us: shards(): pl.pallas_call(transition_kernel, in_specs=[IN_VMEM] * len(operands), out...]
    ppermute x3, starting transfers between devices: 2.15 us -> 2.68 us  [swap(): return lax.ppermute(value, ('atoms', 'samp'), sides)]
    ppermute x1, waiting for transfers between devices: 0.78 us -> 0.4 us  [shards(): across = lax.ppermute(own, 'pair', swapped)]
    ppermute x2 -> x1, waiting for transfers between devices: 0.01 us -> 0.23 us  [shards(): tiles = (both, lax.ppermute(both, 'samp', swapped))]
  transfers between devices with their start and end apart: 6 -> 5, of which waited for: 1 -> 2; matrix products, arithmetic and copies ran while one was open for 0% -> 0% of each run, Pallas kernels for 29% -> 28%
where the time goes in v17:
time: 15.7 us; the launch traced here: 15.6 us
  Pallas kernels  8.91 us (57%)
  starting transfers between devices  5.7 us (36%)
  waiting for transfers between devices  0.64 us (4%)
  between operations  0.27 us (2%)
    ppermute x1, starting transfers between devices, shards(): across = lax.ppermute(own, 'pair', swapped)  3.02 us
    ppermute x3, starting transfers between devices, swap(): return lax.ppermute(value, ('atoms', 'samp'), sides)  2.68 us
    pallas_call x1, Pallas kernels, shards(): pl.pallas_call(pair_kernel, in_specs=[IN_SMEM] + [IN_HBM] * 2, out_specs=...  2.42 us
    pallas_call x1, Pallas kernels, shards(): pl.pallas_call(functools.partial(inner_kernel, heads), in_specs=[IN_SMEM]...  2.09 us
    pallas_call x1, Pallas kernels, shards(): pl.pallas_call(functools.partial(outer_kernel, heads, blocks), in_specs=[...  2 us
    pallas_call x1, Pallas kernels, shards(): pl.pallas_call(project_kernel, in_specs=[IN_SMEM] + [IN_VMEM] * len(opera...  1.39 us
    pallas_call x1, Pallas kernels, shards(): pl.pallas_call(transition_kernel, in_specs=[IN_VMEM] * len(operands), out...  0.96 us
    ppermute x1, waiting for transfers between devices, shards(): across = lax.ppermute(own, 'pair', swapped)  0.4 us
  transfers between devices with their start and end apart: 5, of which 2 were waited for; matrix products, arithmetic and copies ran while one was open for 0% of the time, Pallas kernels for 28%

profile of v17, /device:TPU:0, one launch (start us, length us, event | category | flops | bytes accessed | tf_op | source)
XLA Modules:
  0.0 15.6 jit_solution(17505188545913396001)
XLA Ops:
  0.0 0.0 copy-start.2
  0.0 0.0 copy-start.1
  0.0 0.0 copy-start.12
  0.0 0.0 copy-start.13
  0.0 0.0 copy-start.10
  0.0 0.0 copy-start.9
  0.0 0.0 copy-start.5
  0.1 0.0 copy-start.4
  0.1 0.0 copy-start.6
  0.1 0.0 copy-start.7
  0.1 0.0 copy-start.8
  0.1 0.0 copy-start.15
  0.1 0.0 copy-start.16
  0.1 2.4 %shard_map.182.own_ref = bf16[2,64,128]{2,1,0:T(8,128)(2,1)S(1)} custom-call(s32[1]{0:T(128)} %bitcast.2.core_ref, bf16[4,128]{1,0:T(4,128)(2,1)} %bitcast.4, bf16[128,64,128]{2,1,0:T(8,128)(2,1)} %pair_hbm.1), custom_call_target="tpu_custom_call" | custom-call | flops 268435456 | bytes 4194304 | tf_op jit(solution)/shard_map/pallas_call | solution.py:500
  2.5 3.0 %collective-permute-start = (bf16[2,64,128]{2,1,0:T(8,128)(2,1)S(1)}, bf16[2,64,128]{2,1,0:T(8,128)(2,1)S(1)}, u32[]{:S(2)}, u32[]{:S(2)}) collective-permute-start(bf16[2,64,128]{2,1,0:T(8,128)(2,1)S(1)} %shard_map.182.own_ref), channel_id=1, source_target_pairs={{0,2},{2,0},{1,3},{3,1},{4,6},{6,4},{5,7},{7,5},{8,10},{10,8},{9,1... | collective-permute-start | bytes 98312 | tf_op jit(solution)/shard_map/ppermute | solution.py:516
  5.6 0.0 copy-done.2
  5.6 0.0 copy-done.1
  5.6 0.0 copy-done.12
  5.6 0.0 copy-done.11
  5.6 0.0 copy-done.14
  5.6 0.0 copy-done.13
  5.6 0.0 copy-done.10
  5.6 0.0 copy-done.9
  5.6 0.0 copy-done.5
  5.6 0.0 copy-done.4
  5.6 0.0 copy-start
  5.6 0.0 copy-start.3
  5.7 1.4 %shard_map.181 = (bf16[3,512,128]{2,1,0:T(8,128)(2,1)S(1)}, bf16[3,512,128]{2,1,0:T(8,128)(2,1)S(1)}, bf16[3,512,128]{2,1,0:T(8,128)(2,1)S(1)}, bf16[3,512,128]{...) custom-call(s32[1]{0:T(128)} %bitcast.at_ref, ...), custom_call_target="tpu_custom_call" | custom-call | flops 503316480 | bytes 4194304 | tf_op jit(solution)/shard_map/pallas_call | solution.py:532
  7.0 0.4 %collective-permute-done.across_ref = bf16[2,64,128]{2,1,0:T(8,128)(2,1)S(1)} collective-permute-done((bf16[2,64,128]{2,1,0:T(8,128)(2,1)S(1)}, bf16[2,64,128]{2,1,0:T(8,128)(2,1)S(1)}, u32[]{:S(2)}, u32[]{:S(2)}) %collective-permute-start) | collective-permute-done | bytes 32800 | tf_op jit(solution)/shard_map/ppermute | solution.py:516
  7.5 0.0 collective-permute-start.1
  7.5 0.0 copy-done.6
  7.5 0.0 copy-done.7
  7.5 0.0 copy-done.8
  7.5 0.0 copy-done.15
  7.5 0.0 copy-done.16
  7.5 1.0 %shard_map.184 = (bf16[512,128]{1,0:T(8,128)(2,1)S(1)}, bf16[3,512,128]{2,1,0:T(8,128)(2,1)S(1)}) custom-call(bf16[512,128]{1,0:T(8,128)(2,1)S(1)} %get-tuple-element.30.cond_norm_ref, bf16[3,512,128]{2,1,0:T(8,128)(2,1)S(1)} %get-tuple-element.31.trans_norm_ref, bf16[128,128]{1,0:T(8,128)(2,1)S(1)} %copy-done.15, bf16[128,128]{1,0:T(8,128)(2,1)S(1)} %copy-done.16, ...), custom_call_target="tpu_custom_call" | custom-call | flops 503316480 | bytes 4194304 | tf_op jit(solution)/shard_map/pallas_call | solution.py:555
  8.5 0.2 %collective-permute-done.1.refs_1_ = bf16[2,2,64,128]{3,2,1,0:T(8,128)(2,1)S(1)} collective-permute-done((bf16[2,2,64,128]{3,2,1,0:T(8,128)(2,1)S(1)}, bf16[2,2,64,128]{3,2,1,0:T(8,128)(2,1)S(1)}, u32[]{:S(2)}, u32[]{:S(2)}) %collective-permute-start.1) | collective-permute-done | bytes 65568 | tf_op jit(solution)/shard_map/ppermute | solution.py:552
  8.7 0.1 shard_map.185
  8.8 2.2 %collective-permute-start.2 = (bf16[240,128]{1,0:T(8,128)(2,1)S(1)}, bf16[240,128]{1,0:T(8,128)(2,1)S(1)}, u32[]{:S(2)}, u32[]{:S(2)}) collective-permute-start(bf16[240,128]{1,0:T(8,128)(2,1)S(1)} %get-tuple-element.36), channel_id=1, source_target_pairs={{0,4},{1,5},{4,0},{5,1},{8,9},{9,8},{12,13},{13,12},{2,6},{3,7},{6... | collective-permute-start | bytes 184328 | tf_op jit(solution)/shard_map/ppermute | solution.py:591
  10.9 0.0 collective-permute-start.3
  10.9 0.5 %collective-permute-start.4 = (bf16[240,128]{1,0:T(8,128)(2,1)S(1)}, bf16[240,128]{1,0:T(8,128)(2,1)S(1)}, u32[]{:S(2)}, u32[]{:S(2)}) collective-permute-start(bf16[240,128]{1,0:T(8,128)(2,1)S(1)} %get-tuple-element.38), channel_id=1, source_target_pairs={{0,1},{1,0},{4,5},{5,4},{8,12},{9,13},{12,8},{13,9},{2,3},{3,2},{6... | collective-permute-start | bytes 184328 | tf_op jit(solution)/shard_map/ppermute | solution.py:591
  11.5 0.0 copy-done
  11.5 0.0 copy-done.3
  11.5 2.1 %shard_map.186.inner_ref = bf16[3,384,128]{2,1,0:T(8,128)(2,1)S(1)} custom-call(s32[1]{0:T(128)} %bitcast.at_ref, s32[4,64]{1,0:T(4,128)S(1)} %copy-done.3, bf16[3,512,128]{2,1,0:T(8,128)(2,1)S(1)} %get-tuple-element.22.query_ref, bf16[3,512,128]{2,1,0:T(8,128)(2,1)S(1)} %get-tuple-element.23.key_ref.own_key_ref, ...), custom_call_target="tpu_custom_call" | custom-call | flops 603979776 | bytes 4194304 | tf_op jit(solution)/shard_map/pallas_call | solution.py:597
  13.6 0.0 collective-permute-done.2.early_ref
  13.6 0.0 collective-permute-done.3.second_ref
  13.6 0.0 collective-permute-done.4.late_ref
  13.6 2.0 %shard_map.187 = bf16[3,512,128]{2,1,0:T(8,128)(2,1)} custom-call(s32[1]{0:T(128)} %bitcast.at_ref, s32[4,64]{1,0:T(4,128)S(1)} %copy-done.3, bf16[3,512,128]{2,1,0:T(8,128)(2,1)S(1)} %get-tuple-element.22.query_ref, bf16[3,512,128]{2,1,0:T(8,128)(2,1)S(1)} %get-tuple-element.23.key_ref.own_key_ref, ...), custom_call_target="tpu_custom_call" | custom-call | flops 201326592 | bytes 4194304 | tf_op jit(solution)/shard_map/pallas_call | solution.py:612
  (3 shorter events, 0.0 us)
Async XLA Ops:
  0.0 5.6 %copy-start.2 = (bf16[128,128]{1,0:T(8,128)(2,1)S(1)}, bf16[128,128]{1,0:T(8,128)(2,1)}, u32[]{:S(2)}) copy-start(bf16[128,128]{1,0:T(8,128)(2,1)} %w_value.3) | copy-start | bytes 98308
  0.0 5.6 %copy-start.1 = (bf16[128,128]{1,0:T(8,128)(2,1)S(1)}, bf16[128,128]{1,0:T(8,128)(2,1)}, u32[]{:S(2)}) copy-start(bf16[128,128]{1,0:T(8,128)(2,1)} %w_key.3) | copy-start | bytes 98308
  0.0 5.6 %copy-start.12 = (bf16[128,128]{1,0:T(8,128)(2,1)S(1)}, bf16[128,128]{1,0:T(8,128)(2,1)}, u32[]{:S(2)}) copy-start(bf16[128,128]{1,0:T(8,128)(2,1)} %ada_trans_shift.1) | copy-start | bytes 98308
  0.0 5.6 %copy-start.11 = (bf16[128,128]{1,0:T(8,128)(2,1)S(1)}, bf16[128,128]{1,0:T(8,128)(2,1)}, u32[]{:S(2)}) copy-start(bf16[128,128]{1,0:T(8,128)(2,1)} %ada_trans_scale.1) | copy-start | bytes 98308
  0.0 5.6 %copy-start.14 = (bf16[128,128]{1,0:T(8,128)(2,1)S(1)}, bf16[128,128]{1,0:T(8,128)(2,1)}, u32[]{:S(2)}) copy-start(bf16[128,128]{1,0:T(8,128)(2,1)} %w_gate.1) | copy-start | bytes 98308
  0.0 5.6 %copy-start.13 = (bf16[128,128]{1,0:T(8,128)(2,1)S(1)}, bf16[128,128]{1,0:T(8,128)(2,1)}, u32[]{:S(2)}) copy-start(bf16[128,128]{1,0:T(8,128)(2,1)} %w_query.1) | copy-start | bytes 98308
  0.0 5.6 %copy-start.10 = (bf16[128,128]{1,0:T(8,128)(2,1)S(1)}, bf16[128,128]{1,0:T(8,128)(2,1)}, u32[]{:S(2)}) copy-start(bf16[128,128]{1,0:T(8,128)(2,1)} %ada_attn_shift.1) | copy-start | bytes 98308
  0.0 5.6 %copy-start.9 = (bf16[128,128]{1,0:T(8,128)(2,1)S(1)}, bf16[128,128]{1,0:T(8,128)(2,1)}, u32[]{:S(2)}) copy-start(bf16[128,128]{1,0:T(8,128)(2,1)} %ada_attn_scale.1) | copy-start | bytes 98308
  0.0 5.6 %copy-start.5 = (bf16[512,128]{1,0:T(8,128)(2,1)S(1)}, bf16[512,128]{1,0:T(8,128)(2,1)}, u32[]{:S(2)}) copy-start(bf16[512,128]{1,0:T(8,128)(2,1)} %cond_ref.1) | copy-start | bytes 393220
  0.1 5.6 %copy-start.4 = (bf16[3,512,128]{2,1,0:T(8,128)(2,1)S(1)}, bf16[3,512,128]{2,1,0:T(8,128)(2,1)}, u32[]{:S(2)}) copy-start(bf16[3,512,128]{2,1,0:T(8,128)(2,1)} %single_ref.1) | copy-start | bytes 1179652
  0.1 7.4 %copy-start.6 = (bf16[128,256]{1,0:T(8,128)(2,1)S(1)}, bf16[128,256]{1,0:T(8,128)(2,1)}, u32[]{:S(2)}) copy-start(bf16[128,256]{1,0:T(8,128)(2,1)} %w_swish.1) | copy-start | bytes 196612
  0.1 7.4 %copy-start.7 = (bf16[128,256]{1,0:T(8,128)(2,1)S(1)}, bf16[128,256]{1,0:T(8,128)(2,1)}, u32[]{:S(2)}) copy-start(bf16[128,256]{1,0:T(8,128)(2,1)} %w_linear.1) | copy-start | bytes 196612
  0.1 7.4 %copy-start.8 = (bf16[256,128]{1,0:T(8,128)(2,1)S(1)}, bf16[256,128]{1,0:T(8,128)(2,1)}, u32[]{:S(2)}) copy-start(bf16[256,128]{1,0:T(8,128)(2,1)} %w_down.1) | copy-start | bytes 196612
  0.1 7.4 %copy-start.15 = (bf16[128,128]{1,0:T(8,128)(2,1)S(1)}, bf16[128,128]{1,0:T(8,128)(2,1)}, u32[]{:S(2)}) copy-start(bf16[128,128]{1,0:T(8,128)(2,1)} %attn_gate.1) | copy-start | bytes 98308
  0.1 7.4 %copy-start.16 = (bf16[128,128]{1,0:T(8,128)(2,1)S(1)}, bf16[128,128]{1,0:T(8,128)(2,1)}, u32[]{:S(2)}) copy-start(bf16[128,128]{1,0:T(8,128)(2,1)} %trans_gate.1) | copy-start | bytes 98308
  2.5 4.9 %collective-permute-start = (bf16[2,64,128]{2,1,0:T(8,128)(2,1)S(1)}, bf16[2,64,128]{2,1,0:T(8,128)(2,1)S(1)}, u32[]{:S(2)}, u32[]{:S(2)}) collective-permute-start(bf16[2,64,128]{2,1,0:T(8,128)(2,1)S(1)} %shard_map.182.own_ref), channel_id=1, source_target_pairs={{0,2},{2,0},{1,3},{3,1},{4,6},{6,4},{5,7},{7,5},{8,10},{10,8},{9,1... | collective-permute-start | bytes 98312 | tf_op jit(solution)/shard_map/ppermute | solution.py:516
  5.6 5.8 %copy-start = (bf16[128,128]{1,0:T(8,128)(2,1)S(1)}, bf16[128,128]{1,0:T(8,128)(2,1)}, u32[]{:S(2)}) copy-start(bf16[128,128]{1,0:T(8,128)(2,1)} %w_out_ref.3) | copy-start | bytes 98308
  5.6 5.8 %copy-start.3 = (s32[4,64]{1,0:T(4,128)S(1)}, s32[4,64]{1,0:T(4,128)}, u32[]{:S(2)}) copy-start(s32[4,64]{1,0:T(4,128)} %counts_ref.3) | copy-start | bytes 3076
  7.5 1.3 %collective-permute-start.1 = (bf16[2,2,64,128]{3,2,1,0:T(8,128)(2,1)S(1)}, bf16[2,2,64,128]{3,2,1,0:T(8,128)(2,1)S(1)}, u32[]{:S(2)}, u32[]{:S(2)}) collective-permute-start(bf16[2,2,64,128]{3,2,1,0:T(8,128)(2,1)S(1)} %get-tuple-element.27.refs_0_), channel_id=1, source_target_pairs={{0,1},{1,0},{2,3},{3,2},{4,5},{5,4},{6,7},{7,6},{8,9},{9,8},{10,11... | collective-permute-start | bytes 196616 | tf_op jit(solution)/shard_map/ppermute | solution.py:552
  8.8 4.8 %collective-permute-start.2 = (bf16[240,128]{1,0:T(8,128)(2,1)S(1)}, bf16[240,128]{1,0:T(8,128)(2,1)S(1)}, u32[]{:S(2)}, u32[]{:S(2)}) collective-permute-start(bf16[240,128]{1,0:T(8,128)(2,1)S(1)} %get-tuple-element.36), channel_id=1, source_target_pairs={{0,4},{1,5},{4,0},{5,1},{8,9},{9,8},{12,13},{13,12},{2,6},{3,7},{6... | collective-permute-start | bytes 184328 | tf_op jit(solution)/shard_map/ppermute | solution.py:591
  10.9 2.6 %collective-permute-start.3 = (bf16[240,128]{1,0:T(8,128)(2,1)S(1)}, bf16[240,128]{1,0:T(8,128)(2,1)S(1)}, u32[]{:S(2)}, u32[]{:S(2)}) collective-permute-start(bf16[240,128]{1,0:T(8,128)(2,1)S(1)} %get-tuple-element.37), channel_id=1, source_target_pairs={{0,1},{1,0},{4,8},{5,9},{8,4},{9,5},{12,13},{13,12},{2,3},{3,2},{6... | collective-permute-start | bytes 184328 | tf_op jit(solution)/shard_map/ppermute | solution.py:591
  10.9 2.6 %collective-permute-start.4 = (bf16[240,128]{1,0:T(8,128)(2,1)S(1)}, bf16[240,128]{1,0:T(8,128)(2,1)S(1)}, u32[]{:S(2)}, u32[]{:S(2)}) collective-permute-start(bf16[240,128]{1,0:T(8,128)(2,1)S(1)} %get-tuple-element.38), channel_id=1, source_target_pairs={{0,1},{1,0},{4,5},{5,4},{8,12},{9,13},{12,8},{13,9},{2,3},{3,2},{6... | collective-permute-start | bytes 184328 | tf_op jit(solution)/shard_map/ppermute | solution.py:591

commit v18 on v16

--- a/solution.py
+++ b/solution.py
@@ -97,14 +97,14 @@
     centre = twice(centring(width))
     slot = iota((cols, lanes), 1) % group
 
-    @pl.loop(0, rows // group)
-    def _(chunk):
+    chunks = []
+    for chunk in range(rows // group):
         for part in range(2):
             pair_copy(chunk * 2 + part).wait()
-
-        pair = pair_ref[pl.ds(chunk * group, group)].reshape(group * cols, width)
-        centred = dot(side_by_side(pair), centre)
-        mixed = dot(centred.astype(BF16), mix).reshape(half, cols, 2 * lanes)
+        pair = pair_ref[chunk * group : (chunk + 1) * group].reshape(group * cols, width)
+        chunks.append(dot(side_by_side(pair), centre))
+    mixes = [dot(centred.astype(BF16), mix).reshape(half, cols, 2 * lanes) for centred in chunks]
+    for chunk, (centred, mixed) in enumerate(zip(chunks, mixes)):
         variances = [
             mean_square(centred[:, part * width : (part + 1) * width]).reshape(half, cols, 1)
             for part in range(2)
@@ -115,8 +115,7 @@
             side = slice(i // half * lanes, (i // half + 1) * lanes)
             total = jnp.where(slot == i, mixed[i % half, :, side], total)
             spread_out = jnp.where(slot == i, variances[i // half][i % half], spread_out)
-        bias = (total * lax.rsqrt(spread_out + EPSILON)).astype(BF16)
-        tile_ref[chunk] = bias
+        tile_ref[chunk] = (total * lax.rsqrt(spread_out + EPSILON)).astype(BF16)
 
 
 def beside(first, second):
@@ -150,7 +149,7 @@
     far_ref,
 ):
     samples, atoms_here, width = single_ref.shape
-    step = math.gcd(atoms_here, 256)
+    step = math.gcd(atoms_here, 512)
     for start in range(0, atoms_here, step):
         at = slice(start, start + step)
         cond = layer_norm(cond_ref[at, :]).astype(BF16)
@@ -194,7 +193,7 @@
 
 
 def select_kernel(blocks, at_ref, pair_ref, core_ref, *refs):
-    *tile_refs, _, __, ___, near_ref, far_ref, ____, held_ref, again_ref = refs
+    *tile_refs, _, __, ___, near_ref, far_ref, ____, held_ref = refs
     groups, cols, lanes = tile_refs[0].shape[-3:]
     rows = groups * EDGE
     device_at, place = at_ref[0], (pair_ref[0], core_ref[0])
@@ -204,7 +203,6 @@
         tile = tile_of(tile_refs, place, jnp.clip(beside, 0, blocks - 1))
         tile = jnp.where(above, tile[:, cols - EDGE :], tile[:, :EDGE])
         send_ref[send_ref.shape[0] - rows :, :] = tile.reshape(rows, lanes)
-    again_ref[...] = near_ref[...]
     held_ref[...] = tile_of(tile_refs, place, device_at).reshape(groups * cols, lanes)
 
 
@@ -355,9 +353,8 @@
     inner_ref,
     w_key,
     w_value,
-    early_ref,
+    first_ref,
     second_ref,
-    late_ref,
     out_hbm,
     key_ref,
     value_ref,
@@ -381,8 +378,7 @@
     whole.start()
 
     even = device_at % 2 == 0
-    first = jnp.where(device_at % 4 < 2, early_ref[...], late_ref[...])
-    second = second_ref[...]
+    first, second = first_ref[...], second_ref[...]
     arrived = (jnp.where(even, second, first), jnp.where(even, first, second))
     count = samples * EDGE
     edges = jnp.concatenate([rows[:count] for rows in arrived], 0)
@@ -528,25 +524,24 @@
 
     operands = (*tiles, near, far, opened)
     first = 3 + len(tiles)
-    near, far, opened, held, again = pl.pallas_call(
+    near, far, opened, held = pl.pallas_call(
         functools.partial(select_kernel, blocks),
         in_specs=[IN_SMEM] * 3 + [IN_VMEM] * len(operands),
-        out_specs=[IN_VMEM] * 5,
+        out_specs=[IN_VMEM] * 4,
         out_shape=[
             sent,
             sent,
             pltpu.VMEM((atoms_here, width), BF16),
             pltpu.VMEM((groups * cols, lanes), BF16),
-            sent,
         ],
         input_output_aliases={first: 0, first + 1: 1, first + 2: 2},
         compiler_params=params,
     )(at, pair_at, core_at, *map(in_vmem, operands))
 
-    def swap(value, start, step):
+    def swap(value, start):
         cores = lax.axis_size("samp")
         other_of = {}
-        for i in range(start, blocks - 1, step):
+        for i in range(start, blocks - 1, 2):
             other_of[i], other_of[i + 1] = i + 1, i
         sides = []
         for i in range(blocks):
@@ -555,7 +550,7 @@
                 sides.append((i * cores + core, target[0] * cores + target[1]))
         return lax.ppermute(value, ("atoms", "samp"), sides)
 
-    early, second, later = swap(near, 0, 4), swap(far, 1, 2), swap(again, 2, 4)
+    first, second = swap(near, 0), swap(far, 1)
 
     margin = -(-EDGE // Q_WIN) * Q_WIN
     operands = (query, keys, values, gate, opened, trans, w_out, held)
@@ -573,7 +568,7 @@
     )(at, atom_counts, *map(in_vmem, operands))
 
     reach = margin - Q_WIN + K_WIN
-    operands += (inner, w_key, w_value, early, second, later)
+    operands += (inner, w_key, w_value, first, second)
     return pl.pallas_call(
         functools.partial(outer_kernel, heads, blocks),
         in_specs=[IN_SMEM] + [IN_VMEM] * (1 + len(operands)),

time: 15.4 us -> 15.6 us (1.013); the launches traced: 15.3 us -> 15.3 us
  waiting for transfers between devices: 0.81 us -> 1.51 us
  starting transfers between devices: 5.29 us -> 4.78 us
    ppermute x3 -> x2, starting transfers between devices: 2.15 us -> 1.64 us  [swap(): return lax.ppermute(value, ('atoms', 'samp'), sides)]
    ppermute x3 -> x2, waiting for transfers between devices: 0.03 us -> 0.53 us  [swap(): return lax.ppermute(value, ('atoms', 'samp'), sides)]
    pallas_call x1, Pallas kernels: 2.37 us -> 2.17 us  [shards(): pl.pallas_call(project_kernel, in_specs=[IN_SMEM] + [IN_VMEM] * len(opera...]
    ppermute x1, waiting for transfers between devices: 0.78 us -> 0.98 us  [shards(): across = lax.ppermute(own, 'pair', swapped)]
  transfers between devices with their start and end apart: 6 -> 5, of which waited for: 1 -> 2; matrix products, arithmetic and copies ran while one was open for 0% -> 0% of each run, Pallas kernels for 29% -> 28%
where the time goes in v18:
time: 15.6 us; the launch traced here: 15.3 us
  Pallas kernels  8.72 us (56%)
  starting transfers between devices  4.78 us (31%)
  waiting for transfers between devices  1.51 us (10%)
  between operations  0.24 us (2%)
    ppermute x1, starting transfers between devices, shards(): lax.ppermute(own, ('pair', 'samp'), [(0, 3), (1, 2), (2, 1), (3, 0)])  2.46 us
    pallas_call x1, Pallas kernels, shards(): pl.pallas_call(pair_kernel, in_specs=[IN_SMEM] + [IN_HBM] * 2, out_specs=...  2.4 us
    pallas_call x1, Pallas kernels, shards(): pl.pallas_call(project_kernel, in_specs=[IN_SMEM] + [IN_VMEM] * len(opera...  2.17 us
    pallas_call x1, Pallas kernels, shards(): pl.pallas_call(functools.partial(inner_kernel, heads), in_specs=[IN_SMEM]...  2.11 us
    pallas_call x1, Pallas kernels, shards(): pl.pallas_call(functools.partial(outer_kernel, heads, blocks), in_specs=[...  2 us
    ppermute x2, starting transfers between devices, swap(): return lax.ppermute(value, ('atoms', 'samp'), sides)  1.64 us
    ppermute x1, waiting for transfers between devices, shards(): across = lax.ppermute(own, 'pair', swapped)  0.98 us
    ppermute x1, starting transfers between devices, shards(): across = lax.ppermute(own, 'pair', swapped)  0.64 us
  transfers between devices with their start and end apart: 5, of which 2 were waited for; matrix products, arithmetic and copies ran while one was open for 0% of the time, Pallas kernels for 28%

profile of v18, /device:TPU:0, one launch (start us, length us, event | category | flops | bytes accessed | tf_op | source)
XLA Modules:
  0.0 15.3 jit_solution(14976685682693005667)
XLA Ops:
  0.0 0.0 copy-start.2
  0.0 0.0 copy-start.1
  0.0 0.0 copy-start.14
  0.0 0.0 copy-start.8
  0.0 0.0 copy-start.7
  0.0 0.0 copy-start.6
  0.0 0.0 copy-start.12
  0.0 0.0 copy-start.11
  0.0 0.0 copy-start.13
  0.1 0.0 copy-start.16
  0.1 0.0 copy-start.15
  0.1 0.0 copy-start.10
  0.1 0.0 copy-start.9
  0.1 0.0 copy-start.5
  0.1 0.0 copy-start.4
  0.1 2.4 %shard_map.182.refs_0_ = bf16[2,64,128]{2,1,0:T(8,128)(2,1)S(1)} custom-call(s32[1]{0:T(128)} %bitcast.2.core_ref, bf16[4,128]{1,0:T(4,128)(2,1)} %bitcast.4, bf16[128,64,128]{2,1,0:T(8,128)(2,1)} %pair_hbm.1), custom_call_target="tpu_custom_call" | custom-call | flops 268435456 | bytes 4194304 | tf_op jit(solution)/shard_map/pallas_call | solution.py:476
  2.5 0.0 copy-start
  2.5 0.0 copy-start.3
  2.6 2.5 %collective-permute-start.2 = (bf16[2,64,128]{2,1,0:T(8,128)(2,1)S(1)}, bf16[2,64,128]{2,1,0:T(8,128)(2,1)S(1)}, u32[]{:S(2)}, u32[]{:S(2)}) collective-permute-start(bf16[2,64,128]{2,1,0:T(8,128)(2,1)S(1)} %shard_map.182.refs_0_), channel_id=1, source_target_pairs={{0,3},{1,2},{2,1},{3,0},{4,7},{5,6},{6,5},{7,4},{8,11},{9,10},{10,... | collective-permute-start | bytes 98312 | tf_op jit(solution)/shard_map/ppermute | solution.py:493
  5.0 0.6 %collective-permute-start.1 = (bf16[2,64,128]{2,1,0:T(8,128)(2,1)S(1)}, bf16[2,64,128]{2,1,0:T(8,128)(2,1)S(1)}, u32[]{:S(2)}, u32[]{:S(2)}) collective-permute-start(bf16[2,64,128]{2,1,0:T(8,128)(2,1)S(1)} %shard_map.182.refs_0_), channel_id=1, source_target_pairs={{0,2},{2,0},{1,3},{3,1},{4,6},{6,4},{5,7},{7,5},{8,10},{10,8},{9,1... | collective-permute-start | bytes 98312 | tf_op jit(solution)/shard_map/ppermute | solution.py:492
  5.7 0.0 collective-permute-start
  5.7 0.0 copy-done.2
  5.7 0.0 copy-done.1
  5.7 0.0 copy-done.14
  5.7 0.0 copy-done.8
  5.7 0.0 copy-done.7
  5.7 0.0 copy-done.6
  5.7 0.0 copy-done.12
  5.7 0.0 copy-done.11
  5.7 0.0 copy-done.13
  5.8 0.0 copy-done.16
  5.8 0.0 copy-done.15
  5.8 0.0 copy-done.10
  5.8 0.0 copy-done.9
  5.8 0.0 copy-done.5
  5.8 0.0 copy-done.4
  5.8 2.2 %shard_map.181 = (bf16[3,512,128]{2,1,0:T(8,128)(2,1)S(1)}, bf16[3,512,128]{2,1,0:T(8,128)(2,1)S(1)}, bf16[3,512,128]{2,1,0:T(8,128)(2,1)S(1)}, bf16[3,512,128]{...) custom-call(s32[1]{0:T(128)} %bitcast.at_ref, ...), custom_call_target="tpu_custom_call" | custom-call | flops 1006632960 | bytes 4194304 | tf_op jit(solution)/shard_map/pallas_call | solution.py:515
  8.0 0.0 collective-permute-done.2.refs_3_
  8.0 1.0 %collective-permute-done.1.refs_2_ = bf16[2,64,128]{2,1,0:T(8,128)(2,1)S(1)} collective-permute-done((bf16[2,64,128]{2,1,0:T(8,128)(2,1)S(1)}, bf16[2,64,128]{2,1,0:T(8,128)(2,1)S(1)}, u32[]{:S(2)}, u32[]{:S(2)}) %collective-permute-start.1) | collective-permute-done | bytes 32800 | tf_op jit(solution)/shard_map/ppermute | solution.py:492
  9.0 0.0 collective-permute-done.refs_1_
  9.0 1.6 %collective-permute-start.3 = (bf16[240,128]{1,0:T(8,128)(2,1)S(1)}, bf16[240,128]{1,0:T(8,128)(2,1)S(1)}, u32[]{:S(2)}, u32[]{:S(2)}) collective-permute-start(bf16[240,128]{1,0:T(8,128)(2,1)S(1)} %get-tuple-element.27), channel_id=1, source_target_pairs={{0,4},{1,5},{4,0},{5,1},{8,12},{9,13},{12,8},{13,9},{2,6},{3,7},{6... | collective-permute-start | bytes 184328 | tf_op jit(solution)/shard_map/ppermute | solution.py:551
  10.7 0.0 collective-permute-start.4
  10.7 0.0 copy-done
  10.7 0.0 copy-done.3
  10.7 2.1 %shard_map.184.inner_ref = bf16[3,384,128]{2,1,0:T(8,128)(2,1)S(1)} custom-call(s32[1]{0:T(128)} %bitcast.at_ref, s32[4,64]{1,0:T(4,128)S(1)} %copy-done.3, bf16[3,512,128]{2,1,0:T(8,128)(2,1)S(1)} %get-tuple-element.17.query_ref, bf16[3,512,128]{2,1,0:T(8,128)(2,1)S(1)} %get-tuple-element.18.key_ref.own_key_ref, ...), custom_call_target="tpu_custom_call" | custom-call | flops 603979776 | bytes 4194304 | tf_op jit(solution)/shard_map/pallas_call | solution.py:557
  12.8 0.5 %collective-permute-done.3.first_ref = bf16[240,128]{1,0:T(8,128)(2,1)S(1)} collective-permute-done((bf16[240,128]{1,0:T(8,128)(2,1)S(1)}, bf16[240,128]{1,0:T(8,128)(2,1)S(1)}, u32[]{:S(2)}, u32[]{:S(2)}) %collective-permute-start.3) | collective-permute-done | bytes 61472 | tf_op jit(solution)/shard_map/ppermute | solution.py:551
  13.3 0.0 collective-permute-done.4.second_ref
  13.3 2.0 %shard_map.185 = bf16[3,512,128]{2,1,0:T(8,128)(2,1)} custom-call(s32[1]{0:T(128)} %bitcast.at_ref, s32[4,64]{1,0:T(4,128)S(1)} %copy-done.3, bf16[3,512,128]{2,1,0:T(8,128)(2,1)S(1)} %get-tuple-element.17.query_ref, bf16[3,512,128]{2,1,0:T(8,128)(2,1)S(1)} %get-tuple-element.18.key_ref.own_key_ref, ...), custom_call_target="tpu_custom_call" | custom-call | flops 201326592 | bytes 4194304 | tf_op jit(solution)/shard_map/pallas_call | solution.py:572
  (1 shorter events, 0.0 us)
Async XLA Ops:
  0.0 5.7 %copy-start.2 = (bf16[128,128]{1,0:T(8,128)(2,1)S(1)}, bf16[128,128]{1,0:T(8,128)(2,1)}, u32[]{:S(2)}) copy-start(bf16[128,128]{1,0:T(8,128)(2,1)} %w_value.3) | copy-start | bytes 98308
  0.0 5.7 %copy-start.1 = (bf16[128,128]{1,0:T(8,128)(2,1)S(1)}, bf16[128,128]{1,0:T(8,128)(2,1)}, u32[]{:S(2)}) copy-start(bf16[128,128]{1,0:T(8,128)(2,1)} %w_key.3) | copy-start | bytes 98308
  0.0 5.7 %copy-start.14 = (bf16[128,128]{1,0:T(8,128)(2,1)S(1)}, bf16[128,128]{1,0:T(8,128)(2,1)}, u32[]{:S(2)}) copy-start(bf16[128,128]{1,0:T(8,128)(2,1)} %trans_gate.1) | copy-start | bytes 98308
  0.0 5.7 %copy-start.8 = (bf16[256,128]{1,0:T(8,128)(2,1)S(1)}, bf16[256,128]{1,0:T(8,128)(2,1)}, u32[]{:S(2)}) copy-start(bf16[256,128]{1,0:T(8,128)(2,1)} %w_down.1) | copy-start | bytes 196612
  0.0 5.7 %copy-start.7 = (bf16[128,256]{1,0:T(8,128)(2,1)S(1)}, bf16[128,256]{1,0:T(8,128)(2,1)}, u32[]{:S(2)}) copy-start(bf16[128,256]{1,0:T(8,128)(2,1)} %w_linear.1) | copy-start | bytes 196612
  0.0 5.7 %copy-start.6 = (bf16[128,256]{1,0:T(8,128)(2,1)S(1)}, bf16[128,256]{1,0:T(8,128)(2,1)}, u32[]{:S(2)}) copy-start(bf16[128,256]{1,0:T(8,128)(2,1)} %w_swish.1) | copy-start | bytes 196612
  0.0 5.7 %copy-start.12 = (bf16[128,128]{1,0:T(8,128)(2,1)S(1)}, bf16[128,128]{1,0:T(8,128)(2,1)}, u32[]{:S(2)}) copy-start(bf16[128,128]{1,0:T(8,128)(2,1)} %ada_trans_shift.1) | copy-start | bytes 98308
  0.0 5.7 %copy-start.11 = (bf16[128,128]{1,0:T(8,128)(2,1)S(1)}, bf16[128,128]{1,0:T(8,128)(2,1)}, u32[]{:S(2)}) copy-start(bf16[128,128]{1,0:T(8,128)(2,1)} %ada_trans.1) | copy-start | bytes 98308
  0.0 5.7 %copy-start.13 = (bf16[128,128]{1,0:T(8,128)(2,1)S(1)}, bf16[128,128]{1,0:T(8,128)(2,1)}, u32[]{:S(2)}) copy-start(bf16[128,128]{1,0:T(8,128)(2,1)} %attn_gate.1) | copy-start | bytes 98308
  0.1 5.7 %copy-start.16 = (bf16[128,128]{1,0:T(8,128)(2,1)S(1)}, bf16[128,128]{1,0:T(8,128)(2,1)}, u32[]{:S(2)}) copy-start(bf16[128,128]{1,0:T(8,128)(2,1)} %w_gate.1) | copy-start | bytes 98308
  0.1 5.7 %copy-start.15 = (bf16[128,128]{1,0:T(8,128)(2,1)S(1)}, bf16[128,128]{1,0:T(8,128)(2,1)}, u32[]{:S(2)}) copy-start(bf16[128,128]{1,0:T(8,128)(2,1)} %w_query.1) | copy-start | bytes 98308
  0.1 5.7 %copy-start.10 = (bf16[128,128]{1,0:T(8,128)(2,1)S(1)}, bf16[128,128]{1,0:T(8,128)(2,1)}, u32[]{:S(2)}) copy-start(bf16[128,128]{1,0:T(8,128)(2,1)} %ada_attn_shift.1) | copy-start | bytes 98308
  0.1 5.7 %copy-start.9 = (bf16[128,128]{1,0:T(8,128)(2,1)S(1)}, bf16[128,128]{1,0:T(8,128)(2,1)}, u32[]{:S(2)}) copy-start(bf16[128,128]{1,0:T(8,128)(2,1)} %ada_attn.1) | copy-start | bytes 98308
  0.1 5.7 %copy-start.5 = (bf16[512,128]{1,0:T(8,128)(2,1)S(1)}, bf16[512,128]{1,0:T(8,128)(2,1)}, u32[]{:S(2)}) copy-start(bf16[512,128]{1,0:T(8,128)(2,1)} %cond_ref.1) | copy-start | bytes 393220
  0.1 5.7 %copy-start.4 = (bf16[3,512,128]{2,1,0:T(8,128)(2,1)S(1)}, bf16[3,512,128]{2,1,0:T(8,128)(2,1)}, u32[]{:S(2)}) copy-start(bf16[3,512,128]{2,1,0:T(8,128)(2,1)} %single_ref.1) | copy-start | bytes 1179652
  2.5 8.2 %copy-start = (bf16[128,128]{1,0:T(8,128)(2,1)S(1)}, bf16[128,128]{1,0:T(8,128)(2,1)}, u32[]{:S(2)}) copy-start(bf16[128,128]{1,0:T(8,128)(2,1)} %w_out_ref.3) | copy-start | bytes 98308
  2.5 8.1 %copy-start.3 = (s32[4,64]{1,0:T(4,128)S(1)}, s32[4,64]{1,0:T(4,128)}, u32[]{:S(2)}) copy-start(s32[4,64]{1,0:T(4,128)} %counts_ref.3) | copy-start | bytes 3076
  2.6 5.4 %collective-permute-start.2 = (bf16[2,64,128]{2,1,0:T(8,128)(2,1)S(1)}, bf16[2,64,128]{2,1,0:T(8,128)(2,1)S(1)}, u32[]{:S(2)}, u32[]{:S(2)}) collective-permute-start(bf16[2,64,128]{2,1,0:T(8,128)(2,1)S(1)} %shard_map.182.refs_0_), channel_id=1, source_target_pairs={{0,3},{1,2},{2,1},{3,0},{4,7},{5,6},{6,5},{7,4},{8,11},{9,10},{10,... | collective-permute-start | bytes 98312 | tf_op jit(solution)/shard_map/ppermute | solution.py:493
  5.0 4.0 %collective-permute-start.1 = (bf16[2,64,128]{2,1,0:T(8,128)(2,1)S(1)}, bf16[2,64,128]{2,1,0:T(8,128)(2,1)S(1)}, u32[]{:S(2)}, u32[]{:S(2)}) collective-permute-start(bf16[2,64,128]{2,1,0:T(8,128)(2,1)S(1)} %shard_map.182.refs_0_), channel_id=1, source_target_pairs={{0,2},{2,0},{1,3},{3,1},{4,6},{6,4},{5,7},{7,5},{8,10},{10,8},{9,1... | collective-permute-start | bytes 98312 | tf_op jit(solution)/shard_map/ppermute | solution.py:492
  5.7 3.3 %collective-permute-start = (bf16[2,64,128]{2,1,0:T(8,128)(2,1)S(1)}, bf16[2,64,128]{2,1,0:T(8,128)(2,1)S(1)}, u32[]{:S(2)}, u32[]{:S(2)}) collective-permute-start(bf16[2,64,128]{2,1,0:T(8,128)(2,1)S(1)} %shard_map.182.refs_0_), channel_id=1, source_target_pairs={{0,1},{1,0},{2,3},{3,2},{4,5},{5,4},{6,7},{7,6},{8,9},{9,8},{10,11... | collective-permute-start | bytes 98312 | tf_op jit(solution)/shard_map/ppermute | solution.py:494
  9.0 4.3 %collective-permute-start.3 = (bf16[240,128]{1,0:T(8,128)(2,1)S(1)}, bf16[240,128]{1,0:T(8,128)(2,1)S(1)}, u32[]{:S(2)}, u32[]{:S(2)}) collective-permute-start(bf16[240,128]{1,0:T(8,128)(2,1)S(1)} %get-tuple-element.27), channel_id=1, source_target_pairs={{0,4},{1,5},{4,0},{5,1},{8,12},{9,13},{12,8},{13,9},{2,6},{3,7},{6... | collective-permute-start | bytes 184328 | tf_op jit(solution)/shard_map/ppermute | solution.py:551
  10.7 2.7 %collective-permute-start.4 = (bf16[240,128]{1,0:T(8,128)(2,1)S(1)}, bf16[240,128]{1,0:T(8,128)(2,1)S(1)}, u32[]{:S(2)}, u32[]{:S(2)}) collective-permute-start(bf16[240,128]{1,0:T(8,128)(2,1)S(1)} %get-tuple-element.28), channel_id=1, source_target_pairs={{0,1},{1,0},{4,8},{5,9},{8,4},{9,5},{12,13},{13,12},{2,3},{3,2},{6... | collective-permute-start | bytes 184328 | tf_op jit(solution)/shard_map/ppermute | solution.py:551

commit v19 on v18

--- a/solution.py
+++ b/solution.py
@@ -126,59 +126,52 @@
     at_ref,
     single_ref,
     cond_ref,
-    ada_attn,
+    ada_attn_scale,
     ada_attn_shift,
-    ada_trans,
-    ada_trans_shift,
-    attn_gate,
-    trans_gate,
     w_key,
     w_value,
     w_query,
     w_gate,
-    w_swish,
-    w_linear,
-    w_down,
-    query_ref,
-    key_ref,
-    value_ref,
-    gate_ref,
-    open_ref,
-    trans_ref,
-    near_ref,
-    far_ref,
+    *refs,
 ):
+    late_hbm, refs = refs[:7], refs[7:]
+    query_ref, key_ref, value_ref, gate_ref, open_ref, trans_ref, near_ref, far_ref = refs[:8]
+    late_refs, sem = refs[8:15], refs[15]
+    ada_trans_scale, ada_trans_shift, attn_gate, trans_gate, w_swish, w_linear, w_down = late_refs
     samples, atoms_here, width = single_ref.shape
-    step = math.gcd(atoms_here, 512)
-    for start in range(0, atoms_here, step):
-        at = slice(start, start + step)
-        cond = layer_norm(cond_ref[at, :]).astype(BF16)
-        single = layer_norm(single_ref[:, at, :].reshape(-1, width))
-        single = single.reshape(samples, step, width)
-        normed = attn_norm(cond, single, beside(ada_attn, ada_attn_shift))
-        if start == 0:
-            heads_of = [normed[sample, :EDGE] for sample in range(samples)]
-        if start + step == atoms_here:
-            tails_of = [normed[sample, step - EDGE :] for sample in range(samples)]
-        normed = normed.reshape(-1, width)
-        both = dot(normed, beside(w_key, w_value)).astype(BF16).reshape(samples, step, 2 * width)
-        key_ref[:, at, :] = both[:, :, :width]
-        value_ref[:, at, :] = both[:, :, width:]
-        both = dot(normed, beside(w_query, w_gate)).reshape(samples, step, 2 * width)
-        query_ref[:, at, :] = both[:, :, :width].astype(BF16)
-        gate_ref[:, at, :] = sigmoid(both[:, :, width:]).astype(BF16)
-        gates = dot(cond, beside(attn_gate, trans_gate))
-        open_ref[at, :] = sigmoid(gates[:, :width]).astype(BF16)
-        normed = attn_norm(cond, single, beside(ada_trans, ada_trans_shift)).reshape(-1, width)
-        swish = dot(normed, w_swish[...])
-        hidden = (swish * sigmoid(swish) * dot(normed, w_linear[...])).astype(BF16)
-        down = dot(hidden, w_down[...]).reshape(samples, step, width)
-        trans_ref[:, at, :] = (sigmoid(gates[:, width:])[None] * down).astype(BF16)
+    copies = [
+        pltpu.make_async_copy(source, target, sem.at[i])
+        for i, (source, target) in enumerate(zip(late_hbm, late_refs))
+    ]
+    for copy in copies:
+        copy.start()
+
+    cond = layer_norm(cond_ref[...]).astype(BF16)
+    single = layer_norm(single_ref[...].reshape(-1, width)).reshape(samples, atoms_here, width)
+    normed = attn_norm(cond, single, beside(ada_attn_scale, ada_attn_shift))
     even = at_ref[0] % 2 == 0
-    for sample, (head, tail) in enumerate(zip(heads_of, tails_of)):
+    for sample in range(samples):
         cut = slice(sample * EDGE, (sample + 1) * EDGE)
+        head, tail = normed[sample, :EDGE], normed[sample, atoms_here - EDGE :]
         near_ref[cut, :] = jnp.where(even, tail, head)
         far_ref[cut, :] = jnp.where(even, head, tail)
+    normed = normed.reshape(-1, width)
+    both = dot(normed, beside(w_key, w_value)).astype(BF16).reshape(samples, -1, 2 * width)
+    key_ref[...] = both[:, :, :width]
+    value_ref[...] = both[:, :, width:]
+    both = dot(normed, beside(w_query, w_gate)).reshape(samples, -1, 2 * width)
+    query_ref[...] = both[:, :, :width].astype(BF16)
+    gate_ref[...] = sigmoid(both[:, :, width:]).astype(BF16)
+
+    for copy in copies:
+        copy.wait()
+    gates = dot(cond, beside(attn_gate, trans_gate))
+    open_ref[...] = sigmoid(gates[:, :width]).astype(BF16)
+    normed = attn_norm(cond, single, beside(ada_trans_scale, ada_trans_shift)).reshape(-1, width)
+    swish = dot(normed, w_swish[...])
+    hidden = (swish * sigmoid(swish) * dot(normed, w_linear[...])).astype(BF16)
+    down = dot(hidden, w_down[...]).reshape(samples, -1, width)
+    trans_ref[...] = (sigmoid(gates[:, width:])[None] * down).astype(BF16)
 
 
 def tile_of(refs, place, row_block):
@@ -228,14 +221,24 @@
     return dot(hot, tile).astype(BF16)
 
 
-def attend(heads, reach, windows, query_ref, gate_ref, gated_ref):
-    samples, _, width = query_ref.shape
-    head_dim = width // heads
-    lanes = reach[0].shape[1]
+def head_mask(heads, lanes):
     rows = heads * Q_WIN
     lane_head = iota((rows, lanes), 1) // GROUP % heads
     row_head = iota((rows, lanes), 0) // Q_WIN
-    same_head = (lane_head == row_head).astype(F32).astype(BF16)
+    return (lane_head == row_head).astype(F32).astype(BF16)
+
+
+def picks_of(heads, reach, starts):
+    same_head = head_mask(heads, reach[0].shape[1])
+    return [
+        jnp.concatenate([one_hot(reach, start, Q_WIN)] * heads, 0) * same_head for start in starts
+    ]
+
+
+def attend(heads, windows, query_ref, gate_ref, gated_ref):
+    samples, _, width = query_ref.shape
+    head_dim = width // heads
+    rows = heads * Q_WIN
     own_head = iota((rows, width), 1) // head_dim == iota((rows, width), 0) // Q_WIN
     own_head = own_head.astype(F32).astype(BF16)
     channel_head = iota((Q_WIN, 2 * width), 1) % width // head_dim
@@ -243,8 +246,7 @@
     scaling = LOG2E / math.sqrt(head_dim)
 
     biases = []
-    for start, _, near, mask in windows:
-        pick = jnp.concatenate([one_hot(reach, start, Q_WIN)] * heads, 0) * same_head
+    for _, _, near, pick, mask in windows:
         bias = lax.dot_general(pick, near, LAST, preferred_element_type=F32) * LOG2E
         biases.append(bias if mask is None else jnp.where(mask, bias, MASKED))
     units = [(sample, i) for i in range(len(windows)) for sample in range(samples)]
@@ -255,7 +257,7 @@
         for sample, i in couple:
             query = query_ref[sample, pl.ds(windows[i][0], Q_WIN), :]
             queries.append(jnp.concatenate([query] * heads, 0) * own_head)
-            keys.append(windows[i][1](sample)[0])
+            keys.append(windows[i][1][sample][0])
         if len(couple) == 2:
             blank = jnp.zeros_like(keys[0])
             keys = [jnp.concatenate([keys[0], blank], 1), jnp.concatenate([blank, keys[1]], 1)]
@@ -270,7 +272,7 @@
     tops = [jnp.max(score, axis=-1, keepdims=True) for score in scores]
     raised = [jnp.exp2(score - top).astype(BF16) for score, top in zip(scores, tops)]
     for (sample, i), weight in zip(units, raised):
-        values = windows[i][1](sample)[1]
+        values = windows[i][1][sample][1]
         mixed = dot(weight, jnp.concatenate([values, ones], 1))
         picked = mixed[:Q_WIN]
         for head in range(1, heads):
@@ -294,8 +296,16 @@
     return lane // (heads * GROUP) * GROUP + lane % GROUP
 
 
+def outer_starts(atoms_here):
+    skip = -(-EDGE // Q_WIN)
+    return [
+        [side * (atoms_here - skip * Q_WIN) + i * Q_WIN for i in range(skip)] for side in range(2)
+    ]
+
+
 def inner_kernel(
     heads,
+    blocks,
     at_ref,
     counts_ref,
     query_ref,
@@ -307,6 +317,9 @@
     w_out_ref,
     held_ref,
     out_ref,
+    pick_ref,
+    hot_ref,
+    side_ref,
     near_ref,
     gated_ref,
 ):
@@ -319,29 +332,36 @@
     near_ref[...] = expand(hot, held_ref[...], tok_here // GROUP)
     reach = bounds(counts_ref, device_at, row_tokens(heads, tok_here))
     skip = -(-EDGE // Q_WIN)
-    inner = atoms_here // Q_WIN - 2 * skip
-    batch = math.gcd(inner, 12)
-
-    @pl.loop(0, inner // batch)
-    def _(turn):
-        windows = []
-        for i in range(batch):
-            start = pl.multiple_of((turn * batch + i + skip) * Q_WIN, Q_WIN)
-            cut = pl.ds(pl.multiple_of(start - EDGE, 16), K_WIN)
-            parts = lambda sample, cut=cut: (key_ref[sample, cut, :], value_ref[sample, cut, :])
-            windows.append((start, parts, near_ref[cut, :], None))
-        attend(heads, reach, windows, query_ref, gate_ref, gated_ref)
-
-    cut = slice(skip * Q_WIN, atoms_here - skip * Q_WIN)
+    starts = [window * Q_WIN for window in range(skip, atoms_here // Q_WIN - skip)]
+    windows = []
+    for start, pick in zip(starts, picks_of(heads, reach, starts)):
+        cut = slice(start - EDGE, start - EDGE + K_WIN)
+        parts = [(key_ref[i, cut, :], value_ref[i, cut, :]) for i in range(samples)]
+        windows.append((start, parts, near_ref[cut, :], pick, None))
+    attend(heads, windows, query_ref, gate_ref, gated_ref)
+
+    cut = slice(starts[0], starts[-1] + Q_WIN)
     for sample in range(samples):
         out_ref[sample] = close(sample, cut, gated_ref, open_ref, trans_ref, w_out_ref)
+
+    inside = side_ref.shape[1]
+    sides = (
+        (jnp.maximum(device_at - 1, 0), atoms_here - EDGE, tok_here - EDGE, 0),
+        (jnp.minimum(device_at + 1, blocks - 1), 0, 0, atoms_here - inside),
+    )
+    for side, (block, offset, token, own_start) in enumerate(sides):
+        nearest = bounds(counts_ref, block, iota((tok_here, EDGE), 1) + token)
+        hot_ref[side] = one_hot(nearest, offset, EDGE)
+        side_ref[side] = near_ref[own_start : own_start + inside, :]
+        for i, pick in enumerate(picks_of(heads, reach, outer_starts(atoms_here)[side])):
+            pick_ref[side, i] = pick
 
 
 def outer_kernel(
     heads,
     blocks,
+    groups,
     at_ref,
-    counts_ref,
     query_ref,
     own_key_ref,
     own_value_ref,
@@ -349,28 +369,25 @@
     open_ref,
     trans_ref,
     w_out_ref,
-    held_ref,
     inner_ref,
+    pick_ref,
+    hot_ref,
+    side_ref,
     w_key,
     w_value,
     first_ref,
     second_ref,
     out_hbm,
-    key_ref,
-    value_ref,
-    near_ref,
     gated_ref,
     out_ref,
     sem,
 ):
     samples, atoms_here, width = query_ref.shape
-    tok_here = counts_ref.shape[1]
     device_at = at_ref[0]
     ends = atoms_here * blocks
-    skip = -(-EDGE // Q_WIN)
-    margin = skip * Q_WIN
-    reach_keys = key_ref.shape[2]
-    inside = reach_keys - EDGE
+    starts = outer_starts(atoms_here)
+    margin = len(starts[0]) * Q_WIN
+    inside = side_ref.shape[1]
 
     whole = pltpu.make_async_copy(
         inner_ref, out_hbm.at[:, pl.ds(margin, atoms_here - 2 * margin)], sem.at[0]
@@ -383,45 +400,35 @@
     count = samples * EDGE
     edges = jnp.concatenate([rows[:count] for rows in arrived], 0)
     edges = dot(edges, beside(w_key, w_value)).astype(BF16).reshape(2, samples, EDGE, 2 * width)
-    groups = tok_here // GROUP
-    token = iota((tok_here, tok_here), 1)
-    own_reach = bounds(counts_ref, device_at, token)
-    sides = (
-        (jnp.maximum(device_at - 1, 0), atoms_here - EDGE, 0, EDGE, 0),
-        (jnp.minimum(device_at + 1, blocks - 1), 0, inside, 0, atoms_here - inside),
-    )
-    for side, (block, offset, place, own_place, own_start) in enumerate(sides):
-        for i, (ref, own_ref) in enumerate(((key_ref, own_key_ref), (value_ref, own_value_ref))):
-            ref[side, :, place : place + EDGE, :] = edges[side, :, :, i * width : (i + 1) * width]
-            ref[side, :, own_place : own_place + inside, :] = own_ref[
-                :, own_start : own_start + inside, :
-            ]
-        nearest = iota((tok_here, EDGE), 1) + (tok_here - EDGE if side == 0 else 0)
-        hot = one_hot(bounds(counts_ref, block, nearest), offset, EDGE)
-        near_ref[side, place : place + EDGE, :] = expand(hot, arrived[side][count:], groups)
-        hot = one_hot(own_reach, own_start, inside)
-        near_ref[side, own_place : own_place + inside, :] = expand(hot, held_ref[...], groups)
-
-    reach = bounds(counts_ref, device_at, row_tokens(heads, tok_here))
+
+    def joined(side, edge, own):
+        return jnp.concatenate([own, edge] if side else [edge, own], 0)
+
     windows = []
     for side in range(2):
-        for i in range(skip):
-            start = i * Q_WIN + side * (atoms_here - margin)
+        own = slice(side * (atoms_here - inside), side * (atoms_here - inside) + inside)
+        parts = [
+            (
+                joined(side, edges[side, i, :, :width], own_key_ref[i, own, :]),
+                joined(side, edges[side, i, :, width:], own_value_ref[i, own, :]),
+            )
+            for i in range(samples)
+        ]
+        near = expand(hot_ref[side], arrived[side][count:], groups)
+        near = joined(side, near, side_ref[side])
+        for i, start in enumerate(starts[side]):
             cut = slice(i * Q_WIN, i * Q_WIN + K_WIN)
-            parts = lambda sample, side=side, cut=cut: (
-                key_ref[side, sample, cut, :],
-                value_ref[side, sample, cut, :],
-            )
             key_at = iota((heads * Q_WIN, K_WIN), 1) + (device_at * atoms_here + start - EDGE)
             mask = (key_at >= 0) & (key_at < ends)
-            windows.append((start, parts, near_ref[side, cut, :], mask))
-    attend(heads, reach, windows, query_ref, gate_ref, gated_ref)
+            pieces = [(keys[cut], values[cut]) for keys, values in parts]
+            windows.append((start, pieces, near[cut], pick_ref[side, i], mask))
+    attend(heads, windows, query_ref, gate_ref, gated_ref)
     copies = []
     for side in range(2):
-        cut = slice(side * (atoms_here - margin), side * (atoms_here - margin) + margin)
+        cut = slice(starts[side][0], starts[side][0] + margin)
         for sample in range(samples):
             out_ref[side, sample] = close(sample, cut, gated_ref, open_ref, trans_ref, w_out_ref)
-        target = out_hbm.at[:, pl.ds(side * (atoms_here - margin), margin)]
+        target = out_hbm.at[:, pl.ds(starts[side][0], margin)]
         copies.append(pltpu.make_async_copy(out_ref.at[side], target, sem.at[1 + side]))
         copies[-1].start()
     for copy in copies:
@@ -500,27 +507,23 @@
         atom_cond,
         ada_attn_scale,
         ada_attn_shift,
-        ada_trans_scale,
-        ada_trans_shift,
-        attn_gate,
-        trans_gate,
         w_key,
         w_value,
         w_query,
         w_gate,
-        w_swish,
-        w_linear,
-        w_down,
     )
+    late = (ada_trans_scale, ada_trans_shift, attn_gate, trans_gate, w_swish, w_linear, w_down)
     query, keys, values, gate, opened, trans, near, far = pl.pallas_call(
         project_kernel,
-        in_specs=[IN_SMEM] + [IN_VMEM] * len(operands),
+        in_specs=[IN_SMEM] + [IN_VMEM] * len(operands) + [IN_HBM] * len(late),
         out_specs=[IN_VMEM] * 8,
         out_shape=[pltpu.VMEM(wide, BF16)] * 4
         + [pltpu.VMEM((atoms_here, width), BF16), pltpu.VMEM(wide, BF16), sent, sent],
+        scratch_shapes=[pltpu.VMEM(weight.shape, BF16) for weight in late]
+        + [pltpu.SemaphoreType.DMA((len(late),))],
         compiler_params=params,
         cost_estimate=cost(samples * atoms_here * width * width * 20),
-    )(at, *map(in_vmem, operands))
+    )(at, *map(in_vmem, operands), *map(in_hbm, late))
 
     operands = (*tiles, near, far, opened)
     first = 3 + len(tiles)
@@ -553,38 +556,41 @@
     first, second = swap(near, 0), swap(far, 1)
 
     margin = -(-EDGE // Q_WIN) * Q_WIN
-    operands = (query, keys, values, gate, opened, trans, w_out, held)
-    inner = pl.pallas_call(
-        functools.partial(inner_kernel, heads),
-        in_specs=[IN_SMEM] + [IN_VMEM] * (1 + len(operands)),
-        out_specs=IN_VMEM,
-        out_shape=pltpu.VMEM((samples, atoms_here - 2 * margin, width), BF16),
+    inside = margin - Q_WIN + K_WIN - EDGE
+    expanded = heads * tok_here
+    operands = (query, keys, values, gate, opened, trans, w_out)
+    inner, picks, hots, beside_edges = pl.pallas_call(
+        functools.partial(inner_kernel, heads, blocks),
+        in_specs=[IN_SMEM] + [IN_VMEM] * (2 + len(operands)),
+        out_specs=[IN_VMEM] * 4,
+        out_shape=[
+            pltpu.VMEM((samples, atoms_here - 2 * margin, width), BF16),
+            pltpu.VMEM((2, margin // Q_WIN, heads * Q_WIN, expanded), BF16),
+            pltpu.VMEM((2, EDGE, EDGE), BF16),
+            pltpu.VMEM((2, inside, expanded), BF16),
+        ],
         scratch_shapes=[
-            pltpu.VMEM((atoms_here, heads * tok_here), BF16),
+            pltpu.VMEM((atoms_here, expanded), BF16),
             pltpu.VMEM(wide, BF16),
         ],
         compiler_params=params,
         cost_estimate=cost(samples * atoms_here * width * width * 12),
-    )(at, atom_counts, *map(in_vmem, operands))
-
-    reach = margin - Q_WIN + K_WIN
-    operands += (inner, w_key, w_value, first, second)
+    )(at, atom_counts, *map(in_vmem, (*operands, held)))
+
+    operands += (inner, picks, hots, beside_edges, w_key, w_value, first, second)
     return pl.pallas_call(
-        functools.partial(outer_kernel, heads, blocks),
-        in_specs=[IN_SMEM] + [IN_VMEM] * (1 + len(operands)),
+        functools.partial(outer_kernel, heads, blocks, groups),
+        in_specs=[IN_SMEM] + [IN_VMEM] * len(operands),
         out_specs=IN_HBM,
         out_shape=pltpu.HBM(wide, BF16),
         scratch_shapes=[
-            pltpu.VMEM((2, samples, reach, width), BF16),
-            pltpu.VMEM((2, samples, reach, width), BF16),
-            pltpu.VMEM((2, reach, heads * tok_here), BF16),
             pltpu.VMEM(wide, BF16),
             pltpu.VMEM((2, samples, margin, width), BF16),
             pltpu.SemaphoreType.DMA((3,)),
         ],
         compiler_params=params,
         cost_estimate=cost(samples * atoms_here * width * width * 4),
-    )(at, atom_counts, *map(in_vmem, operands))
+    )(at, *map(in_vmem, operands))
 
 
 def solution(mesh):

time: 15.6 us -> 15.3 us (0.981)
  the two profiles are of different devices: /device:TPU:0 before, /device:TPU:22 now
where the time goes in v19:
time: 15.3 us; the launch traced here: 15.1 us
  Pallas kernels  9.15 us (60%)
  starting transfers between devices  3.57 us (23%)
  waiting for transfers between devices  2.13 us (14%)
  between operations  0.17 us (1%)
    pallas_call x1, Pallas kernels, shards(): pl.pallas_call(project_kernel, in_specs=[IN_SMEM] + [IN_VMEM] * len(opera...  2.99 us
    pallas_call x1, Pallas kernels, shards(): pl.pallas_call(pair_kernel, in_specs=[IN_SMEM] + [IN_HBM] * 2, out_specs=...  2.37 us
    ppermute x2, waiting for transfers between devices, swap(): return lax.ppermute(value, ('atoms', 'samp'), sides)  2.12 us
    pallas_call x1, Pallas kernels, shards(): pl.pallas_call(functools.partial(inner_kernel, heads, blocks), in_specs=[...  2.09 us
    ppermute x2, starting transfers between devices, swap(): return lax.ppermute(value, ('atoms', 'samp'), sides)  1.65 us
    pallas_call x1, Pallas kernels, shards(): pl.pallas_call(functools.partial(outer_kernel, heads, blocks, groups), in...  1.64 us
    ppermute x1, starting transfers between devices, shards(): across = lax.ppermute(own, 'pair', swapped)  1.42 us
    ppermute x1, starting transfers between devices, shards(): tiles = (own, lax.ppermute(own, 'samp', swapped), across, diagonal)  0.43 us
  transfers between devices with their start and end apart: 5, of which 2 were waited for; matrix products, arithmetic and copies ran while one was open for 0% of the time, Pallas kernels for 34%

profile of v19, /device:TPU:22, one launch (start us, length us, event | category | flops | bytes accessed | tf_op | source)
XLA Modules:
  0.0 15.1 jit_solution(3321710258351567830)
XLA Ops:
  0.0 0.0 copy-start.1
  0.0 0.0 copy-start
  0.0 0.0 copy-start.8
  0.0 0.0 copy-start.7
  0.0 0.0 copy-start.6
  0.0 0.0 copy-start.5
  0.0 0.0 copy-start.4
  0.0 0.0 copy-start.3
  0.1 2.4 %shard_map.182.refs_0_ = bf16[2,64,128]{2,1,0:T(8,128)(2,1)S(1)} custom-call(s32[1]{0:T(128)} %bitcast.2.core_ref, bf16[4,128]{1,0:T(4,128)(2,1)} %bitcast.4, bf16[128,64,128]{2,1,0:T(8,128)(2,1)} %pair_hbm.1), custom_call_target="tpu_custom_call" | custom-call | flops 268435456 | bytes 4194304 | tf_op jit(solution)/shard_map/pallas_call | solution.py:483
  2.4 0.0 copy-start.2
  2.5 0.0 copy-start.9
  2.5 0.1 collective-permute-start.2
  2.5 1.4 %collective-permute-start.1 = (bf16[2,64,128]{2,1,0:T(8,128)(2,1)S(1)}, bf16[2,64,128]{2,1,0:T(8,128)(2,1)S(1)}, u32[]{:S(2)}, u32[]{:S(2)}) collective-permute-start(bf16[2,64,128]{2,1,0:T(8,128)(2,1)S(1)} %shard_map.182.refs_0_), channel_id=1, source_target_pairs={{0,2},{2,0},{1,3},{3,1},{4,6},{6,4},{5,7},{7,5},{8,10},{10,8},{9,1... | collective-permute-start | bytes 98312 | tf_op jit(solution)/shard_map/ppermute | solution.py:499
  4.0 0.4 %collective-permute-start = (bf16[2,64,128]{2,1,0:T(8,128)(2,1)S(1)}, bf16[2,64,128]{2,1,0:T(8,128)(2,1)S(1)}, u32[]{:S(2)}, u32[]{:S(2)}) collective-permute-start(bf16[2,64,128]{2,1,0:T(8,128)(2,1)S(1)} %shard_map.182.refs_0_), channel_id=1, source_target_pairs={{0,1},{1,0},{2,3},{3,2},{4,5},{5,4},{6,7},{7,6},{8,9},{9,8},{10,11... | collective-permute-start | bytes 98312 | tf_op jit(solution)/shard_map/ppermute | solution.py:501
  4.4 0.0 copy-done.1
  4.4 0.0 copy-done
  4.4 0.0 copy-done.8
  4.4 0.0 copy-done.7
  4.4 0.0 copy-done.6
  4.4 0.0 copy-done.5
  4.4 0.0 copy-done.4
  4.4 0.0 copy-done.3
  4.4 3.0 %shard_map.181 = (bf16[3,512,128]{2,1,0:T(8,128)(2,1)S(1)}, bf16[3,512,128]{2,1,0:T(8,128)(2,1)S(1)}, bf16[3,512,128]{2,1,0:T(8,128)(2,1)S(1)}, bf16[3,512,128]{...) custom-call(s32[1]{0:T(128)} %bitcast.at_ref, ...), custom_call_target="tpu_custom_call" | custom-call | flops 1006632960 | bytes 4194304 | tf_op jit(solution)/shard_map/pallas_call | solution.py:516
  7.5 0.0 collective-permute-done.2.refs_3_
  7.5 0.0 collective-permute-done.1.refs_2_
  7.5 0.0 collective-permute-done.refs_1_
  7.5 1.6 %collective-permute-start.3 = (bf16[240,128]{1,0:T(8,128)(2,1)S(1)}, bf16[240,128]{1,0:T(8,128)(2,1)S(1)}, u32[]{:S(2)}, u32[]{:S(2)}) collective-permute-start(bf16[240,128]{1,0:T(8,128)(2,1)S(1)} %get-tuple-element.35), channel_id=1, source_target_pairs={{0,4},{1,5},{4,0},{5,1},{8,12},{9,13},{12,8},{13,9},{2,6},{3,7},{6... | collective-permute-start | bytes 184328 | tf_op jit(solution)/shard_map/ppermute | solution.py:554
  9.2 0.0 collective-permute-start.4
  9.2 0.0 copy-done.2
  9.2 0.0 copy-done.9
  9.2 2.1 %shard_map.184 = (bf16[3,384,128]{2,1,0:T(8,128)(2,1)S(1)}, bf16[2,2,128,256]{3,2,1,0:T(8,128)(2,1)S(1)}, bf16[2,48,48]{2,1,0:T(8,128)(2,1)S(1)}, bf16[2,112,256]{2,1,0:T(8,128)(2,1)S(1)}) custom-call(s32[1]{0:T(128)} %bitcast.at_ref, s32[4,64]{1,0:T(4,128)S(1)} %copy-done.9, bf16[3,512,128]{2,1,0:T(8,128)(2,1)S(1)} %get-tuple-element.21.query_ref, ...), custom_call_target="tpu_custom_call" | custom-call | flops 603979776 | bytes 4194304 | tf_op jit(solution)/shard_map/pallas_call | solution.py:562
  11.3 0.5 %collective-permute-done.3.first_ref = bf16[240,128]{1,0:T(8,128)(2,1)S(1)} collective-permute-done((bf16[240,128]{1,0:T(8,128)(2,1)S(1)}, bf16[240,128]{1,0:T(8,128)(2,1)S(1)}, u32[]{:S(2)}, u32[]{:S(2)}) %collective-permute-start.3) | collective-permute-done | bytes 61472 | tf_op jit(solution)/shard_map/ppermute | solution.py:554
  11.8 1.6 %collective-permute-done.4.second_ref = bf16[240,128]{1,0:T(8,128)(2,1)S(1)} collective-permute-done((bf16[240,128]{1,0:T(8,128)(2,1)S(1)}, bf16[240,128]{1,0:T(8,128)(2,1)S(1)}, u32[]{:S(2)}, u32[]{:S(2)}) %collective-permute-start.4) | collective-permute-done | bytes 61472 | tf_op jit(solution)/shard_map/ppermute | solution.py:554
  13.4 1.6 %shard_map.185 = bf16[3,512,128]{2,1,0:T(8,128)(2,1)} custom-call(s32[1]{0:T(128)} %bitcast.at_ref, bf16[3,512,128]{2,1,0:T(8,128)(2,1)S(1)} %get-tuple-element.21.query_ref, bf16[3,512,128]{2,1,0:T(8,128)(2,1)S(1)} %get-tuple-element.22.key_ref.own_key_ref, bf16[3,512,128]{2,1,0:T(8,128)(2,1)S(1)} %get-tuple-element.23.value_ref.own_value_ref, ...), custom_call_target="tpu_custom_call" | custom-call | flops 201326592 | bytes 4194304 | tf_op jit(solution)/shard_map/pallas_call | solution.py:581
  (1 shorter events, 0.0 us)
Async XLA Ops:
  0.0 4.4 %copy-start.1 = (bf16[128,128]{1,0:T(8,128)(2,1)S(1)}, bf16[128,128]{1,0:T(8,128)(2,1)}, u32[]{:S(2)}) copy-start(bf16[128,128]{1,0:T(8,128)(2,1)} %w_value.3) | copy-start | bytes 98308
  0.0 4.4 %copy-start = (bf16[128,128]{1,0:T(8,128)(2,1)S(1)}, bf16[128,128]{1,0:T(8,128)(2,1)}, u32[]{:S(2)}) copy-start(bf16[128,128]{1,0:T(8,128)(2,1)} %w_key.3) | copy-start | bytes 98308
  0.0 4.4 %copy-start.8 = (bf16[128,128]{1,0:T(8,128)(2,1)S(1)}, bf16[128,128]{1,0:T(8,128)(2,1)}, u32[]{:S(2)}) copy-start(bf16[128,128]{1,0:T(8,128)(2,1)} %w_gate.1) | copy-start | bytes 98308
  0.0 4.4 %copy-start.7 = (bf16[128,128]{1,0:T(8,128)(2,1)S(1)}, bf16[128,128]{1,0:T(8,128)(2,1)}, u32[]{:S(2)}) copy-start(bf16[128,128]{1,0:T(8,128)(2,1)} %w_query.1) | copy-start | bytes 98308
  0.0 4.4 %copy-start.6 = (bf16[128,128]{1,0:T(8,128)(2,1)S(1)}, bf16[128,128]{1,0:T(8,128)(2,1)}, u32[]{:S(2)}) copy-start(bf16[128,128]{1,0:T(8,128)(2,1)} %ada_attn_shift.1) | copy-start | bytes 98308
  0.0 4.4 %copy-start.5 = (bf16[128,128]{1,0:T(8,128)(2,1)S(1)}, bf16[128,128]{1,0:T(8,128)(2,1)}, u32[]{:S(2)}) copy-start(bf16[128,128]{1,0:T(8,128)(2,1)} %ada_attn_scale.1) | copy-start | bytes 98308
  0.0 4.4 %copy-start.4 = (bf16[512,128]{1,0:T(8,128)(2,1)S(1)}, bf16[512,128]{1,0:T(8,128)(2,1)}, u32[]{:S(2)}) copy-start(bf16[512,128]{1,0:T(8,128)(2,1)} %cond_ref.1) | copy-start | bytes 393220
  0.0 4.4 %copy-start.3 = (bf16[3,512,128]{2,1,0:T(8,128)(2,1)S(1)}, bf16[3,512,128]{2,1,0:T(8,128)(2,1)}, u32[]{:S(2)}) copy-start(bf16[3,512,128]{2,1,0:T(8,128)(2,1)} %single_ref.1) | copy-start | bytes 1179652
  2.4 6.7 %copy-start.2 = (bf16[128,128]{1,0:T(8,128)(2,1)S(1)}, bf16[128,128]{1,0:T(8,128)(2,1)}, u32[]{:S(2)}) copy-start(bf16[128,128]{1,0:T(8,128)(2,1)} %w_out_ref.3) | copy-start | bytes 98308
  2.5 6.7 %copy-start.9 = (s32[4,64]{1,0:T(4,128)S(1)}, s32[4,64]{1,0:T(4,128)}, u32[]{:S(2)}) copy-start(s32[4,64]{1,0:T(4,128)} %counts_ref.1) | copy-start | bytes 3076
  2.5 5.0 %collective-permute-start.2 = (bf16[2,64,128]{2,1,0:T(8,128)(2,1)S(1)}, bf16[2,64,128]{2,1,0:T(8,128)(2,1)S(1)}, u32[]{:S(2)}, u32[]{:S(2)}) collective-permute-start(bf16[2,64,128]{2,1,0:T(8,128)(2,1)S(1)} %shard_map.182.refs_0_), channel_id=1, source_target_pairs={{0,3},{1,2},{2,1},{3,0},{4,7},{5,6},{6,5},{7,4},{8,11},{9,10},{10,... | collective-permute-start | bytes 98312 | tf_op jit(solution)/shard_map/ppermute | solution.py:500
  2.5 4.9 %collective-permute-start.1 = (bf16[2,64,128]{2,1,0:T(8,128)(2,1)S(1)}, bf16[2,64,128]{2,1,0:T(8,128)(2,1)S(1)}, u32[]{:S(2)}, u32[]{:S(2)}) collective-permute-start(bf16[2,64,128]{2,1,0:T(8,128)(2,1)S(1)} %shard_map.182.refs_0_), channel_id=1, source_target_pairs={{0,2},{2,0},{1,3},{3,1},{4,6},{6,4},{5,7},{7,5},{8,10},{10,8},{9,1... | collective-permute-start | bytes 98312 | tf_op jit(solution)/shard_map/ppermute | solution.py:499
  4.0 3.5 %collective-permute-start = (bf16[2,64,128]{2,1,0:T(8,128)(2,1)S(1)}, bf16[2,64,128]{2,1,0:T(8,128)(2,1)S(1)}, u32[]{:S(2)}, u32[]{:S(2)}) collective-permute-start(bf16[2,64,128]{2,1,0:T(8,128)(2,1)S(1)} %shard_map.182.refs_0_), channel_id=1, source_target_pairs={{0,1},{1,0},{2,3},{3,2},{4,5},{5,4},{6,7},{7,6},{8,9},{9,8},{10,11... | collective-permute-start | bytes 98312 | tf_op jit(solution)/shard_map/ppermute | solution.py:501
  7.5 4.3 %collective-permute-start.3 = (bf16[240,128]{1,0:T(8,128)(2,1)S(1)}, bf16[240,128]{1,0:T(8,128)(2,1)S(1)}, u32[]{:S(2)}, u32[]{:S(2)}) collective-permute-start(bf16[240,128]{1,0:T(8,128)(2,1)S(1)} %get-tuple-element.35), channel_id=1, source_target_pairs={{0,4},{1,5},{4,0},{5,1},{8,12},{9,13},{12,8},{13,9},{2,6},{3,7},{6... | collective-permute-start | bytes 184328 | tf_op jit(solution)/shard_map/ppermute | solution.py:554
  9.2 4.2 %collective-permute-start.4 = (bf16[240,128]{1,0:T(8,128)(2,1)S(1)}, bf16[240,128]{1,0:T(8,128)(2,1)S(1)}, u32[]{:S(2)}, u32[]{:S(2)}) collective-permute-start(bf16[240,128]{1,0:T(8,128)(2,1)S(1)} %get-tuple-element.36), channel_id=1, source_target_pairs={{0,1},{1,0},{4,8},{5,9},{8,4},{9,5},{12,13},{13,12},{2,3},{3,2},{6... | collective-permute-start | bytes 184328 | tf_op jit(solution)/shard_map/ppermute | solution.py:554

commit v20 on v19

--- a/solution.py
+++ b/solution.py
@@ -48,6 +48,10 @@
 def centring(width):
     same = iota((width, width), 0) == iota((width, width), 1)
     return jnp.where(same, 1.0 - 1.0 / width, -1.0 / width).astype(BF16)
+
+
+def averaging(width):
+    return jnp.full((width, width), 1.0 / width, BF16)
 
 
 def mean_square(centred):
@@ -104,10 +108,16 @@
         pair = pair_ref[chunk * group : (chunk + 1) * group].reshape(group * cols, width)
         chunks.append(dot(side_by_side(pair), centre))
     mixes = [dot(centred.astype(BF16), mix).reshape(half, cols, 2 * lanes) for centred in chunks]
+    squares = [(centred[:, :width] * centred[:, :width]).astype(BF16) for centred in chunks]
+    averages = [
+        dot(jnp.concatenate(squares[i : i + 2], 1), twice(averaging(width)))
+        for i in range(0, len(squares), 2)
+    ]
     for chunk, (centred, mixed) in enumerate(zip(chunks, mixes)):
+        pick = slice(chunk % 2 * width, (chunk % 2 + 1) * width)
         variances = [
-            mean_square(centred[:, part * width : (part + 1) * width]).reshape(half, cols, 1)
-            for part in range(2)
+            averages[chunk // 2][:, pick].reshape(half, cols, width),
+            mean_square(centred[:, width:]).reshape(half, cols, 1),
         ]
         total = jnp.zeros((cols, lanes), F32)
         spread_out = jnp.zeros((cols, lanes), F32)
@@ -123,7 +133,7 @@
 
 
 def project_kernel(
-    at_ref,
+    core_ref,
     single_ref,
     cond_ref,
     ada_attn_scale,
@@ -149,12 +159,12 @@
     cond = layer_norm(cond_ref[...]).astype(BF16)
     single = layer_norm(single_ref[...].reshape(-1, width)).reshape(samples, atoms_here, width)
     normed = attn_norm(cond, single, beside(ada_attn_scale, ada_attn_shift))
-    even = at_ref[0] % 2 == 0
+    down = core_ref[0] == 0
     for sample in range(samples):
         cut = slice(sample * EDGE, (sample + 1) * EDGE)
         head, tail = normed[sample, :EDGE], normed[sample, atoms_here - EDGE :]
-        near_ref[cut, :] = jnp.where(even, tail, head)
-        far_ref[cut, :] = jnp.where(even, head, tail)
+        near_ref[cut, :] = jnp.where(down, head, tail)
+        far_ref[cut, :] = jnp.where(down, tail, head)
     normed = normed.reshape(-1, width)
     both = dot(normed, beside(w_key, w_value)).astype(BF16).reshape(samples, -1, 2 * width)
     key_ref[...] = both[:, :, :width]
@@ -190,8 +200,8 @@
     groups, cols, lanes = tile_refs[0].shape[-3:]
     rows = groups * EDGE
     device_at, place = at_ref[0], (pair_ref[0], core_ref[0])
-    for send_ref, parity in ((near_ref, 0), (far_ref, 1)):
-        above = device_at % 2 == parity
+    for send_ref, core in ((near_ref, 1), (far_ref, 0)):
+        above = core_ref[0] == core
         beside = jnp.where(above, device_at + 1, device_at - 1)
         tile = tile_of(tile_refs, place, jnp.clip(beside, 0, blocks - 1))
         tile = jnp.where(above, tile[:, cols - EDGE :], tile[:, :EDGE])
@@ -362,6 +372,7 @@
     blocks,
     groups,
     at_ref,
+    core_ref,
     query_ref,
     own_key_ref,
     own_value_ref,
@@ -394,9 +405,9 @@
     )
     whole.start()
 
-    even = device_at % 2 == 0
+    down = core_ref[0] == 0
     first, second = first_ref[...], second_ref[...]
-    arrived = (jnp.where(even, second, first), jnp.where(even, first, second))
+    arrived = (jnp.where(down, second, first), jnp.where(down, first, second))
     count = samples * EDGE
     edges = jnp.concatenate([rows[:count] for rows in arrived], 0)
     edges = dot(edges, beside(w_key, w_value)).astype(BF16).reshape(2, samples, EDGE, 2 * width)
@@ -523,7 +534,7 @@
         + [pltpu.SemaphoreType.DMA((len(late),))],
         compiler_params=params,
         cost_estimate=cost(samples * atoms_here * width * width * 20),
-    )(at, *map(in_vmem, operands), *map(in_hbm, late))
+    )(core_at, *map(in_vmem, operands), *map(in_hbm, late))
 
     operands = (*tiles, near, far, opened)
     first = 3 + len(tiles)
@@ -541,19 +552,11 @@
         compiler_params=params,
     )(at, pair_at, core_at, *map(in_vmem, operands))
 
-    def swap(value, start):
-        cores = lax.axis_size("samp")
-        other_of = {}
-        for i in range(start, blocks - 1, 2):
-            other_of[i], other_of[i + 1] = i + 1, i
-        sides = []
-        for i in range(blocks):
-            for core in range(cores):
-                target = (other_of[i], core) if i in other_of else (i, (core + 1) % cores)
-                sides.append((i * cores + core, target[0] * cores + target[1]))
-        return lax.ppermute(value, ("atoms", "samp"), sides)
-
-    first, second = swap(near, 0), swap(far, 1)
+    down = [(2 * i, 2 * (i - 1)) for i in range(1, blocks)] + [(0, 1)]
+    up = [(2 * i + 1, 2 * (i + 1) + 1) for i in range(blocks - 1)] + [(2 * blocks - 1, 2 * blocks - 2)]
+    cycle = down + up
+    first = lax.ppermute(near, ("atoms", "samp"), cycle)
+    second = lax.ppermute(far, ("atoms", "samp"), [(target, source) for source, target in cycle])
 
     margin = -(-EDGE // Q_WIN) * Q_WIN
     inside = margin - Q_WIN + K_WIN - EDGE
@@ -580,7 +583,7 @@
     operands += (inner, picks, hots, beside_edges, w_key, w_value, first, second)
     return pl.pallas_call(
         functools.partial(outer_kernel, heads, blocks, groups),
-        in_specs=[IN_SMEM] + [IN_VMEM] * len(operands),
+        in_specs=[IN_SMEM] * 2 + [IN_VMEM] * len(operands),
         out_specs=IN_HBM,
         out_shape=pltpu.HBM(wide, BF16),
         scratch_shapes=[
@@ -590,7 +593,7 @@
         ],
         compiler_params=params,
         cost_estimate=cost(samples * atoms_here * width * width * 4),
-    )(at, *map(in_vmem, operands))
+    )(at, core_at, *map(in_vmem, operands))
 
 
 def solution(mesh):

time: 15.3 us -> 15.1 us (0.987)
  the two profiles are of different devices: /device:TPU:22 before, /device:TPU:0 now
where the time goes in v20:
time: 15.1 us; the launch traced here: 14.9 us
  Pallas kernels  9.09 us (60%)
  starting transfers between devices  5.18 us (34%)
  waiting for transfers between devices  0.45 us (3%)
    pallas_call x1, Pallas kernels, shards(): pl.pallas_call(project_kernel, in_specs=[IN_SMEM] + [IN_VMEM] * len(opera...  2.99 us
    ppermute x1, starting transfers between devices, shards(): lax.ppermute(own, ('pair', 'samp'), [(0, 3), (1, 2), (2, 1), (3, 0)])  2.43 us
    pallas_call x1, Pallas kernels, shards(): pl.pallas_call(pair_kernel, in_specs=[IN_SMEM] + [IN_HBM] * 2, out_specs=...  2.33 us
    pallas_call x1, Pallas kernels, shards(): pl.pallas_call(functools.partial(inner_kernel, heads, blocks), in_specs=[...  2.08 us
    ppermute x1, starting transfers between devices, shards(): lax.ppermute(far, ('atoms', 'samp'), [(target, source) for source, target...  1.75 us
    pallas_call x1, Pallas kernels, shards(): pl.pallas_call(functools.partial(outer_kernel, heads, blocks, groups), in...  1.64 us
    ppermute x1, starting transfers between devices, shards(): across = lax.ppermute(own, 'pair', swapped)  0.67 us
  transfers between devices with their start and end apart: 5, of which 2 were waited for; matrix products, arithmetic and copies ran while one was open for 0% of the time, Pallas kernels for 34%

profile of v20, /device:TPU:0, one launch (start us, length us, event | category | flops | bytes accessed | tf_op | source)
XLA Modules:
  0.0 14.9 jit_solution(10830715430913026724)
XLA Ops:
  0.0 0.0 copy-start.1
  0.0 0.0 copy-start
  0.0 0.0 copy-start.8
  0.0 0.0 copy-start.7
  0.0 0.0 copy-start.6
  0.0 0.0 copy-start.5
  0.0 0.0 copy-start.4
  0.0 0.0 copy-start.3
  0.0 2.3 %shard_map.182.refs_0_ = bf16[2,64,128]{2,1,0:T(8,128)(2,1)S(1)} custom-call(s32[1]{0:T(128)} %bitcast.1.core_ref, bf16[4,128]{1,0:T(4,128)(2,1)} %bitcast.4, bf16[128,64,128]{2,1,0:T(8,128)(2,1)} %pair_hbm.1), custom_call_target="tpu_custom_call" | custom-call | flops 268435456 | bytes 4194304 | tf_op jit(solution)/shard_map/pallas_call | solution.py:494
  2.4 0.0 copy-start.2
  2.4 0.0 copy-start.9
  2.4 2.4 %collective-permute-start.2 = (bf16[2,64,128]{2,1,0:T(8,128)(2,1)S(1)}, bf16[2,64,128]{2,1,0:T(8,128)(2,1)S(1)}, u32[]{:S(2)}, u32[]{:S(2)}) collective-permute-start(bf16[2,64,128]{2,1,0:T(8,128)(2,1)S(1)} %shard_map.182.refs_0_), channel_id=1, source_target_pairs={{0,3},{1,2},{2,1},{3,0},{4,7},{5,6},{6,5},{7,4},{8,11},{9,10},{10,... | collective-permute-start | bytes 98312 | tf_op jit(solution)/shard_map/ppermute | solution.py:511
  4.8 0.7 %collective-permute-start.1 = (bf16[2,64,128]{2,1,0:T(8,128)(2,1)S(1)}, bf16[2,64,128]{2,1,0:T(8,128)(2,1)S(1)}, u32[]{:S(2)}, u32[]{:S(2)}) collective-permute-start(bf16[2,64,128]{2,1,0:T(8,128)(2,1)S(1)} %shard_map.182.refs_0_), channel_id=1, source_target_pairs={{0,2},{2,0},{1,3},{3,1},{4,6},{6,4},{5,7},{7,5},{8,10},{10,8},{9,1... | collective-permute-start | bytes 98312 | tf_op jit(solution)/shard_map/ppermute | solution.py:510
  5.5 0.0 collective-permute-start
  5.6 0.0 copy-done.1
  5.6 0.0 copy-done
  5.6 0.0 copy-done.8
  5.6 0.0 copy-done.7
  5.6 0.0 copy-done.6
  5.6 0.0 copy-done.5
  5.6 0.0 copy-done.4
  5.6 0.0 copy-done.3
  5.6 3.0 %shard_map.181 = (bf16[3,512,128]{2,1,0:T(8,128)(2,1)S(1)}, bf16[3,512,128]{2,1,0:T(8,128)(2,1)S(1)}, bf16[3,512,128]{2,1,0:T(8,128)(2,1)S(1)}, bf16[3,512,128]{...) custom-call(s32[1]{0:T(128)} %bitcast.1.core_ref, ...), custom_call_target="tpu_custom_call" | custom-call | flops 1006632960 | bytes 4194304 | tf_op jit(solution)/shard_map/pallas_call | solution.py:527
  8.6 0.0 collective-permute-done.2.refs_3_
  8.6 0.2 %collective-permute-done.1.refs_2_ = bf16[2,64,128]{2,1,0:T(8,128)(2,1)S(1)} collective-permute-done((bf16[2,64,128]{2,1,0:T(8,128)(2,1)S(1)}, bf16[2,64,128]{2,1,0:T(8,128)(2,1)S(1)}, u32[]{:S(2)}, u32[]{:S(2)}) %collective-permute-start.1) | collective-permute-done | bytes 32800 | tf_op jit(solution)/shard_map/ppermute | solution.py:510
  8.8 0.0 collective-permute-done.refs_1_
  8.9 0.3 %collective-permute-start.3 = (bf16[240,128]{1,0:T(8,128)(2,1)S(1)}, bf16[240,128]{1,0:T(8,128)(2,1)S(1)}, u32[]{:S(2)}, u32[]{:S(2)}) collective-permute-start(bf16[240,128]{1,0:T(8,128)(2,1)S(1)} %get-tuple-element.35), channel_id=1, source_target_pairs={{4,0},{8,4},{12,8},{0,1},{1,5},{5,9},{9,13},{13,12},{6,2},{10,6},{... | collective-permute-start | bytes 184328 | tf_op jit(solution)/shard_map/ppermute | solution.py:558
  9.2 1.8 %collective-permute-start.4 = (bf16[240,128]{1,0:T(8,128)(2,1)S(1)}, bf16[240,128]{1,0:T(8,128)(2,1)S(1)}, u32[]{:S(2)}, u32[]{:S(2)}) collective-permute-start(bf16[240,128]{1,0:T(8,128)(2,1)S(1)} %get-tuple-element.36), channel_id=1, source_target_pairs={{0,4},{4,8},{8,12},{1,0},{5,1},{9,5},{13,9},{12,13},{2,6},{6,10},{... | collective-permute-start | bytes 184328 | tf_op jit(solution)/shard_map/ppermute | solution.py:559
  10.9 0.0 copy-done.2
  10.9 0.0 copy-done.9
  10.9 2.1 %shard_map.184 = (bf16[3,384,128]{2,1,0:T(8,128)(2,1)S(1)}, bf16[2,2,128,256]{3,2,1,0:T(8,128)(2,1)S(1)}, bf16[2,48,48]{2,1,0:T(8,128)(2,1)S(1)}, bf16[2,112,256]{2,1,0:T(8,128)(2,1)S(1)}) custom-call(s32[1]{0:T(128)} %bitcast.at_ref, s32[4,64]{1,0:T(4,128)S(1)} %copy-done.9, bf16[3,512,128]{2,1,0:T(8,128)(2,1)S(1)} %get-tuple-element.21.query_ref, ...), custom_call_target="tpu_custom_call" | custom-call | flops 603979776 | bytes 4194304 | tf_op jit(solution)/shard_map/pallas_call | solution.py:565
  13.0 0.2 %collective-permute-done.3.first_ref = bf16[240,128]{1,0:T(8,128)(2,1)S(1)} collective-permute-done((bf16[240,128]{1,0:T(8,128)(2,1)S(1)}, bf16[240,128]{1,0:T(8,128)(2,1)S(1)}, u32[]{:S(2)}, u32[]{:S(2)}) %collective-permute-start.3) | collective-permute-done | bytes 61472 | tf_op jit(solution)/shard_map/ppermute | solution.py:558
  13.2 0.0 collective-permute-done.4.second_ref
  13.3 1.6 %shard_map.185 = bf16[3,512,128]{2,1,0:T(8,128)(2,1)} custom-call(s32[1]{0:T(128)} %bitcast.at_ref, s32[1]{0:T(128)} %bitcast.1.core_ref, bf16[3,512,128]{2,1,0:T(8,128)(2,1)S(1)} %get-tuple-element.21.query_ref, bf16[3,512,128]{2,1,0:T(8,128)(2,1)S(1)} %get-tuple-element.22.key_ref.own_key_ref, ...), custom_call_target="tpu_custom_call" | custom-call | flops 201326592 | bytes 4194304 | tf_op jit(solution)/shard_map/pallas_call | solution.py:584
  (1 shorter events, 0.0 us)
Async XLA Ops:
  0.0 5.6 %copy-start.1 = (bf16[128,128]{1,0:T(8,128)(2,1)S(1)}, bf16[128,128]{1,0:T(8,128)(2,1)}, u32[]{:S(2)}) copy-start(bf16[128,128]{1,0:T(8,128)(2,1)} %w_value.3) | copy-start | bytes 98308
  0.0 5.6 %copy-start = (bf16[128,128]{1,0:T(8,128)(2,1)S(1)}, bf16[128,128]{1,0:T(8,128)(2,1)}, u32[]{:S(2)}) copy-start(bf16[128,128]{1,0:T(8,128)(2,1)} %w_key.3) | copy-start | bytes 98308
  0.0 5.6 %copy-start.8 = (bf16[128,128]{1,0:T(8,128)(2,1)S(1)}, bf16[128,128]{1,0:T(8,128)(2,1)}, u32[]{:S(2)}) copy-start(bf16[128,128]{1,0:T(8,128)(2,1)} %w_gate.1) | copy-start | bytes 98308
  0.0 5.6 %copy-start.7 = (bf16[128,128]{1,0:T(8,128)(2,1)S(1)}, bf16[128,128]{1,0:T(8,128)(2,1)}, u32[]{:S(2)}) copy-start(bf16[128,128]{1,0:T(8,128)(2,1)} %w_query.1) | copy-start | bytes 98308
  0.0 5.6 %copy-start.6 = (bf16[128,128]{1,0:T(8,128)(2,1)S(1)}, bf16[128,128]{1,0:T(8,128)(2,1)}, u32[]{:S(2)}) copy-start(bf16[128,128]{1,0:T(8,128)(2,1)} %ada_attn_shift.1) | copy-start | bytes 98308
  0.0 5.6 %copy-start.5 = (bf16[128,128]{1,0:T(8,128)(2,1)S(1)}, bf16[128,128]{1,0:T(8,128)(2,1)}, u32[]{:S(2)}) copy-start(bf16[128,128]{1,0:T(8,128)(2,1)} %ada_attn_scale.1) | copy-start | bytes 98308
  0.0 5.6 %copy-start.4 = (bf16[512,128]{1,0:T(8,128)(2,1)S(1)}, bf16[512,128]{1,0:T(8,128)(2,1)}, u32[]{:S(2)}) copy-start(bf16[512,128]{1,0:T(8,128)(2,1)} %cond_ref.1) | copy-start | bytes 393220
  0.0 5.6 %copy-start.3 = (bf16[3,512,128]{2,1,0:T(8,128)(2,1)S(1)}, bf16[3,512,128]{2,1,0:T(8,128)(2,1)}, u32[]{:S(2)}) copy-start(bf16[3,512,128]{2,1,0:T(8,128)(2,1)} %single_ref.1) | copy-start | bytes 1179652
  2.4 8.6 %copy-start.2 = (bf16[128,128]{1,0:T(8,128)(2,1)S(1)}, bf16[128,128]{1,0:T(8,128)(2,1)}, u32[]{:S(2)}) copy-start(bf16[128,128]{1,0:T(8,128)(2,1)} %w_out_ref.3) | copy-start | bytes 98308
  2.4 8.5 %copy-start.9 = (s32[4,64]{1,0:T(4,128)S(1)}, s32[4,64]{1,0:T(4,128)}, u32[]{:S(2)}) copy-start(s32[4,64]{1,0:T(4,128)} %counts_ref.1) | copy-start | bytes 3076
  2.4 6.2 %collective-permute-start.2 = (bf16[2,64,128]{2,1,0:T(8,128)(2,1)S(1)}, bf16[2,64,128]{2,1,0:T(8,128)(2,1)S(1)}, u32[]{:S(2)}, u32[]{:S(2)}) collective-permute-start(bf16[2,64,128]{2,1,0:T(8,128)(2,1)S(1)} %shard_map.182.refs_0_), channel_id=1, source_target_pairs={{0,3},{1,2},{2,1},{3,0},{4,7},{5,6},{6,5},{7,4},{8,11},{9,10},{10,... | collective-permute-start | bytes 98312 | tf_op jit(solution)/shard_map/ppermute | solution.py:511
  4.8 4.0 %collective-permute-start.1 = (bf16[2,64,128]{2,1,0:T(8,128)(2,1)S(1)}, bf16[2,64,128]{2,1,0:T(8,128)(2,1)S(1)}, u32[]{:S(2)}, u32[]{:S(2)}) collective-permute-start(bf16[2,64,128]{2,1,0:T(8,128)(2,1)S(1)} %shard_map.182.refs_0_), channel_id=1, source_target_pairs={{0,2},{2,0},{1,3},{3,1},{4,6},{6,4},{5,7},{7,5},{8,10},{10,8},{9,1... | collective-permute-start | bytes 98312 | tf_op jit(solution)/shard_map/ppermute | solution.py:510
  5.5 3.3 %collective-permute-start = (bf16[2,64,128]{2,1,0:T(8,128)(2,1)S(1)}, bf16[2,64,128]{2,1,0:T(8,128)(2,1)S(1)}, u32[]{:S(2)}, u32[]{:S(2)}) collective-permute-start(bf16[2,64,128]{2,1,0:T(8,128)(2,1)S(1)} %shard_map.182.refs_0_), channel_id=1, source_target_pairs={{0,1},{1,0},{2,3},{3,2},{4,5},{5,4},{6,7},{7,6},{8,9},{9,8},{10,11... | collective-permute-start | bytes 98312 | tf_op jit(solution)/shard_map/ppermute | solution.py:512
  8.9 4.4 %collective-permute-start.3 = (bf16[240,128]{1,0:T(8,128)(2,1)S(1)}, bf16[240,128]{1,0:T(8,128)(2,1)S(1)}, u32[]{:S(2)}, u32[]{:S(2)}) collective-permute-start(bf16[240,128]{1,0:T(8,128)(2,1)S(1)} %get-tuple-element.35), channel_id=1, source_target_pairs={{4,0},{8,4},{12,8},{0,1},{1,5},{5,9},{9,13},{13,12},{6,2},{10,6},{... | collective-permute-start | bytes 184328 | tf_op jit(solution)/shard_map/ppermute | solution.py:558
  9.2 4.1 %collective-permute-start.4 = (bf16[240,128]{1,0:T(8,128)(2,1)S(1)}, bf16[240,128]{1,0:T(8,128)(2,1)S(1)}, u32[]{:S(2)}, u32[]{:S(2)}) collective-permute-start(bf16[240,128]{1,0:T(8,128)(2,1)S(1)} %get-tuple-element.36), channel_id=1, source_target_pairs={{0,4},{4,8},{8,12},{1,0},{5,1},{9,5},{13,9},{12,13},{2,6},{6,10},{... | collective-permute-start | bytes 184328 | tf_op jit(solution)/shard_map/ppermute | solution.py:559

commit v21 on v20

--- a/solution.py
+++ b/solution.py
@@ -81,32 +81,32 @@
     group = GROUP
     lanes = heads * group
     half = group // 2
-    pieces = rows // half
+    piece = rows // pair_sem.shape[0]
     row_start = core_ref[0] * rows
 
     def pair_copy(i):
-        source = pair_hbm.at[pl.ds(row_start + i * half, half)]
-        return pltpu.make_async_copy(source, pair_ref.at[pl.ds(i * half, half)], pair_sem.at[i])
+        source = pair_hbm.at[pl.ds(row_start + i * piece, piece)]
+        return pltpu.make_async_copy(source, pair_ref.at[pl.ds(i * piece, piece)], pair_sem.at[i])
 
     w_pair_copy = pltpu.make_async_copy(w_pair_hbm, w_pair_ref, sem)
+    for i in range(pair_sem.shape[0]):
+        pair_copy(i).start()
     w_pair_copy.start()
-    for i in range(pieces):
-        pair_copy(i).start()
+
+    centre = twice(centring(width))
+    chunks = []
+    for chunk in range(rows // group):
+        for i in range(group // piece):
+            pair_copy(chunk * (group // piece) + i).wait()
+        pair = pair_ref[chunk * group : (chunk + 1) * group].reshape(group * cols, width)
+        chunks.append(dot(side_by_side(pair), centre))
     w_pair_copy.wait()
     w_pair = w_pair_ref[...].astype(F32)
     spread = jnp.concatenate(
         [jnp.broadcast_to(w_pair[h : h + 1], (group, width)) for h in range(heads)], 0
     )
     mix = twice(spread.T.astype(BF16))
-    centre = twice(centring(width))
     slot = iota((cols, lanes), 1) % group
-
-    chunks = []
-    for chunk in range(rows // group):
-        for part in range(2):
-            pair_copy(chunk * 2 + part).wait()
-        pair = pair_ref[chunk * group : (chunk + 1) * group].reshape(group * cols, width)
-        chunks.append(dot(side_by_side(pair), centre))
     mixes = [dot(centred.astype(BF16), mix).reshape(half, cols, 2 * lanes) for centred in chunks]
     squares = [(centred[:, :width] * centred[:, :width]).astype(BF16) for centred in chunks]
     averages = [
@@ -499,7 +499,7 @@
         scratch_shapes=[
             pltpu.VMEM((heads, width), BF16),
             pltpu.VMEM((tok_here, cols, width), BF16),
-            pltpu.SemaphoreType.DMA((2 * groups,)),
+            pltpu.SemaphoreType.DMA((8 * groups,)),
             pltpu.SemaphoreType.DMA,
         ],
         compiler_params=params,

time: 15.1 us -> 15.7 us (1.040)
  Pallas kernels: 9.09 us -> 9.66 us
    pallas_call x1, Pallas kernels: 2.33 us -> 2.9 us  [shards(): pl.pallas_call(pair_kernel, in_specs=[IN_SMEM] + [IN_HBM] * 2, out_specs=...]
  transfers between devices with their start and end apart: 5 -> 5, of which waited for: 2 -> 2; matrix products, arithmetic and copies ran while one was open for 0% -> 0% of each run, Pallas kernels for 34% -> 33%
where the time goes in v21:
time: 15.7 us; the launch traced here: 15.5 us
  Pallas kernels  9.66 us (62%)
  starting transfers between devices  5.21 us (33%)
  waiting for transfers between devices  0.45 us (3%)
    pallas_call x1, Pallas kernels, shards(): pl.pallas_call(project_kernel, in_specs=[IN_SMEM] + [IN_VMEM] * len(opera...  2.99 us
    pallas_call x1, Pallas kernels, shards(): pl.pallas_call(pair_kernel, in_specs=[IN_SMEM] + [IN_HBM] * 2, out_specs=...  2.9 us
    ppermute x1, starting transfers between devices, shards(): lax.ppermute(own, ('pair', 'samp'), [(0, 3), (1, 2), (2, 1), (3, 0)])  2.48 us
    pallas_call x1, Pallas kernels, shards(): pl.pallas_call(functools.partial(inner_kernel, heads, blocks), in_specs=[...  2.08 us
    ppermute x1, starting transfers between devices, shards(): lax.ppermute(far, ('atoms', 'samp'), [(target, source) for source, target...  1.75 us
    pallas_call x1, Pallas kernels, shards(): pl.pallas_call(functools.partial(outer_kernel, heads, blocks, groups), in...  1.64 us
    ppermute x1, starting transfers between devices, shards(): across = lax.ppermute(own, 'pair', swapped)  0.65 us
  transfers between devices with their start and end apart: 5, of which 2 were waited for; matrix products, arithmetic and copies ran while one was open for 0% of the time, Pallas kernels for 33%

profile of v21, /device:TPU:0, one launch (start us, length us, event | category | flops | bytes accessed | tf_op | source)
XLA Modules:
  0.0 15.5 jit_solution(17834266282951168312)
XLA Ops:
  0.0 0.0 copy-start.1
  0.0 0.0 copy-start
  0.0 0.0 copy-start.8
  0.0 0.0 copy-start.7
  0.0 0.0 copy-start.6
  0.0 0.0 copy-start.5
  0.0 0.0 copy-start.4
  0.0 0.0 copy-start.3
  0.0 2.9 %shard_map.182.refs_0_ = bf16[2,64,128]{2,1,0:T(8,128)(2,1)S(1)} custom-call(s32[1]{0:T(128)} %bitcast.1.core_ref, bf16[4,128]{1,0:T(4,128)(2,1)} %bitcast.4, bf16[128,64,128]{2,1,0:T(8,128)(2,1)} %pair_hbm.1), custom_call_target="tpu_custom_call" | custom-call | flops 268435456 | bytes 4194304 | tf_op jit(solution)/shard_map/pallas_call | solution.py:494
  3.0 0.0 copy-start.2
  3.0 0.0 copy-start.9
  3.0 2.5 %collective-permute-start.2 = (bf16[2,64,128]{2,1,0:T(8,128)(2,1)S(1)}, bf16[2,64,128]{2,1,0:T(8,128)(2,1)S(1)}, u32[]{:S(2)}, u32[]{:S(2)}) collective-permute-start(bf16[2,64,128]{2,1,0:T(8,128)(2,1)S(1)} %shard_map.182.refs_0_), channel_id=1, source_target_pairs={{0,3},{1,2},{2,1},{3,0},{4,7},{5,6},{6,5},{7,4},{8,11},{9,10},{10,... | collective-permute-start | bytes 98312 | tf_op jit(solution)/shard_map/ppermute | solution.py:511
  5.5 0.6 %collective-permute-start.1 = (bf16[2,64,128]{2,1,0:T(8,128)(2,1)S(1)}, bf16[2,64,128]{2,1,0:T(8,128)(2,1)S(1)}, u32[]{:S(2)}, u32[]{:S(2)}) collective-permute-start(bf16[2,64,128]{2,1,0:T(8,128)(2,1)S(1)} %shard_map.182.refs_0_), channel_id=1, source_target_pairs={{0,2},{2,0},{1,3},{3,1},{4,6},{6,4},{5,7},{7,5},{8,10},{10,8},{9,1... | collective-permute-start | bytes 98312 | tf_op jit(solution)/shard_map/ppermute | solution.py:510
  6.1 0.0 collective-permute-start
  6.2 0.0 copy-done.1
  6.2 0.0 copy-done
  6.2 0.0 copy-done.8
  6.2 0.0 copy-done.7
  6.2 0.0 copy-done.6
  6.2 0.0 copy-done.5
  6.2 0.0 copy-done.4
  6.2 0.0 copy-done.3
  6.2 3.0 %shard_map.181 = (bf16[3,512,128]{2,1,0:T(8,128)(2,1)S(1)}, bf16[3,512,128]{2,1,0:T(8,128)(2,1)S(1)}, bf16[3,512,128]{2,1,0:T(8,128)(2,1)S(1)}, bf16[3,512,128]{...) custom-call(s32[1]{0:T(128)} %bitcast.1.core_ref, ...), custom_call_target="tpu_custom_call" | custom-call | flops 1006632960 | bytes 4194304 | tf_op jit(solution)/shard_map/pallas_call | solution.py:527
  9.2 0.0 collective-permute-done.2.refs_3_
  9.2 0.2 %collective-permute-done.1.refs_2_ = bf16[2,64,128]{2,1,0:T(8,128)(2,1)S(1)} collective-permute-done((bf16[2,64,128]{2,1,0:T(8,128)(2,1)S(1)}, bf16[2,64,128]{2,1,0:T(8,128)(2,1)S(1)}, u32[]{:S(2)}, u32[]{:S(2)}) %collective-permute-start.1) | collective-permute-done | bytes 32800 | tf_op jit(solution)/shard_map/ppermute | solution.py:510
  9.4 0.0 collective-permute-done.refs_1_
  9.5 0.3 %collective-permute-start.3 = (bf16[240,128]{1,0:T(8,128)(2,1)S(1)}, bf16[240,128]{1,0:T(8,128)(2,1)S(1)}, u32[]{:S(2)}, u32[]{:S(2)}) collective-permute-start(bf16[240,128]{1,0:T(8,128)(2,1)S(1)} %get-tuple-element.35), channel_id=1, source_target_pairs={{4,0},{8,4},{12,8},{0,1},{1,5},{5,9},{9,13},{13,12},{6,2},{10,6},{... | collective-permute-start | bytes 184328 | tf_op jit(solution)/shard_map/ppermute | solution.py:558
  9.8 1.8 %collective-permute-start.4 = (bf16[240,128]{1,0:T(8,128)(2,1)S(1)}, bf16[240,128]{1,0:T(8,128)(2,1)S(1)}, u32[]{:S(2)}, u32[]{:S(2)}) collective-permute-start(bf16[240,128]{1,0:T(8,128)(2,1)S(1)} %get-tuple-element.36), channel_id=1, source_target_pairs={{0,4},{4,8},{8,12},{1,0},{5,1},{9,5},{13,9},{12,13},{2,6},{6,10},{... | collective-permute-start | bytes 184328 | tf_op jit(solution)/shard_map/ppermute | solution.py:559
  11.5 0.0 copy-done.2
  11.5 0.0 copy-done.9
  11.5 2.1 %shard_map.184 = (bf16[3,384,128]{2,1,0:T(8,128)(2,1)S(1)}, bf16[2,2,128,256]{3,2,1,0:T(8,128)(2,1)S(1)}, bf16[2,48,48]{2,1,0:T(8,128)(2,1)S(1)}, bf16[2,112,256]{2,1,0:T(8,128)(2,1)S(1)}) custom-call(s32[1]{0:T(128)} %bitcast.at_ref, s32[4,64]{1,0:T(4,128)S(1)} %copy-done.9, bf16[3,512,128]{2,1,0:T(8,128)(2,1)S(1)} %get-tuple-element.21.query_ref, ...), custom_call_target="tpu_custom_call" | custom-call | flops 603979776 | bytes 4194304 | tf_op jit(solution)/shard_map/pallas_call | solution.py:565
  13.6 0.2 %collective-permute-done.3.first_ref = bf16[240,128]{1,0:T(8,128)(2,1)S(1)} collective-permute-done((bf16[240,128]{1,0:T(8,128)(2,1)S(1)}, bf16[240,128]{1,0:T(8,128)(2,1)S(1)}, u32[]{:S(2)}, u32[]{:S(2)}) %collective-permute-start.3) | collective-permute-done | bytes 61472 | tf_op jit(solution)/shard_map/ppermute | solution.py:558
  13.9 0.0 collective-permute-done.4.second_ref
  13.9 1.6 %shard_map.185 = bf16[3,512,128]{2,1,0:T(8,128)(2,1)} custom-call(s32[1]{0:T(128)} %bitcast.at_ref, s32[1]{0:T(128)} %bitcast.1.core_ref, bf16[3,512,128]{2,1,0:T(8,128)(2,1)S(1)} %get-tuple-element.21.query_ref, bf16[3,512,128]{2,1,0:T(8,128)(2,1)S(1)} %get-tuple-element.22.key_ref.own_key_ref, ...), custom_call_target="tpu_custom_call" | custom-call | flops 201326592 | bytes 4194304 | tf_op jit(solution)/shard_map/pallas_call | solution.py:584
  (1 shorter events, 0.0 us)
Async XLA Ops:
  0.0 6.2 %copy-start.1 = (bf16[128,128]{1,0:T(8,128)(2,1)S(1)}, bf16[128,128]{1,0:T(8,128)(2,1)}, u32[]{:S(2)}) copy-start(bf16[128,128]{1,0:T(8,128)(2,1)} %w_value.3) | copy-start | bytes 98308
  0.0 6.2 %copy-start = (bf16[128,128]{1,0:T(8,128)(2,1)S(1)}, bf16[128,128]{1,0:T(8,128)(2,1)}, u32[]{:S(2)}) copy-start(bf16[128,128]{1,0:T(8,128)(2,1)} %w_key.3) | copy-start | bytes 98308
  0.0 6.2 %copy-start.8 = (bf16[128,128]{1,0:T(8,128)(2,1)S(1)}, bf16[128,128]{1,0:T(8,128)(2,1)}, u32[]{:S(2)}) copy-start(bf16[128,128]{1,0:T(8,128)(2,1)} %w_gate.1) | copy-start | bytes 98308
  0.0 6.2 %copy-start.7 = (bf16[128,128]{1,0:T(8,128)(2,1)S(1)}, bf16[128,128]{1,0:T(8,128)(2,1)}, u32[]{:S(2)}) copy-start(bf16[128,128]{1,0:T(8,128)(2,1)} %w_query.1) | copy-start | bytes 98308
  0.0 6.2 %copy-start.6 = (bf16[128,128]{1,0:T(8,128)(2,1)S(1)}, bf16[128,128]{1,0:T(8,128)(2,1)}, u32[]{:S(2)}) copy-start(bf16[128,128]{1,0:T(8,128)(2,1)} %ada_attn_shift.1) | copy-start | bytes 98308
  0.0 6.2 %copy-start.5 = (bf16[128,128]{1,0:T(8,128)(2,1)S(1)}, bf16[128,128]{1,0:T(8,128)(2,1)}, u32[]{:S(2)}) copy-start(bf16[128,128]{1,0:T(8,128)(2,1)} %ada_attn_scale.1) | copy-start | bytes 98308
  0.0 6.2 %copy-start.4 = (bf16[512,128]{1,0:T(8,128)(2,1)S(1)}, bf16[512,128]{1,0:T(8,128)(2,1)}, u32[]{:S(2)}) copy-start(bf16[512,128]{1,0:T(8,128)(2,1)} %cond_ref.1) | copy-start | bytes 393220
  0.0 6.2 %copy-start.3 = (bf16[3,512,128]{2,1,0:T(8,128)(2,1)S(1)}, bf16[3,512,128]{2,1,0:T(8,128)(2,1)}, u32[]{:S(2)}) copy-start(bf16[3,512,128]{2,1,0:T(8,128)(2,1)} %single_ref.1) | copy-start | bytes 1179652
  3.0 8.6 %copy-start.2 = (bf16[128,128]{1,0:T(8,128)(2,1)S(1)}, bf16[128,128]{1,0:T(8,128)(2,1)}, u32[]{:S(2)}) copy-start(bf16[128,128]{1,0:T(8,128)(2,1)} %w_out_ref.3) | copy-start | bytes 98308
  3.0 8.6 %copy-start.9 = (s32[4,64]{1,0:T(4,128)S(1)}, s32[4,64]{1,0:T(4,128)}, u32[]{:S(2)}) copy-start(s32[4,64]{1,0:T(4,128)} %counts_ref.1) | copy-start | bytes 3076
  3.0 6.2 %collective-permute-start.2 = (bf16[2,64,128]{2,1,0:T(8,128)(2,1)S(1)}, bf16[2,64,128]{2,1,0:T(8,128)(2,1)S(1)}, u32[]{:S(2)}, u32[]{:S(2)}) collective-permute-start(bf16[2,64,128]{2,1,0:T(8,128)(2,1)S(1)} %shard_map.182.refs_0_), channel_id=1, source_target_pairs={{0,3},{1,2},{2,1},{3,0},{4,7},{5,6},{6,5},{7,4},{8,11},{9,10},{10,... | collective-permute-start | bytes 98312 | tf_op jit(solution)/shard_map/ppermute | solution.py:511
  5.5 4.0 %collective-permute-start.1 = (bf16[2,64,128]{2,1,0:T(8,128)(2,1)S(1)}, bf16[2,64,128]{2,1,0:T(8,128)(2,1)S(1)}, u32[]{:S(2)}, u32[]{:S(2)}) collective-permute-start(bf16[2,64,128]{2,1,0:T(8,128)(2,1)S(1)} %shard_map.182.refs_0_), channel_id=1, source_target_pairs={{0,2},{2,0},{1,3},{3,1},{4,6},{6,4},{5,7},{7,5},{8,10},{10,8},{9,1... | collective-permute-start | bytes 98312 | tf_op jit(solution)/shard_map/ppermute | solution.py:510
  6.1 3.3 %collective-permute-start = (bf16[2,64,128]{2,1,0:T(8,128)(2,1)S(1)}, bf16[2,64,128]{2,1,0:T(8,128)(2,1)S(1)}, u32[]{:S(2)}, u32[]{:S(2)}) collective-permute-start(bf16[2,64,128]{2,1,0:T(8,128)(2,1)S(1)} %shard_map.182.refs_0_), channel_id=1, source_target_pairs={{0,1},{1,0},{2,3},{3,2},{4,5},{5,4},{6,7},{7,6},{8,9},{9,8},{10,11... | collective-permute-start | bytes 98312 | tf_op jit(solution)/shard_map/ppermute | solution.py:512
  9.5 4.4 %collective-permute-start.3 = (bf16[240,128]{1,0:T(8,128)(2,1)S(1)}, bf16[240,128]{1,0:T(8,128)(2,1)S(1)}, u32[]{:S(2)}, u32[]{:S(2)}) collective-permute-start(bf16[240,128]{1,0:T(8,128)(2,1)S(1)} %get-tuple-element.35), channel_id=1, source_target_pairs={{4,0},{8,4},{12,8},{0,1},{1,5},{5,9},{9,13},{13,12},{6,2},{10,6},{... | collective-permute-start | bytes 184328 | tf_op jit(solution)/shard_map/ppermute | solution.py:558
  9.8 4.1 %collective-permute-start.4 = (bf16[240,128]{1,0:T(8,128)(2,1)S(1)}, bf16[240,128]{1,0:T(8,128)(2,1)S(1)}, u32[]{:S(2)}, u32[]{:S(2)}) collective-permute-start(bf16[240,128]{1,0:T(8,128)(2,1)S(1)} %get-tuple-element.36), channel_id=1, source_target_pairs={{0,4},{4,8},{8,12},{1,0},{5,1},{9,5},{13,9},{12,13},{2,6},{6,10},{... | collective-permute-start | bytes 184328 | tf_op jit(solution)/shard_map/ppermute | solution.py:559

commit v22 on v20

--- a/solution.py
+++ b/solution.py
@@ -81,16 +81,15 @@
     group = GROUP
     lanes = heads * group
     half = group // 2
-    pieces = rows // half
     row_start = core_ref[0] * rows
 
     def pair_copy(i):
-        source = pair_hbm.at[pl.ds(row_start + i * half, half)]
-        return pltpu.make_async_copy(source, pair_ref.at[pl.ds(i * half, half)], pair_sem.at[i])
+        source = pair_hbm.at[pl.ds(row_start + i * group, group)]
+        return pltpu.make_async_copy(source, pair_ref.at[pl.ds(i * group, group)], pair_sem.at[i])
 
     w_pair_copy = pltpu.make_async_copy(w_pair_hbm, w_pair_ref, sem)
     w_pair_copy.start()
-    for i in range(pieces):
+    for i in range(rows // group):
         pair_copy(i).start()
     w_pair_copy.wait()
     w_pair = w_pair_ref[...].astype(F32)
@@ -103,12 +102,11 @@
 
     chunks = []
     for chunk in range(rows // group):
-        for part in range(2):
-            pair_copy(chunk * 2 + part).wait()
+        pair_copy(chunk).wait()
         pair = pair_ref[chunk * group : (chunk + 1) * group].reshape(group * cols, width)
-        chunks.append(dot(side_by_side(pair), centre))
-    mixes = [dot(centred.astype(BF16), mix).reshape(half, cols, 2 * lanes) for centred in chunks]
-    squares = [(centred[:, :width] * centred[:, :width]).astype(BF16) for centred in chunks]
+        chunks.append(dot(side_by_side(pair), centre).astype(BF16))
+    mixes = [dot(centred, mix).reshape(half, cols, 2 * lanes) for centred in chunks]
+    squares = [centred[:, :width] * centred[:, :width] for centred in chunks]
     averages = [
         dot(jnp.concatenate(squares[i : i + 2], 1), twice(averaging(width)))
         for i in range(0, len(squares), 2)
@@ -117,7 +115,7 @@
         pick = slice(chunk % 2 * width, (chunk % 2 + 1) * width)
         variances = [
             averages[chunk // 2][:, pick].reshape(half, cols, width),
-            mean_square(centred[:, width:]).reshape(half, cols, 1),
+            mean_square(centred[:, width:].astype(F32)).reshape(half, cols, 1),
         ]
         total = jnp.zeros((cols, lanes), F32)
         spread_out = jnp.zeros((cols, lanes), F32)
@@ -499,7 +497,7 @@
         scratch_shapes=[
             pltpu.VMEM((heads, width), BF16),
             pltpu.VMEM((tok_here, cols, width), BF16),
-            pltpu.SemaphoreType.DMA((2 * groups,)),
+            pltpu.SemaphoreType.DMA((groups,)),
             pltpu.SemaphoreType.DMA,
         ],
         compiler_params=params,

time: 15.1 us -> 15 us (level)
  no operation moved by 1% of the time
where the time goes in v22:
time: 15 us; the launch traced here: 14.8 us
  Pallas kernels  9.02 us (60%)
  starting transfers between devices  5.21 us (35%)
  waiting for transfers between devices  0.44 us (3%)
    pallas_call x1, Pallas kernels, shards(): pl.pallas_call(project_kernel, in_specs=[IN_SMEM] + [IN_VMEM] * len(opera...  2.99 us
    ppermute x1, starting transfers between devices, shards(): lax.ppermute(own, ('pair', 'samp'), [(0, 3), (1, 2), (2, 1), (3, 0)])  2.49 us
    pallas_call x1, Pallas kernels, shards(): pl.pallas_call(pair_kernel, in_specs=[IN_SMEM] + [IN_HBM] * 2, out_specs=...  2.26 us
    pallas_call x1, Pallas kernels, shards(): pl.pallas_call(functools.partial(inner_kernel, heads, blocks), in_specs=[...  2.08 us
    ppermute x1, starting transfers between devices, shards(): lax.ppermute(far, ('atoms', 'samp'), [(target, source) for source, target...  1.75 us
    pallas_call x1, Pallas kernels, shards(): pl.pallas_call(functools.partial(outer_kernel, heads, blocks, groups), in...  1.64 us
    ppermute x1, starting transfers between devices, shards(): across = lax.ppermute(own, 'pair', swapped)  0.64 us
  transfers between devices with their start and end apart: 5, of which 2 were waited for; matrix products, arithmetic and copies ran while one was open for 0% of the time, Pallas kernels for 34%

profile of v22, /device:TPU:0, one launch (start us, length us, event | category | flops | bytes accessed | tf_op | source)
XLA Modules:
  0.0 14.8 jit_solution(15806029412386405917)
XLA Ops:
  0.0 0.0 copy-start.1
  0.0 0.0 copy-start
  0.0 0.0 copy-start.8
  0.0 0.0 copy-start.7
  0.0 0.0 copy-start.6
  0.0 0.0 copy-start.5
  0.0 0.0 copy-start.4
  0.0 0.0 copy-start.3
  0.0 2.3 %shard_map.182.refs_0_ = bf16[2,64,128]{2,1,0:T(8,128)(2,1)S(1)} custom-call(s32[1]{0:T(128)} %bitcast.1.core_ref, bf16[4,128]{1,0:T(4,128)(2,1)} %bitcast.4, bf16[128,64,128]{2,1,0:T(8,128)(2,1)} %pair_hbm.1), custom_call_target="tpu_custom_call" | custom-call | flops 268435456 | bytes 4194304 | tf_op jit(solution)/shard_map/pallas_call | solution.py:492
  2.3 0.0 copy-start.2
  2.3 0.0 copy-start.9
  2.3 2.5 %collective-permute-start.2 = (bf16[2,64,128]{2,1,0:T(8,128)(2,1)S(1)}, bf16[2,64,128]{2,1,0:T(8,128)(2,1)S(1)}, u32[]{:S(2)}, u32[]{:S(2)}) collective-permute-start(bf16[2,64,128]{2,1,0:T(8,128)(2,1)S(1)} %shard_map.182.refs_0_), channel_id=1, source_target_pairs={{0,3},{1,2},{2,1},{3,0},{4,7},{5,6},{6,5},{7,4},{8,11},{9,10},{10,... | collective-permute-start | bytes 98312 | tf_op jit(solution)/shard_map/ppermute | solution.py:509
  4.8 0.6 %collective-permute-start.1 = (bf16[2,64,128]{2,1,0:T(8,128)(2,1)S(1)}, bf16[2,64,128]{2,1,0:T(8,128)(2,1)S(1)}, u32[]{:S(2)}, u32[]{:S(2)}) collective-permute-start(bf16[2,64,128]{2,1,0:T(8,128)(2,1)S(1)} %shard_map.182.refs_0_), channel_id=1, source_target_pairs={{0,2},{2,0},{1,3},{3,1},{4,6},{6,4},{5,7},{7,5},{8,10},{10,8},{9,1... | collective-permute-start | bytes 98312 | tf_op jit(solution)/shard_map/ppermute | solution.py:508
  5.5 0.0 collective-permute-start
  5.5 0.0 copy-done.1
  5.5 0.0 copy-done
  5.5 0.0 copy-done.8
  5.5 0.0 copy-done.7
  5.5 0.0 copy-done.6
  5.5 0.0 copy-done.5
  5.5 0.0 copy-done.4
  5.6 0.0 copy-done.3
  5.6 3.0 %shard_map.181 = (bf16[3,512,128]{2,1,0:T(8,128)(2,1)S(1)}, bf16[3,512,128]{2,1,0:T(8,128)(2,1)S(1)}, bf16[3,512,128]{2,1,0:T(8,128)(2,1)S(1)}, bf16[3,512,128]{...) custom-call(s32[1]{0:T(128)} %bitcast.1.core_ref, ...), custom_call_target="tpu_custom_call" | custom-call | flops 1006632960 | bytes 4194304 | tf_op jit(solution)/shard_map/pallas_call | solution.py:525
  8.6 0.0 collective-permute-done.2.refs_3_
  8.6 0.2 %collective-permute-done.1.refs_2_ = bf16[2,64,128]{2,1,0:T(8,128)(2,1)S(1)} collective-permute-done((bf16[2,64,128]{2,1,0:T(8,128)(2,1)S(1)}, bf16[2,64,128]{2,1,0:T(8,128)(2,1)S(1)}, u32[]{:S(2)}, u32[]{:S(2)}) %collective-permute-start.1) | collective-permute-done | bytes 32800 | tf_op jit(solution)/shard_map/ppermute | solution.py:508
  8.8 0.0 collective-permute-done.refs_1_
  8.9 0.3 %collective-permute-start.3 = (bf16[240,128]{1,0:T(8,128)(2,1)S(1)}, bf16[240,128]{1,0:T(8,128)(2,1)S(1)}, u32[]{:S(2)}, u32[]{:S(2)}) collective-permute-start(bf16[240,128]{1,0:T(8,128)(2,1)S(1)} %get-tuple-element.35), channel_id=1, source_target_pairs={{4,0},{8,4},{12,8},{0,1},{1,5},{5,9},{9,13},{13,12},{6,2},{10,6},{... | collective-permute-start | bytes 184328 | tf_op jit(solution)/shard_map/ppermute | solution.py:556
  9.1 1.7 %collective-permute-start.4 = (bf16[240,128]{1,0:T(8,128)(2,1)S(1)}, bf16[240,128]{1,0:T(8,128)(2,1)S(1)}, u32[]{:S(2)}, u32[]{:S(2)}) collective-permute-start(bf16[240,128]{1,0:T(8,128)(2,1)S(1)} %get-tuple-element.36), channel_id=1, source_target_pairs={{0,4},{4,8},{8,12},{1,0},{5,1},{9,5},{13,9},{12,13},{2,6},{6,10},{... | collective-permute-start | bytes 184328 | tf_op jit(solution)/shard_map/ppermute | solution.py:557
  10.9 0.0 copy-done.2
  10.9 0.0 copy-done.9
  10.9 2.1 %shard_map.184 = (bf16[3,384,128]{2,1,0:T(8,128)(2,1)S(1)}, bf16[2,2,128,256]{3,2,1,0:T(8,128)(2,1)S(1)}, bf16[2,48,48]{2,1,0:T(8,128)(2,1)S(1)}, bf16[2,112,256]{2,1,0:T(8,128)(2,1)S(1)}) custom-call(s32[1]{0:T(128)} %bitcast.at_ref, s32[4,64]{1,0:T(4,128)S(1)} %copy-done.9, bf16[3,512,128]{2,1,0:T(8,128)(2,1)S(1)} %get-tuple-element.21.query_ref, ...), custom_call_target="tpu_custom_call" | custom-call | flops 603979776 | bytes 4194304 | tf_op jit(solution)/shard_map/pallas_call | solution.py:563
  13.0 0.2 %collective-permute-done.3.first_ref = bf16[240,128]{1,0:T(8,128)(2,1)S(1)} collective-permute-done((bf16[240,128]{1,0:T(8,128)(2,1)S(1)}, bf16[240,128]{1,0:T(8,128)(2,1)S(1)}, u32[]{:S(2)}, u32[]{:S(2)}) %collective-permute-start.3) | collective-permute-done | bytes 61472 | tf_op jit(solution)/shard_map/ppermute | solution.py:556
  13.2 0.0 collective-permute-done.4.second_ref
  13.2 1.6 %shard_map.185 = bf16[3,512,128]{2,1,0:T(8,128)(2,1)} custom-call(s32[1]{0:T(128)} %bitcast.at_ref, s32[1]{0:T(128)} %bitcast.1.core_ref, bf16[3,512,128]{2,1,0:T(8,128)(2,1)S(1)} %get-tuple-element.21.query_ref, bf16[3,512,128]{2,1,0:T(8,128)(2,1)S(1)} %get-tuple-element.22.key_ref.own_key_ref, ...), custom_call_target="tpu_custom_call" | custom-call | flops 201326592 | bytes 4194304 | tf_op jit(solution)/shard_map/pallas_call | solution.py:582
  (1 shorter events, 0.0 us)
Async XLA Ops:
  0.0 5.5 %copy-start.1 = (bf16[128,128]{1,0:T(8,128)(2,1)S(1)}, bf16[128,128]{1,0:T(8,128)(2,1)}, u32[]{:S(2)}) copy-start(bf16[128,128]{1,0:T(8,128)(2,1)} %w_value.3) | copy-start | bytes 98308
  0.0 5.5 %copy-start = (bf16[128,128]{1,0:T(8,128)(2,1)S(1)}, bf16[128,128]{1,0:T(8,128)(2,1)}, u32[]{:S(2)}) copy-start(bf16[128,128]{1,0:T(8,128)(2,1)} %w_key.3) | copy-start | bytes 98308
  0.0 5.5 %copy-start.8 = (bf16[128,128]{1,0:T(8,128)(2,1)S(1)}, bf16[128,128]{1,0:T(8,128)(2,1)}, u32[]{:S(2)}) copy-start(bf16[128,128]{1,0:T(8,128)(2,1)} %w_gate.1) | copy-start | bytes 98308
  0.0 5.5 %copy-start.7 = (bf16[128,128]{1,0:T(8,128)(2,1)S(1)}, bf16[128,128]{1,0:T(8,128)(2,1)}, u32[]{:S(2)}) copy-start(bf16[128,128]{1,0:T(8,128)(2,1)} %w_query.1) | copy-start | bytes 98308
  0.0 5.5 %copy-start.6 = (bf16[128,128]{1,0:T(8,128)(2,1)S(1)}, bf16[128,128]{1,0:T(8,128)(2,1)}, u32[]{:S(2)}) copy-start(bf16[128,128]{1,0:T(8,128)(2,1)} %ada_attn_shift.1) | copy-start | bytes 98308
  0.0 5.5 %copy-start.5 = (bf16[128,128]{1,0:T(8,128)(2,1)S(1)}, bf16[128,128]{1,0:T(8,128)(2,1)}, u32[]{:S(2)}) copy-start(bf16[128,128]{1,0:T(8,128)(2,1)} %ada_attn_scale.1) | copy-start | bytes 98308
  0.0 5.5 %copy-start.4 = (bf16[512,128]{1,0:T(8,128)(2,1)S(1)}, bf16[512,128]{1,0:T(8,128)(2,1)}, u32[]{:S(2)}) copy-start(bf16[512,128]{1,0:T(8,128)(2,1)} %cond_ref.1) | copy-start | bytes 393220
  0.0 5.5 %copy-start.3 = (bf16[3,512,128]{2,1,0:T(8,128)(2,1)S(1)}, bf16[3,512,128]{2,1,0:T(8,128)(2,1)}, u32[]{:S(2)}) copy-start(bf16[3,512,128]{2,1,0:T(8,128)(2,1)} %single_ref.1) | copy-start | bytes 1179652
  2.3 8.6 %copy-start.2 = (bf16[128,128]{1,0:T(8,128)(2,1)S(1)}, bf16[128,128]{1,0:T(8,128)(2,1)}, u32[]{:S(2)}) copy-start(bf16[128,128]{1,0:T(8,128)(2,1)} %w_out_ref.3) | copy-start | bytes 98308
  2.3 8.6 %copy-start.9 = (s32[4,64]{1,0:T(4,128)S(1)}, s32[4,64]{1,0:T(4,128)}, u32[]{:S(2)}) copy-start(s32[4,64]{1,0:T(4,128)} %counts_ref.1) | copy-start | bytes 3076
  2.3 6.2 %collective-permute-start.2 = (bf16[2,64,128]{2,1,0:T(8,128)(2,1)S(1)}, bf16[2,64,128]{2,1,0:T(8,128)(2,1)S(1)}, u32[]{:S(2)}, u32[]{:S(2)}) collective-permute-start(bf16[2,64,128]{2,1,0:T(8,128)(2,1)S(1)} %shard_map.182.refs_0_), channel_id=1, source_target_pairs={{0,3},{1,2},{2,1},{3,0},{4,7},{5,6},{6,5},{7,4},{8,11},{9,10},{10,... | collective-permute-start | bytes 98312 | tf_op jit(solution)/shard_map/ppermute | solution.py:509
  4.8 4.0 %collective-permute-start.1 = (bf16[2,64,128]{2,1,0:T(8,128)(2,1)S(1)}, bf16[2,64,128]{2,1,0:T(8,128)(2,1)S(1)}, u32[]{:S(2)}, u32[]{:S(2)}) collective-permute-start(bf16[2,64,128]{2,1,0:T(8,128)(2,1)S(1)} %shard_map.182.refs_0_), channel_id=1, source_target_pairs={{0,2},{2,0},{1,3},{3,1},{4,6},{6,4},{5,7},{7,5},{8,10},{10,8},{9,1... | collective-permute-start | bytes 98312 | tf_op jit(solution)/shard_map/ppermute | solution.py:508
  5.5 3.3 %collective-permute-start = (bf16[2,64,128]{2,1,0:T(8,128)(2,1)S(1)}, bf16[2,64,128]{2,1,0:T(8,128)(2,1)S(1)}, u32[]{:S(2)}, u32[]{:S(2)}) collective-permute-start(bf16[2,64,128]{2,1,0:T(8,128)(2,1)S(1)} %shard_map.182.refs_0_), channel_id=1, source_target_pairs={{0,1},{1,0},{2,3},{3,2},{4,5},{5,4},{6,7},{7,6},{8,9},{9,8},{10,11... | collective-permute-start | bytes 98312 | tf_op jit(solution)/shard_map/ppermute | solution.py:510
  8.9 4.3 %collective-permute-start.3 = (bf16[240,128]{1,0:T(8,128)(2,1)S(1)}, bf16[240,128]{1,0:T(8,128)(2,1)S(1)}, u32[]{:S(2)}, u32[]{:S(2)}) collective-permute-start(bf16[240,128]{1,0:T(8,128)(2,1)S(1)} %get-tuple-element.35), channel_id=1, source_target_pairs={{4,0},{8,4},{12,8},{0,1},{1,5},{5,9},{9,13},{13,12},{6,2},{10,6},{... | collective-permute-start | bytes 184328 | tf_op jit(solution)/shard_map/ppermute | solution.py:556
  9.1 4.1 %collective-permute-start.4 = (bf16[240,128]{1,0:T(8,128)(2,1)S(1)}, bf16[240,128]{1,0:T(8,128)(2,1)S(1)}, u32[]{:S(2)}, u32[]{:S(2)}) collective-permute-start(bf16[240,128]{1,0:T(8,128)(2,1)S(1)} %get-tuple-element.36), channel_id=1, source_target_pairs={{0,4},{4,8},{8,12},{1,0},{5,1},{9,5},{13,9},{12,13},{2,6},{6,10},{... | collective-permute-start | bytes 184328 | tf_op jit(solution)/shard_map/ppermute | solution.py:557

commit v23 on v22

--- a/solution.py
+++ b/solution.py
@@ -48,10 +48,6 @@
 def centring(width):
     same = iota((width, width), 0) == iota((width, width), 1)
     return jnp.where(same, 1.0 - 1.0 / width, -1.0 / width).astype(BF16)
-
-
-def averaging(width):
-    return jnp.full((width, width), 1.0 / width, BF16)
 
 
 def mean_square(centred):
@@ -106,17 +102,12 @@
         pair = pair_ref[chunk * group : (chunk + 1) * group].reshape(group * cols, width)
         chunks.append(dot(side_by_side(pair), centre).astype(BF16))
     mixes = [dot(centred, mix).reshape(half, cols, 2 * lanes) for centred in chunks]
-    squares = [centred[:, :width] * centred[:, :width] for centred in chunks]
-    averages = [
-        dot(jnp.concatenate(squares[i : i + 2], 1), twice(averaging(width)))
-        for i in range(0, len(squares), 2)
-    ]
     for chunk, (centred, mixed) in enumerate(zip(chunks, mixes)):
-        pick = slice(chunk % 2 * width, (chunk % 2 + 1) * width)
         variances = [
-            averages[chunk // 2][:, pick].reshape(half, cols, width),
-            mean_square(centred[:, width:].astype(F32)).reshape(half, cols, 1),
+            mean_square(centred[:, part * width : (part + 1) * width].astype(F32))
+            for part in range(2)
         ]
+        variances = [variance.reshape(half, cols, 1) for variance in variances]
         total = jnp.zeros((cols, lanes), F32)
         spread_out = jnp.zeros((cols, lanes), F32)
         for i in range(group):
@@ -187,7 +178,7 @@
         return refs[0][row_block]
     pair_at, core_at = place
     owners = 2
-    mine, theirs, across, diagonal = [ref[...] for ref in refs]
+    mine, theirs, diagonal, across = [ref[...] for ref in refs]
     near = jnp.where(row_block % owners == core_at, mine, theirs)
     far = jnp.where(row_block % owners == core_at, across, diagonal)
     return jnp.where(row_block // owners == pair_at, near, far)
@@ -507,7 +498,7 @@
         swapped = [(0, 1), (1, 0)]
         across = lax.ppermute(own, "pair", swapped)
         diagonal = lax.ppermute(own, ("pair", "samp"), [(0, 3), (1, 2), (2, 1), (3, 0)])
-        tiles = (own, lax.ppermute(own, "samp", swapped), across, diagonal)
+        tiles = (own, lax.ppermute(own, "samp", swapped), diagonal, across)
     else:
         tiles = (lax.all_gather(own, ("pair", "samp")),)
 

time: 15 us -> 15 us (level)
  waiting for transfers between devices: 0.44 us -> 0.27 us
    ppermute x1, starting transfers between devices: 2.49 us -> 0.01 us  [shards(): lax.ppermute(own, ('pair', 'samp'), [(0, 3), (1, 2), (2, 1), (3, 0)])]
    ppermute x1, starting transfers between devices: 0.64 us -> 3.04 us  [shards(): across = lax.ppermute(own, 'pair', swapped)]
    ppermute x1, waiting for transfers between devices: 0.22 us -> 0.01 us  [shards(): across = lax.ppermute(own, 'pair', swapped)]
    ppermute x1, waiting for transfers between devices: 0.01 us -> 0.16 us  [shards(): lax.ppermute(own, ('pair', 'samp'), [(0, 3), (1, 2), (2, 1), (3, 0)])]
    ppermute x1, starting transfers between devices: 0.04 us -> 0.19 us  [shards(): tiles = (own, lax.ppermute(own, 'samp', swapped), diagonal, across)]
where the time goes in v23:
time: 15 us; the launch traced here: 14.8 us
  Pallas kernels  9.07 us (60%)
  starting transfers between devices  5.28 us (35%)
  waiting for transfers between devices  0.27 us (2%)
    ppermute x1, starting transfers between devices, shards(): across = lax.ppermute(own, 'pair', swapped)  3.04 us
    pallas_call x1, Pallas kernels, shards(): pl.pallas_call(project_kernel, in_specs=[IN_SMEM] + [IN_VMEM] * len(opera...  2.99 us
    pallas_call x1, Pallas kernels, shards(): pl.pallas_call(pair_kernel, in_specs=[IN_SMEM] + [IN_HBM] * 2, out_specs=...  2.31 us
    pallas_call x1, Pallas kernels, shards(): pl.pallas_call(functools.partial(inner_kernel, heads, blocks), in_specs=[...  2.08 us
    ppermute x1, starting transfers between devices, shards(): lax.ppermute(far, ('atoms', 'samp'), [(target, source) for source, target...  1.84 us
    pallas_call x1, Pallas kernels, shards(): pl.pallas_call(functools.partial(outer_kernel, heads, blocks, groups), in...  1.64 us
  transfers between devices with their start and end apart: 5, of which 2 were waited for; matrix products, arithmetic and copies ran while one was open for 0% of the time, Pallas kernels for 34%

profile of v23, /device:TPU:0, one launch (start us, length us, event | category | flops | bytes accessed | tf_op | source)
XLA Modules:
  0.0 14.8 jit_solution(5751277114477851006)
XLA Ops:
  0.0 0.0 copy-start.1
  0.0 0.0 copy-start
  0.0 0.0 copy-start.8
  0.0 0.0 copy-start.7
  0.0 0.0 copy-start.6
  0.0 0.0 copy-start.5
  0.0 0.0 copy-start.4
  0.0 0.0 copy-start.3
  0.0 2.3 %shard_map.182.refs_0_ = bf16[2,64,128]{2,1,0:T(8,128)(2,1)S(1)} custom-call(s32[1]{0:T(128)} %bitcast.1.core_ref, bf16[4,128]{1,0:T(4,128)(2,1)} %bitcast.4, bf16[128,64,128]{2,1,0:T(8,128)(2,1)} %pair_hbm.1), custom_call_target="tpu_custom_call" | custom-call | flops 268435456 | bytes 4194304 | tf_op jit(solution)/shard_map/pallas_call | solution.py:483
  2.4 0.0 copy-start.2
  2.4 0.0 copy-start.9
  2.4 3.0 %collective-permute-start.2 = (bf16[2,64,128]{2,1,0:T(8,128)(2,1)S(1)}, bf16[2,64,128]{2,1,0:T(8,128)(2,1)S(1)}, u32[]{:S(2)}, u32[]{:S(2)}) collective-permute-start(bf16[2,64,128]{2,1,0:T(8,128)(2,1)S(1)} %shard_map.182.refs_0_), channel_id=1, source_target_pairs={{0,2},{2,0},{1,3},{3,1},{4,6},{6,4},{5,7},{7,5},{8,10},{10,8},{9,1... | collective-permute-start | bytes 98312 | tf_op jit(solution)/shard_map/ppermute | solution.py:499
  5.4 0.0 collective-permute-start.1
  5.4 0.2 %collective-permute-start = (bf16[2,64,128]{2,1,0:T(8,128)(2,1)S(1)}, bf16[2,64,128]{2,1,0:T(8,128)(2,1)S(1)}, u32[]{:S(2)}, u32[]{:S(2)}) collective-permute-start(bf16[2,64,128]{2,1,0:T(8,128)(2,1)S(1)} %shard_map.182.refs_0_), channel_id=1, source_target_pairs={{0,1},{1,0},{2,3},{3,2},{4,5},{5,4},{6,7},{7,6},{8,9},{9,8},{10,11... | collective-permute-start | bytes 98312 | tf_op jit(solution)/shard_map/ppermute | solution.py:501
  5.6 0.0 copy-done.1
  5.6 0.0 copy-done
  5.6 0.0 copy-done.8
  5.6 0.0 copy-done.7
  5.6 0.0 copy-done.6
  5.6 0.0 copy-done.5
  5.7 0.0 copy-done.4
  5.7 0.0 copy-done.3
  5.7 3.0 %shard_map.181 = (bf16[3,512,128]{2,1,0:T(8,128)(2,1)S(1)}, bf16[3,512,128]{2,1,0:T(8,128)(2,1)S(1)}, bf16[3,512,128]{2,1,0:T(8,128)(2,1)S(1)}, bf16[3,512,128]{...) custom-call(s32[1]{0:T(128)} %bitcast.1.core_ref, ...), custom_call_target="tpu_custom_call" | custom-call | flops 1006632960 | bytes 4194304 | tf_op jit(solution)/shard_map/pallas_call | solution.py:516
  8.7 0.0 collective-permute-done.2.refs_3_
  8.7 0.2 %collective-permute-done.1.refs_2_ = bf16[2,64,128]{2,1,0:T(8,128)(2,1)S(1)} collective-permute-done((bf16[2,64,128]{2,1,0:T(8,128)(2,1)S(1)}, bf16[2,64,128]{2,1,0:T(8,128)(2,1)S(1)}, u32[]{:S(2)}, u32[]{:S(2)}) %collective-permute-start.1) | collective-permute-done | bytes 32800 | tf_op jit(solution)/shard_map/ppermute | solution.py:500
  8.9 0.0 collective-permute-done.refs_1_
  8.9 0.2 %collective-permute-start.3 = (bf16[240,128]{1,0:T(8,128)(2,1)S(1)}, bf16[240,128]{1,0:T(8,128)(2,1)S(1)}, u32[]{:S(2)}, u32[]{:S(2)}) collective-permute-start(bf16[240,128]{1,0:T(8,128)(2,1)S(1)} %get-tuple-element.35), channel_id=1, source_target_pairs={{4,0},{8,4},{12,8},{0,1},{1,5},{5,9},{9,13},{13,12},{6,2},{10,6},{... | collective-permute-start | bytes 184328 | tf_op jit(solution)/shard_map/ppermute | solution.py:547
  9.1 1.8 %collective-permute-start.4 = (bf16[240,128]{1,0:T(8,128)(2,1)S(1)}, bf16[240,128]{1,0:T(8,128)(2,1)S(1)}, u32[]{:S(2)}, u32[]{:S(2)}) collective-permute-start(bf16[240,128]{1,0:T(8,128)(2,1)S(1)} %get-tuple-element.36), channel_id=1, source_target_pairs={{0,4},{4,8},{8,12},{1,0},{5,1},{9,5},{13,9},{12,13},{2,6},{6,10},{... | collective-permute-start | bytes 184328 | tf_op jit(solution)/shard_map/ppermute | solution.py:548
  10.9 0.0 copy-done.2
  11.0 0.0 copy-done.9
  11.0 2.1 %shard_map.184 = (bf16[3,384,128]{2,1,0:T(8,128)(2,1)S(1)}, bf16[2,2,128,256]{3,2,1,0:T(8,128)(2,1)S(1)}, bf16[2,48,48]{2,1,0:T(8,128)(2,1)S(1)}, bf16[2,112,256]{2,1,0:T(8,128)(2,1)S(1)}) custom-call(s32[1]{0:T(128)} %bitcast.at_ref, s32[4,64]{1,0:T(4,128)S(1)} %copy-done.9, bf16[3,512,128]{2,1,0:T(8,128)(2,1)S(1)} %get-tuple-element.21.query_ref, ...), custom_call_target="tpu_custom_call" | custom-call | flops 603979776 | bytes 4194304 | tf_op jit(solution)/shard_map/pallas_call | solution.py:554
  13.0 0.1 collective-permute-done.3.first_ref
  13.1 0.0 collective-permute-done.4.second_ref
  13.1 1.6 %shard_map.185 = bf16[3,512,128]{2,1,0:T(8,128)(2,1)} custom-call(s32[1]{0:T(128)} %bitcast.at_ref, s32[1]{0:T(128)} %bitcast.1.core_ref, bf16[3,512,128]{2,1,0:T(8,128)(2,1)S(1)} %get-tuple-element.21.query_ref, bf16[3,512,128]{2,1,0:T(8,128)(2,1)S(1)} %get-tuple-element.22.key_ref.own_key_ref, ...), custom_call_target="tpu_custom_call" | custom-call | flops 201326592 | bytes 4194304 | tf_op jit(solution)/shard_map/pallas_call | solution.py:573
  (1 shorter events, 0.0 us)
Async XLA Ops:
  0.0 5.6 %copy-start.1 = (bf16[128,128]{1,0:T(8,128)(2,1)S(1)}, bf16[128,128]{1,0:T(8,128)(2,1)}, u32[]{:S(2)}) copy-start(bf16[128,128]{1,0:T(8,128)(2,1)} %w_value.3) | copy-start | bytes 98308
  0.0 5.6 %copy-start = (bf16[128,128]{1,0:T(8,128)(2,1)S(1)}, bf16[128,128]{1,0:T(8,128)(2,1)}, u32[]{:S(2)}) copy-start(bf16[128,128]{1,0:T(8,128)(2,1)} %w_key.3) | copy-start | bytes 98308
  0.0 5.6 %copy-start.8 = (bf16[128,128]{1,0:T(8,128)(2,1)S(1)}, bf16[128,128]{1,0:T(8,128)(2,1)}, u32[]{:S(2)}) copy-start(bf16[128,128]{1,0:T(8,128)(2,1)} %w_gate.1) | copy-start | bytes 98308
  0.0 5.6 %copy-start.7 = (bf16[128,128]{1,0:T(8,128)(2,1)S(1)}, bf16[128,128]{1,0:T(8,128)(2,1)}, u32[]{:S(2)}) copy-start(bf16[128,128]{1,0:T(8,128)(2,1)} %w_query.1) | copy-start | bytes 98308
  0.0 5.6 %copy-start.6 = (bf16[128,128]{1,0:T(8,128)(2,1)S(1)}, bf16[128,128]{1,0:T(8,128)(2,1)}, u32[]{:S(2)}) copy-start(bf16[128,128]{1,0:T(8,128)(2,1)} %ada_attn_shift.1) | copy-start | bytes 98308
  0.0 5.6 %copy-start.5 = (bf16[128,128]{1,0:T(8,128)(2,1)S(1)}, bf16[128,128]{1,0:T(8,128)(2,1)}, u32[]{:S(2)}) copy-start(bf16[128,128]{1,0:T(8,128)(2,1)} %ada_attn_scale.1) | copy-start | bytes 98308
  0.0 5.6 %copy-start.4 = (bf16[512,128]{1,0:T(8,128)(2,1)S(1)}, bf16[512,128]{1,0:T(8,128)(2,1)}, u32[]{:S(2)}) copy-start(bf16[512,128]{1,0:T(8,128)(2,1)} %cond_ref.1) | copy-start | bytes 393220
  0.0 5.6 %copy-start.3 = (bf16[3,512,128]{2,1,0:T(8,128)(2,1)S(1)}, bf16[3,512,128]{2,1,0:T(8,128)(2,1)}, u32[]{:S(2)}) copy-start(bf16[3,512,128]{2,1,0:T(8,128)(2,1)} %single_ref.1) | copy-start | bytes 1179652
  2.4 8.6 %copy-start.2 = (bf16[128,128]{1,0:T(8,128)(2,1)S(1)}, bf16[128,128]{1,0:T(8,128)(2,1)}, u32[]{:S(2)}) copy-start(bf16[128,128]{1,0:T(8,128)(2,1)} %w_out_ref.3) | copy-start | bytes 98308
  2.4 8.6 %copy-start.9 = (s32[4,64]{1,0:T(4,128)S(1)}, s32[4,64]{1,0:T(4,128)}, u32[]{:S(2)}) copy-start(s32[4,64]{1,0:T(4,128)} %counts_ref.1) | copy-start | bytes 3076
  2.4 6.3 %collective-permute-start.2 = (bf16[2,64,128]{2,1,0:T(8,128)(2,1)S(1)}, bf16[2,64,128]{2,1,0:T(8,128)(2,1)S(1)}, u32[]{:S(2)}, u32[]{:S(2)}) collective-permute-start(bf16[2,64,128]{2,1,0:T(8,128)(2,1)S(1)} %shard_map.182.refs_0_), channel_id=1, source_target_pairs={{0,2},{2,0},{1,3},{3,1},{4,6},{6,4},{5,7},{7,5},{8,10},{10,8},{9,1... | collective-permute-start | bytes 98312 | tf_op jit(solution)/shard_map/ppermute | solution.py:499
  5.4 3.4 %collective-permute-start.1 = (bf16[2,64,128]{2,1,0:T(8,128)(2,1)S(1)}, bf16[2,64,128]{2,1,0:T(8,128)(2,1)S(1)}, u32[]{:S(2)}, u32[]{:S(2)}) collective-permute-start(bf16[2,64,128]{2,1,0:T(8,128)(2,1)S(1)} %shard_map.182.refs_0_), channel_id=1, source_target_pairs={{0,3},{1,2},{2,1},{3,0},{4,7},{5,6},{6,5},{7,4},{8,11},{9,10},{10,... | collective-permute-start | bytes 98312 | tf_op jit(solution)/shard_map/ppermute | solution.py:500
  5.4 3.4 %collective-permute-start = (bf16[2,64,128]{2,1,0:T(8,128)(2,1)S(1)}, bf16[2,64,128]{2,1,0:T(8,128)(2,1)S(1)}, u32[]{:S(2)}, u32[]{:S(2)}) collective-permute-start(bf16[2,64,128]{2,1,0:T(8,128)(2,1)S(1)} %shard_map.182.refs_0_), channel_id=1, source_target_pairs={{0,1},{1,0},{2,3},{3,2},{4,5},{5,4},{6,7},{7,6},{8,9},{9,8},{10,11... | collective-permute-start | bytes 98312 | tf_op jit(solution)/shard_map/ppermute | solution.py:501
  8.9 4.2 %collective-permute-start.3 = (bf16[240,128]{1,0:T(8,128)(2,1)S(1)}, bf16[240,128]{1,0:T(8,128)(2,1)S(1)}, u32[]{:S(2)}, u32[]{:S(2)}) collective-permute-start(bf16[240,128]{1,0:T(8,128)(2,1)S(1)} %get-tuple-element.35), channel_id=1, source_target_pairs={{4,0},{8,4},{12,8},{0,1},{1,5},{5,9},{9,13},{13,12},{6,2},{10,6},{... | collective-permute-start | bytes 184328 | tf_op jit(solution)/shard_map/ppermute | solution.py:547
  9.1 4.0 %collective-permute-start.4 = (bf16[240,128]{1,0:T(8,128)(2,1)S(1)}, bf16[240,128]{1,0:T(8,128)(2,1)S(1)}, u32[]{:S(2)}, u32[]{:S(2)}) collective-permute-start(bf16[240,128]{1,0:T(8,128)(2,1)S(1)} %get-tuple-element.36), channel_id=1, source_target_pairs={{0,4},{4,8},{8,12},{1,0},{5,1},{9,5},{13,9},{12,13},{2,6},{6,10},{... | collective-permute-start | bytes 184328 | tf_op jit(solution)/shard_map/ppermute | solution.py:548

commit v24 on v22

--- a/solution.py
+++ b/solution.py
@@ -193,17 +193,38 @@
     return jnp.where(row_block // owners == pair_at, near, far)
 
 
+def shifted(values, lanes):
+    return pltpu.roll(values, lanes % values.shape[1], 1)
+
+
+def unpacked(rows, side):
+    half = EDGE // 2
+    whole, packed = rows[:EDGE], rows[EDGE:].astype(F32)
+    if side == 0:
+        part = jnp.concatenate([packed, shifted(packed, -GROUP // 2)], 0).astype(BF16)
+        return jnp.concatenate([whole, part], 1)
+    part = jnp.concatenate([shifted(packed, GROUP // 2), packed], 0).astype(BF16)
+    return jnp.concatenate([part, whole], 1)
+
+
 def select_kernel(blocks, at_ref, pair_ref, core_ref, *refs):
     *tile_refs, _, __, ___, near_ref, far_ref, ____, held_ref = refs
     groups, cols, lanes = tile_refs[0].shape[-3:]
-    rows = groups * EDGE
     device_at, place = at_ref[0], (pair_ref[0], core_ref[0])
+    half = EDGE // 2
     for send_ref, core in ((near_ref, 1), (far_ref, 0)):
         above = core_ref[0] == core
         beside = jnp.where(above, device_at + 1, device_at - 1)
         tile = tile_of(tile_refs, place, jnp.clip(beside, 0, blocks - 1))
         tile = jnp.where(above, tile[:, cols - EDGE :], tile[:, :EDGE])
-        send_ref[send_ref.shape[0] - rows :, :] = tile.reshape(rows, lanes)
+        whole = jnp.where(above, tile[0], tile[1])
+        part = jnp.where(above, tile[1], tile[0]).astype(F32)
+        first, last = part[:half], part[half:]
+        first = jnp.where(above, first, shifted(first, -GROUP // 2))
+        last = jnp.where(above, shifted(last, GROUP // 2), last)
+        low = iota((half, lanes), 1) % GROUP < GROUP // 2
+        packed = jnp.where(low, first, last).astype(BF16)
+        send_ref[send_ref.shape[0] - EDGE - half :, :] = jnp.concatenate([whole, packed], 0)
     held_ref[...] = tile_of(tile_refs, place, device_at).reshape(groups * cols, lanes)
 
 
@@ -243,7 +264,7 @@
     ]
 
 
-def attend(heads, windows, query_ref, gate_ref, gated_ref):
+def attend(heads, windows, query_ref, gate_ref, gated_ref, paired=0):
     samples, _, width = query_ref.shape
     head_dim = width // heads
     rows = heads * Q_WIN
@@ -278,16 +299,38 @@
         for j, (_, i) in enumerate(couple):
             scores.append(product[:, j * K_WIN : (j + 1) * K_WIN] * scaling + biases[i])
     tops = [jnp.max(score, axis=-1, keepdims=True) for score in scores]
-    raised = [jnp.exp2(score - top).astype(BF16) for score, top in zip(scores, tops)]
-    for (sample, i), weight in zip(units, raised):
-        values = windows[i][1][sample][1]
-        mixed = dot(weight, jnp.concatenate([values, ones], 1))
-        picked = mixed[:Q_WIN]
+    raised = [jnp.exp2(score - top) for score, top in zip(scores, tops)]
+
+    def by_head(parts, like):
+        picked = jnp.broadcast_to(parts[:Q_WIN], (Q_WIN, like.shape[1]))
         for head in range(1, heads):
-            picked = jnp.where(
-                channel_head == head, mixed[head * Q_WIN : (head + 1) * Q_WIN], picked
-            )
-        attended = picked[:, :width] * pl.reciprocal(picked[:, width:], approx=True)
+            part = parts[head * Q_WIN : (head + 1) * Q_WIN]
+            picked = jnp.where(like == head, part, picked)
+        return picked
+
+    mixes = []
+    for first in range(0, len(units), 2):
+        couple = units[first : first + 2]
+        values = [windows[i][1][sample][1] for sample, i in couple]
+        weights = [weight.astype(BF16) for weight in raised[first : first + 2]]
+        if paired and first // 2 % paired == 0 and len(couple) == 2:
+            blank = jnp.zeros_like(values[0])
+            values = [
+                jnp.concatenate([values[0], blank], 1),
+                jnp.concatenate([blank, values[1]], 1),
+            ]
+            both = dot(jnp.concatenate(weights, 1), jnp.concatenate(values, 0))
+            for j in range(2):
+                total = jnp.sum(raised[first + j], axis=-1, keepdims=True)
+                narrow = channel_head[:, :width]
+                attended = by_head(both[:, j * width : (j + 1) * width], narrow)
+                mixes.append((attended, by_head(total, narrow)))
+        else:
+            for value, weight in zip(values, weights):
+                picked = by_head(dot(weight, jnp.concatenate([value, ones], 1)), channel_head)
+                mixes.append((picked[:, :width], picked[:, width:]))
+    for (sample, i), (attended, total) in zip(units, mixes):
+        attended = attended * pl.reciprocal(total, approx=True)
         at = pl.ds(windows[i][0], Q_WIN)
         gate = gate_ref[sample, at, :].astype(F32)
         gated_ref[sample, at, :] = (gate * attended).astype(BF16)
@@ -346,7 +389,7 @@
         cut = slice(start - EDGE, start - EDGE + K_WIN)
         parts = [(key_ref[i, cut, :], value_ref[i, cut, :]) for i in range(samples)]
         windows.append((start, parts, near_ref[cut, :], pick, None))
-    attend(heads, windows, query_ref, gate_ref, gated_ref)
+    attend(heads, windows, query_ref, gate_ref, gated_ref, paired=2)
 
     cut = slice(starts[0], starts[-1] + Q_WIN)
     for sample in range(samples):
@@ -368,7 +411,6 @@
 def outer_kernel(
     heads,
     blocks,
-    groups,
     at_ref,
     core_ref,
     query_ref,
@@ -423,7 +465,7 @@
             )
             for i in range(samples)
         ]
-        near = expand(hot_ref[side], arrived[side][count:], groups)
+        near = dot(hot_ref[side], unpacked(arrived[side][count:], side)).astype(BF16)
         near = joined(side, near, side_ref[side])
         for i, start in enumerate(starts[side]):
             cut = slice(i * Q_WIN, i * Q_WIN + K_WIN)
@@ -474,6 +516,7 @@
     groups = tok_here // GROUP
     pairs = lax.axis_size("pair")
     assert pair_cond.shape[0] == lax.axis_size("samp") * tok_here
+    assert groups == 2 and tok_here - EDGE == GROUP // 2
     at = device_at.astype(jnp.int32).reshape(1)
     pair_at = lax.axis_index("pair").astype(jnp.int32).reshape(1)
     core_at = lax.axis_index("samp").astype(jnp.int32).reshape(1)
@@ -488,7 +531,7 @@
     def cost(products):
         return pl.CostEstimate(flops=2 * products, bytes_accessed=4 << 20, transcendentals=0)
 
-    sent = pltpu.VMEM((samples * EDGE + groups * EDGE, lanes), BF16)
+    sent = pltpu.VMEM((samples * EDGE + EDGE + EDGE // 2, lanes), BF16)
     own = pl.pallas_call(
         pair_kernel,
         in_specs=[IN_SMEM] + [IN_HBM] * 2,
@@ -580,7 +623,7 @@
 
     operands += (inner, picks, hots, beside_edges, w_key, w_value, first, second)
     return pl.pallas_call(
-        functools.partial(outer_kernel, heads, blocks, groups),
+        functools.partial(outer_kernel, heads, blocks),
         in_specs=[IN_SMEM] * 2 + [IN_VMEM] * len(operands),
         out_specs=IN_HBM,
         out_shape=pltpu.HBM(wide, BF16),

time: 15 us -> 15 us (level)
  no operation moved by 1% of the time
where the time goes in v24:
time: 15 us; the launch traced here: 14.8 us
  Pallas kernels  9.06 us (60%)
  starting transfers between devices  5.2 us (35%)
  waiting for transfers between devices  0.36 us (2%)
    pallas_call x1, Pallas kernels, shards(): pl.pallas_call(project_kernel, in_specs=[IN_SMEM] + [IN_VMEM] * len(opera...  2.99 us
    ppermute x1, starting transfers between devices, shards(): lax.ppermute(own, ('pair', 'samp'), [(0, 3), (1, 2), (2, 1), (3, 0)])  2.49 us
    pallas_call x1, Pallas kernels, shards(): pl.pallas_call(pair_kernel, in_specs=[IN_SMEM] + [IN_HBM] * 2, out_specs=...  2.26 us
    pallas_call x1, Pallas kernels, shards(): pl.pallas_call(functools.partial(inner_kernel, heads, blocks), in_specs=[...  1.99 us
    ppermute x1, starting transfers between devices, shards(): lax.ppermute(far, ('atoms', 'samp'), [(target, source) for source, target...  1.75 us
    pallas_call x1, Pallas kernels, shards(): pl.pallas_call(functools.partial(outer_kernel, heads, blocks), in_specs=[...  1.7 us
    ppermute x1, starting transfers between devices, shards(): across = lax.ppermute(own, 'pair', swapped)  0.64 us
  transfers between devices with their start and end apart: 5, of which 2 were waited for; matrix products, arithmetic and copies ran while one was open for 0% of the time, Pallas kernels for 34%

profile of v24, /device:TPU:0, one launch (start us, length us, event | category | flops | bytes accessed | tf_op | source)
XLA Modules:
  0.0 14.8 jit_solution(11413084587215808097)
XLA Ops:
  0.0 0.0 copy-start.1
  0.0 0.0 copy-start
  0.0 0.0 copy-start.8
  0.0 0.0 copy-start.7
  0.0 0.0 copy-start.6
  0.0 0.0 copy-start.5
  0.0 0.0 copy-start.4
  0.0 0.0 copy-start.3
  0.0 2.3 %shard_map.182.refs_0_ = bf16[2,64,128]{2,1,0:T(8,128)(2,1)S(1)} custom-call(s32[1]{0:T(128)} %bitcast.1.core_ref, bf16[4,128]{1,0:T(4,128)(2,1)} %bitcast.4, bf16[128,64,128]{2,1,0:T(8,128)(2,1)} %pair_hbm.1), custom_call_target="tpu_custom_call" | custom-call | flops 268435456 | bytes 4194304 | tf_op jit(solution)/shard_map/pallas_call | solution.py:535
  2.3 0.0 copy-start.2
  2.3 0.0 copy-start.9
  2.3 2.5 %collective-permute-start.2 = (bf16[2,64,128]{2,1,0:T(8,128)(2,1)S(1)}, bf16[2,64,128]{2,1,0:T(8,128)(2,1)S(1)}, u32[]{:S(2)}, u32[]{:S(2)}) collective-permute-start(bf16[2,64,128]{2,1,0:T(8,128)(2,1)S(1)} %shard_map.182.refs_0_), channel_id=1, source_target_pairs={{0,3},{1,2},{2,1},{3,0},{4,7},{5,6},{6,5},{7,4},{8,11},{9,10},{10,... | collective-permute-start | bytes 98312 | tf_op jit(solution)/shard_map/ppermute | solution.py:552
  4.8 0.6 %collective-permute-start.1 = (bf16[2,64,128]{2,1,0:T(8,128)(2,1)S(1)}, bf16[2,64,128]{2,1,0:T(8,128)(2,1)S(1)}, u32[]{:S(2)}, u32[]{:S(2)}) collective-permute-start(bf16[2,64,128]{2,1,0:T(8,128)(2,1)S(1)} %shard_map.182.refs_0_), channel_id=1, source_target_pairs={{0,2},{2,0},{1,3},{3,1},{4,6},{6,4},{5,7},{7,5},{8,10},{10,8},{9,1... | collective-permute-start | bytes 98312 | tf_op jit(solution)/shard_map/ppermute | solution.py:551
  5.5 0.0 collective-permute-start
  5.5 0.0 copy-done.1
  5.5 0.0 copy-done
  5.5 0.0 copy-done.8
  5.5 0.0 copy-done.7
  5.5 0.0 copy-done.6
  5.5 0.0 copy-done.5
  5.5 0.0 copy-done.4
  5.6 0.0 copy-done.3
  5.6 3.0 %shard_map.181 = (bf16[3,512,128]{2,1,0:T(8,128)(2,1)S(1)}, bf16[3,512,128]{2,1,0:T(8,128)(2,1)S(1)}, bf16[3,512,128]{2,1,0:T(8,128)(2,1)S(1)}, bf16[3,512,128]{...) custom-call(s32[1]{0:T(128)} %bitcast.1.core_ref, ...), custom_call_target="tpu_custom_call" | custom-call | flops 1006632960 | bytes 4194304 | tf_op jit(solution)/shard_map/pallas_call | solution.py:568
  8.6 0.0 collective-permute-done.2.refs_3_
  8.6 0.2 %collective-permute-done.1.refs_2_ = bf16[2,64,128]{2,1,0:T(8,128)(2,1)S(1)} collective-permute-done((bf16[2,64,128]{2,1,0:T(8,128)(2,1)S(1)}, bf16[2,64,128]{2,1,0:T(8,128)(2,1)S(1)}, u32[]{:S(2)}, u32[]{:S(2)}) %collective-permute-start.1) | collective-permute-done | bytes 32800 | tf_op jit(solution)/shard_map/ppermute | solution.py:551
  8.8 0.0 collective-permute-done.refs_1_
  8.8 0.1 shard_map.183
  8.9 0.3 %collective-permute-start.3 = (bf16[216,128]{1,0:T(8,128)(2,1)S(1)}, bf16[216,128]{1,0:T(8,128)(2,1)S(1)}, u32[]{:S(2)}, u32[]{:S(2)}) collective-permute-start(bf16[216,128]{1,0:T(8,128)(2,1)S(1)} %get-tuple-element.35), channel_id=1, source_target_pairs={{4,0},{8,4},{12,8},{0,1},{1,5},{5,9},{9,13},{13,12},{6,2},{10,6},{... | collective-permute-start | bytes 165896 | tf_op jit(solution)/shard_map/ppermute | solution.py:599
  9.2 1.8 %collective-permute-start.4 = (bf16[216,128]{1,0:T(8,128)(2,1)S(1)}, bf16[216,128]{1,0:T(8,128)(2,1)S(1)}, u32[]{:S(2)}, u32[]{:S(2)}) collective-permute-start(bf16[216,128]{1,0:T(8,128)(2,1)S(1)} %get-tuple-element.36), channel_id=1, source_target_pairs={{0,4},{4,8},{8,12},{1,0},{5,1},{9,5},{13,9},{12,13},{2,6},{6,10},{... | collective-permute-start | bytes 165896 | tf_op jit(solution)/shard_map/ppermute | solution.py:600
  11.0 0.0 copy-done.2
  11.0 0.0 copy-done.9
  11.0 2.0 %shard_map.184 = (bf16[3,384,128]{2,1,0:T(8,128)(2,1)S(1)}, bf16[2,2,128,256]{3,2,1,0:T(8,128)(2,1)S(1)}, bf16[2,48,48]{2,1,0:T(8,128)(2,1)S(1)}, bf16[2,112,256]{2,1,0:T(8,128)(2,1)S(1)}) custom-call(s32[1]{0:T(128)} %bitcast.at_ref, s32[4,64]{1,0:T(4,128)S(1)} %copy-done.9, bf16[3,512,128]{2,1,0:T(8,128)(2,1)S(1)} %get-tuple-element.21.query_ref, ...), custom_call_target="tpu_custom_call" | custom-call | flops 603979776 | bytes 4194304 | tf_op jit(solution)/shard_map/pallas_call | solution.py:606
  13.0 0.1 collective-permute-done.3.first_ref
  13.1 0.0 collective-permute-done.4.second_ref
  13.1 1.7 %shard_map.185 = bf16[3,512,128]{2,1,0:T(8,128)(2,1)} custom-call(s32[1]{0:T(128)} %bitcast.at_ref, s32[1]{0:T(128)} %bitcast.1.core_ref, bf16[3,512,128]{2,1,0:T(8,128)(2,1)S(1)} %get-tuple-element.21.query_ref, bf16[3,512,128]{2,1,0:T(8,128)(2,1)S(1)} %get-tuple-element.22.key_ref.own_key_ref, ...), custom_call_target="tpu_custom_call" | custom-call | flops 201326592 | bytes 4194304 | tf_op jit(solution)/shard_map/pallas_call | solution.py:625
Async XLA Ops:
  0.0 5.5 %copy-start.1 = (bf16[128,128]{1,0:T(8,128)(2,1)S(1)}, bf16[128,128]{1,0:T(8,128)(2,1)}, u32[]{:S(2)}) copy-start(bf16[128,128]{1,0:T(8,128)(2,1)} %w_value.3) | copy-start | bytes 98308
  0.0 5.5 %copy-start = (bf16[128,128]{1,0:T(8,128)(2,1)S(1)}, bf16[128,128]{1,0:T(8,128)(2,1)}, u32[]{:S(2)}) copy-start(bf16[128,128]{1,0:T(8,128)(2,1)} %w_key.3) | copy-start | bytes 98308
  0.0 5.5 %copy-start.8 = (bf16[128,128]{1,0:T(8,128)(2,1)S(1)}, bf16[128,128]{1,0:T(8,128)(2,1)}, u32[]{:S(2)}) copy-start(bf16[128,128]{1,0:T(8,128)(2,1)} %w_gate.1) | copy-start | bytes 98308
  0.0 5.5 %copy-start.7 = (bf16[128,128]{1,0:T(8,128)(2,1)S(1)}, bf16[128,128]{1,0:T(8,128)(2,1)}, u32[]{:S(2)}) copy-start(bf16[128,128]{1,0:T(8,128)(2,1)} %w_query.1) | copy-start | bytes 98308
  0.0 5.5 %copy-start.6 = (bf16[128,128]{1,0:T(8,128)(2,1)S(1)}, bf16[128,128]{1,0:T(8,128)(2,1)}, u32[]{:S(2)}) copy-start(bf16[128,128]{1,0:T(8,128)(2,1)} %ada_attn_shift.1) | copy-start | bytes 98308
  0.0 5.5 %copy-start.5 = (bf16[128,128]{1,0:T(8,128)(2,1)S(1)}, bf16[128,128]{1,0:T(8,128)(2,1)}, u32[]{:S(2)}) copy-start(bf16[128,128]{1,0:T(8,128)(2,1)} %ada_attn_scale.1) | copy-start | bytes 98308
  0.0 5.5 %copy-start.4 = (bf16[512,128]{1,0:T(8,128)(2,1)S(1)}, bf16[512,128]{1,0:T(8,128)(2,1)}, u32[]{:S(2)}) copy-start(bf16[512,128]{1,0:T(8,128)(2,1)} %cond_ref.1) | copy-start | bytes 393220
  0.0 5.5 %copy-start.3 = (bf16[3,512,128]{2,1,0:T(8,128)(2,1)S(1)}, bf16[3,512,128]{2,1,0:T(8,128)(2,1)}, u32[]{:S(2)}) copy-start(bf16[3,512,128]{2,1,0:T(8,128)(2,1)} %single_ref.1) | copy-start | bytes 1179652
  2.3 8.6 %copy-start.2 = (bf16[128,128]{1,0:T(8,128)(2,1)S(1)}, bf16[128,128]{1,0:T(8,128)(2,1)}, u32[]{:S(2)}) copy-start(bf16[128,128]{1,0:T(8,128)(2,1)} %w_out_ref.3) | copy-start | bytes 98308
  2.3 8.6 %copy-start.9 = (s32[4,64]{1,0:T(4,128)S(1)}, s32[4,64]{1,0:T(4,128)}, u32[]{:S(2)}) copy-start(s32[4,64]{1,0:T(4,128)} %counts_ref.1) | copy-start | bytes 3076
  2.3 6.2 %collective-permute-start.2 = (bf16[2,64,128]{2,1,0:T(8,128)(2,1)S(1)}, bf16[2,64,128]{2,1,0:T(8,128)(2,1)S(1)}, u32[]{:S(2)}, u32[]{:S(2)}) collective-permute-start(bf16[2,64,128]{2,1,0:T(8,128)(2,1)S(1)} %shard_map.182.refs_0_), channel_id=1, source_target_pairs={{0,3},{1,2},{2,1},{3,0},{4,7},{5,6},{6,5},{7,4},{8,11},{9,10},{10,... | collective-permute-start | bytes 98312 | tf_op jit(solution)/shard_map/ppermute | solution.py:552
  4.8 4.0 %collective-permute-start.1 = (bf16[2,64,128]{2,1,0:T(8,128)(2,1)S(1)}, bf16[2,64,128]{2,1,0:T(8,128)(2,1)S(1)}, u32[]{:S(2)}, u32[]{:S(2)}) collective-permute-start(bf16[2,64,128]{2,1,0:T(8,128)(2,1)S(1)} %shard_map.182.refs_0_), channel_id=1, source_target_pairs={{0,2},{2,0},{1,3},{3,1},{4,6},{6,4},{5,7},{7,5},{8,10},{10,8},{9,1... | collective-permute-start | bytes 98312 | tf_op jit(solution)/shard_map/ppermute | solution.py:551
  5.5 3.3 %collective-permute-start = (bf16[2,64,128]{2,1,0:T(8,128)(2,1)S(1)}, bf16[2,64,128]{2,1,0:T(8,128)(2,1)S(1)}, u32[]{:S(2)}, u32[]{:S(2)}) collective-permute-start(bf16[2,64,128]{2,1,0:T(8,128)(2,1)S(1)} %shard_map.182.refs_0_), channel_id=1, source_target_pairs={{0,1},{1,0},{2,3},{3,2},{4,5},{5,4},{6,7},{7,6},{8,9},{9,8},{10,11... | collective-permute-start | bytes 98312 | tf_op jit(solution)/shard_map/ppermute | solution.py:553
  8.9 4.2 %collective-permute-start.3 = (bf16[216,128]{1,0:T(8,128)(2,1)S(1)}, bf16[216,128]{1,0:T(8,128)(2,1)S(1)}, u32[]{:S(2)}, u32[]{:S(2)}) collective-permute-start(bf16[216,128]{1,0:T(8,128)(2,1)S(1)} %get-tuple-element.35), channel_id=1, source_target_pairs={{4,0},{8,4},{12,8},{0,1},{1,5},{5,9},{9,13},{13,12},{6,2},{10,6},{... | collective-permute-start | bytes 165896 | tf_op jit(solution)/shard_map/ppermute | solution.py:599
  9.2 3.9 %collective-permute-start.4 = (bf16[216,128]{1,0:T(8,128)(2,1)S(1)}, bf16[216,128]{1,0:T(8,128)(2,1)S(1)}, u32[]{:S(2)}, u32[]{:S(2)}) collective-permute-start(bf16[216,128]{1,0:T(8,128)(2,1)S(1)} %get-tuple-element.36), channel_id=1, source_target_pairs={{0,4},{4,8},{8,12},{1,0},{5,1},{9,5},{13,9},{12,13},{2,6},{6,10},{... | collective-permute-start | bytes 165896 | tf_op jit(solution)/shard_map/ppermute | solution.py:600

commit v25 on v24

--- a/solution.py
+++ b/solution.py
@@ -75,7 +75,20 @@
     return (sigmoid(mixed[:, :width])[None] * single + mixed[None, :, width:]).astype(BF16)
 
 
-def pair_kernel(core_ref, w_pair_hbm, pair_hbm, tile_ref, w_pair_ref, pair_ref, pair_sem, sem):
+def pair_kernel(
+    core_ref,
+    w_pair_hbm,
+    pair_hbm,
+    single_hbm,
+    cond_hbm,
+    tile_ref,
+    single_ref,
+    cond_ref,
+    w_pair_ref,
+    pair_ref,
+    pair_sem,
+    sem,
+):
     rows, cols, width = pair_ref.shape
     heads = w_pair_ref.shape[0]
     group = GROUP
@@ -87,10 +100,16 @@
         source = pair_hbm.at[pl.ds(row_start + i * group, group)]
         return pltpu.make_async_copy(source, pair_ref.at[pl.ds(i * group, group)], pair_sem.at[i])
 
-    w_pair_copy = pltpu.make_async_copy(w_pair_hbm, w_pair_ref, sem)
+    w_pair_copy = pltpu.make_async_copy(w_pair_hbm, w_pair_ref, sem.at[0])
+    atom_copies = [
+        pltpu.make_async_copy(single_hbm, single_ref, sem.at[1]),
+        pltpu.make_async_copy(cond_hbm, cond_ref, sem.at[2]),
+    ]
     w_pair_copy.start()
     for i in range(rows // group):
         pair_copy(i).start()
+    for copy in atom_copies:
+        copy.start()
     w_pair_copy.wait()
     w_pair = w_pair_ref[...].astype(F32)
     spread = jnp.concatenate(
@@ -124,6 +143,8 @@
             total = jnp.where(slot == i, mixed[i % half, :, side], total)
             spread_out = jnp.where(slot == i, variances[i // half][i % half], spread_out)
         tile_ref[chunk] = (total * lax.rsqrt(spread_out + EPSILON)).astype(BF16)
+    for copy in atom_copies:
+        copy.wait()
 
 
 def beside(first, second):
@@ -532,20 +553,24 @@
         return pl.CostEstimate(flops=2 * products, bytes_accessed=4 << 20, transcendentals=0)
 
     sent = pltpu.VMEM((samples * EDGE + EDGE + EDGE // 2, lanes), BF16)
-    own = pl.pallas_call(
+    own, single, cond = pl.pallas_call(
         pair_kernel,
-        in_specs=[IN_SMEM] + [IN_HBM] * 2,
-        out_specs=IN_VMEM,
-        out_shape=pltpu.VMEM((groups, cols, lanes), BF16),
+        in_specs=[IN_SMEM] + [IN_HBM] * 4,
+        out_specs=[IN_VMEM] * 3,
+        out_shape=[
+            pltpu.VMEM((groups, cols, lanes), BF16),
+            pltpu.VMEM(wide, BF16),
+            pltpu.VMEM(atom_cond.shape, BF16),
+        ],
         scratch_shapes=[
             pltpu.VMEM((heads, width), BF16),
             pltpu.VMEM((tok_here, cols, width), BF16),
             pltpu.SemaphoreType.DMA((groups,)),
-            pltpu.SemaphoreType.DMA,
+            pltpu.SemaphoreType.DMA((3,)),
         ],
         compiler_params=params,
         cost_estimate=cost(tok_here * cols * width * width * 2),
-    )(core_at, *map(in_hbm, (w_pair.T, pair_cond)))
+    )(core_at, *map(in_hbm, (w_pair.T, pair_cond, atom_single, atom_cond)))
     if pairs == 2:
         swapped = [(0, 1), (1, 0)]
         across = lax.ppermute(own, "pair", swapped)
@@ -555,8 +580,8 @@
         tiles = (lax.all_gather(own, ("pair", "samp")),)
 
     operands = (
-        atom_single,
-        atom_cond,
+        single,
+        cond,
         ada_attn_scale,
         ada_attn_shift,
         w_key,

time: 15 us -> 15 us (level)
  no operation moved by 1% of the time
where the time goes in v25:
time: 15 us; the launch traced here: 14.8 us
  Pallas kernels  9.08 us (61%)
  starting transfers between devices  5.17 us (34%)
  waiting for transfers between devices  0.45 us (3%)
    pallas_call x1, Pallas kernels, shards(): pl.pallas_call(project_kernel, in_specs=[IN_SMEM] + [IN_VMEM] * len(opera...  2.99 us
    ppermute x1, starting transfers between devices, shards(): lax.ppermute(own, ('pair', 'samp'), [(0, 3), (1, 2), (2, 1), (3, 0)])  2.46 us
    pallas_call x1, Pallas kernels, shards(): pl.pallas_call(pair_kernel, in_specs=[IN_SMEM] + [IN_HBM] * 4, out_specs=...  2.28 us
    pallas_call x1, Pallas kernels, shards(): pl.pallas_call(functools.partial(inner_kernel, heads, blocks), in_specs=[...  1.99 us
    ppermute x1, starting transfers between devices, shards(): lax.ppermute(far, ('atoms', 'samp'), [(target, source) for source, target...  1.78 us
    pallas_call x1, Pallas kernels, shards(): pl.pallas_call(functools.partial(outer_kernel, heads, blocks), in_specs=[...  1.7 us
    ppermute x1, starting transfers between devices, shards(): across = lax.ppermute(own, 'pair', swapped)  0.63 us
  transfers between devices with their start and end apart: 5, of which 2 were waited for; matrix products, arithmetic and copies ran while one was open for 0% of the time, Pallas kernels for 34%

profile of v25, /device:TPU:0, one launch (start us, length us, event | category | flops | bytes accessed | tf_op | source)
XLA Modules:
  0.0 14.8 jit_solution(5252189774610637601)
XLA Ops:
  0.0 0.0 copy-start.1
  0.0 0.0 copy-start
  0.0 0.0 copy-start.6
  0.0 0.0 copy-start.5
  0.0 0.0 copy-start.4
  0.0 0.0 copy-start.3
  0.0 2.3 %shard_map.181 = (bf16[2,64,128]{2,1,0:T(8,128)(2,1)S(1)}, bf16[3,512,128]{2,1,0:T(8,128)(2,1)S(1)}, bf16[512,128]{1,0:T(8,128)(2,1)S(1)}) custom-call(s32[1]{0:T(128)} %bitcast.1.core_ref, bf16[4,128]{1,0:T(4,128)(2,1)} %bitcast.4, bf16[128,64,128]{2,1,0:T(8,128)(2,1)} %pair_hbm.1, bf16[3,512,128]{2,1,0:T(8,128)(2,1)} %single_hbm.1, bf16[512,128]{1,0:T(8,128)(2,1)} %cond_hbm.1), custom_call_target="tpu_custom_call" | custom-call | flops 268435456 | bytes 4194304 | tf_op jit(solution)/shard_map/pallas_call | solution.py:556
  2.3 0.0 copy-start.2
  2.3 0.0 copy-start.7
  2.3 2.5 %collective-permute-start.2 = (bf16[2,64,128]{2,1,0:T(8,128)(2,1)S(1)}, bf16[2,64,128]{2,1,0:T(8,128)(2,1)S(1)}, u32[]{:S(2)}, u32[]{:S(2)}) collective-permute-start(bf16[2,64,128]{2,1,0:T(8,128)(2,1)S(1)} %get-tuple-element.30.refs_0_), channel_id=1, source_target_pairs={{0,3},{1,2},{2,1},{3,0},{4,7},{5,6},{6,5},{7,4},{8,11},{9,10},{10,... | collective-permute-start | bytes 98312 | tf_op jit(solution)/shard_map/ppermute | solution.py:577
  4.8 0.6 %collective-permute-start.1 = (bf16[2,64,128]{2,1,0:T(8,128)(2,1)S(1)}, bf16[2,64,128]{2,1,0:T(8,128)(2,1)S(1)}, u32[]{:S(2)}, u32[]{:S(2)}) collective-permute-start(bf16[2,64,128]{2,1,0:T(8,128)(2,1)S(1)} %get-tuple-element.30.refs_0_), channel_id=1, source_target_pairs={{0,2},{2,0},{1,3},{3,1},{4,6},{6,4},{5,7},{7,5},{8,10},{10,8},{9,1... | collective-permute-start | bytes 98312 | tf_op jit(solution)/shard_map/ppermute | solution.py:576
  5.4 0.0 collective-permute-start
  5.5 0.0 copy-done.1
  5.5 0.0 copy-done
  5.5 0.0 copy-done.6
  5.5 0.0 copy-done.5
  5.5 0.0 copy-done.4
  5.5 0.0 copy-done.3
  5.5 3.0 %shard_map.182 = (bf16[3,512,128]{2,1,0:T(8,128)(2,1)S(1)}, bf16[3,512,128]{2,1,0:T(8,128)(2,1)S(1)}, bf16[3,512,128]{2,1,0:T(8,128)(2,1)S(1)}, bf16[3,512,128]{...) custom-call(s32[1]{0:T(128)} %bitcast.1.core_ref, ...), custom_call_target="tpu_custom_call" | custom-call | flops 1006632960 | bytes 4194304 | tf_op jit(solution)/shard_map/pallas_call | solution.py:593
  8.5 0.0 collective-permute-done.2.refs_3_
  8.5 0.2 %collective-permute-done.1.refs_2_ = bf16[2,64,128]{2,1,0:T(8,128)(2,1)S(1)} collective-permute-done((bf16[2,64,128]{2,1,0:T(8,128)(2,1)S(1)}, bf16[2,64,128]{2,1,0:T(8,128)(2,1)S(1)}, u32[]{:S(2)}, u32[]{:S(2)}) %collective-permute-start.1) | collective-permute-done | bytes 32800 | tf_op jit(solution)/shard_map/ppermute | solution.py:576
  8.8 0.0 collective-permute-done.refs_1_
  8.8 0.1 shard_map.183
  8.9 0.3 %collective-permute-start.3 = (bf16[216,128]{1,0:T(8,128)(2,1)S(1)}, bf16[216,128]{1,0:T(8,128)(2,1)S(1)}, u32[]{:S(2)}, u32[]{:S(2)}) collective-permute-start(bf16[216,128]{1,0:T(8,128)(2,1)S(1)} %get-tuple-element.41), channel_id=1, source_target_pairs={{4,0},{8,4},{12,8},{0,1},{1,5},{5,9},{9,13},{13,12},{6,2},{10,6},{... | collective-permute-start | bytes 165896 | tf_op jit(solution)/shard_map/ppermute | solution.py:624
  9.2 1.8 %collective-permute-start.4 = (bf16[216,128]{1,0:T(8,128)(2,1)S(1)}, bf16[216,128]{1,0:T(8,128)(2,1)S(1)}, u32[]{:S(2)}, u32[]{:S(2)}) collective-permute-start(bf16[216,128]{1,0:T(8,128)(2,1)S(1)} %get-tuple-element.42), channel_id=1, source_target_pairs={{0,4},{4,8},{8,12},{1,0},{5,1},{9,5},{13,9},{12,13},{2,6},{6,10},{... | collective-permute-start | bytes 165896 | tf_op jit(solution)/shard_map/ppermute | solution.py:625
  10.9 0.0 copy-done.2
  10.9 0.0 copy-done.7
  10.9 2.0 %shard_map.184 = (bf16[3,384,128]{2,1,0:T(8,128)(2,1)S(1)}, bf16[2,2,128,256]{3,2,1,0:T(8,128)(2,1)S(1)}, bf16[2,48,48]{2,1,0:T(8,128)(2,1)S(1)}, bf16[2,112,256]{2,1,0:T(8,128)(2,1)S(1)}) custom-call(s32[1]{0:T(128)} %bitcast.at_ref, s32[4,64]{1,0:T(4,128)S(1)} %copy-done.7, bf16[3,512,128]{2,1,0:T(8,128)(2,1)S(1)} %get-tuple-element.26.query_ref, ...), custom_call_target="tpu_custom_call" | custom-call | flops 603979776 | bytes 4194304 | tf_op jit(solution)/shard_map/pallas_call | solution.py:631
  12.9 0.2 %collective-permute-done.3.first_ref = bf16[216,128]{1,0:T(8,128)(2,1)S(1)} collective-permute-done((bf16[216,128]{1,0:T(8,128)(2,1)S(1)}, bf16[216,128]{1,0:T(8,128)(2,1)S(1)}, u32[]{:S(2)}, u32[]{:S(2)}) %collective-permute-start.3) | collective-permute-done | bytes 55328 | tf_op jit(solution)/shard_map/ppermute | solution.py:624
  13.1 0.0 collective-permute-done.4.second_ref
  13.1 1.7 %shard_map.185 = bf16[3,512,128]{2,1,0:T(8,128)(2,1)} custom-call(s32[1]{0:T(128)} %bitcast.at_ref, s32[1]{0:T(128)} %bitcast.1.core_ref, bf16[3,512,128]{2,1,0:T(8,128)(2,1)S(1)} %get-tuple-element.26.query_ref, bf16[3,512,128]{2,1,0:T(8,128)(2,1)S(1)} %get-tuple-element.27.key_ref.own_key_ref, ...), custom_call_target="tpu_custom_call" | custom-call | flops 201326592 | bytes 4194304 | tf_op jit(solution)/shard_map/pallas_call | solution.py:650
Async XLA Ops:
  0.0 5.5 %copy-start.1 = (bf16[128,128]{1,0:T(8,128)(2,1)S(1)}, bf16[128,128]{1,0:T(8,128)(2,1)}, u32[]{:S(2)}) copy-start(bf16[128,128]{1,0:T(8,128)(2,1)} %w_value.3) | copy-start | bytes 98308
  0.0 5.5 %copy-start = (bf16[128,128]{1,0:T(8,128)(2,1)S(1)}, bf16[128,128]{1,0:T(8,128)(2,1)}, u32[]{:S(2)}) copy-start(bf16[128,128]{1,0:T(8,128)(2,1)} %w_key.3) | copy-start | bytes 98308
  0.0 5.5 %copy-start.6 = (bf16[128,128]{1,0:T(8,128)(2,1)S(1)}, bf16[128,128]{1,0:T(8,128)(2,1)}, u32[]{:S(2)}) copy-start(bf16[128,128]{1,0:T(8,128)(2,1)} %w_gate.1) | copy-start | bytes 98308
  0.0 5.5 %copy-start.5 = (bf16[128,128]{1,0:T(8,128)(2,1)S(1)}, bf16[128,128]{1,0:T(8,128)(2,1)}, u32[]{:S(2)}) copy-start(bf16[128,128]{1,0:T(8,128)(2,1)} %w_query.1) | copy-start | bytes 98308
  0.0 5.5 %copy-start.4 = (bf16[128,128]{1,0:T(8,128)(2,1)S(1)}, bf16[128,128]{1,0:T(8,128)(2,1)}, u32[]{:S(2)}) copy-start(bf16[128,128]{1,0:T(8,128)(2,1)} %ada_attn_shift.1) | copy-start | bytes 98308
  0.0 5.5 %copy-start.3 = (bf16[128,128]{1,0:T(8,128)(2,1)S(1)}, bf16[128,128]{1,0:T(8,128)(2,1)}, u32[]{:S(2)}) copy-start(bf16[128,128]{1,0:T(8,128)(2,1)} %ada_attn_scale.1) | copy-start | bytes 98308
  2.3 8.6 %copy-start.2 = (bf16[128,128]{1,0:T(8,128)(2,1)S(1)}, bf16[128,128]{1,0:T(8,128)(2,1)}, u32[]{:S(2)}) copy-start(bf16[128,128]{1,0:T(8,128)(2,1)} %w_out_ref.3) | copy-start | bytes 98308
  2.3 8.6 %copy-start.7 = (s32[4,64]{1,0:T(4,128)S(1)}, s32[4,64]{1,0:T(4,128)}, u32[]{:S(2)}) copy-start(s32[4,64]{1,0:T(4,128)} %counts_ref.1) | copy-start | bytes 3076
  2.3 6.2 %collective-permute-start.2 = (bf16[2,64,128]{2,1,0:T(8,128)(2,1)S(1)}, bf16[2,64,128]{2,1,0:T(8,128)(2,1)S(1)}, u32[]{:S(2)}, u32[]{:S(2)}) collective-permute-start(bf16[2,64,128]{2,1,0:T(8,128)(2,1)S(1)} %get-tuple-element.30.refs_0_), channel_id=1, source_target_pairs={{0,3},{1,2},{2,1},{3,0},{4,7},{5,6},{6,5},{7,4},{8,11},{9,10},{10,... | collective-permute-start | bytes 98312 | tf_op jit(solution)/shard_map/ppermute | solution.py:577
  4.8 4.0 %collective-permute-start.1 = (bf16[2,64,128]{2,1,0:T(8,128)(2,1)S(1)}, bf16[2,64,128]{2,1,0:T(8,128)(2,1)S(1)}, u32[]{:S(2)}, u32[]{:S(2)}) collective-permute-start(bf16[2,64,128]{2,1,0:T(8,128)(2,1)S(1)} %get-tuple-element.30.refs_0_), channel_id=1, source_target_pairs={{0,2},{2,0},{1,3},{3,1},{4,6},{6,4},{5,7},{7,5},{8,10},{10,8},{9,1... | collective-permute-start | bytes 98312 | tf_op jit(solution)/shard_map/ppermute | solution.py:576
  5.4 3.3 %collective-permute-start = (bf16[2,64,128]{2,1,0:T(8,128)(2,1)S(1)}, bf16[2,64,128]{2,1,0:T(8,128)(2,1)S(1)}, u32[]{:S(2)}, u32[]{:S(2)}) collective-permute-start(bf16[2,64,128]{2,1,0:T(8,128)(2,1)S(1)} %get-tuple-element.30.refs_0_), channel_id=1, source_target_pairs={{0,1},{1,0},{2,3},{3,2},{4,5},{5,4},{6,7},{7,6},{8,9},{9,8},{10,11... | collective-permute-start | bytes 98312 | tf_op jit(solution)/shard_map/ppermute | solution.py:578
  8.9 4.2 %collective-permute-start.3 = (bf16[216,128]{1,0:T(8,128)(2,1)S(1)}, bf16[216,128]{1,0:T(8,128)(2,1)S(1)}, u32[]{:S(2)}, u32[]{:S(2)}) collective-permute-start(bf16[216,128]{1,0:T(8,128)(2,1)S(1)} %get-tuple-element.41), channel_id=1, source_target_pairs={{4,0},{8,4},{12,8},{0,1},{1,5},{5,9},{9,13},{13,12},{6,2},{10,6},{... | collective-permute-start | bytes 165896 | tf_op jit(solution)/shard_map/ppermute | solution.py:624
  9.2 4.0 %collective-permute-start.4 = (bf16[216,128]{1,0:T(8,128)(2,1)S(1)}, bf16[216,128]{1,0:T(8,128)(2,1)S(1)}, u32[]{:S(2)}, u32[]{:S(2)}) collective-permute-start(bf16[216,128]{1,0:T(8,128)(2,1)S(1)} %get-tuple-element.42), channel_id=1, source_target_pairs={{0,4},{4,8},{8,12},{1,0},{5,1},{9,5},{13,9},{12,13},{2,6},{6,10},{... | collective-permute-start | bytes 165896 | tf_op jit(solution)/shard_map/ppermute | solution.py:625

commit v26 on v24

--- a/solution.py
+++ b/solution.py
@@ -106,23 +106,17 @@
         pair = pair_ref[chunk * group : (chunk + 1) * group].reshape(group * cols, width)
         chunks.append(dot(side_by_side(pair), centre).astype(BF16))
     mixes = [dot(centred, mix).reshape(half, cols, 2 * lanes) for centred in chunks]
-    squares = [centred[:, :width] * centred[:, :width] for centred in chunks]
+    average = twice(averaging(width))
     averages = [
-        dot(jnp.concatenate(squares[i : i + 2], 1), twice(averaging(width)))
-        for i in range(0, len(squares), 2)
+        dot(centred * centred, average).reshape(half, cols, 2 * lanes) for centred in chunks
     ]
-    for chunk, (centred, mixed) in enumerate(zip(chunks, mixes)):
-        pick = slice(chunk % 2 * width, (chunk % 2 + 1) * width)
-        variances = [
-            averages[chunk // 2][:, pick].reshape(half, cols, width),
-            mean_square(centred[:, width:].astype(F32)).reshape(half, cols, 1),
-        ]
+    for chunk, (mixed, variance) in enumerate(zip(mixes, averages)):
         total = jnp.zeros((cols, lanes), F32)
         spread_out = jnp.zeros((cols, lanes), F32)
         for i in range(group):
             side = slice(i // half * lanes, (i // half + 1) * lanes)
             total = jnp.where(slot == i, mixed[i % half, :, side], total)
-            spread_out = jnp.where(slot == i, variances[i // half][i % half], spread_out)
+            spread_out = jnp.where(slot == i, variance[i % half, :, side], spread_out)
         tile_ref[chunk] = (total * lax.rsqrt(spread_out + EPSILON)).astype(BF16)
 
 

time: 15 us -> 15.3 us (1.020)
  Pallas kernels: 9.06 us -> 9.37 us
    pallas_call x1, Pallas kernels: 2.26 us -> 2.58 us  [shards(): pl.pallas_call(pair_kernel, in_specs=[IN_SMEM] + [IN_HBM] * 2, out_specs=...]
  transfers between devices with their start and end apart: 5 -> 5, of which waited for: 2 -> 2; matrix products, arithmetic and copies ran while one was open for 0% -> 0% of each run, Pallas kernels for 34% -> 33%
where the time goes in v26:
time: 15.3 us; the launch traced here: 15.1 us
  Pallas kernels  9.37 us (61%)
  starting transfers between devices  5.2 us (34%)
  waiting for transfers between devices  0.36 us (2%)
    pallas_call x1, Pallas kernels, shards(): pl.pallas_call(project_kernel, in_specs=[IN_SMEM] + [IN_VMEM] * len(opera...  2.99 us
    pallas_call x1, Pallas kernels, shards(): pl.pallas_call(pair_kernel, in_specs=[IN_SMEM] + [IN_HBM] * 2, out_specs=...  2.58 us
    ppermute x1, starting transfers between devices, shards(): lax.ppermute(own, ('pair', 'samp'), [(0, 3), (1, 2), (2, 1), (3, 0)])  2.48 us
    pallas_call x1, Pallas kernels, shards(): pl.pallas_call(functools.partial(inner_kernel, heads, blocks), in_specs=[...  1.99 us
    ppermute x1, starting transfers between devices, shards(): lax.ppermute(far, ('atoms', 'samp'), [(target, source) for source, target...  1.76 us
    pallas_call x1, Pallas kernels, shards(): pl.pallas_call(functools.partial(outer_kernel, heads, blocks), in_specs=[...  1.7 us
    ppermute x1, starting transfers between devices, shards(): across = lax.ppermute(own, 'pair', swapped)  0.64 us
  transfers between devices with their start and end apart: 5, of which 2 were waited for; matrix products, arithmetic and copies ran while one was open for 0% of the time, Pallas kernels for 33%

profile of v26, /device:TPU:0, one launch (start us, length us, event | category | flops | bytes accessed | tf_op | source)
XLA Modules:
  0.0 15.1 jit_solution(18043482195251001394)
XLA Ops:
  0.0 0.0 copy-start.1
  0.0 0.0 copy-start
  0.0 0.0 copy-start.8
  0.0 0.0 copy-start.7
  0.0 0.0 copy-start.6
  0.0 0.0 copy-start.5
  0.0 0.0 copy-start.4
  0.0 0.0 copy-start.3
  0.0 2.6 %shard_map.182.refs_0_ = bf16[2,64,128]{2,1,0:T(8,128)(2,1)S(1)} custom-call(s32[1]{0:T(128)} %bitcast.1.core_ref, bf16[4,128]{1,0:T(4,128)(2,1)} %bitcast.4, bf16[128,64,128]{2,1,0:T(8,128)(2,1)} %pair_hbm.1), custom_call_target="tpu_custom_call" | custom-call | flops 268435456 | bytes 4194304 | tf_op jit(solution)/shard_map/pallas_call | solution.py:529
  2.6 0.0 copy-start.2
  2.6 0.0 copy-start.9
  2.7 2.5 %collective-permute-start.2 = (bf16[2,64,128]{2,1,0:T(8,128)(2,1)S(1)}, bf16[2,64,128]{2,1,0:T(8,128)(2,1)S(1)}, u32[]{:S(2)}, u32[]{:S(2)}) collective-permute-start(bf16[2,64,128]{2,1,0:T(8,128)(2,1)S(1)} %shard_map.182.refs_0_), channel_id=1, source_target_pairs={{0,3},{1,2},{2,1},{3,0},{4,7},{5,6},{6,5},{7,4},{8,11},{9,10},{10,... | collective-permute-start | bytes 98312 | tf_op jit(solution)/shard_map/ppermute | solution.py:546
  5.1 0.6 %collective-permute-start.1 = (bf16[2,64,128]{2,1,0:T(8,128)(2,1)S(1)}, bf16[2,64,128]{2,1,0:T(8,128)(2,1)S(1)}, u32[]{:S(2)}, u32[]{:S(2)}) collective-permute-start(bf16[2,64,128]{2,1,0:T(8,128)(2,1)S(1)} %shard_map.182.refs_0_), channel_id=1, source_target_pairs={{0,2},{2,0},{1,3},{3,1},{4,6},{6,4},{5,7},{7,5},{8,10},{10,8},{9,1... | collective-permute-start | bytes 98312 | tf_op jit(solution)/shard_map/ppermute | solution.py:545
  5.8 0.0 collective-permute-start
  5.8 0.0 copy-done.1
  5.8 0.0 copy-done
  5.8 0.0 copy-done.8
  5.8 0.0 copy-done.7
  5.8 0.0 copy-done.6
  5.8 0.0 copy-done.5
  5.9 0.0 copy-done.4
  5.9 0.0 copy-done.3
  5.9 3.0 %shard_map.181 = (bf16[3,512,128]{2,1,0:T(8,128)(2,1)S(1)}, bf16[3,512,128]{2,1,0:T(8,128)(2,1)S(1)}, bf16[3,512,128]{2,1,0:T(8,128)(2,1)S(1)}, bf16[3,512,128]{...) custom-call(s32[1]{0:T(128)} %bitcast.1.core_ref, ...), custom_call_target="tpu_custom_call" | custom-call | flops 1006632960 | bytes 4194304 | tf_op jit(solution)/shard_map/pallas_call | solution.py:562
  8.9 0.0 collective-permute-done.2.refs_3_
  8.9 0.2 %collective-permute-done.1.refs_2_ = bf16[2,64,128]{2,1,0:T(8,128)(2,1)S(1)} collective-permute-done((bf16[2,64,128]{2,1,0:T(8,128)(2,1)S(1)}, bf16[2,64,128]{2,1,0:T(8,128)(2,1)S(1)}, u32[]{:S(2)}, u32[]{:S(2)}) %collective-permute-start.1) | collective-permute-done | bytes 32800 | tf_op jit(solution)/shard_map/ppermute | solution.py:545
  9.1 0.0 collective-permute-done.refs_1_
  9.1 0.1 shard_map.183
  9.2 0.3 %collective-permute-start.3 = (bf16[216,128]{1,0:T(8,128)(2,1)S(1)}, bf16[216,128]{1,0:T(8,128)(2,1)S(1)}, u32[]{:S(2)}, u32[]{:S(2)}) collective-permute-start(bf16[216,128]{1,0:T(8,128)(2,1)S(1)} %get-tuple-element.35), channel_id=1, source_target_pairs={{4,0},{8,4},{12,8},{0,1},{1,5},{5,9},{9,13},{13,12},{6,2},{10,6},{... | collective-permute-start | bytes 165896 | tf_op jit(solution)/shard_map/ppermute | solution.py:593
  9.5 1.8 %collective-permute-start.4 = (bf16[216,128]{1,0:T(8,128)(2,1)S(1)}, bf16[216,128]{1,0:T(8,128)(2,1)S(1)}, u32[]{:S(2)}, u32[]{:S(2)}) collective-permute-start(bf16[216,128]{1,0:T(8,128)(2,1)S(1)} %get-tuple-element.36), channel_id=1, source_target_pairs={{0,4},{4,8},{8,12},{1,0},{5,1},{9,5},{13,9},{12,13},{2,6},{6,10},{... | collective-permute-start | bytes 165896 | tf_op jit(solution)/shard_map/ppermute | solution.py:594
  11.3 0.0 copy-done.2
  11.3 0.0 copy-done.9
  11.3 2.0 %shard_map.184 = (bf16[3,384,128]{2,1,0:T(8,128)(2,1)S(1)}, bf16[2,2,128,256]{3,2,1,0:T(8,128)(2,1)S(1)}, bf16[2,48,48]{2,1,0:T(8,128)(2,1)S(1)}, bf16[2,112,256]{2,1,0:T(8,128)(2,1)S(1)}) custom-call(s32[1]{0:T(128)} %bitcast.at_ref, s32[4,64]{1,0:T(4,128)S(1)} %copy-done.9, bf16[3,512,128]{2,1,0:T(8,128)(2,1)S(1)} %get-tuple-element.21.query_ref, ...), custom_call_target="tpu_custom_call" | custom-call | flops 603979776 | bytes 4194304 | tf_op jit(solution)/shard_map/pallas_call | solution.py:600
  13.3 0.1 collective-permute-done.3.first_ref
  13.4 0.0 collective-permute-done.4.second_ref
  13.4 1.7 %shard_map.185 = bf16[3,512,128]{2,1,0:T(8,128)(2,1)} custom-call(s32[1]{0:T(128)} %bitcast.at_ref, s32[1]{0:T(128)} %bitcast.1.core_ref, bf16[3,512,128]{2,1,0:T(8,128)(2,1)S(1)} %get-tuple-element.21.query_ref, bf16[3,512,128]{2,1,0:T(8,128)(2,1)S(1)} %get-tuple-element.22.key_ref.own_key_ref, ...), custom_call_target="tpu_custom_call" | custom-call | flops 201326592 | bytes 4194304 | tf_op jit(solution)/shard_map/pallas_call | solution.py:619
Async XLA Ops:
  0.0 5.8 %copy-start.1 = (bf16[128,128]{1,0:T(8,128)(2,1)S(1)}, bf16[128,128]{1,0:T(8,128)(2,1)}, u32[]{:S(2)}) copy-start(bf16[128,128]{1,0:T(8,128)(2,1)} %w_value.3) | copy-start | bytes 98308
  0.0 5.8 %copy-start = (bf16[128,128]{1,0:T(8,128)(2,1)S(1)}, bf16[128,128]{1,0:T(8,128)(2,1)}, u32[]{:S(2)}) copy-start(bf16[128,128]{1,0:T(8,128)(2,1)} %w_key.3) | copy-start | bytes 98308
  0.0 5.8 %copy-start.8 = (bf16[128,128]{1,0:T(8,128)(2,1)S(1)}, bf16[128,128]{1,0:T(8,128)(2,1)}, u32[]{:S(2)}) copy-start(bf16[128,128]{1,0:T(8,128)(2,1)} %w_gate.1) | copy-start | bytes 98308
  0.0 5.8 %copy-start.7 = (bf16[128,128]{1,0:T(8,128)(2,1)S(1)}, bf16[128,128]{1,0:T(8,128)(2,1)}, u32[]{:S(2)}) copy-start(bf16[128,128]{1,0:T(8,128)(2,1)} %w_query.1) | copy-start | bytes 98308
  0.0 5.8 %copy-start.6 = (bf16[128,128]{1,0:T(8,128)(2,1)S(1)}, bf16[128,128]{1,0:T(8,128)(2,1)}, u32[]{:S(2)}) copy-start(bf16[128,128]{1,0:T(8,128)(2,1)} %ada_attn_shift.1) | copy-start | bytes 98308
  0.0 5.8 %copy-start.5 = (bf16[128,128]{1,0:T(8,128)(2,1)S(1)}, bf16[128,128]{1,0:T(8,128)(2,1)}, u32[]{:S(2)}) copy-start(bf16[128,128]{1,0:T(8,128)(2,1)} %ada_attn_scale.1) | copy-start | bytes 98308
  0.0 5.8 %copy-start.4 = (bf16[512,128]{1,0:T(8,128)(2,1)S(1)}, bf16[512,128]{1,0:T(8,128)(2,1)}, u32[]{:S(2)}) copy-start(bf16[512,128]{1,0:T(8,128)(2,1)} %cond_ref.1) | copy-start | bytes 393220
  0.0 5.8 %copy-start.3 = (bf16[3,512,128]{2,1,0:T(8,128)(2,1)S(1)}, bf16[3,512,128]{2,1,0:T(8,128)(2,1)}, u32[]{:S(2)}) copy-start(bf16[3,512,128]{2,1,0:T(8,128)(2,1)} %single_ref.1) | copy-start | bytes 1179652
  2.6 8.6 %copy-start.2 = (bf16[128,128]{1,0:T(8,128)(2,1)S(1)}, bf16[128,128]{1,0:T(8,128)(2,1)}, u32[]{:S(2)}) copy-start(bf16[128,128]{1,0:T(8,128)(2,1)} %w_out_ref.3) | copy-start | bytes 98308
  2.6 8.6 %copy-start.9 = (s32[4,64]{1,0:T(4,128)S(1)}, s32[4,64]{1,0:T(4,128)}, u32[]{:S(2)}) copy-start(s32[4,64]{1,0:T(4,128)} %counts_ref.1) | copy-start | bytes 3076
  2.7 6.2 %collective-permute-start.2 = (bf16[2,64,128]{2,1,0:T(8,128)(2,1)S(1)}, bf16[2,64,128]{2,1,0:T(8,128)(2,1)S(1)}, u32[]{:S(2)}, u32[]{:S(2)}) collective-permute-start(bf16[2,64,128]{2,1,0:T(8,128)(2,1)S(1)} %shard_map.182.refs_0_), channel_id=1, source_target_pairs={{0,3},{1,2},{2,1},{3,0},{4,7},{5,6},{6,5},{7,4},{8,11},{9,10},{10,... | collective-permute-start | bytes 98312 | tf_op jit(solution)/shard_map/ppermute | solution.py:546
  5.1 4.0 %collective-permute-start.1 = (bf16[2,64,128]{2,1,0:T(8,128)(2,1)S(1)}, bf16[2,64,128]{2,1,0:T(8,128)(2,1)S(1)}, u32[]{:S(2)}, u32[]{:S(2)}) collective-permute-start(bf16[2,64,128]{2,1,0:T(8,128)(2,1)S(1)} %shard_map.182.refs_0_), channel_id=1, source_target_pairs={{0,2},{2,0},{1,3},{3,1},{4,6},{6,4},{5,7},{7,5},{8,10},{10,8},{9,1... | collective-permute-start | bytes 98312 | tf_op jit(solution)/shard_map/ppermute | solution.py:545
  5.8 3.3 %collective-permute-start = (bf16[2,64,128]{2,1,0:T(8,128)(2,1)S(1)}, bf16[2,64,128]{2,1,0:T(8,128)(2,1)S(1)}, u32[]{:S(2)}, u32[]{:S(2)}) collective-permute-start(bf16[2,64,128]{2,1,0:T(8,128)(2,1)S(1)} %shard_map.182.refs_0_), channel_id=1, source_target_pairs={{0,1},{1,0},{2,3},{3,2},{4,5},{5,4},{6,7},{7,6},{8,9},{9,8},{10,11... | collective-permute-start | bytes 98312 | tf_op jit(solution)/shard_map/ppermute | solution.py:547
  9.2 4.2 %collective-permute-start.3 = (bf16[216,128]{1,0:T(8,128)(2,1)S(1)}, bf16[216,128]{1,0:T(8,128)(2,1)S(1)}, u32[]{:S(2)}, u32[]{:S(2)}) collective-permute-start(bf16[216,128]{1,0:T(8,128)(2,1)S(1)} %get-tuple-element.35), channel_id=1, source_target_pairs={{4,0},{8,4},{12,8},{0,1},{1,5},{5,9},{9,13},{13,12},{6,2},{10,6},{... | collective-permute-start | bytes 165896 | tf_op jit(solution)/shard_map/ppermute | solution.py:593
  9.5 3.9 %collective-permute-start.4 = (bf16[216,128]{1,0:T(8,128)(2,1)S(1)}, bf16[216,128]{1,0:T(8,128)(2,1)S(1)}, u32[]{:S(2)}, u32[]{:S(2)}) collective-permute-start(bf16[216,128]{1,0:T(8,128)(2,1)S(1)} %get-tuple-element.36), channel_id=1, source_target_pairs={{0,4},{4,8},{8,12},{1,0},{5,1},{9,5},{13,9},{12,13},{2,6},{6,10},{... | collective-permute-start | bytes 165896 | tf_op jit(solution)/shard_map/ppermute | solution.py:594

commit v27 on v26

--- a/solution.py
+++ b/solution.py
@@ -106,17 +106,20 @@
         pair = pair_ref[chunk * group : (chunk + 1) * group].reshape(group * cols, width)
         chunks.append(dot(side_by_side(pair), centre).astype(BF16))
     mixes = [dot(centred, mix).reshape(half, cols, 2 * lanes) for centred in chunks]
-    average = twice(averaging(width))
-    averages = [
-        dot(centred * centred, average).reshape(half, cols, 2 * lanes) for centred in chunks
-    ]
-    for chunk, (mixed, variance) in enumerate(zip(mixes, averages)):
+    squares = chunks[0][:, :width] * chunks[0][:, :width]
+    average = dot(side_by_side(squares), twice(averaging(width)))
+    average = jnp.concatenate([average[:, :width], average[:, width:]], 0)
+    for chunk, (centred, mixed) in enumerate(zip(chunks, mixes)):
+        variances = [average.reshape(half, cols, width)] if chunk == 0 else []
+        for part in range(len(variances), 2):
+            rows_of = centred[:, part * width : (part + 1) * width].astype(F32)
+            variances.append(mean_square(rows_of).reshape(half, cols, 1))
         total = jnp.zeros((cols, lanes), F32)
         spread_out = jnp.zeros((cols, lanes), F32)
         for i in range(group):
             side = slice(i // half * lanes, (i // half + 1) * lanes)
             total = jnp.where(slot == i, mixed[i % half, :, side], total)
-            spread_out = jnp.where(slot == i, variance[i % half, :, side], spread_out)
+            spread_out = jnp.where(slot == i, variances[i // half][i % half], spread_out)
         tile_ref[chunk] = (total * lax.rsqrt(spread_out + EPSILON)).astype(BF16)
 
 
@@ -157,6 +160,8 @@
         head, tail = normed[sample, :EDGE], normed[sample, atoms_here - EDGE :]
         near_ref[cut, :] = jnp.where(down, head, tail)
         far_ref[cut, :] = jnp.where(down, tail, head)
+    for copy in copies:
+        copy.wait()
     normed = normed.reshape(-1, width)
     both = dot(normed, beside(w_key, w_value)).astype(BF16).reshape(samples, -1, 2 * width)
     key_ref[...] = both[:, :, :width]
@@ -165,8 +170,6 @@
     query_ref[...] = both[:, :, :width].astype(BF16)
     gate_ref[...] = sigmoid(both[:, :, width:]).astype(BF16)
 
-    for copy in copies:
-        copy.wait()
     gates = dot(cond, beside(attn_gate, trans_gate))
     open_ref[...] = sigmoid(gates[:, :width]).astype(BF16)
     normed = attn_norm(cond, single, beside(ada_trans_scale, ada_trans_shift)).reshape(-1, width)

time: 15.3 us -> 15 us (0.980)
  Pallas kernels: 9.37 us -> 9.09 us
    pallas_call x1, Pallas kernels: 2.58 us -> 2.27 us  [shards(): pl.pallas_call(pair_kernel, in_specs=[IN_SMEM] + [IN_HBM] * 2, out_specs=...]
  transfers between devices with their start and end apart: 5 -> 5, of which waited for: 2 -> 2; matrix products, arithmetic and copies ran while one was open for 0% -> 0% of each run, Pallas kernels for 33% -> 34%
where the time goes in v27:
time: 15 us; the launch traced here: 14.8 us
  Pallas kernels  9.09 us (61%)
  starting transfers between devices  5.2 us (35%)
  waiting for transfers between devices  0.34 us (2%)
    pallas_call x1, Pallas kernels, shards(): pl.pallas_call(project_kernel, in_specs=[IN_SMEM] + [IN_VMEM] * len(opera...  3.02 us
    ppermute x1, starting transfers between devices, shards(): lax.ppermute(own, ('pair', 'samp'), [(0, 3), (1, 2), (2, 1), (3, 0)])  2.48 us
    pallas_call x1, Pallas kernels, shards(): pl.pallas_call(pair_kernel, in_specs=[IN_SMEM] + [IN_HBM] * 2, out_specs=...  2.27 us
    pallas_call x1, Pallas kernels, shards(): pl.pallas_call(functools.partial(inner_kernel, heads, blocks), in_specs=[...  1.99 us
    ppermute x1, starting transfers between devices, shards(): lax.ppermute(far, ('atoms', 'samp'), [(target, source) for source, target...  1.73 us
    pallas_call x1, Pallas kernels, shards(): pl.pallas_call(functools.partial(outer_kernel, heads, blocks), in_specs=[...  1.7 us
    ppermute x1, starting transfers between devices, shards(): across = lax.ppermute(own, 'pair', swapped)  0.64 us
    ppermute x1, starting transfers between devices, shards(): first = lax.ppermute(near, ('atoms', 'samp'), cycle)  0.31 us
  transfers between devices with their start and end apart: 5, of which 2 were waited for; matrix products, arithmetic and copies ran while one was open for 0% of the time, Pallas kernels for 34%

profile of v27, /device:TPU:0, one launch (start us, length us, event | category | flops | bytes accessed | tf_op | source)
XLA Modules:
  0.0 14.8 jit_solution(11438881090235258540)
XLA Ops:
  0.0 0.0 copy-start.1
  0.0 0.0 copy-start
  0.0 0.0 copy-start.8
  0.0 0.0 copy-start.7
  0.0 0.0 copy-start.6
  0.0 0.0 copy-start.5
  0.0 0.0 copy-start.4
  0.0 0.0 copy-start.3
  0.0 2.3 %shard_map.182.refs_0_ = bf16[2,64,128]{2,1,0:T(8,128)(2,1)S(1)} custom-call(s32[1]{0:T(128)} %bitcast.1.core_ref, bf16[4,128]{1,0:T(4,128)(2,1)} %bitcast.4, bf16[128,64,128]{2,1,0:T(8,128)(2,1)} %pair_hbm.1), custom_call_target="tpu_custom_call" | custom-call | flops 268435456 | bytes 4194304 | tf_op jit(solution)/shard_map/pallas_call | solution.py:532
  2.3 0.0 copy-start.2
  2.3 0.0 copy-start.9
  2.3 2.5 %collective-permute-start.2 = (bf16[2,64,128]{2,1,0:T(8,128)(2,1)S(1)}, bf16[2,64,128]{2,1,0:T(8,128)(2,1)S(1)}, u32[]{:S(2)}, u32[]{:S(2)}) collective-permute-start(bf16[2,64,128]{2,1,0:T(8,128)(2,1)S(1)} %shard_map.182.refs_0_), channel_id=1, source_target_pairs={{0,3},{1,2},{2,1},{3,0},{4,7},{5,6},{6,5},{7,4},{8,11},{9,10},{10,... | collective-permute-start | bytes 98312 | tf_op jit(solution)/shard_map/ppermute | solution.py:549
  4.8 0.6 %collective-permute-start.1 = (bf16[2,64,128]{2,1,0:T(8,128)(2,1)S(1)}, bf16[2,64,128]{2,1,0:T(8,128)(2,1)S(1)}, u32[]{:S(2)}, u32[]{:S(2)}) collective-permute-start(bf16[2,64,128]{2,1,0:T(8,128)(2,1)S(1)} %shard_map.182.refs_0_), channel_id=1, source_target_pairs={{0,2},{2,0},{1,3},{3,1},{4,6},{6,4},{5,7},{7,5},{8,10},{10,8},{9,1... | collective-permute-start | bytes 98312 | tf_op jit(solution)/shard_map/ppermute | solution.py:548
  5.5 0.0 collective-permute-start
  5.5 0.0 copy-done.1
  5.5 0.0 copy-done
  5.5 0.0 copy-done.8
  5.5 0.0 copy-done.7
  5.5 0.0 copy-done.6
  5.5 0.0 copy-done.5
  5.5 0.0 copy-done.4
  5.6 0.0 copy-done.3
  5.6 3.0 %shard_map.181 = (bf16[3,512,128]{2,1,0:T(8,128)(2,1)S(1)}, bf16[3,512,128]{2,1,0:T(8,128)(2,1)S(1)}, bf16[3,512,128]{2,1,0:T(8,128)(2,1)S(1)}, bf16[3,512,128]{...) custom-call(s32[1]{0:T(128)} %bitcast.1.core_ref, ...), custom_call_target="tpu_custom_call" | custom-call | flops 1006632960 | bytes 4194304 | tf_op jit(solution)/shard_map/pallas_call | solution.py:565
  8.6 0.0 collective-permute-done.2.refs_3_
  8.6 0.2 %collective-permute-done.1.refs_2_ = bf16[2,64,128]{2,1,0:T(8,128)(2,1)S(1)} collective-permute-done((bf16[2,64,128]{2,1,0:T(8,128)(2,1)S(1)}, bf16[2,64,128]{2,1,0:T(8,128)(2,1)S(1)}, u32[]{:S(2)}, u32[]{:S(2)}) %collective-permute-start.1) | collective-permute-done | bytes 32800 | tf_op jit(solution)/shard_map/ppermute | solution.py:548
  8.8 0.0 collective-permute-done.refs_1_
  8.8 0.1 shard_map.183
  8.9 0.3 %collective-permute-start.3 = (bf16[216,128]{1,0:T(8,128)(2,1)S(1)}, bf16[216,128]{1,0:T(8,128)(2,1)S(1)}, u32[]{:S(2)}, u32[]{:S(2)}) collective-permute-start(bf16[216,128]{1,0:T(8,128)(2,1)S(1)} %get-tuple-element.35), channel_id=1, source_target_pairs={{4,0},{8,4},{12,8},{0,1},{1,5},{5,9},{9,13},{13,12},{6,2},{10,6},{... | collective-permute-start | bytes 165896 | tf_op jit(solution)/shard_map/ppermute | solution.py:596
  9.2 1.7 %collective-permute-start.4 = (bf16[216,128]{1,0:T(8,128)(2,1)S(1)}, bf16[216,128]{1,0:T(8,128)(2,1)S(1)}, u32[]{:S(2)}, u32[]{:S(2)}) collective-permute-start(bf16[216,128]{1,0:T(8,128)(2,1)S(1)} %get-tuple-element.36), channel_id=1, source_target_pairs={{0,4},{4,8},{8,12},{1,0},{5,1},{9,5},{13,9},{12,13},{2,6},{6,10},{... | collective-permute-start | bytes 165896 | tf_op jit(solution)/shard_map/ppermute | solution.py:597
  11.0 0.0 copy-done.2
  11.0 0.0 copy-done.9
  11.0 2.0 %shard_map.184 = (bf16[3,384,128]{2,1,0:T(8,128)(2,1)S(1)}, bf16[2,2,128,256]{3,2,1,0:T(8,128)(2,1)S(1)}, bf16[2,48,48]{2,1,0:T(8,128)(2,1)S(1)}, bf16[2,112,256]{2,1,0:T(8,128)(2,1)S(1)}) custom-call(s32[1]{0:T(128)} %bitcast.at_ref, s32[4,64]{1,0:T(4,128)S(1)} %copy-done.9, bf16[3,512,128]{2,1,0:T(8,128)(2,1)S(1)} %get-tuple-element.21.query_ref, ...), custom_call_target="tpu_custom_call" | custom-call | flops 603979776 | bytes 4194304 | tf_op jit(solution)/shard_map/pallas_call | solution.py:603
  13.0 0.1 collective-permute-done.3.first_ref
  13.1 0.0 collective-permute-done.4.second_ref
  13.1 1.7 %shard_map.185 = bf16[3,512,128]{2,1,0:T(8,128)(2,1)} custom-call(s32[1]{0:T(128)} %bitcast.at_ref, s32[1]{0:T(128)} %bitcast.1.core_ref, bf16[3,512,128]{2,1,0:T(8,128)(2,1)S(1)} %get-tuple-element.21.query_ref, bf16[3,512,128]{2,1,0:T(8,128)(2,1)S(1)} %get-tuple-element.22.key_ref.own_key_ref, ...), custom_call_target="tpu_custom_call" | custom-call | flops 201326592 | bytes 4194304 | tf_op jit(solution)/shard_map/pallas_call | solution.py:622
Async XLA Ops:
  0.0 5.5 %copy-start.1 = (bf16[128,128]{1,0:T(8,128)(2,1)S(1)}, bf16[128,128]{1,0:T(8,128)(2,1)}, u32[]{:S(2)}) copy-start(bf16[128,128]{1,0:T(8,128)(2,1)} %w_value.3) | copy-start | bytes 98308
  0.0 5.5 %copy-start = (bf16[128,128]{1,0:T(8,128)(2,1)S(1)}, bf16[128,128]{1,0:T(8,128)(2,1)}, u32[]{:S(2)}) copy-start(bf16[128,128]{1,0:T(8,128)(2,1)} %w_key.3) | copy-start | bytes 98308
  0.0 5.5 %copy-start.8 = (bf16[128,128]{1,0:T(8,128)(2,1)S(1)}, bf16[128,128]{1,0:T(8,128)(2,1)}, u32[]{:S(2)}) copy-start(bf16[128,128]{1,0:T(8,128)(2,1)} %w_gate.1) | copy-start | bytes 98308
  0.0 5.5 %copy-start.7 = (bf16[128,128]{1,0:T(8,128)(2,1)S(1)}, bf16[128,128]{1,0:T(8,128)(2,1)}, u32[]{:S(2)}) copy-start(bf16[128,128]{1,0:T(8,128)(2,1)} %w_query.1) | copy-start | bytes 98308
  0.0 5.5 %copy-start.6 = (bf16[128,128]{1,0:T(8,128)(2,1)S(1)}, bf16[128,128]{1,0:T(8,128)(2,1)}, u32[]{:S(2)}) copy-start(bf16[128,128]{1,0:T(8,128)(2,1)} %ada_attn_shift.1) | copy-start | bytes 98308
  0.0 5.5 %copy-start.5 = (bf16[128,128]{1,0:T(8,128)(2,1)S(1)}, bf16[128,128]{1,0:T(8,128)(2,1)}, u32[]{:S(2)}) copy-start(bf16[128,128]{1,0:T(8,128)(2,1)} %ada_attn_scale.1) | copy-start | bytes 98308
  0.0 5.5 %copy-start.4 = (bf16[512,128]{1,0:T(8,128)(2,1)S(1)}, bf16[512,128]{1,0:T(8,128)(2,1)}, u32[]{:S(2)}) copy-start(bf16[512,128]{1,0:T(8,128)(2,1)} %cond_ref.1) | copy-start | bytes 393220
  0.0 5.5 %copy-start.3 = (bf16[3,512,128]{2,1,0:T(8,128)(2,1)S(1)}, bf16[3,512,128]{2,1,0:T(8,128)(2,1)}, u32[]{:S(2)}) copy-start(bf16[3,512,128]{2,1,0:T(8,128)(2,1)} %single_ref.1) | copy-start | bytes 1179652
  2.3 8.6 %copy-start.2 = (bf16[128,128]{1,0:T(8,128)(2,1)S(1)}, bf16[128,128]{1,0:T(8,128)(2,1)}, u32[]{:S(2)}) copy-start(bf16[128,128]{1,0:T(8,128)(2,1)} %w_out_ref.3) | copy-start | bytes 98308
  2.3 8.6 %copy-start.9 = (s32[4,64]{1,0:T(4,128)S(1)}, s32[4,64]{1,0:T(4,128)}, u32[]{:S(2)}) copy-start(s32[4,64]{1,0:T(4,128)} %counts_ref.1) | copy-start | bytes 3076
  2.3 6.3 %collective-permute-start.2 = (bf16[2,64,128]{2,1,0:T(8,128)(2,1)S(1)}, bf16[2,64,128]{2,1,0:T(8,128)(2,1)S(1)}, u32[]{:S(2)}, u32[]{:S(2)}) collective-permute-start(bf16[2,64,128]{2,1,0:T(8,128)(2,1)S(1)} %shard_map.182.refs_0_), channel_id=1, source_target_pairs={{0,3},{1,2},{2,1},{3,0},{4,7},{5,6},{6,5},{7,4},{8,11},{9,10},{10,... | collective-permute-start | bytes 98312 | tf_op jit(solution)/shard_map/ppermute | solution.py:549
  4.8 4.0 %collective-permute-start.1 = (bf16[2,64,128]{2,1,0:T(8,128)(2,1)S(1)}, bf16[2,64,128]{2,1,0:T(8,128)(2,1)S(1)}, u32[]{:S(2)}, u32[]{:S(2)}) collective-permute-start(bf16[2,64,128]{2,1,0:T(8,128)(2,1)S(1)} %shard_map.182.refs_0_), channel_id=1, source_target_pairs={{0,2},{2,0},{1,3},{3,1},{4,6},{6,4},{5,7},{7,5},{8,10},{10,8},{9,1... | collective-permute-start | bytes 98312 | tf_op jit(solution)/shard_map/ppermute | solution.py:548
  5.5 3.3 %collective-permute-start = (bf16[2,64,128]{2,1,0:T(8,128)(2,1)S(1)}, bf16[2,64,128]{2,1,0:T(8,128)(2,1)S(1)}, u32[]{:S(2)}, u32[]{:S(2)}) collective-permute-start(bf16[2,64,128]{2,1,0:T(8,128)(2,1)S(1)} %shard_map.182.refs_0_), channel_id=1, source_target_pairs={{0,1},{1,0},{2,3},{3,2},{4,5},{5,4},{6,7},{7,6},{8,9},{9,8},{10,11... | collective-permute-start | bytes 98312 | tf_op jit(solution)/shard_map/ppermute | solution.py:550
  8.9 4.2 %collective-permute-start.3 = (bf16[216,128]{1,0:T(8,128)(2,1)S(1)}, bf16[216,128]{1,0:T(8,128)(2,1)S(1)}, u32[]{:S(2)}, u32[]{:S(2)}) collective-permute-start(bf16[216,128]{1,0:T(8,128)(2,1)S(1)} %get-tuple-element.35), channel_id=1, source_target_pairs={{4,0},{8,4},{12,8},{0,1},{1,5},{5,9},{9,13},{13,12},{6,2},{10,6},{... | collective-permute-start | bytes 165896 | tf_op jit(solution)/shard_map/ppermute | solution.py:596
  9.2 3.9 %collective-permute-start.4 = (bf16[216,128]{1,0:T(8,128)(2,1)S(1)}, bf16[216,128]{1,0:T(8,128)(2,1)S(1)}, u32[]{:S(2)}, u32[]{:S(2)}) collective-permute-start(bf16[216,128]{1,0:T(8,128)(2,1)S(1)} %get-tuple-element.36), channel_id=1, source_target_pairs={{0,4},{4,8},{8,12},{1,0},{5,1},{9,5},{13,9},{12,13},{2,6},{6,10},{... | collective-permute-start | bytes 165896 | tf_op jit(solution)/shard_map/ppermute | solution.py:597

commit v28 on v27

--- a/solution.py
+++ b/solution.py
@@ -100,17 +100,17 @@
     centre = twice(centring(width))
     slot = iota((cols, lanes), 1) % group
 
-    chunks = []
     for chunk in range(rows // group):
         pair_copy(chunk).wait()
         pair = pair_ref[chunk * group : (chunk + 1) * group].reshape(group * cols, width)
-        chunks.append(dot(side_by_side(pair), centre).astype(BF16))
-    mixes = [dot(centred, mix).reshape(half, cols, 2 * lanes) for centred in chunks]
-    squares = chunks[0][:, :width] * chunks[0][:, :width]
-    average = dot(side_by_side(squares), twice(averaging(width)))
-    average = jnp.concatenate([average[:, :width], average[:, width:]], 0)
-    for chunk, (centred, mixed) in enumerate(zip(chunks, mixes)):
-        variances = [average.reshape(half, cols, width)] if chunk == 0 else []
+        centred = dot(side_by_side(pair), centre).astype(BF16)
+        mixed = dot(centred, mix).reshape(half, cols, 2 * lanes)
+        variances = []
+        if chunk == 0:
+            squares = side_by_side(centred[:, :width] * centred[:, :width])
+            average = dot(squares, twice(averaging(width)))
+            average = jnp.concatenate([average[:, :width], average[:, width:]], 0)
+            variances.append(average.reshape(half, cols, width))
         for part in range(len(variances), 2):
             rows_of = centred[:, part * width : (part + 1) * width].astype(F32)
             variances.append(mean_square(rows_of).reshape(half, cols, 1))

time: 15 us -> 15.1 us (level)
  no operation moved by 1% of the time
where the time goes in v28:
time: 15.1 us; the launch traced here: 14.9 us
  Pallas kernels  9.17 us (61%)
  starting transfers between devices  5.2 us (34%)
  waiting for transfers between devices  0.34 us (2%)
    pallas_call x1, Pallas kernels, shards(): pl.pallas_call(project_kernel, in_specs=[IN_SMEM] + [IN_VMEM] * len(opera...  3.01 us
    ppermute x1, starting transfers between devices, shards(): lax.ppermute(own, ('pair', 'samp'), [(0, 3), (1, 2), (2, 1), (3, 0)])  2.48 us
    pallas_call x1, Pallas kernels, shards(): pl.pallas_call(pair_kernel, in_specs=[IN_SMEM] + [IN_HBM] * 2, out_specs=...  2.35 us
    pallas_call x1, Pallas kernels, shards(): pl.pallas_call(functools.partial(inner_kernel, heads, blocks), in_specs=[...  1.99 us
    ppermute x1, starting transfers between devices, shards(): lax.ppermute(far, ('atoms', 'samp'), [(target, source) for source, target...  1.73 us
    pallas_call x1, Pallas kernels, shards(): pl.pallas_call(functools.partial(outer_kernel, heads, blocks), in_specs=[...  1.7 us
    ppermute x1, starting transfers between devices, shards(): across = lax.ppermute(own, 'pair', swapped)  0.64 us
    ppermute x1, starting transfers between devices, shards(): first = lax.ppermute(near, ('atoms', 'samp'), cycle)  0.31 us
  transfers between devices with their start and end apart: 5, of which 2 were waited for; matrix products, arithmetic and copies ran while one was open for 0% of the time, Pallas kernels for 34%

profile of v28, /device:TPU:0, one launch (start us, length us, event | category | flops | bytes accessed | tf_op | source)
XLA Modules:
  0.0 14.9 jit_solution(8216831970270576481)
XLA Ops:
  0.0 0.0 copy-start.1
  0.0 0.0 copy-start
  0.0 0.0 copy-start.8
  0.0 0.0 copy-start.7
  0.0 0.0 copy-start.6
  0.0 0.0 copy-start.5
  0.0 0.0 copy-start.4
  0.0 0.0 copy-start.3
  0.0 2.4 %shard_map.182.refs_0_ = bf16[2,64,128]{2,1,0:T(8,128)(2,1)S(1)} custom-call(s32[1]{0:T(128)} %bitcast.1.core_ref, bf16[4,128]{1,0:T(4,128)(2,1)} %bitcast.4, bf16[128,64,128]{2,1,0:T(8,128)(2,1)} %pair_hbm.1), custom_call_target="tpu_custom_call" | custom-call | flops 268435456 | bytes 4194304 | tf_op jit(solution)/shard_map/pallas_call | solution.py:532
  2.4 0.0 copy-start.2
  2.4 0.0 copy-start.9
  2.4 2.5 %collective-permute-start.2 = (bf16[2,64,128]{2,1,0:T(8,128)(2,1)S(1)}, bf16[2,64,128]{2,1,0:T(8,128)(2,1)S(1)}, u32[]{:S(2)}, u32[]{:S(2)}) collective-permute-start(bf16[2,64,128]{2,1,0:T(8,128)(2,1)S(1)} %shard_map.182.refs_0_), channel_id=1, source_target_pairs={{0,3},{1,2},{2,1},{3,0},{4,7},{5,6},{6,5},{7,4},{8,11},{9,10},{10,... | collective-permute-start | bytes 98312 | tf_op jit(solution)/shard_map/ppermute | solution.py:549
  4.9 0.6 %collective-permute-start.1 = (bf16[2,64,128]{2,1,0:T(8,128)(2,1)S(1)}, bf16[2,64,128]{2,1,0:T(8,128)(2,1)S(1)}, u32[]{:S(2)}, u32[]{:S(2)}) collective-permute-start(bf16[2,64,128]{2,1,0:T(8,128)(2,1)S(1)} %shard_map.182.refs_0_), channel_id=1, source_target_pairs={{0,2},{2,0},{1,3},{3,1},{4,6},{6,4},{5,7},{7,5},{8,10},{10,8},{9,1... | collective-permute-start | bytes 98312 | tf_op jit(solution)/shard_map/ppermute | solution.py:548
  5.6 0.0 collective-permute-start
  5.6 0.0 copy-done.1
  5.6 0.0 copy-done
  5.6 0.0 copy-done.8
  5.6 0.0 copy-done.7
  5.6 0.0 copy-done.6
  5.6 0.0 copy-done.5
  5.6 0.0 copy-done.4
  5.6 0.0 copy-done.3
  5.6 3.0 %shard_map.181 = (bf16[3,512,128]{2,1,0:T(8,128)(2,1)S(1)}, bf16[3,512,128]{2,1,0:T(8,128)(2,1)S(1)}, bf16[3,512,128]{2,1,0:T(8,128)(2,1)S(1)}, bf16[3,512,128]{...) custom-call(s32[1]{0:T(128)} %bitcast.1.core_ref, ...), custom_call_target="tpu_custom_call" | custom-call | flops 1006632960 | bytes 4194304 | tf_op jit(solution)/shard_map/pallas_call | solution.py:565
  8.7 0.0 collective-permute-done.2.refs_3_
  8.7 0.2 %collective-permute-done.1.refs_2_ = bf16[2,64,128]{2,1,0:T(8,128)(2,1)S(1)} collective-permute-done((bf16[2,64,128]{2,1,0:T(8,128)(2,1)S(1)}, bf16[2,64,128]{2,1,0:T(8,128)(2,1)S(1)}, u32[]{:S(2)}, u32[]{:S(2)}) %collective-permute-start.1) | collective-permute-done | bytes 32800 | tf_op jit(solution)/shard_map/ppermute | solution.py:548
  8.9 0.0 collective-permute-done.refs_1_
  8.9 0.1 shard_map.183
  9.0 0.3 %collective-permute-start.3 = (bf16[216,128]{1,0:T(8,128)(2,1)S(1)}, bf16[216,128]{1,0:T(8,128)(2,1)S(1)}, u32[]{:S(2)}, u32[]{:S(2)}) collective-permute-start(bf16[216,128]{1,0:T(8,128)(2,1)S(1)} %get-tuple-element.35), channel_id=1, source_target_pairs={{4,0},{8,4},{12,8},{0,1},{1,5},{5,9},{9,13},{13,12},{6,2},{10,6},{... | collective-permute-start | bytes 165896 | tf_op jit(solution)/shard_map/ppermute | solution.py:596
  9.3 1.7 %collective-permute-start.4 = (bf16[216,128]{1,0:T(8,128)(2,1)S(1)}, bf16[216,128]{1,0:T(8,128)(2,1)S(1)}, u32[]{:S(2)}, u32[]{:S(2)}) collective-permute-start(bf16[216,128]{1,0:T(8,128)(2,1)S(1)} %get-tuple-element.36), channel_id=1, source_target_pairs={{0,4},{4,8},{8,12},{1,0},{5,1},{9,5},{13,9},{12,13},{2,6},{6,10},{... | collective-permute-start | bytes 165896 | tf_op jit(solution)/shard_map/ppermute | solution.py:597
  11.1 0.0 copy-done.2
  11.1 0.0 copy-done.9
  11.1 2.0 %shard_map.184 = (bf16[3,384,128]{2,1,0:T(8,128)(2,1)S(1)}, bf16[2,2,128,256]{3,2,1,0:T(8,128)(2,1)S(1)}, bf16[2,48,48]{2,1,0:T(8,128)(2,1)S(1)}, bf16[2,112,256]{2,1,0:T(8,128)(2,1)S(1)}) custom-call(s32[1]{0:T(128)} %bitcast.at_ref, s32[4,64]{1,0:T(4,128)S(1)} %copy-done.9, bf16[3,512,128]{2,1,0:T(8,128)(2,1)S(1)} %get-tuple-element.21.query_ref, ...), custom_call_target="tpu_custom_call" | custom-call | flops 603979776 | bytes 4194304 | tf_op jit(solution)/shard_map/pallas_call | solution.py:603
  13.1 0.1 collective-permute-done.3.first_ref
  13.2 0.0 collective-permute-done.4.second_ref
  13.2 1.7 %shard_map.185 = bf16[3,512,128]{2,1,0:T(8,128)(2,1)} custom-call(s32[1]{0:T(128)} %bitcast.at_ref, s32[1]{0:T(128)} %bitcast.1.core_ref, bf16[3,512,128]{2,1,0:T(8,128)(2,1)S(1)} %get-tuple-element.21.query_ref, bf16[3,512,128]{2,1,0:T(8,128)(2,1)S(1)} %get-tuple-element.22.key_ref.own_key_ref, ...), custom_call_target="tpu_custom_call" | custom-call | flops 201326592 | bytes 4194304 | tf_op jit(solution)/shard_map/pallas_call | solution.py:622
Async XLA Ops:
  0.0 5.6 %copy-start.1 = (bf16[128,128]{1,0:T(8,128)(2,1)S(1)}, bf16[128,128]{1,0:T(8,128)(2,1)}, u32[]{:S(2)}) copy-start(bf16[128,128]{1,0:T(8,128)(2,1)} %w_value.3) | copy-start | bytes 98308
  0.0 5.6 %copy-start = (bf16[128,128]{1,0:T(8,128)(2,1)S(1)}, bf16[128,128]{1,0:T(8,128)(2,1)}, u32[]{:S(2)}) copy-start(bf16[128,128]{1,0:T(8,128)(2,1)} %w_key.3) | copy-start | bytes 98308
  0.0 5.6 %copy-start.8 = (bf16[128,128]{1,0:T(8,128)(2,1)S(1)}, bf16[128,128]{1,0:T(8,128)(2,1)}, u32[]{:S(2)}) copy-start(bf16[128,128]{1,0:T(8,128)(2,1)} %w_gate.1) | copy-start | bytes 98308
  0.0 5.6 %copy-start.7 = (bf16[128,128]{1,0:T(8,128)(2,1)S(1)}, bf16[128,128]{1,0:T(8,128)(2,1)}, u32[]{:S(2)}) copy-start(bf16[128,128]{1,0:T(8,128)(2,1)} %w_query.1) | copy-start | bytes 98308
  0.0 5.6 %copy-start.6 = (bf16[128,128]{1,0:T(8,128)(2,1)S(1)}, bf16[128,128]{1,0:T(8,128)(2,1)}, u32[]{:S(2)}) copy-start(bf16[128,128]{1,0:T(8,128)(2,1)} %ada_attn_shift.1) | copy-start | bytes 98308
  0.0 5.6 %copy-start.5 = (bf16[128,128]{1,0:T(8,128)(2,1)S(1)}, bf16[128,128]{1,0:T(8,128)(2,1)}, u32[]{:S(2)}) copy-start(bf16[128,128]{1,0:T(8,128)(2,1)} %ada_attn_scale.1) | copy-start | bytes 98308
  0.0 5.6 %copy-start.4 = (bf16[512,128]{1,0:T(8,128)(2,1)S(1)}, bf16[512,128]{1,0:T(8,128)(2,1)}, u32[]{:S(2)}) copy-start(bf16[512,128]{1,0:T(8,128)(2,1)} %cond_ref.1) | copy-start | bytes 393220
  0.0 5.6 %copy-start.3 = (bf16[3,512,128]{2,1,0:T(8,128)(2,1)S(1)}, bf16[3,512,128]{2,1,0:T(8,128)(2,1)}, u32[]{:S(2)}) copy-start(bf16[3,512,128]{2,1,0:T(8,128)(2,1)} %single_ref.1) | copy-start | bytes 1179652
  2.4 8.6 %copy-start.2 = (bf16[128,128]{1,0:T(8,128)(2,1)S(1)}, bf16[128,128]{1,0:T(8,128)(2,1)}, u32[]{:S(2)}) copy-start(bf16[128,128]{1,0:T(8,128)(2,1)} %w_out_ref.3) | copy-start | bytes 98308
  2.4 8.6 %copy-start.9 = (s32[4,64]{1,0:T(4,128)S(1)}, s32[4,64]{1,0:T(4,128)}, u32[]{:S(2)}) copy-start(s32[4,64]{1,0:T(4,128)} %counts_ref.1) | copy-start | bytes 3076
  2.4 6.2 %collective-permute-start.2 = (bf16[2,64,128]{2,1,0:T(8,128)(2,1)S(1)}, bf16[2,64,128]{2,1,0:T(8,128)(2,1)S(1)}, u32[]{:S(2)}, u32[]{:S(2)}) collective-permute-start(bf16[2,64,128]{2,1,0:T(8,128)(2,1)S(1)} %shard_map.182.refs_0_), channel_id=1, source_target_pairs={{0,3},{1,2},{2,1},{3,0},{4,7},{5,6},{6,5},{7,4},{8,11},{9,10},{10,... | collective-permute-start | bytes 98312 | tf_op jit(solution)/shard_map/ppermute | solution.py:549
  4.9 4.0 %collective-permute-start.1 = (bf16[2,64,128]{2,1,0:T(8,128)(2,1)S(1)}, bf16[2,64,128]{2,1,0:T(8,128)(2,1)S(1)}, u32[]{:S(2)}, u32[]{:S(2)}) collective-permute-start(bf16[2,64,128]{2,1,0:T(8,128)(2,1)S(1)} %shard_map.182.refs_0_), channel_id=1, source_target_pairs={{0,2},{2,0},{1,3},{3,1},{4,6},{6,4},{5,7},{7,5},{8,10},{10,8},{9,1... | collective-permute-start | bytes 98312 | tf_op jit(solution)/shard_map/ppermute | solution.py:548
  5.6 3.3 %collective-permute-start = (bf16[2,64,128]{2,1,0:T(8,128)(2,1)S(1)}, bf16[2,64,128]{2,1,0:T(8,128)(2,1)S(1)}, u32[]{:S(2)}, u32[]{:S(2)}) collective-permute-start(bf16[2,64,128]{2,1,0:T(8,128)(2,1)S(1)} %shard_map.182.refs_0_), channel_id=1, source_target_pairs={{0,1},{1,0},{2,3},{3,2},{4,5},{5,4},{6,7},{7,6},{8,9},{9,8},{10,11... | collective-permute-start | bytes 98312 | tf_op jit(solution)/shard_map/ppermute | solution.py:550
  9.0 4.2 %collective-permute-start.3 = (bf16[216,128]{1,0:T(8,128)(2,1)S(1)}, bf16[216,128]{1,0:T(8,128)(2,1)S(1)}, u32[]{:S(2)}, u32[]{:S(2)}) collective-permute-start(bf16[216,128]{1,0:T(8,128)(2,1)S(1)} %get-tuple-element.35), channel_id=1, source_target_pairs={{4,0},{8,4},{12,8},{0,1},{1,5},{5,9},{9,13},{13,12},{6,2},{10,6},{... | collective-permute-start | bytes 165896 | tf_op jit(solution)/shard_map/ppermute | solution.py:596
  9.3 3.9 %collective-permute-start.4 = (bf16[216,128]{1,0:T(8,128)(2,1)S(1)}, bf16[216,128]{1,0:T(8,128)(2,1)S(1)}, u32[]{:S(2)}, u32[]{:S(2)}) collective-permute-start(bf16[216,128]{1,0:T(8,128)(2,1)S(1)} %get-tuple-element.36), channel_id=1, source_target_pairs={{0,4},{4,8},{8,12},{1,0},{5,1},{9,5},{13,9},{12,13},{2,6},{6,10},{... | collective-permute-start | bytes 165896 | tf_op jit(solution)/shard_map/ppermute | solution.py:597

commit v29 on v27

--- a/solution.py
+++ b/solution.py
@@ -50,10 +50,6 @@
     return jnp.where(same, 1.0 - 1.0 / width, -1.0 / width).astype(BF16)
 
 
-def averaging(width):
-    return jnp.full((width, width), 1.0 / width, BF16)
-
-
 def mean_square(centred):
     return jnp.mean(centred * centred, axis=-1, keepdims=True)
 
@@ -96,30 +92,30 @@
     spread = jnp.concatenate(
         [jnp.broadcast_to(w_pair[h : h + 1], (group, width)) for h in range(heads)], 0
     )
-    mix = twice(spread.T.astype(BF16))
+    weight = spread.T.astype(BF16)
+    low = iota((width, lanes), 1) % group < half
+    blank = jnp.zeros_like(weight)
+
+    def shared(columns):
+        return jnp.concatenate([jnp.where(low, columns, blank), jnp.where(low, blank, columns)], 0)
+
+    mix = shared(weight)
+    average = shared(jnp.full((width, lanes), 1.0 / width, BF16))
     centre = twice(centring(width))
-    slot = iota((cols, lanes), 1) % group
+    slot = iota((cols, lanes), 1) % half
 
     chunks = []
     for chunk in range(rows // group):
         pair_copy(chunk).wait()
         pair = pair_ref[chunk * group : (chunk + 1) * group].reshape(group * cols, width)
         chunks.append(dot(side_by_side(pair), centre).astype(BF16))
-    mixes = [dot(centred, mix).reshape(half, cols, 2 * lanes) for centred in chunks]
-    squares = chunks[0][:, :width] * chunks[0][:, :width]
-    average = dot(side_by_side(squares), twice(averaging(width)))
-    average = jnp.concatenate([average[:, :width], average[:, width:]], 0)
-    for chunk, (centred, mixed) in enumerate(zip(chunks, mixes)):
-        variances = [average.reshape(half, cols, width)] if chunk == 0 else []
-        for part in range(len(variances), 2):
-            rows_of = centred[:, part * width : (part + 1) * width].astype(F32)
-            variances.append(mean_square(rows_of).reshape(half, cols, 1))
-        total = jnp.zeros((cols, lanes), F32)
-        spread_out = jnp.zeros((cols, lanes), F32)
-        for i in range(group):
-            side = slice(i // half * lanes, (i // half + 1) * lanes)
-            total = jnp.where(slot == i, mixed[i % half, :, side], total)
-            spread_out = jnp.where(slot == i, variances[i // half][i % half], spread_out)
+    mixes = [dot(centred, mix).reshape(half, cols, lanes) for centred in chunks]
+    variances = [dot(centred * centred, average).reshape(half, cols, lanes) for centred in chunks]
+    for chunk, (mixed, variance) in enumerate(zip(mixes, variances)):
+        total, spread_out = mixed[0], variance[0]
+        for i in range(1, half):
+            total = jnp.where(slot == i, mixed[i], total)
+            spread_out = jnp.where(slot == i, variance[i], spread_out)
         tile_ref[chunk] = (total * lax.rsqrt(spread_out + EPSILON)).astype(BF16)
 
 

time: 15 us -> 15.3 us (1.020)
  Pallas kernels: 9.09 us -> 9.37 us
    pallas_call x1, Pallas kernels: 2.27 us -> 2.55 us  [shards(): pl.pallas_call(pair_kernel, in_specs=[IN_SMEM] + [IN_HBM] * 2, out_specs=...]
  transfers between devices with their start and end apart: 5 -> 5, of which waited for: 2 -> 2; matrix products, arithmetic and copies ran while one was open for 0% -> 0% of each run, Pallas kernels for 34% -> 33%
where the time goes in v29:
time: 15.3 us; the launch traced here: 15.1 us
  Pallas kernels  9.37 us (61%)
  starting transfers between devices  5.2 us (34%)
  waiting for transfers between devices  0.34 us (2%)
    pallas_call x1, Pallas kernels, shards(): pl.pallas_call(project_kernel, in_specs=[IN_SMEM] + [IN_VMEM] * len(opera...  3.02 us
    pallas_call x1, Pallas kernels, shards(): pl.pallas_call(pair_kernel, in_specs=[IN_SMEM] + [IN_HBM] * 2, out_specs=...  2.55 us
    ppermute x1, starting transfers between devices, shards(): lax.ppermute(own, ('pair', 'samp'), [(0, 3), (1, 2), (2, 1), (3, 0)])  2.48 us
    pallas_call x1, Pallas kernels, shards(): pl.pallas_call(functools.partial(inner_kernel, heads, blocks), in_specs=[...  1.99 us
    ppermute x1, starting transfers between devices, shards(): lax.ppermute(far, ('atoms', 'samp'), [(target, source) for source, target...  1.73 us
    pallas_call x1, Pallas kernels, shards(): pl.pallas_call(functools.partial(outer_kernel, heads, blocks), in_specs=[...  1.69 us
    ppermute x1, starting transfers between devices, shards(): across = lax.ppermute(own, 'pair', swapped)  0.64 us
    ppermute x1, starting transfers between devices, shards(): first = lax.ppermute(near, ('atoms', 'samp'), cycle)  0.31 us
  transfers between devices with their start and end apart: 5, of which 2 were waited for; matrix products, arithmetic and copies ran while one was open for 0% of the time, Pallas kernels for 33%

profile of v29, /device:TPU:0, one launch (start us, length us, event | category | flops | bytes accessed | tf_op | source)
XLA Modules:
  0.0 15.1 jit_solution(17930753810969128463)
XLA Ops:
  0.0 0.0 copy-start.1
  0.0 0.0 copy-start
  0.0 0.0 copy-start.8
  0.0 0.0 copy-start.7
  0.0 0.0 copy-start.6
  0.0 0.0 copy-start.5
  0.0 0.0 copy-start.4
  0.0 0.0 copy-start.3
  0.0 2.6 %shard_map.182.refs_0_ = bf16[2,64,128]{2,1,0:T(8,128)(2,1)S(1)} custom-call(s32[1]{0:T(128)} %bitcast.1.core_ref, bf16[4,128]{1,0:T(4,128)(2,1)} %bitcast.4, bf16[128,64,128]{2,1,0:T(8,128)(2,1)} %pair_hbm.1), custom_call_target="tpu_custom_call" | custom-call | flops 268435456 | bytes 4194304 | tf_op jit(solution)/shard_map/pallas_call | solution.py:528
  2.6 0.0 copy-start.2
  2.6 0.0 copy-start.9
  2.6 2.5 %collective-permute-start.2 = (bf16[2,64,128]{2,1,0:T(8,128)(2,1)S(1)}, bf16[2,64,128]{2,1,0:T(8,128)(2,1)S(1)}, u32[]{:S(2)}, u32[]{:S(2)}) collective-permute-start(bf16[2,64,128]{2,1,0:T(8,128)(2,1)S(1)} %shard_map.182.refs_0_), channel_id=1, source_target_pairs={{0,3},{1,2},{2,1},{3,0},{4,7},{5,6},{6,5},{7,4},{8,11},{9,10},{10,... | collective-permute-start | bytes 98312 | tf_op jit(solution)/shard_map/ppermute | solution.py:545
  5.1 0.6 %collective-permute-start.1 = (bf16[2,64,128]{2,1,0:T(8,128)(2,1)S(1)}, bf16[2,64,128]{2,1,0:T(8,128)(2,1)S(1)}, u32[]{:S(2)}, u32[]{:S(2)}) collective-permute-start(bf16[2,64,128]{2,1,0:T(8,128)(2,1)S(1)} %shard_map.182.refs_0_), channel_id=1, source_target_pairs={{0,2},{2,0},{1,3},{3,1},{4,6},{6,4},{5,7},{7,5},{8,10},{10,8},{9,1... | collective-permute-start | bytes 98312 | tf_op jit(solution)/shard_map/ppermute | solution.py:544
  5.8 0.0 collective-permute-start
  5.8 0.0 copy-done.1
  5.8 0.0 copy-done
  5.8 0.0 copy-done.8
  5.8 0.0 copy-done.7
  5.8 0.0 copy-done.6
  5.8 0.0 copy-done.5
  5.8 0.0 copy-done.4
  5.8 0.0 copy-done.3
  5.8 3.0 %shard_map.181 = (bf16[3,512,128]{2,1,0:T(8,128)(2,1)S(1)}, bf16[3,512,128]{2,1,0:T(8,128)(2,1)S(1)}, bf16[3,512,128]{2,1,0:T(8,128)(2,1)S(1)}, bf16[3,512,128]{...) custom-call(s32[1]{0:T(128)} %bitcast.1.core_ref, ...), custom_call_target="tpu_custom_call" | custom-call | flops 1006632960 | bytes 4194304 | tf_op jit(solution)/shard_map/pallas_call | solution.py:561
  8.9 0.0 collective-permute-done.2.refs_3_
  8.9 0.2 %collective-permute-done.1.refs_2_ = bf16[2,64,128]{2,1,0:T(8,128)(2,1)S(1)} collective-permute-done((bf16[2,64,128]{2,1,0:T(8,128)(2,1)S(1)}, bf16[2,64,128]{2,1,0:T(8,128)(2,1)S(1)}, u32[]{:S(2)}, u32[]{:S(2)}) %collective-permute-start.1) | collective-permute-done | bytes 32800 | tf_op jit(solution)/shard_map/ppermute | solution.py:544
  9.1 0.0 collective-permute-done.refs_1_
  9.1 0.1 shard_map.183
  9.2 0.3 %collective-permute-start.3 = (bf16[216,128]{1,0:T(8,128)(2,1)S(1)}, bf16[216,128]{1,0:T(8,128)(2,1)S(1)}, u32[]{:S(2)}, u32[]{:S(2)}) collective-permute-start(bf16[216,128]{1,0:T(8,128)(2,1)S(1)} %get-tuple-element.35), channel_id=1, source_target_pairs={{4,0},{8,4},{12,8},{0,1},{1,5},{5,9},{9,13},{13,12},{6,2},{10,6},{... | collective-permute-start | bytes 165896 | tf_op jit(solution)/shard_map/ppermute | solution.py:592
  9.5 1.7 %collective-permute-start.4 = (bf16[216,128]{1,0:T(8,128)(2,1)S(1)}, bf16[216,128]{1,0:T(8,128)(2,1)S(1)}, u32[]{:S(2)}, u32[]{:S(2)}) collective-permute-start(bf16[216,128]{1,0:T(8,128)(2,1)S(1)} %get-tuple-element.36), channel_id=1, source_target_pairs={{0,4},{4,8},{8,12},{1,0},{5,1},{9,5},{13,9},{12,13},{2,6},{6,10},{... | collective-permute-start | bytes 165896 | tf_op jit(solution)/shard_map/ppermute | solution.py:593
  11.2 0.0 copy-done.2
  11.3 0.0 copy-done.9
  11.3 2.0 %shard_map.184 = (bf16[3,384,128]{2,1,0:T(8,128)(2,1)S(1)}, bf16[2,2,128,256]{3,2,1,0:T(8,128)(2,1)S(1)}, bf16[2,48,48]{2,1,0:T(8,128)(2,1)S(1)}, bf16[2,112,256]{2,1,0:T(8,128)(2,1)S(1)}) custom-call(s32[1]{0:T(128)} %bitcast.at_ref, s32[4,64]{1,0:T(4,128)S(1)} %copy-done.9, bf16[3,512,128]{2,1,0:T(8,128)(2,1)S(1)} %get-tuple-element.21.query_ref, ...), custom_call_target="tpu_custom_call" | custom-call | flops 603979776 | bytes 4194304 | tf_op jit(solution)/shard_map/pallas_call | solution.py:599
  13.2 0.1 collective-permute-done.3.first_ref
  13.4 0.0 collective-permute-done.4.second_ref
  13.4 1.7 %shard_map.185 = bf16[3,512,128]{2,1,0:T(8,128)(2,1)} custom-call(s32[1]{0:T(128)} %bitcast.at_ref, s32[1]{0:T(128)} %bitcast.1.core_ref, bf16[3,512,128]{2,1,0:T(8,128)(2,1)S(1)} %get-tuple-element.21.query_ref, bf16[3,512,128]{2,1,0:T(8,128)(2,1)S(1)} %get-tuple-element.22.key_ref.own_key_ref, ...), custom_call_target="tpu_custom_call" | custom-call | flops 201326592 | bytes 4194304 | tf_op jit(solution)/shard_map/pallas_call | solution.py:618
Async XLA Ops:
  0.0 5.8 %copy-start.1 = (bf16[128,128]{1,0:T(8,128)(2,1)S(1)}, bf16[128,128]{1,0:T(8,128)(2,1)}, u32[]{:S(2)}) copy-start(bf16[128,128]{1,0:T(8,128)(2,1)} %w_value.3) | copy-start | bytes 98308
  0.0 5.8 %copy-start = (bf16[128,128]{1,0:T(8,128)(2,1)S(1)}, bf16[128,128]{1,0:T(8,128)(2,1)}, u32[]{:S(2)}) copy-start(bf16[128,128]{1,0:T(8,128)(2,1)} %w_key.3) | copy-start | bytes 98308
  0.0 5.8 %copy-start.8 = (bf16[128,128]{1,0:T(8,128)(2,1)S(1)}, bf16[128,128]{1,0:T(8,128)(2,1)}, u32[]{:S(2)}) copy-start(bf16[128,128]{1,0:T(8,128)(2,1)} %w_gate.1) | copy-start | bytes 98308
  0.0 5.8 %copy-start.7 = (bf16[128,128]{1,0:T(8,128)(2,1)S(1)}, bf16[128,128]{1,0:T(8,128)(2,1)}, u32[]{:S(2)}) copy-start(bf16[128,128]{1,0:T(8,128)(2,1)} %w_query.1) | copy-start | bytes 98308
  0.0 5.8 %copy-start.6 = (bf16[128,128]{1,0:T(8,128)(2,1)S(1)}, bf16[128,128]{1,0:T(8,128)(2,1)}, u32[]{:S(2)}) copy-start(bf16[128,128]{1,0:T(8,128)(2,1)} %ada_attn_shift.1) | copy-start | bytes 98308
  0.0 5.8 %copy-start.5 = (bf16[128,128]{1,0:T(8,128)(2,1)S(1)}, bf16[128,128]{1,0:T(8,128)(2,1)}, u32[]{:S(2)}) copy-start(bf16[128,128]{1,0:T(8,128)(2,1)} %ada_attn_scale.1) | copy-start | bytes 98308
  0.0 5.8 %copy-start.4 = (bf16[512,128]{1,0:T(8,128)(2,1)S(1)}, bf16[512,128]{1,0:T(8,128)(2,1)}, u32[]{:S(2)}) copy-start(bf16[512,128]{1,0:T(8,128)(2,1)} %cond_ref.1) | copy-start | bytes 393220
  0.0 5.8 %copy-start.3 = (bf16[3,512,128]{2,1,0:T(8,128)(2,1)S(1)}, bf16[3,512,128]{2,1,0:T(8,128)(2,1)}, u32[]{:S(2)}) copy-start(bf16[3,512,128]{2,1,0:T(8,128)(2,1)} %single_ref.1) | copy-start | bytes 1179652
  2.6 8.6 %copy-start.2 = (bf16[128,128]{1,0:T(8,128)(2,1)S(1)}, bf16[128,128]{1,0:T(8,128)(2,1)}, u32[]{:S(2)}) copy-start(bf16[128,128]{1,0:T(8,128)(2,1)} %w_out_ref.3) | copy-start | bytes 98308
  2.6 8.6 %copy-start.9 = (s32[4,64]{1,0:T(4,128)S(1)}, s32[4,64]{1,0:T(4,128)}, u32[]{:S(2)}) copy-start(s32[4,64]{1,0:T(4,128)} %counts_ref.1) | copy-start | bytes 3076
  2.6 6.2 %collective-permute-start.2 = (bf16[2,64,128]{2,1,0:T(8,128)(2,1)S(1)}, bf16[2,64,128]{2,1,0:T(8,128)(2,1)S(1)}, u32[]{:S(2)}, u32[]{:S(2)}) collective-permute-start(bf16[2,64,128]{2,1,0:T(8,128)(2,1)S(1)} %shard_map.182.refs_0_), channel_id=1, source_target_pairs={{0,3},{1,2},{2,1},{3,0},{4,7},{5,6},{6,5},{7,4},{8,11},{9,10},{10,... | collective-permute-start | bytes 98312 | tf_op jit(solution)/shard_map/ppermute | solution.py:545
  5.1 4.0 %collective-permute-start.1 = (bf16[2,64,128]{2,1,0:T(8,128)(2,1)S(1)}, bf16[2,64,128]{2,1,0:T(8,128)(2,1)S(1)}, u32[]{:S(2)}, u32[]{:S(2)}) collective-permute-start(bf16[2,64,128]{2,1,0:T(8,128)(2,1)S(1)} %shard_map.182.refs_0_), channel_id=1, source_target_pairs={{0,2},{2,0},{1,3},{3,1},{4,6},{6,4},{5,7},{7,5},{8,10},{10,8},{9,1... | collective-permute-start | bytes 98312 | tf_op jit(solution)/shard_map/ppermute | solution.py:544
  5.8 3.3 %collective-permute-start = (bf16[2,64,128]{2,1,0:T(8,128)(2,1)S(1)}, bf16[2,64,128]{2,1,0:T(8,128)(2,1)S(1)}, u32[]{:S(2)}, u32[]{:S(2)}) collective-permute-start(bf16[2,64,128]{2,1,0:T(8,128)(2,1)S(1)} %shard_map.182.refs_0_), channel_id=1, source_target_pairs={{0,1},{1,0},{2,3},{3,2},{4,5},{5,4},{6,7},{7,6},{8,9},{9,8},{10,11... | collective-permute-start | bytes 98312 | tf_op jit(solution)/shard_map/ppermute | solution.py:546
  9.2 4.2 %collective-permute-start.3 = (bf16[216,128]{1,0:T(8,128)(2,1)S(1)}, bf16[216,128]{1,0:T(8,128)(2,1)S(1)}, u32[]{:S(2)}, u32[]{:S(2)}) collective-permute-start(bf16[216,128]{1,0:T(8,128)(2,1)S(1)} %get-tuple-element.35), channel_id=1, source_target_pairs={{4,0},{8,4},{12,8},{0,1},{1,5},{5,9},{9,13},{13,12},{6,2},{10,6},{... | collective-permute-start | bytes 165896 | tf_op jit(solution)/shard_map/ppermute | solution.py:592
  9.5 3.9 %collective-permute-start.4 = (bf16[216,128]{1,0:T(8,128)(2,1)S(1)}, bf16[216,128]{1,0:T(8,128)(2,1)S(1)}, u32[]{:S(2)}, u32[]{:S(2)}) collective-permute-start(bf16[216,128]{1,0:T(8,128)(2,1)S(1)} %get-tuple-element.36), channel_id=1, source_target_pairs={{0,4},{4,8},{8,12},{1,0},{5,1},{9,5},{13,9},{12,13},{2,6},{6,10},{... | collective-permute-start | bytes 165896 | tf_op jit(solution)/shard_map/ppermute | solution.py:593

commit v30 on v27

--- a/solution.py
+++ b/solution.py
@@ -96,7 +96,10 @@
     spread = jnp.concatenate(
         [jnp.broadcast_to(w_pair[h : h + 1], (group, width)) for h in range(heads)], 0
     )
-    mix = twice(spread.T.astype(BF16))
+    weight = spread.T.astype(BF16)
+    low = iota((width, lanes), 1) % group < half
+    blank = jnp.zeros_like(weight)
+    mix = jnp.concatenate([jnp.where(low, weight, blank), jnp.where(low, blank, weight)], 0)
     centre = twice(centring(width))
     slot = iota((cols, lanes), 1) % group
 
@@ -105,7 +108,7 @@
         pair_copy(chunk).wait()
         pair = pair_ref[chunk * group : (chunk + 1) * group].reshape(group * cols, width)
         chunks.append(dot(side_by_side(pair), centre).astype(BF16))
-    mixes = [dot(centred, mix).reshape(half, cols, 2 * lanes) for centred in chunks]
+    mixes = [dot(centred, mix).reshape(half, cols, lanes) for centred in chunks]
     squares = chunks[0][:, :width] * chunks[0][:, :width]
     average = dot(side_by_side(squares), twice(averaging(width)))
     average = jnp.concatenate([average[:, :width], average[:, width:]], 0)
@@ -114,11 +117,11 @@
         for part in range(len(variances), 2):
             rows_of = centred[:, part * width : (part + 1) * width].astype(F32)
             variances.append(mean_square(rows_of).reshape(half, cols, 1))
-        total = jnp.zeros((cols, lanes), F32)
+        total = mixed[0]
+        for i in range(1, half):
+            total = jnp.where(slot % half == i, mixed[i], total)
         spread_out = jnp.zeros((cols, lanes), F32)
         for i in range(group):
-            side = slice(i // half * lanes, (i // half + 1) * lanes)
-            total = jnp.where(slot == i, mixed[i % half, :, side], total)
             spread_out = jnp.where(slot == i, variances[i // half][i % half], spread_out)
         tile_ref[chunk] = (total * lax.rsqrt(spread_out + EPSILON)).astype(BF16)
 

time: 15 us -> 15 us (level)
  no operation moved by 1% of the time
where the time goes in v30:
time: 15 us; the launch traced here: 14.8 us
  Pallas kernels  9.07 us (60%)
  starting transfers between devices  5.19 us (35%)
  waiting for transfers between devices  0.33 us (2%)
    pallas_call x1, Pallas kernels, shards(): pl.pallas_call(project_kernel, in_specs=[IN_SMEM] + [IN_VMEM] * len(opera...  3.02 us
    ppermute x1, starting transfers between devices, shards(): lax.ppermute(own, ('pair', 'samp'), [(0, 3), (1, 2), (2, 1), (3, 0)])  2.47 us
    pallas_call x1, Pallas kernels, shards(): pl.pallas_call(pair_kernel, in_specs=[IN_SMEM] + [IN_HBM] * 2, out_specs=...  2.25 us
    pallas_call x1, Pallas kernels, shards(): pl.pallas_call(functools.partial(inner_kernel, heads, blocks), in_specs=[...  1.99 us
    ppermute x1, starting transfers between devices, shards(): lax.ppermute(far, ('atoms', 'samp'), [(target, source) for source, target...  1.73 us
    pallas_call x1, Pallas kernels, shards(): pl.pallas_call(functools.partial(outer_kernel, heads, blocks), in_specs=[...  1.7 us
    ppermute x1, starting transfers between devices, shards(): across = lax.ppermute(own, 'pair', swapped)  0.64 us
    ppermute x1, starting transfers between devices, shards(): first = lax.ppermute(near, ('atoms', 'samp'), cycle)  0.31 us
  transfers between devices with their start and end apart: 5, of which 2 were waited for; matrix products, arithmetic and copies ran while one was open for 0% of the time, Pallas kernels for 34%

profile of v30, /device:TPU:0, one launch (start us, length us, event | category | flops | bytes accessed | tf_op | source)
XLA Modules:
  0.0 14.8 jit_solution(7098116515195275928)
XLA Ops:
  0.0 0.0 copy-start.1
  0.0 0.0 copy-start
  0.0 0.0 copy-start.8
  0.0 0.0 copy-start.7
  0.0 0.0 copy-start.6
  0.0 0.0 copy-start.5
  0.0 0.0 copy-start.4
  0.0 0.0 copy-start.3
  0.0 2.3 %shard_map.182.refs_0_ = bf16[2,64,128]{2,1,0:T(8,128)(2,1)S(1)} custom-call(s32[1]{0:T(128)} %bitcast.1.core_ref, bf16[4,128]{1,0:T(4,128)(2,1)} %bitcast.4, bf16[128,64,128]{2,1,0:T(8,128)(2,1)} %pair_hbm.1), custom_call_target="tpu_custom_call" | custom-call | flops 268435456 | bytes 4194304 | tf_op jit(solution)/shard_map/pallas_call | solution.py:535
  2.3 0.0 copy-start.2
  2.3 0.0 copy-start.9
  2.3 2.5 %collective-permute-start.2 = (bf16[2,64,128]{2,1,0:T(8,128)(2,1)S(1)}, bf16[2,64,128]{2,1,0:T(8,128)(2,1)S(1)}, u32[]{:S(2)}, u32[]{:S(2)}) collective-permute-start(bf16[2,64,128]{2,1,0:T(8,128)(2,1)S(1)} %shard_map.182.refs_0_), channel_id=1, source_target_pairs={{0,3},{1,2},{2,1},{3,0},{4,7},{5,6},{6,5},{7,4},{8,11},{9,10},{10,... | collective-permute-start | bytes 98312 | tf_op jit(solution)/shard_map/ppermute | solution.py:552
  4.8 0.6 %collective-permute-start.1 = (bf16[2,64,128]{2,1,0:T(8,128)(2,1)S(1)}, bf16[2,64,128]{2,1,0:T(8,128)(2,1)S(1)}, u32[]{:S(2)}, u32[]{:S(2)}) collective-permute-start(bf16[2,64,128]{2,1,0:T(8,128)(2,1)S(1)} %shard_map.182.refs_0_), channel_id=1, source_target_pairs={{0,2},{2,0},{1,3},{3,1},{4,6},{6,4},{5,7},{7,5},{8,10},{10,8},{9,1... | collective-permute-start | bytes 98312 | tf_op jit(solution)/shard_map/ppermute | solution.py:551
  5.4 0.0 collective-permute-start
  5.5 0.0 copy-done.1
  5.5 0.0 copy-done
  5.5 0.0 copy-done.8
  5.5 0.0 copy-done.7
  5.5 0.0 copy-done.6
  5.5 0.0 copy-done.5
  5.5 0.0 copy-done.4
  5.5 0.0 copy-done.3
  5.5 3.0 %shard_map.181 = (bf16[3,512,128]{2,1,0:T(8,128)(2,1)S(1)}, bf16[3,512,128]{2,1,0:T(8,128)(2,1)S(1)}, bf16[3,512,128]{2,1,0:T(8,128)(2,1)S(1)}, bf16[3,512,128]{...) custom-call(s32[1]{0:T(128)} %bitcast.1.core_ref, ...), custom_call_target="tpu_custom_call" | custom-call | flops 1006632960 | bytes 4194304 | tf_op jit(solution)/shard_map/pallas_call | solution.py:568
  8.6 0.0 collective-permute-done.2.refs_3_
  8.6 0.2 %collective-permute-done.1.refs_2_ = bf16[2,64,128]{2,1,0:T(8,128)(2,1)S(1)} collective-permute-done((bf16[2,64,128]{2,1,0:T(8,128)(2,1)S(1)}, bf16[2,64,128]{2,1,0:T(8,128)(2,1)S(1)}, u32[]{:S(2)}, u32[]{:S(2)}) %collective-permute-start.1) | collective-permute-done | bytes 32800 | tf_op jit(solution)/shard_map/ppermute | solution.py:551
  8.8 0.0 collective-permute-done.refs_1_
  8.8 0.1 shard_map.183
  8.9 0.3 %collective-permute-start.3 = (bf16[216,128]{1,0:T(8,128)(2,1)S(1)}, bf16[216,128]{1,0:T(8,128)(2,1)S(1)}, u32[]{:S(2)}, u32[]{:S(2)}) collective-permute-start(bf16[216,128]{1,0:T(8,128)(2,1)S(1)} %get-tuple-element.35), channel_id=1, source_target_pairs={{4,0},{8,4},{12,8},{0,1},{1,5},{5,9},{9,13},{13,12},{6,2},{10,6},{... | collective-permute-start | bytes 165896 | tf_op jit(solution)/shard_map/ppermute | solution.py:599
  9.2 1.7 %collective-permute-start.4 = (bf16[216,128]{1,0:T(8,128)(2,1)S(1)}, bf16[216,128]{1,0:T(8,128)(2,1)S(1)}, u32[]{:S(2)}, u32[]{:S(2)}) collective-permute-start(bf16[216,128]{1,0:T(8,128)(2,1)S(1)} %get-tuple-element.36), channel_id=1, source_target_pairs={{0,4},{4,8},{8,12},{1,0},{5,1},{9,5},{13,9},{12,13},{2,6},{6,10},{... | collective-permute-start | bytes 165896 | tf_op jit(solution)/shard_map/ppermute | solution.py:600
  10.9 0.0 copy-done.2
  10.9 0.0 copy-done.9
  10.9 2.0 %shard_map.184 = (bf16[3,384,128]{2,1,0:T(8,128)(2,1)S(1)}, bf16[2,2,128,256]{3,2,1,0:T(8,128)(2,1)S(1)}, bf16[2,48,48]{2,1,0:T(8,128)(2,1)S(1)}, bf16[2,112,256]{2,1,0:T(8,128)(2,1)S(1)}) custom-call(s32[1]{0:T(128)} %bitcast.at_ref, s32[4,64]{1,0:T(4,128)S(1)} %copy-done.9, bf16[3,512,128]{2,1,0:T(8,128)(2,1)S(1)} %get-tuple-element.21.query_ref, ...), custom_call_target="tpu_custom_call" | custom-call | flops 603979776 | bytes 4194304 | tf_op jit(solution)/shard_map/pallas_call | solution.py:606
  12.9 0.1 collective-permute-done.3.first_ref
  13.1 0.0 collective-permute-done.4.second_ref
  13.1 1.7 %shard_map.185 = bf16[3,512,128]{2,1,0:T(8,128)(2,1)} custom-call(s32[1]{0:T(128)} %bitcast.at_ref, s32[1]{0:T(128)} %bitcast.1.core_ref, bf16[3,512,128]{2,1,0:T(8,128)(2,1)S(1)} %get-tuple-element.21.query_ref, bf16[3,512,128]{2,1,0:T(8,128)(2,1)S(1)} %get-tuple-element.22.key_ref.own_key_ref, ...), custom_call_target="tpu_custom_call" | custom-call | flops 201326592 | bytes 4194304 | tf_op jit(solution)/shard_map/pallas_call | solution.py:625
Async XLA Ops:
  0.0 5.5 %copy-start.1 = (bf16[128,128]{1,0:T(8,128)(2,1)S(1)}, bf16[128,128]{1,0:T(8,128)(2,1)}, u32[]{:S(2)}) copy-start(bf16[128,128]{1,0:T(8,128)(2,1)} %w_value.3) | copy-start | bytes 98308
  0.0 5.5 %copy-start = (bf16[128,128]{1,0:T(8,128)(2,1)S(1)}, bf16[128,128]{1,0:T(8,128)(2,1)}, u32[]{:S(2)}) copy-start(bf16[128,128]{1,0:T(8,128)(2,1)} %w_key.3) | copy-start | bytes 98308
  0.0 5.5 %copy-start.8 = (bf16[128,128]{1,0:T(8,128)(2,1)S(1)}, bf16[128,128]{1,0:T(8,128)(2,1)}, u32[]{:S(2)}) copy-start(bf16[128,128]{1,0:T(8,128)(2,1)} %w_gate.1) | copy-start | bytes 98308
  0.0 5.5 %copy-start.7 = (bf16[128,128]{1,0:T(8,128)(2,1)S(1)}, bf16[128,128]{1,0:T(8,128)(2,1)}, u32[]{:S(2)}) copy-start(bf16[128,128]{1,0:T(8,128)(2,1)} %w_query.1) | copy-start | bytes 98308
  0.0 5.5 %copy-start.6 = (bf16[128,128]{1,0:T(8,128)(2,1)S(1)}, bf16[128,128]{1,0:T(8,128)(2,1)}, u32[]{:S(2)}) copy-start(bf16[128,128]{1,0:T(8,128)(2,1)} %ada_attn_shift.1) | copy-start | bytes 98308
  0.0 5.5 %copy-start.5 = (bf16[128,128]{1,0:T(8,128)(2,1)S(1)}, bf16[128,128]{1,0:T(8,128)(2,1)}, u32[]{:S(2)}) copy-start(bf16[128,128]{1,0:T(8,128)(2,1)} %ada_attn_scale.1) | copy-start | bytes 98308
  0.0 5.5 %copy-start.4 = (bf16[512,128]{1,0:T(8,128)(2,1)S(1)}, bf16[512,128]{1,0:T(8,128)(2,1)}, u32[]{:S(2)}) copy-start(bf16[512,128]{1,0:T(8,128)(2,1)} %cond_ref.1) | copy-start | bytes 393220
  0.0 5.5 %copy-start.3 = (bf16[3,512,128]{2,1,0:T(8,128)(2,1)S(1)}, bf16[3,512,128]{2,1,0:T(8,128)(2,1)}, u32[]{:S(2)}) copy-start(bf16[3,512,128]{2,1,0:T(8,128)(2,1)} %single_ref.1) | copy-start | bytes 1179652
  2.3 8.6 %copy-start.2 = (bf16[128,128]{1,0:T(8,128)(2,1)S(1)}, bf16[128,128]{1,0:T(8,128)(2,1)}, u32[]{:S(2)}) copy-start(bf16[128,128]{1,0:T(8,128)(2,1)} %w_out_ref.3) | copy-start | bytes 98308
  2.3 8.6 %copy-start.9 = (s32[4,64]{1,0:T(4,128)S(1)}, s32[4,64]{1,0:T(4,128)}, u32[]{:S(2)}) copy-start(s32[4,64]{1,0:T(4,128)} %counts_ref.1) | copy-start | bytes 3076
  2.3 6.2 %collective-permute-start.2 = (bf16[2,64,128]{2,1,0:T(8,128)(2,1)S(1)}, bf16[2,64,128]{2,1,0:T(8,128)(2,1)S(1)}, u32[]{:S(2)}, u32[]{:S(2)}) collective-permute-start(bf16[2,64,128]{2,1,0:T(8,128)(2,1)S(1)} %shard_map.182.refs_0_), channel_id=1, source_target_pairs={{0,3},{1,2},{2,1},{3,0},{4,7},{5,6},{6,5},{7,4},{8,11},{9,10},{10,... | collective-permute-start | bytes 98312 | tf_op jit(solution)/shard_map/ppermute | solution.py:552
  4.8 4.0 %collective-permute-start.1 = (bf16[2,64,128]{2,1,0:T(8,128)(2,1)S(1)}, bf16[2,64,128]{2,1,0:T(8,128)(2,1)S(1)}, u32[]{:S(2)}, u32[]{:S(2)}) collective-permute-start(bf16[2,64,128]{2,1,0:T(8,128)(2,1)S(1)} %shard_map.182.refs_0_), channel_id=1, source_target_pairs={{0,2},{2,0},{1,3},{3,1},{4,6},{6,4},{5,7},{7,5},{8,10},{10,8},{9,1... | collective-permute-start | bytes 98312 | tf_op jit(solution)/shard_map/ppermute | solution.py:551
  5.4 3.3 %collective-permute-start = (bf16[2,64,128]{2,1,0:T(8,128)(2,1)S(1)}, bf16[2,64,128]{2,1,0:T(8,128)(2,1)S(1)}, u32[]{:S(2)}, u32[]{:S(2)}) collective-permute-start(bf16[2,64,128]{2,1,0:T(8,128)(2,1)S(1)} %shard_map.182.refs_0_), channel_id=1, source_target_pairs={{0,1},{1,0},{2,3},{3,2},{4,5},{5,4},{6,7},{7,6},{8,9},{9,8},{10,11... | collective-permute-start | bytes 98312 | tf_op jit(solution)/shard_map/ppermute | solution.py:553
  8.9 4.2 %collective-permute-start.3 = (bf16[216,128]{1,0:T(8,128)(2,1)S(1)}, bf16[216,128]{1,0:T(8,128)(2,1)S(1)}, u32[]{:S(2)}, u32[]{:S(2)}) collective-permute-start(bf16[216,128]{1,0:T(8,128)(2,1)S(1)} %get-tuple-element.35), channel_id=1, source_target_pairs={{4,0},{8,4},{12,8},{0,1},{1,5},{5,9},{9,13},{13,12},{6,2},{10,6},{... | collective-permute-start | bytes 165896 | tf_op jit(solution)/shard_map/ppermute | solution.py:599
  9.2 3.9 %collective-permute-start.4 = (bf16[216,128]{1,0:T(8,128)(2,1)S(1)}, bf16[216,128]{1,0:T(8,128)(2,1)S(1)}, u32[]{:S(2)}, u32[]{:S(2)}) collective-permute-start(bf16[216,128]{1,0:T(8,128)(2,1)S(1)} %get-tuple-element.36), channel_id=1, source_target_pairs={{0,4},{4,8},{8,12},{1,0},{5,1},{9,5},{13,9},{12,13},{2,6},{6,10},{... | collective-permute-start | bytes 165896 | tf_op jit(solution)/shard_map/ppermute | solution.py:600

commit v31 on v27

--- a/solution.py
+++ b/solution.py
@@ -470,7 +470,7 @@
             mask = (key_at >= 0) & (key_at < ends)
             pieces = [(keys[cut], values[cut]) for keys, values in parts]
             windows.append((start, pieces, near[cut], pick_ref[side, i], mask))
-    attend(heads, windows, query_ref, gate_ref, gated_ref)
+    attend(heads, windows, query_ref, gate_ref, gated_ref, paired=2)
     copies = []
     for side in range(2):
         cut = slice(starts[side][0], starts[side][0] + margin)

time: 15 us -> 15 us (level)
  no operation moved by 1% of the time
where the time goes in v31:
time: 15 us; the launch traced here: 14.8 us
  Pallas kernels  9.1 us (61%)
  starting transfers between devices  5.2 us (35%)
  waiting for transfers between devices  0.34 us (2%)
    pallas_call x1, Pallas kernels, shards(): pl.pallas_call(project_kernel, in_specs=[IN_SMEM] + [IN_VMEM] * len(opera...  3.02 us
    ppermute x1, starting transfers between devices, shards(): lax.ppermute(own, ('pair', 'samp'), [(0, 3), (1, 2), (2, 1), (3, 0)])  2.48 us
    pallas_call x1, Pallas kernels, shards(): pl.pallas_call(pair_kernel, in_specs=[IN_SMEM] + [IN_HBM] * 2, out_specs=...  2.27 us
    pallas_call x1, Pallas kernels, shards(): pl.pallas_call(functools.partial(inner_kernel, heads, blocks), in_specs=[...  1.99 us
    ppermute x1, starting transfers between devices, shards(): lax.ppermute(far, ('atoms', 'samp'), [(target, source) for source, target...  1.73 us
    pallas_call x1, Pallas kernels, shards(): pl.pallas_call(functools.partial(outer_kernel, heads, blocks), in_specs=[...  1.71 us
    ppermute x1, starting transfers between devices, shards(): across = lax.ppermute(own, 'pair', swapped)  0.64 us
    ppermute x1, starting transfers between devices, shards(): first = lax.ppermute(near, ('atoms', 'samp'), cycle)  0.31 us
  transfers between devices with their start and end apart: 5, of which 2 were waited for; matrix products, arithmetic and copies ran while one was open for 0% of the time, Pallas kernels for 34%

profile of v31, /device:TPU:0, one launch (start us, length us, event | category | flops | bytes accessed | tf_op | source)
XLA Modules:
  0.0 14.8 jit_solution(11598099856691890607)
XLA Ops:
  0.0 0.0 copy-start.1
  0.0 0.0 copy-start
  0.0 0.0 copy-start.8
  0.0 0.0 copy-start.7
  0.0 0.0 copy-start.6
  0.0 0.0 copy-start.5
  0.0 0.0 copy-start.4
  0.0 0.0 copy-start.3
  0.0 2.3 %shard_map.182.refs_0_ = bf16[2,64,128]{2,1,0:T(8,128)(2,1)S(1)} custom-call(s32[1]{0:T(128)} %bitcast.1.core_ref, bf16[4,128]{1,0:T(4,128)(2,1)} %bitcast.4, bf16[128,64,128]{2,1,0:T(8,128)(2,1)} %pair_hbm.1), custom_call_target="tpu_custom_call" | custom-call | flops 268435456 | bytes 4194304 | tf_op jit(solution)/shard_map/pallas_call | solution.py:532
  2.3 0.0 copy-start.2
  2.3 0.0 copy-start.9
  2.3 2.5 %collective-permute-start.2 = (bf16[2,64,128]{2,1,0:T(8,128)(2,1)S(1)}, bf16[2,64,128]{2,1,0:T(8,128)(2,1)S(1)}, u32[]{:S(2)}, u32[]{:S(2)}) collective-permute-start(bf16[2,64,128]{2,1,0:T(8,128)(2,1)S(1)} %shard_map.182.refs_0_), channel_id=1, source_target_pairs={{0,3},{1,2},{2,1},{3,0},{4,7},{5,6},{6,5},{7,4},{8,11},{9,10},{10,... | collective-permute-start | bytes 98312 | tf_op jit(solution)/shard_map/ppermute | solution.py:549
  4.8 0.6 %collective-permute-start.1 = (bf16[2,64,128]{2,1,0:T(8,128)(2,1)S(1)}, bf16[2,64,128]{2,1,0:T(8,128)(2,1)S(1)}, u32[]{:S(2)}, u32[]{:S(2)}) collective-permute-start(bf16[2,64,128]{2,1,0:T(8,128)(2,1)S(1)} %shard_map.182.refs_0_), channel_id=1, source_target_pairs={{0,2},{2,0},{1,3},{3,1},{4,6},{6,4},{5,7},{7,5},{8,10},{10,8},{9,1... | collective-permute-start | bytes 98312 | tf_op jit(solution)/shard_map/ppermute | solution.py:548
  5.5 0.0 collective-permute-start
  5.5 0.0 copy-done.1
  5.5 0.0 copy-done
  5.5 0.0 copy-done.8
  5.5 0.0 copy-done.7
  5.5 0.0 copy-done.6
  5.5 0.0 copy-done.5
  5.5 0.0 copy-done.4
  5.6 0.0 copy-done.3
  5.6 3.0 %shard_map.181 = (bf16[3,512,128]{2,1,0:T(8,128)(2,1)S(1)}, bf16[3,512,128]{2,1,0:T(8,128)(2,1)S(1)}, bf16[3,512,128]{2,1,0:T(8,128)(2,1)S(1)}, bf16[3,512,128]{...) custom-call(s32[1]{0:T(128)} %bitcast.1.core_ref, ...), custom_call_target="tpu_custom_call" | custom-call | flops 1006632960 | bytes 4194304 | tf_op jit(solution)/shard_map/pallas_call | solution.py:565
  8.6 0.0 collective-permute-done.2.refs_3_
  8.6 0.2 %collective-permute-done.1.refs_2_ = bf16[2,64,128]{2,1,0:T(8,128)(2,1)S(1)} collective-permute-done((bf16[2,64,128]{2,1,0:T(8,128)(2,1)S(1)}, bf16[2,64,128]{2,1,0:T(8,128)(2,1)S(1)}, u32[]{:S(2)}, u32[]{:S(2)}) %collective-permute-start.1) | collective-permute-done | bytes 32800 | tf_op jit(solution)/shard_map/ppermute | solution.py:548
  8.8 0.0 collective-permute-done.refs_1_
  8.8 0.1 shard_map.183
  8.9 0.3 %collective-permute-start.3 = (bf16[216,128]{1,0:T(8,128)(2,1)S(1)}, bf16[216,128]{1,0:T(8,128)(2,1)S(1)}, u32[]{:S(2)}, u32[]{:S(2)}) collective-permute-start(bf16[216,128]{1,0:T(8,128)(2,1)S(1)} %get-tuple-element.35), channel_id=1, source_target_pairs={{4,0},{8,4},{12,8},{0,1},{1,5},{5,9},{9,13},{13,12},{6,2},{10,6},{... | collective-permute-start | bytes 165896 | tf_op jit(solution)/shard_map/ppermute | solution.py:596
  9.2 1.7 %collective-permute-start.4 = (bf16[216,128]{1,0:T(8,128)(2,1)S(1)}, bf16[216,128]{1,0:T(8,128)(2,1)S(1)}, u32[]{:S(2)}, u32[]{:S(2)}) collective-permute-start(bf16[216,128]{1,0:T(8,128)(2,1)S(1)} %get-tuple-element.36), channel_id=1, source_target_pairs={{0,4},{4,8},{8,12},{1,0},{5,1},{9,5},{13,9},{12,13},{2,6},{6,10},{... | collective-permute-start | bytes 165896 | tf_op jit(solution)/shard_map/ppermute | solution.py:597
  11.0 0.0 copy-done.2
  11.0 0.0 copy-done.9
  11.0 2.0 %shard_map.184 = (bf16[3,384,128]{2,1,0:T(8,128)(2,1)S(1)}, bf16[2,2,128,256]{3,2,1,0:T(8,128)(2,1)S(1)}, bf16[2,48,48]{2,1,0:T(8,128)(2,1)S(1)}, bf16[2,112,256]{2,1,0:T(8,128)(2,1)S(1)}) custom-call(s32[1]{0:T(128)} %bitcast.at_ref, s32[4,64]{1,0:T(4,128)S(1)} %copy-done.9, bf16[3,512,128]{2,1,0:T(8,128)(2,1)S(1)} %get-tuple-element.21.query_ref, ...), custom_call_target="tpu_custom_call" | custom-call | flops 603979776 | bytes 4194304 | tf_op jit(solution)/shard_map/pallas_call | solution.py:603
  13.0 0.1 collective-permute-done.3.first_ref
  13.1 0.0 collective-permute-done.4.second_ref
  13.1 1.7 %shard_map.185 = bf16[3,512,128]{2,1,0:T(8,128)(2,1)} custom-call(s32[1]{0:T(128)} %bitcast.at_ref, s32[1]{0:T(128)} %bitcast.1.core_ref, bf16[3,512,128]{2,1,0:T(8,128)(2,1)S(1)} %get-tuple-element.21.query_ref, bf16[3,512,128]{2,1,0:T(8,128)(2,1)S(1)} %get-tuple-element.22.key_ref.own_key_ref, ...), custom_call_target="tpu_custom_call" | custom-call | flops 201326592 | bytes 4194304 | tf_op jit(solution)/shard_map/pallas_call | solution.py:622
Async XLA Ops:
  0.0 5.5 %copy-start.1 = (bf16[128,128]{1,0:T(8,128)(2,1)S(1)}, bf16[128,128]{1,0:T(8,128)(2,1)}, u32[]{:S(2)}) copy-start(bf16[128,128]{1,0:T(8,128)(2,1)} %w_value.3) | copy-start | bytes 98308
  0.0 5.5 %copy-start = (bf16[128,128]{1,0:T(8,128)(2,1)S(1)}, bf16[128,128]{1,0:T(8,128)(2,1)}, u32[]{:S(2)}) copy-start(bf16[128,128]{1,0:T(8,128)(2,1)} %w_key.3) | copy-start | bytes 98308
  0.0 5.5 %copy-start.8 = (bf16[128,128]{1,0:T(8,128)(2,1)S(1)}, bf16[128,128]{1,0:T(8,128)(2,1)}, u32[]{:S(2)}) copy-start(bf16[128,128]{1,0:T(8,128)(2,1)} %w_gate.1) | copy-start | bytes 98308
  0.0 5.5 %copy-start.7 = (bf16[128,128]{1,0:T(8,128)(2,1)S(1)}, bf16[128,128]{1,0:T(8,128)(2,1)}, u32[]{:S(2)}) copy-start(bf16[128,128]{1,0:T(8,128)(2,1)} %w_query.1) | copy-start | bytes 98308
  0.0 5.5 %copy-start.6 = (bf16[128,128]{1,0:T(8,128)(2,1)S(1)}, bf16[128,128]{1,0:T(8,128)(2,1)}, u32[]{:S(2)}) copy-start(bf16[128,128]{1,0:T(8,128)(2,1)} %ada_attn_shift.1) | copy-start | bytes 98308
  0.0 5.5 %copy-start.5 = (bf16[128,128]{1,0:T(8,128)(2,1)S(1)}, bf16[128,128]{1,0:T(8,128)(2,1)}, u32[]{:S(2)}) copy-start(bf16[128,128]{1,0:T(8,128)(2,1)} %ada_attn_scale.1) | copy-start | bytes 98308
  0.0 5.5 %copy-start.4 = (bf16[512,128]{1,0:T(8,128)(2,1)S(1)}, bf16[512,128]{1,0:T(8,128)(2,1)}, u32[]{:S(2)}) copy-start(bf16[512,128]{1,0:T(8,128)(2,1)} %cond_ref.1) | copy-start | bytes 393220
  0.0 5.5 %copy-start.3 = (bf16[3,512,128]{2,1,0:T(8,128)(2,1)S(1)}, bf16[3,512,128]{2,1,0:T(8,128)(2,1)}, u32[]{:S(2)}) copy-start(bf16[3,512,128]{2,1,0:T(8,128)(2,1)} %single_ref.1) | copy-start | bytes 1179652
  2.3 8.6 %copy-start.2 = (bf16[128,128]{1,0:T(8,128)(2,1)S(1)}, bf16[128,128]{1,0:T(8,128)(2,1)}, u32[]{:S(2)}) copy-start(bf16[128,128]{1,0:T(8,128)(2,1)} %w_out_ref.3) | copy-start | bytes 98308
  2.3 8.6 %copy-start.9 = (s32[4,64]{1,0:T(4,128)S(1)}, s32[4,64]{1,0:T(4,128)}, u32[]{:S(2)}) copy-start(s32[4,64]{1,0:T(4,128)} %counts_ref.1) | copy-start | bytes 3076
  2.3 6.3 %collective-permute-start.2 = (bf16[2,64,128]{2,1,0:T(8,128)(2,1)S(1)}, bf16[2,64,128]{2,1,0:T(8,128)(2,1)S(1)}, u32[]{:S(2)}, u32[]{:S(2)}) collective-permute-start(bf16[2,64,128]{2,1,0:T(8,128)(2,1)S(1)} %shard_map.182.refs_0_), channel_id=1, source_target_pairs={{0,3},{1,2},{2,1},{3,0},{4,7},{5,6},{6,5},{7,4},{8,11},{9,10},{10,... | collective-permute-start | bytes 98312 | tf_op jit(solution)/shard_map/ppermute | solution.py:549
  4.8 4.0 %collective-permute-start.1 = (bf16[2,64,128]{2,1,0:T(8,128)(2,1)S(1)}, bf16[2,64,128]{2,1,0:T(8,128)(2,1)S(1)}, u32[]{:S(2)}, u32[]{:S(2)}) collective-permute-start(bf16[2,64,128]{2,1,0:T(8,128)(2,1)S(1)} %shard_map.182.refs_0_), channel_id=1, source_target_pairs={{0,2},{2,0},{1,3},{3,1},{4,6},{6,4},{5,7},{7,5},{8,10},{10,8},{9,1... | collective-permute-start | bytes 98312 | tf_op jit(solution)/shard_map/ppermute | solution.py:548
  5.5 3.3 %collective-permute-start = (bf16[2,64,128]{2,1,0:T(8,128)(2,1)S(1)}, bf16[2,64,128]{2,1,0:T(8,128)(2,1)S(1)}, u32[]{:S(2)}, u32[]{:S(2)}) collective-permute-start(bf16[2,64,128]{2,1,0:T(8,128)(2,1)S(1)} %shard_map.182.refs_0_), channel_id=1, source_target_pairs={{0,1},{1,0},{2,3},{3,2},{4,5},{5,4},{6,7},{7,6},{8,9},{9,8},{10,11... | collective-permute-start | bytes 98312 | tf_op jit(solution)/shard_map/ppermute | solution.py:550
  8.9 4.2 %collective-permute-start.3 = (bf16[216,128]{1,0:T(8,128)(2,1)S(1)}, bf16[216,128]{1,0:T(8,128)(2,1)S(1)}, u32[]{:S(2)}, u32[]{:S(2)}) collective-permute-start(bf16[216,128]{1,0:T(8,128)(2,1)S(1)} %get-tuple-element.35), channel_id=1, source_target_pairs={{4,0},{8,4},{12,8},{0,1},{1,5},{5,9},{9,13},{13,12},{6,2},{10,6},{... | collective-permute-start | bytes 165896 | tf_op jit(solution)/shard_map/ppermute | solution.py:596
  9.2 3.9 %collective-permute-start.4 = (bf16[216,128]{1,0:T(8,128)(2,1)S(1)}, bf16[216,128]{1,0:T(8,128)(2,1)S(1)}, u32[]{:S(2)}, u32[]{:S(2)}) collective-permute-start(bf16[216,128]{1,0:T(8,128)(2,1)S(1)} %get-tuple-element.36), channel_id=1, source_target_pairs={{0,4},{4,8},{8,12},{1,0},{5,1},{9,5},{13,9},{12,13},{2,6},{6,10},{... | collective-permute-start | bytes 165896 | tf_op jit(solution)/shard_map/ppermute | solution.py:597
